TPU v7x, 32 devices: a whole 2x2x4 slice. The times are simulated.
32 devices in a mesh: wide: 8 (over z, y), narrow: 4 (over x, core).
Axes of the slice: x: 2, y: 2, z: 4, core: 2. Of those that a mesh axis runs over, the one named last changes fastest.
Arguments:
- tokens: bfloat16 [4096, 2048], P('wide', 'narrow'), may hold values from -6 to 6
- cotangent: bfloat16 [4096, 2048], P('wide', 'narrow'), may hold values from -6 to 6
- ln_gain: bfloat16 [2048], P(('narrow', 'wide')), may hold values from 0.5 to 1.5
- ln_shift: bfloat16 [2048], P(('narrow', 'wide')), may hold values from -1.75 to 1.75
- w_query: bfloat16 [2048, 2048], P('wide', 'narrow'), may hold values from -0.125 to 0.125
- b_query: bfloat16 [2048], P(('narrow', 'wide')), may hold values from -1.75 to 1.75
- w_key: bfloat16 [2048, 2048], P('wide', 'narrow'), may hold values from -0.125 to 0.125
- b_key: bfloat16 [2048], P(('narrow', 'wide')), may hold values from -1.75 to 1.75
- w_value: bfloat16 [2048, 2048], P('wide', 'narrow'), may hold values from -0.125 to 0.125
- b_value: bfloat16 [2048], P(('narrow', 'wide')), may hold values from -1.75 to 1.75
- w_dense: bfloat16 [2048, 2048], P('narrow', 'wide'), may hold values from -4 to 4
- b_dense: bfloat16 [2048], P(('narrow', 'wide')), may hold values from -1.75 to 1.75
- w_fc1: bfloat16 [2048, 8192], P('wide', 'narrow'), may hold values from -0.125 to 0.125
- b_fc1: bfloat16 [8192], P(('narrow', 'wide')), may hold values from -1.75 to 1.75
- w_fc2: bfloat16 [8192, 2048], P('narrow', 'wide'), may hold values from -0.0625 to 0.0625
- b_fc2: bfloat16 [2048], P(('narrow', 'wide')), may hold values from -1.75 to 1.75
Outputs:
- output: bfloat16 [4096, 2048], P('wide', 'narrow')
- input_grad: float32 [4096, 2048], P('wide', 'narrow')
- grad_ln_gain: float32 [2048], P(('narrow', 'wide'))
- grad_ln_shift: float32 [2048], P(('narrow', 'wide'))
- grad_w_query: float32 [2048, 2048], P('wide', 'narrow')
- grad_b_query: float32 [2048], P(('narrow', 'wide'))
- grad_w_key: float32 [2048, 2048], P('wide', 'narrow')
- grad_b_key: float32 [2048], P(('narrow', 'wide'))
- grad_w_value: float32 [2048, 2048], P('wide', 'narrow')
- grad_b_value: float32 [2048], P(('narrow', 'wide'))
- grad_w_dense: float32 [2048, 2048], P('narrow', 'wide')
- grad_b_dense: float32 [2048], P(('narrow', 'wide'))
- grad_w_fc1: float32 [2048, 8192], P('wide', 'narrow')
- grad_b_fc1: float32 [8192], P(('narrow', 'wide'))
- grad_w_fc2: float32 [8192, 2048], P('narrow', 'wide')
- grad_b_fc2: float32 [2048], P(('narrow', 'wide'))
All inputs are finite; a program needn't handle non-finite values.
Results may differ from a plain program's by a relative error of at most 0.015.
Values may be sent and summed in bfloat16 or wider, within the bound.
No kernel may reach another device: no remote copies, remote signals or barrier semaphores. Data moves between devices by JAX's collectives and lax.ppermute only.
A program may use at most 192 MiB of HBM per device.

v0:
```python
from functools import partial
import math

import jax
import jax.numpy as jnp
from jax import lax
from jax.sharding import PartitionSpec as P

D = 2048
HEAD_DIM = 64
ROT = 32
SEQ_SHARDS = 4


epsilon = 1e-05


def passed_along(value, axis, steps):
    count = lax.axis_size(axis)
    leading, last = (max(0, -steps), min(count, count - steps))
    return lax.ppermute(value, axis, [(source, source + steps) for source in range(leading, last)])


def matmul(left_side, right_side):
    return jnp.dot(left_side, right_side, preferred_element_type=jnp.float32)


def contract_rows(left_side, right_side):
    return lax.dot_general(
        left_side, right_side, (((0,), (0,)), ((), ())), preferred_element_type=jnp.float32
    )


def contract_cols(left_side, right_side):
    return lax.dot_general(
        left_side, right_side, (((1,), (1,)), ((), ())), preferred_element_type=jnp.float32
    )


def rotary_tables(places):
    halves = jnp.arange(ROT // 2).astype(jnp.float32)
    inverse = jnp.exp(halves * (-2.0 * math.log(10000.0) / ROT))
    phases = places[:, None] * inverse[None, :]
    phases = jnp.concatenate([phases, phases], axis=-1)
    return (jnp.cos(phases)[:, None, :], jnp.sin(phases)[:, None, :])


def rotate(values, cosine, sine_table):
    leading = values[..., :ROT]
    middle = ROT // 2
    turned = jnp.concatenate([-leading[..., middle:], leading[..., :middle]], axis=-1)
    return jnp.concatenate([leading * cosine + turned * sine_table, values[..., ROT:]], axis=-1)


def body(
    tokens,
    cotangent,
    ln_gain,
    ln_shift,
    w_query,
    b_query,
    w_key,
    b_key,
    w_value,
    b_value,
    w_dense,
    b_dense,
    w_fc1,
    b_fc1,
    w_fc2,
    b_fc2,
):
    row_count = tokens.shape[0]
    local_x = tokens.astype(jnp.float32)
    gathered = (
        lax.all_gather(ln_gain, "wide", axis=0, tiled=True),
        lax.all_gather(ln_shift, "wide", axis=0, tiled=True),
        lax.all_gather(w_query, "wide", axis=0, tiled=True),
        lax.all_gather(b_query, "wide", axis=0, tiled=True),
        lax.all_gather(w_key, "wide", axis=0, tiled=True),
        lax.all_gather(b_key, "wide", axis=0, tiled=True),
        lax.all_gather(w_value, "wide", axis=0, tiled=True),
        lax.all_gather(b_value, "wide", axis=0, tiled=True),
        lax.all_gather(w_dense, "wide", axis=1, tiled=True),
        lax.all_gather(b_dense, "wide", axis=0, tiled=True),
        lax.all_gather(w_fc1, "wide", axis=0, tiled=True),
        lax.all_gather(b_fc1, "wide", axis=0, tiled=True),
        lax.all_gather(w_fc2, "wide", axis=1, tiled=True),
        lax.all_gather(b_fc2, "wide", axis=0, tiled=True),
    )
    (
        gain_full,
        shift_full,
        query_weight,
        query_bias,
        key_weight,
        key_bias,
        value_weight,
        value_bias,
        dense_weight,
        dense_bias,
        up_weight,
        up_bias,
        down_weight,
        down_bias,
    ) = gathered
    row_sums = lax.psum((jnp.sum(local_x, axis=1), jnp.sum(local_x * local_x, axis=1)), "narrow")
    row_mean = row_sums[0] / D
    inverse_std = lax.rsqrt(row_sums[1] / D - row_mean * row_mean + epsilon)
    standard = (local_x - row_mean[:, None]) * inverse_std[:, None]
    normed_local = (
        standard * gain_full.astype(jnp.float32) + shift_full.astype(jnp.float32)
    ).astype(jnp.bfloat16)
    normed = lax.all_gather(normed_local, "narrow", axis=1, tiled=True)
    local_width = query_weight.shape[1]
    local_heads = local_width // HEAD_DIM
    head_shape = (row_count, local_heads, HEAD_DIM)
    place_index = lax.axis_index("wide") % SEQ_SHARDS
    local_places = jnp.arange(row_count, dtype=jnp.int32)
    query_places = place_index * row_count + local_places
    cosine, sine_table = rotary_tables(query_places.astype(jnp.float32))
    factor = 1.0 / math.sqrt(HEAD_DIM)
    queries = (
        rotate(
            (matmul(normed, query_weight) + query_bias.astype(jnp.float32)).reshape(head_shape),
            cosine,
            sine_table,
        )
        * factor
    )
    queries = queries.astype(jnp.bfloat16).reshape(row_count, local_width)
    keys_here = rotate(
        (matmul(normed, key_weight) + key_bias.astype(jnp.float32)).reshape(head_shape),
        cosine,
        sine_table,
    )
    keys_here = keys_here.astype(jnp.bfloat16).reshape(row_count, local_width)
    values_here = (matmul(normed, value_weight) + value_bias.astype(jnp.float32)).astype(
        jnp.bfloat16
    )
    key_blocks = [keys_here]
    value_blocks = [values_here]
    place_blocks = [query_places]
    for offset in range(1, SEQ_SHARDS):
        arrived_key, arrived_value = passed_along((keys_here, values_here), "wide", offset)
        key_blocks = [arrived_key] + key_blocks
        value_blocks = [arrived_value] + value_blocks
        place_blocks = [(place_index - offset) * row_count + local_places] + place_blocks
    all_keys = jnp.concatenate(key_blocks, axis=0)
    all_values = jnp.concatenate(value_blocks, axis=0)
    key_places = jnp.concatenate(place_blocks, axis=0)
    key_count = all_keys.shape[0]
    allowed = (key_places[None, :] >= 0) & (key_places[None, :] <= query_places[:, None])

    def by_head(flat_rows, total_rows):
        return flat_rows.reshape(total_rows, local_heads, HEAD_DIM).transpose(1, 0, 2)

    def attend(head_parts):
        query_head, key_head, value_head = head_parts
        scores = jnp.where(allowed, contract_cols(query_head, key_head), -1e30)
        row_max = jnp.max(scores, axis=1, keepdims=True)
        weights = jnp.exp(scores - row_max)
        weight_sum = jnp.sum(weights, axis=1, keepdims=True)
        probabilities = (weights / weight_sum).astype(jnp.bfloat16)
        return (matmul(probabilities, value_head), row_max[:, 0] + jnp.log(weight_sum[:, 0]))

    query_heads = by_head(queries, row_count)
    key_heads = by_head(all_keys, key_count)
    value_heads = by_head(all_values, key_count)
    head_out, log_sums = lax.map(attend, (query_heads, key_heads, value_heads))
    attended = head_out.transpose(1, 0, 2).reshape(row_count, local_width).astype(jnp.bfloat16)
    up_input = matmul(normed, up_weight) + up_bias.astype(jnp.float32)
    up_output, gelu_pull = jax.vjp(partial(jax.nn.gelu, approximate=True), up_input)
    up_short = up_output.astype(jnp.bfloat16)
    partial_sum = matmul(attended, dense_weight) + matmul(up_short, down_weight)
    branch_total = lax.psum_scatter(
        partial_sum.astype(jnp.bfloat16), "narrow", scatter_dimension=1, tiled=True
    ).astype(jnp.float32)
    output = (
        local_x + branch_total + dense_bias.astype(jnp.float32) + down_bias.astype(jnp.float32)
    ).astype(jnp.bfloat16)
    grad_out_local = jnp.sum(cotangent.astype(jnp.float32), axis=0)
    cotangent_full = lax.all_gather(cotangent, "narrow", axis=1, tiled=True)
    back_gain, back_query, back_key, back_value, back_dense, back_up, back_down = (
        gain_full,
        query_weight,
        key_weight,
        value_weight,
        dense_weight,
        up_weight,
        down_weight,
    )
    up_grad = gelu_pull(contract_cols(cotangent_full, back_down))[0].astype(jnp.bfloat16)
    grad_down = contract_rows(up_short, cotangent_full)
    grad_up = contract_rows(normed, up_grad)
    grad_up_bias = jnp.sum(up_grad.astype(jnp.float32), axis=0)
    attended_grad = contract_cols(cotangent_full, back_dense).astype(jnp.bfloat16)
    grad_dense = contract_rows(attended, cotangent_full)

    def attend_back(head_parts):
        query_head, key_head, value_head, out_grad, log_sum = head_parts
        scores = contract_cols(query_head, key_head)
        probabilities = jnp.where(allowed, jnp.exp(scores - log_sum[:, None]), 0.0)
        prob_grad = contract_cols(out_grad, value_head)
        row_dot = jnp.sum(probabilities * prob_grad, axis=1, keepdims=True)
        score_grad = (probabilities * (prob_grad - row_dot)).astype(jnp.bfloat16)
        return (
            matmul(score_grad, key_head),
            contract_rows(score_grad, query_head),
            contract_rows(probabilities.astype(jnp.bfloat16), out_grad),
        )

    query_grads, key_grads, value_grads = lax.map(
        attend_back,
        (query_heads, key_heads, value_heads, by_head(attended_grad, row_count), log_sums),
    )
    key_flat_grads = key_grads.transpose(1, 0, 2).reshape(key_count, local_width)
    value_flat_grads = value_grads.transpose(1, 0, 2).reshape(key_count, local_width)
    own_start = (SEQ_SHARDS - 1) * row_count
    key_sum = key_flat_grads[own_start:]
    value_sum = value_flat_grads[own_start:]
    for offset in range(1, SEQ_SHARDS):
        begin = (SEQ_SHARDS - 1 - offset) * row_count
        arrived_key, arrived_value = passed_along(
            (
                key_flat_grads[begin : begin + row_count],
                value_flat_grads[begin : begin + row_count],
            ),
            "wide",
            -offset,
        )
        key_sum = key_sum + arrived_key
        value_sum = value_sum + arrived_value
    query_pre = (
        rotate(query_grads.transpose(1, 0, 2) * factor, cosine, -sine_table)
        .reshape(row_count, local_width)
        .astype(jnp.bfloat16)
    )
    key_pre = (
        rotate(key_sum.reshape(head_shape), cosine, -sine_table)
        .reshape(row_count, local_width)
        .astype(jnp.bfloat16)
    )
    value_pre = value_sum.astype(jnp.bfloat16)
    grad_query = contract_rows(normed, query_pre)
    grad_key = contract_rows(normed, key_pre)
    grad_value = contract_rows(normed, value_pre)
    query_bias_grad = jnp.sum(query_pre.astype(jnp.float32), axis=0)
    key_bias_grad = jnp.sum(key_pre.astype(jnp.float32), axis=0)
    value_bias_grad = jnp.sum(value_pre.astype(jnp.float32), axis=0)
    normed_grad = (
        contract_cols(up_grad, back_up)
        + contract_cols(query_pre, back_query)
        + contract_cols(key_pre, back_key)
        + contract_cols(value_pre, back_value)
    )
    standard_grad = lax.psum_scatter(
        normed_grad.astype(jnp.bfloat16), "narrow", scatter_dimension=1, tiled=True
    ).astype(jnp.float32)
    grad_gain_part = jnp.sum(standard_grad * standard, axis=0)
    grad_shift_part = jnp.sum(standard_grad, axis=0)
    scaled_grad = standard_grad * back_gain.astype(jnp.float32)
    back_sums = lax.psum(
        (jnp.sum(scaled_grad, axis=1), jnp.sum(scaled_grad * standard, axis=1)), "narrow"
    )
    input_grad = (
        scaled_grad - back_sums[0][:, None] / D - standard * (back_sums[1][:, None] / D)
    ) * inverse_std[:, None] + cotangent.astype(jnp.float32)
    reduced = (
        lax.psum_scatter(
            grad_gain_part.astype(jnp.bfloat16), "wide", scatter_dimension=0, tiled=True
        ).astype(jnp.float32),
        lax.psum_scatter(
            grad_shift_part.astype(jnp.bfloat16), "wide", scatter_dimension=0, tiled=True
        ).astype(jnp.float32),
        lax.psum_scatter(
            grad_query.astype(jnp.bfloat16), "wide", scatter_dimension=0, tiled=True
        ).astype(jnp.float32),
        lax.psum_scatter(
            query_bias_grad.astype(jnp.bfloat16), "wide", scatter_dimension=0, tiled=True
        ).astype(jnp.float32),
        lax.psum_scatter(
            grad_key.astype(jnp.bfloat16), "wide", scatter_dimension=0, tiled=True
        ).astype(jnp.float32),
        lax.psum_scatter(
            key_bias_grad.astype(jnp.bfloat16), "wide", scatter_dimension=0, tiled=True
        ).astype(jnp.float32),
        lax.psum_scatter(
            grad_value.astype(jnp.bfloat16), "wide", scatter_dimension=0, tiled=True
        ).astype(jnp.float32),
        lax.psum_scatter(
            value_bias_grad.astype(jnp.bfloat16), "wide", scatter_dimension=0, tiled=True
        ).astype(jnp.float32),
        lax.psum_scatter(
            grad_dense.astype(jnp.bfloat16), "wide", scatter_dimension=1, tiled=True
        ).astype(jnp.float32),
        lax.psum_scatter(
            grad_out_local.astype(jnp.bfloat16), "wide", scatter_dimension=0, tiled=True
        ).astype(jnp.float32),
        lax.psum_scatter(
            grad_up.astype(jnp.bfloat16), "wide", scatter_dimension=0, tiled=True
        ).astype(jnp.float32),
        lax.psum_scatter(
            grad_up_bias.astype(jnp.bfloat16), "wide", scatter_dimension=0, tiled=True
        ).astype(jnp.float32),
        lax.psum_scatter(
            grad_down.astype(jnp.bfloat16), "wide", scatter_dimension=1, tiled=True
        ).astype(jnp.float32),
    )
    return (
        output,
        input_grad,
        reduced[0],
        reduced[1],
        reduced[2],
        reduced[3],
        reduced[4],
        reduced[5],
        reduced[6],
        reduced[7],
        reduced[8],
        reduced[9],
        reduced[10],
        reduced[11],
        reduced[12],
        reduced[9],
    )


def solution(mesh):
    in_specs = (
        P("wide", "narrow"),
        P("wide", "narrow"),
        P(("narrow", "wide")),
        P(("narrow", "wide")),
        P("wide", "narrow"),
        P(("narrow", "wide")),
        P("wide", "narrow"),
        P(("narrow", "wide")),
        P("wide", "narrow"),
        P(("narrow", "wide")),
        P("narrow", "wide"),
        P(("narrow", "wide")),
        P("wide", "narrow"),
        P(("narrow", "wide")),
        P("narrow", "wide"),
        P(("narrow", "wide")),
    )
    out_specs = (
        P("wide", "narrow"),
        P("wide", "narrow"),
        P(("narrow", "wide")),
        P(("narrow", "wide")),
        P("wide", "narrow"),
        P(("narrow", "wide")),
        P("wide", "narrow"),
        P(("narrow", "wide")),
        P("wide", "narrow"),
        P(("narrow", "wide")),
        P("narrow", "wide"),
        P(("narrow", "wide")),
        P("wide", "narrow"),
        P(("narrow", "wide")),
        P("narrow", "wide"),
        P(("narrow", "wide")),
    )
    return jax.shard_map(body, mesh=mesh, in_specs=in_specs, out_specs=out_specs, check_vma=False)
```

profile of v0, /device:TPU:0, one launch (start us, length us, event | category | flops | bytes accessed | tf_op | source)
XLA Modules:
  0.0 1367.5 jit_solution(17611837205912794349)
XLA Ops:
  13.5 23.3 %all-reduce.17 = (bf16[512]{0:T(512)(128)(2,1)S(1)}, bf16[512]{0:T(512)(128)(2,1)S(1)}, bf16[512]{0:T(512)(128)(2,1)S(1)}, bf16[512]{0:T(512)(128)(2,1)S(1)}, bf16[512]{0:T(512)(128)(2,1)S(1)}) all-reduce(bf16[512]{0:T(512)(128)(2,1)S(1)} %dynamic-update-slice.1, ...), channel_id=1, replica_groups=mesh['wide'=8,'narrow'=4] {'wide'}, use_global_device_ids=true, to_apply=%add.1 | all-reduce | flops 2560 | bytes 10240
  38.2 5.7 all-reduce.15
  52.5 14.2 %all-gather.10.cloned.1.call-done = bf16[512,2048]{1,0:T(8,128)(2,1)} async-done(((bf16[512,512]{1,0:T(8,128)(2,1)}), bf16[512,2048]{1,0:T(8,128)(2,1)}) %all-gather.10.cloned.1.call-update) | async-done | bytes 2097168 | tf_op jit(solution)/shard_map/all_gather | solution.py:114
  66.8 51.5 %all-gather.14.cloned.1.call-done = bf16[2048,512]{1,0:T(8,128)(2,1)} async-done(((bf16[256,512]{1,0:T(8,128)(2,1)}), bf16[2048,512]{1,0:T(8,128)(2,1)}) %all-gather.14.cloned.1.call-update) | async-done | bytes 2097168 | tf_op jit(solution)/shard_map/all_gather | solution.py:80
  118.2 3.5 convolution_add_fusion.1
  122.0 3.4 collective-permute-start
  128.3 4.2 collective-permute-start.2
  132.4 53.1 %all-gather.16.cloned.1.call-done = bf16[2048,512]{1,0:T(8,128)(2,1)} async-done(((bf16[256,512]{1,0:T(8,128)(2,1)}), bf16[2048,512]{1,0:T(8,128)(2,1)}) %all-gather.16.cloned.1.call-update) | async-done | bytes 2097168 | tf_op jit(solution)/shard_map/all_gather | solution.py:82
  185.6 4.3 fusion.50
  189.8 5.2 collective-permute-start.3
  195.1 3.6 collective-permute-start.4
  198.7 47.9 %all-gather.12.cloned.1.call-done = bf16[2048,512]{1,0:T(8,128)(2,1)} async-done(((bf16[256,512]{1,0:T(8,128)(2,1)}), bf16[2048,512]{1,0:T(8,128)(2,1)}) %all-gather.12.cloned.1.call-update) | async-done | bytes 2097168 | tf_op jit(solution)/shard_map/all_gather | solution.py:78
  246.5 3.5 convolution_add_fusion.2
  250.9 3.8 collective-permute-start.5
  254.7 21.7 %all-gather.24.cloned.1.call-done = bf16[512,2048]{1,0:T(8,128)(2,1)} async-done(((bf16[512,512]{1,0:T(8,128)(2,1)}), bf16[512,2048]{1,0:T(8,128)(2,1)}) %all-gather.24.cloned.1.call-update) | async-done | bytes 2097168 | tf_op jit(solution)/shard_map/all_gather | solution.py:183
  276.4 53.0 %all-gather.18.cloned.1.call-done = bf16[512,2048]{1,0:T(8,128)(2,1)} async-done(((bf16[512,256]{1,0:T(8,128)(2,1)}), bf16[512,2048]{1,0:T(8,128)(2,1)}) %all-gather.18.cloned.1.call-update) | async-done | bytes 2097168 | tf_op jit(solution)/shard_map/all_gather | solution.py:84
  329.4 3.5 convolution_convert_fusion.6
  349.1 72.1 %while.30 = (s32[]{:T(128)}, bf16[8,512,64]{1,2,0:T(8,128)(2,1)}, f32[8,512]{1,0:T(8,128)S(1)}, bf16[8,512,64]{2,1,0:T(8,128)(2,1)S(1)}, bf16[8,2048,64]{2,1,0:T...) while((s32[]{:T(128)}, bf16[8,512,64]{1,2,0:T(8,128)(2,1)}, ...), condition=%wide.region_7.8_spmd.clone.clone, body=%wide.region_4.7_spmd.clone.sunk.clone | while | flops 277872128 | bytes 30705788 | solution.py:170
  354.1 3.9 fusion.166
  363.0 4.0 fusion.166
  372.0 3.9 fusion.166
  380.9 4.6 fusion.166
  390.5 4.0 fusion.166
  399.4 3.9 fusion.166
  408.3 3.9 fusion.166
  417.2 4.0 fusion.166
  421.2 4.4 convolution_convert_fusion.2
  425.7 83.6 %while.31 = (s32[]{:T(128)}, f32[8,512,64]{1,2,0:T(8,128)S(1)}, f32[8,2048,64]{1,2,0:T(8,128)}, f32[8,2048,64]{1,2,0:T(8,128)}, bf16[8,512,64]{2,1,0:T(8,128)(2,...) while((s32[]{:T(128)}, f32[8,512,64]{1,2,0:T(8,128)S(1)}, ...), condition=%wide.region_11.12_spmd.clone.clone, body=%wide.region_9.11_spmd.clone.sunk.clone | while | flops 681573888 | bytes 34761848 | solution.py:213
  516.7 51.7 %collective-permute-done.10 = f32[512,512]{0,1:T(8,128)S(1)} collective-permute-done((f32[512,512]{0,1:T(8,128)S(1)}, f32[512,512]{0,1:T(8,128)S(1)}, u32[]{:S(2)}, u32[]{:S(2)}) %collective-permute-start.10) | collective-permute-done | bytes 1048608 | tf_op jit(solution)/shard_map/ppermute | solution.py:21
  568.4 45.2 %collective-permute-done.11 = f32[512,512]{0,1:T(8,128)S(1)} collective-permute-done((f32[512,512]{0,1:T(8,128)S(1)}, f32[512,512]{0,1:T(8,128)S(1)}, u32[]{:S(2)}, u32[]{:S(2)}) %collective-permute-start.11) | collective-permute-done | bytes 1048608 | tf_op jit(solution)/shard_map/ppermute | solution.py:21
  623.6 59.7 %collective-permute-done.6 = f32[512,512]{0,1:T(8,128)S(1)} collective-permute-done((f32[512,512]{0,1:T(8,128)S(1)}, f32[512,512]{0,1:T(8,128)S(1)}, u32[]{:S(2)}, u32[]{:S(2)}) %collective-permute-start.6) | collective-permute-done | bytes 1048608 | tf_op jit(solution)/shard_map/ppermute | solution.py:21
  683.2 31.2 %collective-permute-done.7 = f32[512,512]{0,1:T(8,128)S(1)} collective-permute-done((f32[512,512]{0,1:T(8,128)S(1)}, f32[512,512]{0,1:T(8,128)S(1)}, u32[]{:S(2)}, u32[]{:S(2)}) %collective-permute-start.7) | collective-permute-done | bytes 1048608 | tf_op jit(solution)/shard_map/ppermute | solution.py:21
  714.4 35.2 %collective-permute-done.8 = f32[512,512]{0,1:T(8,128)S(1)} collective-permute-done((f32[512,512]{0,1:T(8,128)S(1)}, f32[512,512]{0,1:T(8,128)S(1)}, u32[]{:S(2)}, u32[]{:S(2)}) %collective-permute-start.8) | collective-permute-done | bytes 1048608 | tf_op jit(solution)/shard_map/ppermute | solution.py:21
  754.4 78.8 %all-gather = bf16[8,1,256]{2,1,0:T(2,128)(2,1)S(1)} all-gather(bf16[1,1,256]{2,1,0:T(2,128)(2,1)S(1)} %reshape.234), channel_id=1, replica_groups=mesh['wide'=8,'narrow'=4] {'wide'}, dimensions={0}, use_global_device_ids=true | all-gather | bytes 4608 | tf_op jit(solution)/shard_map/all_gather | solution.py:87
  833.3 4.2 convolution_convert_fusion.4
  837.7 5.1 fusion.93
  846.1 10.5 fusion.91
  856.6 12.1 fusion.81
  868.8 8.1 fusion.92
  879.8 9.3 fusion.80
  891.9 10.1 convolution_convert_fusion.1
  903.6 11.0 convolution_convert_fusion
  923.2 61.0 %reduce-scatter.15.cloned.1.call-done = bf16[256,512]{1,0:T(8,128)(2,1)} async-done(((bf16[2048,512]{1,0:T(8,128)(2,1)}), bf16[256,512]{1,0:T(8,128)(2,1)}) %reduce-scatter.15.cloned.1.call-update) | async-done | bytes 262160 | tf_op jit(solution)/shard_map/reduce_scatter | solution.py:282
  986.0 31.8 %reduce-scatter.11.cloned.1.call-done = bf16[512,512]{1,0:T(8,128)(2,1)} async-done(((bf16[512,2048]{1,0:T(8,128)(2,1)}), bf16[512,512]{1,0:T(8,128)(2,1)}) %reduce-scatter.11.cloned.1.call-update) | async-done | bytes 524304 | tf_op jit(solution)/shard_map/reduce_scatter | solution.py:257
  1020.6 37.1 %all-reduce.16 = (bf16[512]{0:T(512)(128)(2,1)S(1)}, bf16[512]{0:T(512)(128)(2,1)S(1)}, bf16[512]{0:T(512)(128)(2,1)S(1)}, bf16[512]{0:T(512)(128)(2,1)S(1)}, bf...) all-reduce(bf16[512]{0:T(512)(128)(2,1)S(1)} %dynamic-update-slice., ...), channel_id=1, replica_groups=mesh['wide'=8,'narrow'=4] {'wide'}, use_global_device_ids=true, to_apply=%add.6 | all-reduce | flops 6144 | bytes 24576
  1057.8 5.9 all-reduce.14
  1070.1 134.8 %reduce-scatter.21.cloned.1.call-done = bf16[256,2048]{1,0:T(8,128)(2,1)} async-done(((bf16[2048,2048]{1,0:T(8,128)(2,1)}), bf16[256,2048]{1,0:T(8,128)(2,1)}) %reduce-scatter.21.cloned.1.call-update) | async-done | bytes 1048592 | tf_op jit(solution)/shard_map/reduce_scatter | solution.py:300
  1207.7 149.6 %reduce-scatter.23.cloned.1.call-done = bf16[2048,256]{1,0:T(8,128)(2,1)} async-done(((bf16[2048,2048]{1,0:T(8,128)(2,1)}), bf16[2048,256]{1,0:T(8,128)(2,1)}) %reduce-scatter.23.cloned.1.call-update) | async-done | bytes 1048592 | tf_op jit(solution)/shard_map/reduce_scatter | solution.py:306
  (299 shorter events, 215.7 us)
Async XLA Ops:
  7.2 59.6 %all-gather.10.cloned.1.call-start = ((), (), s32[]{:S(2)}) async-start(), calls=%async_computation.8 | async-start | bytes 2621440 | tf_op jit(solution)/shard_map/all_gather | solution.py:114
  36.8 15.4 %copy-start.13 = (f32[512]{0:T(512)}, f32[512]{0:T(512)S(1)}, u32[]{:S(2)}) copy-start(f32[512]{0:T(512)S(1)} %convert_element_type.193) | copy-start | bytes 6148
  46.5 71.7 %all-gather.14.cloned.1.call-start = ((), (), s32[]{:S(2)}) async-start(), calls=%async_computation.10 | async-start | bytes 2359296 | tf_op jit(solution)/shard_map/all_gather | solution.py:80
  47.3 138.3 %all-gather.16.cloned.1.call-start = ((), (), s32[]{:S(2)}) async-start(), calls=%async_computation.11 | async-start | bytes 2359296 | tf_op jit(solution)/shard_map/all_gather | solution.py:82
  48.0 198.5 %all-gather.12.cloned.1.call-start = ((), (), s32[]{:S(2)}) async-start(), calls=%async_computation.9 | async-start | bytes 2359296 | tf_op jit(solution)/shard_map/all_gather | solution.py:78
  48.6 227.8 %all-gather.24.cloned.1.call-start = ((), (), s32[]{:S(2)}) async-start(), calls=%async_computation.16 | async-start | bytes 2621440 | tf_op jit(solution)/shard_map/all_gather | solution.py:183
  49.2 280.2 %all-gather.18.cloned.1.call-start = ((), (), s32[]{:S(2)}) async-start(), calls=%async_computation.12 | async-start | bytes 2359296 | tf_op jit(solution)/shard_map/all_gather | solution.py:84
  49.7 796.4 %all-gather.20.cloned.1.call-start = ((), (), s32[]{:S(2)}) async-start(), calls=%async_computation.13 | async-start | bytes 9437184 | tf_op jit(solution)/shard_map/all_gather | solution.py:86
  50.5 806.1 %all-gather.22.cloned.1.call-start = ((), (), s32[]{:S(2)}) async-start(), calls=%async_computation.14 | async-start | bytes 9437184 | tf_op jit(solution)/shard_map/all_gather | solution.py:88
  51.2 866.6 %reduce-scatter.19.cloned.1.call-start = ((), (), s32[]{:S(2)}) async-start(), calls=%async_computation.21 | async-start | bytes 2359296 | tf_op jit(solution)/shard_map/reduce_scatter | solution.py:294
  122.0 128.0 %copy-start.9 = (bf16[512,8,64]{0,2,1:T(8,128)(2,1)}, bf16[512,8,64]{0,2,1:T(8,128)(2,1)S(1)}, u32[]{:S(2)}) copy-start(bf16[512,8,64]{0,2,1:T(8,128)(2,1)S(1)} %maximum_convert_fusion) | copy-start | bytes 1572868
  122.0 128.9 %collective-permute-start = (bf16[512,512]{0,1:T(8,128)(2,1)S(1)}, bf16[512,512]{0,1:T(8,128)(2,1)S(1)}, u32[]{:S(2)}, u32[]{:S(2)}) collective-permute-start(bf16[512,512]{0,1:T(8,128)(2,1)S(1)} %bitcast.206), channel_id=1, source_target_pairs={{0,12},{4,16},{8,20},{12,24},{16,28},{1,13},{5,17},{9,21},{13,25},... | collective-permute-start | bytes 1572872 | tf_op jit(solution)/shard_map/ppermute | solution.py:21
  125.4 208.8 %collective-permute-start.1 = (bf16[512,512]{0,1:T(8,128)(2,1)S(1)}, bf16[512,512]{0,1:T(8,128)(2,1)S(1)}, u32[]{:S(2)}, u32[]{:S(2)}) collective-permute-start(bf16[512,512]{0,1:T(8,128)(2,1)S(1)} %bitcast.207), channel_id=1, source_target_pairs={{0,8},{4,12},{8,16},{12,20},{16,24},{20,28},{1,9},{5,13},{9,17},{1... | collective-permute-start | bytes 1572872 | tf_op jit(solution)/shard_map/ppermute | solution.py:21
  128.3 206.0 %collective-permute-start.2 = (bf16[512,512]{0,1:T(8,128)(2,1)S(1)}, bf16[512,512]{0,1:T(8,128)(2,1)}, u32[]{:S(2)}, u32[]{:S(2)}) collective-permute-start(bf16[512,512]{0,1:T(8,128)(2,1)S(1)} %bitcast.208), channel_id=1, source_target_pairs={{0,4},{4,8},{8,12},{12,16},{16,20},{20,24},{24,28},{1,5},{5,9},{9,... | collective-permute-start | bytes 1572872 | tf_op jit(solution)/shard_map/ppermute | solution.py:21
  189.8 150.1 %collective-permute-start.3 = (bf16[512,512]{1,0:T(8,128)(2,1)}, bf16[512,512]{1,0:T(8,128)(2,1)}, u32[]{:S(2)}, u32[]{:S(2)}) collective-permute-start(bf16[512,512]{1,0:T(8,128)(2,1)} %fusion.50), channel_id=1, source_target_pairs={{0,12},{4,16},{8,20},{12,24},{16,28},{1,13},{5,17},{9,21},{13,25},... | collective-permute-start | bytes 1572872 | tf_op jit(solution)/shard_map/ppermute | solution.py:21
  195.1 144.9 %collective-permute-start.4 = (bf16[512,512]{1,0:T(8,128)(2,1)}, bf16[512,512]{1,0:T(8,128)(2,1)}, u32[]{:S(2)}, u32[]{:S(2)}) collective-permute-start(bf16[512,512]{1,0:T(8,128)(2,1)} %fusion.50), channel_id=1, source_target_pairs={{0,8},{4,12},{8,16},{12,20},{16,24},{20,28},{1,9},{5,13},{9,17},{1... | collective-permute-start | bytes 1572872 | tf_op jit(solution)/shard_map/ppermute | solution.py:21
  250.9 83.3 %copy-start.11 = (bf16[512,512]{0,1:T(8,128)(2,1)}, bf16[512,512]{0,1:T(8,128)(2,1)S(1)}, u32[]{:S(2)}) copy-start(bf16[512,512]{0,1:T(8,128)(2,1)S(1)} %collective-permute-done) | copy-start | bytes 1572868
  250.9 89.0 %collective-permute-start.5 = (bf16[512,512]{1,0:T(8,128)(2,1)}, bf16[512,512]{1,0:T(8,128)(2,1)}, u32[]{:S(2)}, u32[]{:S(2)}) collective-permute-start(bf16[512,512]{1,0:T(8,128)(2,1)} %fusion.50), channel_id=1, source_target_pairs={{0,4},{4,8},{8,12},{12,16},{16,20},{20,24},{24,28},{1,5},{5,9},{9,... | collective-permute-start | bytes 1572872 | tf_op jit(solution)/shard_map/ppermute | solution.py:21
  421.2 4.5 copy-start.10
  425.6 493.9 %reduce-scatter.17.cloned.1.call-start = ((), (), s32[]{:S(2)}) async-start(), calls=%async_computation.20 | async-start | bytes 2359296 | tf_op jit(solution)/shard_map/reduce_scatter | solution.py:288
  512.3 101.7 %copy-start.19 = (bf16[512,2048]{1,0:T(8,128)(2,1)S(1)}, bf16[512,2048]{1,0:T(8,128)(2,1)}, u32[]{:S(2)}) copy-start(bf16[512,2048]{1,0:T(8,128)(2,1)} %all-gather.10.cloned.1.call-done) | copy-start | bytes 6291460
  512.3 56.1 %collective-permute-start.10 = (f32[512,512]{0,1:T(8,128)S(1)}, f32[512,512]{0,1:T(8,128)S(1)}, u32[]{:S(2)}, u32[]{:S(2)}) collective-permute-start(f32[512,512]{0,1:T(8,128)S(1)} %bitcast.216), channel_id=1, source_target_pairs={{8,0},{12,4},{16,8},{20,12},{24,16},{28,20},{9,1},{13,5},{17,9},{2... | collective-permute-start | bytes 3145736 | tf_op jit(solution)/shard_map/ppermute | solution.py:21
  513.7 99.9 %collective-permute-start.11 = (f32[512,512]{0,1:T(8,128)S(1)}, f32[512,512]{0,1:T(8,128)S(1)}, u32[]{:S(2)}, u32[]{:S(2)}) collective-permute-start(f32[512,512]{0,1:T(8,128)S(1)} %bitcast.215), channel_id=1, source_target_pairs={{12,0},{16,4},{20,8},{24,12},{28,16},{13,1},{17,5},{21,9},{25,13},... | collective-permute-start | bytes 3145736 | tf_op jit(solution)/shard_map/ppermute | solution.py:21
  515.0 98.6 %collective-permute-start.9 = (f32[512,512]{0,1:T(8,128)S(1)}, f32[512,512]{0,1:T(8,128)S(1)}, u32[]{:S(2)}, u32[]{:S(2)}) collective-permute-start(f32[512,512]{0,1:T(8,128)S(1)} %bitcast.213), channel_id=1, source_target_pairs={{4,0},{8,4},{12,8},{16,12},{20,16},{24,20},{28,24},{5,1},{9,5},{13... | collective-permute-start | bytes 3145736 | tf_op jit(solution)/shard_map/ppermute | solution.py:21
  616.7 304.7 %reduce-scatter.13.cloned.1.call-start = ((), (), s32[]{:S(2)}) async-start(), calls=%async_computation.18 | async-start | bytes 2359296 | tf_op jit(solution)/shard_map/reduce_scatter | solution.py:276
  619.5 63.7 %collective-permute-start.6 = (f32[512,512]{0,1:T(8,128)S(1)}, f32[512,512]{0,1:T(8,128)S(1)}, u32[]{:S(2)}, u32[]{:S(2)}) collective-permute-start(f32[512,512]{0,1:T(8,128)S(1)} %bitcast.214), channel_id=1, source_target_pairs={{4,0},{8,4},{12,8},{16,12},{20,16},{24,20},{28,24},{5,1},{9,5},{13... | collective-permute-start | bytes 3145736 | tf_op jit(solution)/shard_map/ppermute | solution.py:21
  620.8 93.6 %collective-permute-start.7 = (f32[512,512]{0,1:T(8,128)S(1)}, f32[512,512]{0,1:T(8,128)S(1)}, u32[]{:S(2)}, u32[]{:S(2)}) collective-permute-start(f32[512,512]{0,1:T(8,128)S(1)} %bitcast.212), channel_id=1, source_target_pairs={{8,0},{12,4},{16,8},{20,12},{24,16},{28,20},{9,1},{13,5},{17,9},{2... | collective-permute-start | bytes 3145736 | tf_op jit(solution)/shard_map/ppermute | solution.py:21
  622.1 127.5 %collective-permute-start.8 = (f32[512,512]{0,1:T(8,128)S(1)}, f32[512,512]{0,1:T(8,128)S(1)}, u32[]{:S(2)}, u32[]{:S(2)}) collective-permute-start(f32[512,512]{0,1:T(8,128)S(1)} %bitcast.211), channel_id=1, source_target_pairs={{12,0},{16,4},{20,8},{24,12},{28,16},{13,1},{17,5},{21,9},{25,13},... | collective-permute-start | bytes 3145736 | tf_op jit(solution)/shard_map/ppermute | solution.py:21
  751.7 2.7 copy-start.22
  754.3 229.9 %reduce-scatter.15.cloned.1.call-start = ((), (), s32[]{:S(2)}) async-start(), calls=%async_computation.19 | async-start | bytes 2359296 | tf_op jit(solution)/shard_map/reduce_scatter | solution.py:282
  837.5 180.3 %reduce-scatter.11.cloned.1.call-start = ((), (), s32[]{:S(2)}) async-start(), calls=%async_computation.17 | async-start | bytes 2621440 | tf_op jit(solution)/shard_map/reduce_scatter | solution.py:257
  837.7 5.1 copy-start.8
  868.8 8.1 copy-start.26
  868.8 8.1 copy-start.1
  868.8 8.1 copy-start.2
  868.8 8.1 copy-start.6
  879.8 9.4 copy-start.5
  879.8 9.3 copy-start.7
  879.8 187.5 %reduce-scatter.9.cloned.1.call-start = ((), (), s32[]{:S(2)}) async-start(), calls=%async_computation.15 | async-start | bytes 2621440 | tf_op jit(solution)/shard_map/reduce_scatter | solution.py:176
  891.8 313.0 %reduce-scatter.21.cloned.1.call-start = ((), (), s32[]{:S(2)}) async-start(), calls=%async_computation.22 | async-start | bytes 9437184 | tf_op jit(solution)/shard_map/reduce_scatter | solution.py:300
  902.0 455.3 %reduce-scatter.23.cloned.1.call-start = ((), (), s32[]{:S(2)}) async-start(), calls=%async_computation.23 | async-start | bytes 9437184 | tf_op jit(solution)/shard_map/reduce_scatter | solution.py:306
  914.6 2.5 copy-start.23
  914.6 2.8 copy-start.24
  915.6 103.3 %copy-start.3 = (bf16[512,512]{1,0:T(8,128)(2,1)S(1)}, bf16[512,512]{1,0:T(8,128)(2,1)}, u32[]{:S(2)}) copy-start(bf16[512,512]{1,0:T(8,128)(2,1)} %param.20) | copy-start | bytes 1572868
  915.6 103.3 %copy-start.14 = (f32[512]{0:T(512)S(1)}, f32[512]{0:T(512)}, u32[]{:S(2)}) copy-start(f32[512]{0:T(512)} %copy-done.13) | copy-start | bytes 6148
  915.7 103.3 %copy-start.16 = (f32[512]{0:T(512)S(1)}, f32[512]{0:T(512)}, u32[]{:S(2)}) copy-start(f32[512]{0:T(512)} %copy-done.15) | copy-start | bytes 6148
  915.7 103.3 %copy-start.18 = (f32[512]{0:T(512)S(1)}, f32[512]{0:T(512)}, u32[]{:S(2)}) copy-start(f32[512]{0:T(512)} %copy-done.17) | copy-start | bytes 6148
  1057.8 302.1 %copy-start.25 = (f32[64]{0:T(128)}, f32[64]{0:T(128)S(1)}, u32[]{:S(2)}) copy-start(f32[64]{0:T(128)S(1)} %dynamic-slice_convert_fusion.1) | copy-start | bytes 772
  (14 other events, 22.6 us)
Sparse Core Ops, SparseCore 0:
  46.6 20.0 all-gather.9
  68.9 49.2 all-gather.13
  120.3 65.1 all-gather.15
  187.5 58.9 all-gather.11
  247.9 28.4 all-gather.23
  278.3 51.0 all-gather.17
  331.5 123.1 all-gather.19
  456.7 183.8 all-gather.21
  644.1 109.6 reduce-scatter.18
  757.2 86.8 reduce-scatter.16
  847.7 66.4 reduce-scatter.12
  917.5 66.6 reduce-scatter.14
  987.3 30.4 reduce-scatter.10
  1020.9 31.4 reduce-scatter.8
  1055.8 149.0 reduce-scatter.20
  1208.8 148.4 reduce-scatter.22
where the time goes:
time: 1380 us; the launch traced here: 1370 us
  waiting for transfers between devices  846 us (61%)
  matrix products  233 us (17%)
  blocking collectives  151 us (11%)
  local copies, waits for them, and re-layouts  45.5 us (3%)
  other arithmetic  42.7 us (3%)
  starting transfers between devices  32.1 us (2%)
  between operations  17.1 us (1%)
    ppermute x12, waiting for transfers between devices, passed_along(): lax.ppermute(value, axis, [(source, source + steps) for source in range(l...  223 us
    reduce_scatter x1, waiting for transfers between devices, body(): lax.psum_scatter(grad_down.astype(jnp.bfloat16), 'wide', scatter_dimensio...  150 us
    reduce_scatter x1, waiting for transfers between devices, body(): lax.psum_scatter(grad_up.astype(jnp.bfloat16), 'wide', scatter_dimension=...  135 us
    dot_general x30, matrix products, contract_cols(): lax.dot_general(left_side, right_side, (((1,), (1,)), ((), ())), preferre...  88.8 us
    dot_general x22, matrix products, matmul(): return jnp.dot(left_side, right_side, preferred_element_type=jnp.float32)  80.5 us
    all_gather x1, blocking collectives, body(): lax.all_gather(b_fc1, 'wide', axis=0, tiled=True)  78.8 us
    dot_general x22, matrix products, contract_rows(): lax.dot_general(left_side, right_side, (((0,), (0,)), ((), ())), preferre...  63.6 us
    reduce_scatter x1, waiting for transfers between devices, body(): lax.psum_scatter(grad_key.astype(jnp.bfloat16), 'wide', scatter_dimension...  61 us
  transfers between devices with their start and end apart: 28, of which 15 were waited for; matrix products, arithmetic and copies ran while one was open for 21% of the time, Pallas kernels for 0%

commit v1 on v0

v1 whole, which is shorter than its diff:
```python
from functools import partial
import math

import jax
import jax.numpy as jnp
import numpy as np
from jax import lax
from jax.experimental import pallas as pl
from jax.experimental.pallas import tpu as pltpu
from jax.sharding import Mesh, PartitionSpec as P

D = 2048
HEAD_DIM = 64
ROT = 32
SEQ_LEN = 2048
EPSILON = 1e-05
BLOCK = 256

WIDE = ("s", "g", "h")
LINE = ("s", "g")
CUBE = ("g", "h", "m", "c")


def matmul(left_side, right_side):
    return jnp.dot(left_side, right_side, preferred_element_type=jnp.float32)


def contract_rows(left_side, right_side):
    return lax.dot_general(
        left_side, right_side, (((0,), (0,)), ((), ())), preferred_element_type=jnp.float32
    )


def contract_cols(left_side, right_side):
    return lax.dot_general(
        left_side, right_side, (((1,), (1,)), ((), ())), preferred_element_type=jnp.float32
    )


def pick(blocks, index, axis=0):
    return lax.dynamic_index_in_dim(blocks, index, axis, keepdims=False)


def shifted(value, axis, step):
    count = lax.axis_size(axis)
    return lax.ppermute(value, axis, [(source, (source + step) % count) for source in range(count)])


def rotary_tables(rows):
    lane = np.arange(2 * HEAD_DIM) % HEAD_DIM
    pair = (lane % (ROT // 2)).astype(np.float32)
    inverse = np.exp(pair * np.float32(-2.0 * math.log(10000.0) / ROT)).astype(np.float32)
    phase = np.arange(rows, dtype=np.float32)[:, None] * inverse[None, :]
    turned = (lane < ROT)[None, :]
    sign = np.where(lane < ROT // 2, -1.0, 1.0)[None, :]
    cosine = np.where(turned, np.cos(phase), 1.0).astype(np.float32)
    sine = np.where(turned, np.sin(phase) * sign, 0.0).astype(np.float32)
    return (cosine, sine)


def norm_kernel(rows, tokens_ref, gain_ref, shift_ref, normed_ref, stats_ref):
    parts = [tokens_ref[0, j].astype(jnp.float32) for j in range(tokens_ref.shape[1])]
    total = sum(jnp.sum(part, axis=1, keepdims=True) for part in parts)
    squares = sum(jnp.sum(part * part, axis=1, keepdims=True) for part in parts)
    mean = total / D
    inverse_std = lax.rsqrt(squares / D - mean * mean + EPSILON)
    width = parts[0].shape[1]
    for j, part in enumerate(parts):
        cols = slice(j * width, (j + 1) * width)
        standard = (part - mean) * inverse_std
        normed_ref[:, cols] = (standard * gain_ref[:, cols] + shift_ref[:, cols]).astype(
            jnp.bfloat16
        )
    stats_ref[...] = jnp.concatenate(
        [jnp.broadcast_to(mean, (rows, 64)), jnp.broadcast_to(inverse_std, (rows, 64))], axis=1
    )


def layer_norm(blocks, gain, shift, row_count):
    row_blocks, col_blocks, _, width = blocks.shape
    rows = 256
    per = row_count // rows
    total_rows = row_blocks * row_count
    return pl.pallas_call(
        partial(norm_kernel, rows),
        grid=(row_blocks * per,),
        in_specs=[
            pl.BlockSpec((1, col_blocks, rows, width), lambda i: (i // per, 0, i % per, 0)),
            pl.BlockSpec((1, D), lambda i: (0, 0)),
            pl.BlockSpec((1, D), lambda i: (0, 0)),
        ],
        out_specs=[
            pl.BlockSpec((rows, D), lambda i: (i, 0)),
            pl.BlockSpec((rows, 128), lambda i: (i, 0)),
        ],
        out_shape=[
            jax.ShapeDtypeStruct((total_rows, D), jnp.bfloat16),
            jax.ShapeDtypeStruct((total_rows, 128), jnp.float32),
        ],
        compiler_params=pltpu.CompilerParams(vmem_limit_bytes=48 * 2**20),
        name="layer_norm",
    )(blocks, gain, shift)


def turn(values, cosine, sine):
    lane = lax.broadcasted_iota(jnp.int32, values.shape, 1) % HEAD_DIM
    width = values.shape[1]
    half = ROT // 2
    partner = jnp.where(
        lane < half, pltpu.roll(values, width - half, 1), pltpu.roll(values, half, 1)
    )
    return values * cosine + partner * sine


def attention_kernel(
    blocks,
    pre_ref,
    grad_ref,
    cosine_ref,
    sine_ref,
    attended_ref,
    pre_grad_ref,
    q_ref,
    k_ref,
    v_ref,
    score_ref,
    slope_ref,
    k_total,
    v_total,
):
    i = pl.program_id(0)
    width = 2 * HEAD_DIM
    factor = 1.0 / math.sqrt(HEAD_DIM)

    @pl.when(i == 0)
    def _():
        def prepare(b, carry):
            rows = pl.ds(pl.multiple_of(b * BLOCK, BLOCK), BLOCK)
            cosine, sine = cosine_ref[rows, :], sine_ref[rows, :]
            pre = pre_ref[rows, :]
            q_ref[rows, :] = (turn(pre[:, :width], cosine, sine) * factor).astype(jnp.bfloat16)
            k_ref[rows, :] = turn(pre[:, width : 2 * width], cosine, sine).astype(jnp.bfloat16)
            v_ref[rows, :] = pre[:, 2 * width :].astype(jnp.bfloat16)
            return carry

        lax.fori_loop(0, blocks, prepare, 0)
        k_total[...] = jnp.zeros_like(k_total)
        v_total[...] = jnp.zeros_like(v_total)

    own = pl.ds(pl.multiple_of(i * BLOCK, BLOCK), BLOCK)
    causal = lax.broadcasted_iota(jnp.int32, (BLOCK, BLOCK), 0) >= lax.broadcasted_iota(
        jnp.int32, (BLOCK, BLOCK), 1
    )
    attended_parts, q_grad_parts = [], []
    for head in range(2):
        cols = slice(head * HEAD_DIM, (head + 1) * HEAD_DIM)
        queries = q_ref[own, cols]
        out_grad = grad_ref[own, cols]

        def lanes(block):
            return [block[:, n : n + 128] for n in range(0, BLOCK, 128)]

        def score(j, best, diagonal):
            rows = pl.ds(pl.multiple_of(j * BLOCK, BLOCK), BLOCK)
            block = contract_cols(queries, k_ref[rows, cols])
            if diagonal:
                block = jnp.where(causal, block, -1e30)
            score_ref[j] = block
            for part in lanes(block):
                best = jnp.maximum(best, part)
            return best

        best = lax.fori_loop(
            0, i, lambda j, b: score(j, b, False), jnp.full((BLOCK, 128), -1e30, jnp.float32)
        )
        row_max = jnp.max(score(i, best, True), axis=1, keepdims=True)

        def weigh(j, carry):
            total, dots = carry
            rows = pl.ds(pl.multiple_of(j * BLOCK, BLOCK), BLOCK)
            weights = jnp.exp(score_ref[j] - row_max)
            slope = contract_cols(out_grad, v_ref[rows, cols])
            score_ref[j] = weights
            slope_ref[j] = slope
            for part in lanes(weights):
                total = total + part
            for part in lanes(weights * slope):
                dots = dots + part
            return total, dots

        zero = jnp.zeros((BLOCK, 128), jnp.float32)
        total, dots = lax.fori_loop(0, i + 1, weigh, (zero, zero))
        scale = 1.0 / jnp.sum(total, axis=1, keepdims=True)
        row_dot = jnp.sum(dots, axis=1, keepdims=True) * scale

        def push(j, carry):
            out, q_grad = carry
            rows = pl.ds(pl.multiple_of(j * BLOCK, BLOCK), BLOCK)
            probs = score_ref[j] * scale
            low = probs.astype(jnp.bfloat16)
            score_grad = (probs * (slope_ref[j] - row_dot)).astype(jnp.bfloat16)
            out = out + matmul(low, v_ref[rows, cols])
            q_grad = q_grad + matmul(score_grad, k_ref[rows, cols])
            k_total[rows, cols] += contract_rows(score_grad, queries)
            v_total[rows, cols] += contract_rows(low, out_grad)
            return out, q_grad

        narrow_zero = jnp.zeros((BLOCK, HEAD_DIM), jnp.float32)
        out, q_grad = lax.fori_loop(0, i + 1, push, (narrow_zero, narrow_zero))
        attended_parts.append(out)
        q_grad_parts.append(q_grad)
    attended_ref[own, :] = jnp.concatenate(attended_parts, axis=1).astype(jnp.bfloat16)
    q_grad = jnp.concatenate(q_grad_parts, axis=1) * factor
    pre_grad_ref[own, :width] = turn(q_grad, cosine_ref[own, :], -sine_ref[own, :]).astype(
        jnp.bfloat16
    )

    @pl.when(i == blocks - 1)
    def _():
        def finish(b, carry):
            rows = pl.ds(pl.multiple_of(b * BLOCK, BLOCK), BLOCK)
            pre_grad_ref[rows, width : 2 * width] = turn(
                k_total[rows, :], cosine_ref[rows, :], -sine_ref[rows, :]
            ).astype(jnp.bfloat16)
            pre_grad_ref[rows, 2 * width :] = v_total[rows, :].astype(jnp.bfloat16)
            return carry

        lax.fori_loop(0, blocks, finish, 0)


def attention(pre, out_grad):
    rows, width = pre.shape[0], 2 * HEAD_DIM
    blocks = rows // BLOCK
    cosine, sine = rotary_tables(rows)
    whole = lambda shape: pl.BlockSpec(shape, lambda i: (0, 0))
    pairs = rows * (rows + BLOCK)
    return pl.pallas_call(
        partial(attention_kernel, blocks),
        grid=(blocks,),
        in_specs=[
            whole((rows, 3 * width)),
            whole((rows, width)),
            whole((rows, width)),
            whole((rows, width)),
        ],
        out_specs=[whole((rows, width)), whole((rows, 3 * width))],
        out_shape=[
            jax.ShapeDtypeStruct((rows, width), jnp.bfloat16),
            jax.ShapeDtypeStruct((rows, 3 * width), jnp.bfloat16),
        ],
        scratch_shapes=[
            pltpu.VMEM((rows, width), jnp.bfloat16),
            pltpu.VMEM((rows, width), jnp.bfloat16),
            pltpu.VMEM((rows, width), jnp.bfloat16),
            pltpu.VMEM((blocks, BLOCK, BLOCK), jnp.float32),
            pltpu.VMEM((blocks, BLOCK, BLOCK), jnp.float32),
            pltpu.VMEM((rows, width), jnp.float32),
            pltpu.VMEM((rows, width), jnp.float32),
        ],
        compiler_params=pltpu.CompilerParams(vmem_limit_bytes=48 * 2**20),
        cost_estimate=pl.CostEstimate(
            flops=6 * pairs * 256 * 2, bytes_accessed=rows * width * 16, transcendentals=pairs
        ),
        name="attention",
    )(pre, out_grad, jnp.asarray(cosine), jnp.asarray(sine))


def gather_columns(shard):
    rows = shard.shape[0]
    own_g, own_h = lax.axis_index("g"), lax.axis_index("h")
    split = shard.reshape(rows, 2, 2, -1)
    mine = pick(split, own_h, 2)
    other = shifted(pick(split, 1 - own_h, 2), "h", 1)
    pair = jnp.stack(
        [jnp.where(own_h == 0, mine, other), jnp.where(own_h == 0, other, mine)], axis=0
    )
    same, cross = pick(pair, own_g, 2), pick(pair, 1 - own_g, 2)
    same = same.reshape(2 * rows, -1)
    cross = cross.reshape(2 * rows, -1)
    count = lax.axis_size(LINE)
    place = lax.axis_index(LINE)
    full = jnp.zeros((count, 2 * rows, same.shape[1]), shard.dtype)
    full = lax.dynamic_update_index_in_dim(full, same, place, 0)
    for step in range(1, count):
        arrived = shifted(cross if step % 2 else same, LINE, step)
        full = lax.dynamic_update_index_in_dim(full, arrived, (place - step) % count, 0)
    return full.reshape(count * 2 * rows, -1)


def scatter_columns(grad):
    count = lax.axis_size(LINE)
    place = lax.axis_index(LINE)
    own_g, own_h = lax.axis_index("g"), lax.axis_index("h")
    cols = grad.shape[1]
    blocks = grad.reshape(count, 2, -1, cols)
    rows = blocks.shape[2]
    same = pick(blocks, place).astype(jnp.float32)
    cross = None
    for step in range(1, count):
        arrived = shifted(pick(blocks, (place + step) % count), LINE, step).astype(jnp.float32)
        if step % 2:
            cross = arrived if cross is None else cross + arrived
        else:
            same = same + arrived
    both = jnp.stack(
        [jnp.where(own_g == 0, same, cross), jnp.where(own_g == 0, cross, same)], axis=0
    )
    mine = pick(both, own_h, 1)
    other = shifted(pick(both, 1 - own_h, 1).astype(jnp.bfloat16), "h", 1).astype(jnp.float32)
    lower, upper = jnp.where(own_h == 0, mine, other), jnp.where(own_h == 0, other, mine)
    return jnp.concatenate([lower[0], upper[0], lower[1], upper[1]], axis=1)


def body(
    tokens,
    cotangent,
    ln_gain,
    ln_shift,
    w_query,
    b_query,
    w_key,
    b_key,
    w_value,
    b_value,
    w_dense,
    b_dense,
    w_fc1,
    b_fc1,
    w_fc2,
    b_fc2,
):
    row_count, feature_count = tokens.shape
    sequences = lax.axis_size("s")
    own_s, own_g, own_h = lax.axis_index("s"), lax.axis_index("g"), lax.axis_index("h")
    own_n = lax.axis_index(("m", "c"))
    wide = lax.axis_size(WIDE)
    weight_rows = w_fc1.shape[0]
    heads_width = w_query.shape[1] // 4
    hidden = w_fc1.shape[1] // 4

    vectors = (ln_gain, ln_shift, b_query, b_key, b_value, b_dense, b_fc2, b_fc1)
    lengths = [vector.shape[0] for vector in vectors]
    packed = jnp.concatenate(vectors)
    lanes = -(-packed.shape[0] // feature_count) * feature_count
    packed = jnp.pad(packed, (0, lanes - packed.shape[0]))
    by_sequence = jnp.zeros((sequences, lanes), packed.dtype)
    by_sequence = lax.dynamic_update_index_in_dim(by_sequence, packed, own_s, 0)
    for step in range(1, sequences):
        by_sequence = lax.dynamic_update_index_in_dim(
            by_sequence, shifted(packed, "s", step), (own_s - step) % sequences, 0
        )
    extra = by_sequence.reshape(-1, feature_count)
    extra_rows = -(-extra.shape[0] // 16) * 16
    extra = jnp.pad(extra, ((0, extra_rows - extra.shape[0]), (0, 0)))
    token_blocks = lax.all_gather(
        jnp.concatenate([tokens, extra], axis=0), CUBE, axis=0, tiled=False
    )
    cotangent_blocks = lax.all_gather(cotangent, CUBE, axis=0, tiled=False)

    up_weight = gather_columns(w_fc1)
    attention_shard = jnp.concatenate(
        [
            part.reshape(weight_rows, 4, heads_width)
            for part in (w_query, w_key, w_value, w_dense.T)
        ],
        axis=2,
    )
    attention_weight = gather_columns(attention_shard.reshape(weight_rows, -1))
    down_weight = gather_columns(w_fc2.T)
    qkv_weight = attention_weight[:, : 3 * heads_width]
    back_weight = jnp.concatenate([attention_weight[:, 3 * heads_width :], down_weight], axis=1)

    table = token_blocks[:, row_count : row_count + sequences * lanes // feature_count, :]
    table = table.reshape(2, 2, 4, sequences, lanes).transpose(2, 3, 0, 1, 4)
    table = table.reshape(4, wide, lanes).astype(jnp.float32)
    pieces, start = [], 0
    for length in lengths:
        pieces.append(table[:, :, start : start + length])
        start += length
    gain = pieces[0].reshape(1, -1)
    shift = pieces[1].reshape(1, -1)
    here = pick(jnp.concatenate(pieces[2:], axis=2), own_n)
    start = 0
    local = []
    for length in lengths[2:]:
        local.append(here[:, start : start + length].reshape(-1))
        start += length
    quarter = 2 * own_g + own_h
    qkv_bias = jnp.concatenate([pick(part.reshape(4, -1), quarter) for part in local[:3]])
    out_bias = local[3] + local[4]
    up_bias = pick(local[5].reshape(4, -1), quarter)

    normed, stats = layer_norm(
        token_blocks.reshape(4, 4, row_count + extra_rows, feature_count), gain, shift, row_count
    )
    cotangent_full = (
        cotangent_blocks.reshape(4, 4, row_count, feature_count)
        .transpose(0, 2, 1, 3)
        .reshape(4 * row_count, 4 * feature_count)
    )

    up_input = matmul(normed, up_weight) + up_bias
    up_output, gelu_pull = jax.vjp(partial(jax.nn.gelu, approximate=True), up_input)
    up_short = up_output.astype(jnp.bfloat16)

    qkv_pre = matmul(normed, qkv_weight) + qkv_bias
    back = matmul(cotangent_full, back_weight)
    attended_grad = back[:, :heads_width].astype(jnp.bfloat16)
    up_grad = gelu_pull(back[:, heads_width:])[0].astype(jnp.bfloat16)
    attended, qkv_grad = attention(qkv_pre, attended_grad)

    grad_down = contract_rows(cotangent_full, up_short).astype(jnp.bfloat16)
    grad_dense = contract_rows(cotangent_full, attended).astype(jnp.bfloat16)
    grad_up = contract_rows(normed, up_grad).astype(jnp.bfloat16)
    grad_qkv = contract_rows(normed, qkv_grad).astype(jnp.bfloat16)

    branch = contract_cols(jnp.concatenate([attended, up_short], axis=1), back_weight)
    normed_grad = contract_cols(
        jnp.concatenate([qkv_grad, up_grad], axis=1),
        jnp.concatenate([qkv_weight, up_weight], axis=1),
    )

    def summed_blocks(partial_sum):
        blocks = partial_sum.astype(jnp.bfloat16).reshape(4, row_count, 4, feature_count)
        blocks = blocks.transpose(0, 2, 1, 3).reshape(16, row_count, feature_count)
        return lax.psum_scatter(blocks, CUBE, scatter_dimension=0, tiled=False).astype(
            jnp.float32
        )

    local_x = tokens.astype(jnp.float32)
    output = (local_x + summed_blocks(branch) + out_bias).astype(jnp.bfloat16)

    grad_down_sum = scatter_columns(grad_down).T
    grad_up_sum = scatter_columns(grad_up)
    grad_attention = scatter_columns(jnp.concatenate([grad_qkv, grad_dense], axis=1))
    grad_attention = grad_attention.reshape(weight_rows, 4, 4, heads_width)
    grad_query, grad_key, grad_value, grad_dense_sum = (
        grad_attention[:, :, n].reshape(weight_rows, -1) for n in range(4)
    )

    standard_grad = summed_blocks(normed_grad)
    own_stats = pick(stats.reshape(4, row_count, 128), quarter)
    row_mean, inverse_std = own_stats[:, :1], own_stats[:, 64:65]
    standard = (local_x - row_mean) * inverse_std
    own_gain = pick(pieces[0].reshape(4, -1), own_n)
    scaled_grad = standard_grad * own_gain
    back_sums = lax.psum(
        (jnp.sum(scaled_grad, axis=1), jnp.sum(scaled_grad * standard, axis=1)), ("m", "c")
    )
    input_grad = (
        scaled_grad - back_sums[0][:, None] / D - standard * (back_sums[1][:, None] / D)
    ) * inverse_std + cotangent.astype(jnp.float32)

    def spread(vector):
        placed = jnp.zeros((4, vector.shape[0]), jnp.float32)
        placed = lax.dynamic_update_index_in_dim(placed, vector, quarter, 0)
        return placed.reshape(wide, -1)

    def column_sums(values):
        return jnp.sum(values.astype(jnp.float32), axis=0)

    qkv_sums = column_sums(qkv_grad)
    terms = [
        jnp.sum(standard_grad * standard, axis=0).reshape(wide, -1),
        jnp.sum(standard_grad, axis=0).reshape(wide, -1),
        spread(qkv_sums[:heads_width]),
        spread(qkv_sums[heads_width : 2 * heads_width]),
        spread(qkv_sums[2 * heads_width :]),
        column_sums(cotangent).reshape(wide, -1),
        spread(column_sums(up_grad)),
    ]
    vector_sums = lax.psum_scatter(
        jnp.concatenate(terms, axis=1), WIDE, scatter_dimension=0, tiled=False
    )
    vector_grads, start = [], 0
    for term in terms:
        vector_grads.append(vector_sums[start : start + term.shape[1]])
        start += term.shape[1]
    return (
        output,
        input_grad,
        vector_grads[0],
        vector_grads[1],
        grad_query,
        vector_grads[2],
        grad_key,
        vector_grads[3],
        grad_value,
        vector_grads[4],
        grad_dense_sum.T,
        vector_grads[5],
        grad_up_sum,
        vector_grads[6],
        grad_down_sum,
        vector_grads[5],
    )


def solution(mesh):
    wide = mesh.shape["wide"]
    inner = Mesh(mesh.devices.reshape(wide // 4, 2, 2, 2, 2), ("s", "g", "h", "m", "c"))
    narrow = ("m", "c")
    acts = P(WIDE, narrow)
    vector = P(narrow + WIDE)
    by_rows = P(WIDE, narrow)
    by_cols = P(narrow, WIDE)
    in_specs = (
        (acts, acts, vector, vector)
        + (by_rows, vector) * 3
        + (by_cols, vector, by_rows, vector, by_cols, vector)
    )
    out_specs = (
        (acts, acts, vector, vector)
        + (by_rows, vector) * 3
        + (by_cols, vector, by_rows, vector, by_cols, vector)
    )
    return jax.shard_map(body, mesh=inner, in_specs=in_specs, out_specs=out_specs, check_vma=False)
```

time: 1380 us -> 704 us (0.51)
  waiting for transfers between devices: 846 us -> 159 us
  matrix products: 233 us -> 83.2 us
  local copies, waits for them, and re-layouts: 45.5 us -> 139 us
  Pallas kernels: 0 us -> 85.6 us
  starting transfers between devices: 32.1 us -> 99 us
  blocking collectives: 151 us -> 90.4 us
  other arithmetic: 42.7 us -> 25.8 us
    reduce_scatter x8 -> x2, waiting for transfers between devices: 377 us -> 0.01 us  [summed_blocks(): lax.psum_scatter(blocks, CUBE, scatter_dimension=0, tiled=False)]
    all_gather x8 -> x2, waiting for transfers between devices: 241 us -> 0.02 us  [the longest x1 0.02 us: body(): lax.all_gather(jnp.concatenate([tokens, extra], axis=0), CUBE, axis=0, ti...]
    pallas_call x0 -> x2, Pallas kernels: none -> 85.6 us  [the longest x1 73.3 us: attention(): pl.pallas_call(partial(attention_kernel, blocks), grid=(blocks,), in_spec...]
    all_gather x1 -> x0, blocking collectives: 78.8 us -> none  [body(): lax.all_gather(b_fc1, 'wide', axis=0, tiled=True)]
    ppermute x12 -> x25, starting transfers between devices: 31.3 us -> 98.8 us  [shifted(): lax.ppermute(value, axis, [(source, (source + step) % count) for source i...]
    dot_general x30 -> x2, matrix products: 88.8 us -> 23.5 us  [contract_cols(): lax.dot_general(left_side, right_side, (((1,), (1,)), ((), ())), preferre...]
    ppermute x12 -> x25, waiting for transfers between devices: 223 us -> 158 us  [shifted(): lax.ppermute(value, axis, [(source, (source + step) % count) for source i...]
    dot_general x22 -> x3, matrix products: 80.5 us -> 29.2 us  [matmul(): return jnp.dot(left_side, right_side, preferred_element_type=jnp.float32)]
  transfers between devices with their start and end apart: 28 -> 29, of which waited for: 15 -> 15; matrix products, arithmetic and copies ran while one was open for 21% -> 26% of each run, Pallas kernels for 0% -> 0%
where the time goes in v1:
time: 704 us; the launch traced here: 697 us
  waiting for transfers between devices  159 us (23%)
  local copies, waits for them, and re-layouts  139 us (20%)
  starting transfers between devices  99 us (14%)
  blocking collectives  90.4 us (13%)
  Pallas kernels  85.6 us (12%)
  matrix products  83.2 us (12%)
  other arithmetic  25.8 us (4%)
  between operations  15.1 us (2%)
    ppermute x25, waiting for transfers between devices, shifted(): lax.ppermute(value, axis, [(source, (source + step) % count) for source i...  158 us
    ppermute x25, starting transfers between devices, shifted(): lax.ppermute(value, axis, [(source, (source + step) % count) for source i...  98.8 us
    pallas_call x1, Pallas kernels, attention(): pl.pallas_call(partial(attention_kernel, blocks), grid=(blocks,), in_spec...  73.3 us
    psum x1, blocking collectives, body(): lax.psum((jnp.sum(scaled_grad, axis=1), jnp.sum(scaled_grad * standard, a...  55.2 us
    unnamed x1, blocking collectives  35.2 us
    dot_general x4, matrix products, contract_rows(): lax.dot_general(left_side, right_side, (((0,), (0,)), ((), ())), preferre...  30.4 us
    reshape x2, local copies, waits for them, and re-layouts, summed_blocks(): partial_sum.astype(jnp.bfloat16).reshape(4, row_count, 4, feature_count)  29.3 us
    dot_general x3, matrix products, matmul(): return jnp.dot(left_side, right_side, preferred_element_type=jnp.float32)  29.2 us
  transfers between devices with their start and end apart: 29, of which 15 were waited for; matrix products, arithmetic and copies ran while one was open for 26% of the time, Pallas kernels for 0%

profile of v1, /device:TPU:0, one launch (start us, length us, event | category | flops | bytes accessed | tf_op | source)
XLA Modules:
  0.0 697.4 jit_solution(16646512033693009012)
XLA Ops:
  8.0 5.4 concatenate.59
  13.4 4.1 collective-permute-start
  31.4 6.9 collective-permute-done.1
  39.5 4.0 collective-permute-start.4
  43.5 6.0 collective-permute-done.9
  50.6 8.0 %collective-permute-done.5 = bf16[256,2,512]{2,0,1:T(8,128)(2,1)} collective-permute-done((bf16[256,2,512]{2,0,1:T(8,128)(2,1)}, bf16[256,2,512]{2,0,1:T(8,128)(2,1)}, u32[]{:S(2)}, u32[]{:S(2)}) %collective-permute-start.5) | collective-permute-done | bytes 524320 | tf_op jit(solution)/shard_map/ppermute | solution.py:46
  60.0 3.7 collective-permute-start.8
  67.5 17.1 %collective-permute-done.2 = bf16[512,512]{1,0:T(8,128)(2,1)S(1)} collective-permute-done((bf16[512,512]{1,0:T(8,128)(2,1)S(1)}, bf16[512,512]{1,0:T(8,128)(2,1)S(1)}, u32[]{:S(2)}, u32[]{:S(2)}) %collective-permute-start.2) | collective-permute-done | bytes 524320 | tf_op jit(solution)/shard_map/ppermute | solution.py:46
  84.6 20.7 %collective-permute-start.7 = (bf16[512,512]{1,0:T(8,128)(2,1)S(1)}, bf16[512,512]{1,0:T(8,128)(2,1)S(1)}, u32[]{:S(2)}, u32[]{:S(2)}) collective-permute-start(bf16[512,512]{1,0:T(8,128)(2,1)S(1)} %bitcast.297), channel_id=1, source_target_pairs={{0,16},{8,24},{16,0},{24,8},{1,17},{9,25},{17,1},{25,9},{2,18},{10... | collective-permute-start | bytes 1572872 | tf_op jit(solution)/shard_map/ppermute | solution.py:46
  107.2 17.4 %collective-permute-start.12 = (bf16[512,512]{1,0:T(8,128)(2,1)S(1)}, bf16[512,512]{1,0:T(8,128)(2,1)S(1)}, u32[]{:S(2)}, u32[]{:S(2)}) collective-permute-start(bf16[512,512]{1,0:T(8,128)(2,1)S(1)} %bitcast.309), channel_id=1, source_target_pairs={{0,24},{8,0},{16,8},{24,16},{1,25},{9,1},{17,9},{25,17},{2,26},{10... | collective-permute-start | bytes 1572872 | tf_op jit(solution)/shard_map/ppermute | solution.py:46
  124.6 5.2 collective-permute-done.3
  130.1 12.0 %collective-permute-done.7 = bf16[512,512]{1,0:T(8,128)(2,1)S(1)} collective-permute-done((bf16[512,512]{1,0:T(8,128)(2,1)S(1)}, bf16[512,512]{1,0:T(8,128)(2,1)S(1)}, u32[]{:S(2)}, u32[]{:S(2)}) %collective-permute-start.7) | collective-permute-done | bytes 524320 | tf_op jit(solution)/shard_map/ppermute | solution.py:46
  143.9 28.2 %collective-permute-done.10 = bf16[512,512]{1,0:T(8,128)(2,1)S(1)} collective-permute-done((bf16[512,512]{1,0:T(8,128)(2,1)S(1)}, bf16[512,512]{1,0:T(8,128)(2,1)S(1)}, u32[]{:S(2)}, u32[]{:S(2)}) %collective-permute-start.10) | collective-permute-done | bytes 524320 | tf_op jit(solution)/shard_map/ppermute | solution.py:46
  172.9 18.7 %collective-permute-done.11 = bf16[512,512]{1,0:T(8,128)(2,1)S(1)} collective-permute-done((bf16[512,512]{1,0:T(8,128)(2,1)S(1)}, bf16[512,512]{1,0:T(8,128)(2,1)S(1)}, u32[]{:S(2)}, u32[]{:S(2)}) %collective-permute-start.11) | collective-permute-done | bytes 524320 | tf_op jit(solution)/shard_map/ppermute | solution.py:46
  193.3 12.2 %copy.135 = bf16[4,4,512,512]{3,1,2,0:T(4,128)(2,1)} copy(bf16[4,4,512,512]{3,2,1,0:T(8,128)(2,1)} %bitcast.290) | data formatting | bytes 16777216 | tf_op jit(solution)/shard_map/reshape | solution.py:397
  205.4 10.3 %copy.172 = bf16[256,8,4,512]{3,1,2,0:T(8,128)(2,1)} copy(bf16[256,8,4,512]{3,2,1,0:T(4,128)(2,1)} %bitcast.282) | data formatting | bytes 16777216
  215.7 9.0 %convolution_bitcast_fusion = f32[2048,640]{1,0:T(8,128)S(1)} fusion(bf16[2048,2048]{1,0:T(8,128)(2,1)} %bitcast.277, bf16[2048,512]{1,0:T(8,128)(2,1)S(1)} %bitcast.292, bf16[2048,128]{1,0:T(8,128)(2,1)S(1)} %slice.211), kind=kOutput, calls=%fused_computation.19 | convolution fusion | flops 5373952000 | bytes 16252928 | tf_op jit(solution)/shard_map/dot_general | solution.py:25
  229.2 12.3 %layer_norm.1 = (bf16[2048,2048]{1,0:T(8,128)(2,1)}, f32[2048,128]{1,0:T(8,128)S(1)}) custom-call(bf16[4,4,528,512]{3,2,1,0:T(8,128)(2,1)} %bitcast.286, f32[1,2048]{1,0:T(1,128)S(1)} %reshape.205.gain_ref, f32[1,2048]{1,0:T(1,128)S(1)} %reshape.206.shift_ref), custom_call_target="tpu_custom_call" | custom-call | tf_op jit(solution)/shard_map/layer_norm/pallas_call | solution.py:84
  241.6 9.9 %convolution_add_fusion.pre_ref = f32[2048,384]{1,0:T(8,128)} fusion(bf16[2048,2048]{1,0:T(8,128)(2,1)} %get-tuple-element.20, f32[384]{0:T(512)S(1)} %pad_maximum_fusion.7, bf16[2048,512]{1,0:T(8,128)(2,1)S(1)} %bitcast.289), kind=kOutput, calls=%fused_computation.23 | convolution fusion | flops 3222011904 | bytes 13109248 | tf_op jit(solution)/shard_map/dot_general | solution.py:25
  251.6 10.3 %convert_reduce_fusion = (f32[512]{0:T(512)S(1)}, bf16[2048,512]{1,0:T(8,128)(2,1)S(1)}, bf16[2048,512]{1,0:T(8,128)(2,1)}) fusion(f32[512]{0:T(512)S(1)} %bitcast.329, f32[2048,640]{1,0:T(8,128)S(1)} %bitcast.321, bf16[2048,2048]{1,0:T(8,128)(2,1)S(1)} %copy-done.23, bf16[2048,512]{1,0:T(8,128)(2,1)} %bitcast.49), kind=kOutput, calls=%fused_computation.11 | convolution fusion | flops 4321181184 | bytes 18878464 | tf_op jit(solution)/shard_map/dot_general | solution.py:25
  261.8 73.3 %attention.1 = (bf16[2048,128]{1,0:T(8,128)(2,1)S(1)}, bf16[2048,384]{1,0:T(8,128)(2,1)S(1)}) custom-call(f32[2048,384]{1,0:T(8,128)} %convolution_add_fusion.pre_ref, bf16[2048,128]{1,0:T(8,128)(2,1)S(1)} %slice.253.grad_ref, f32[2048,128]{1,0:T(8,128)S(1)} %copy-done.2, f32[2048,128]{1,0:T(8,128)S(1)} %copy-done.1), custom_call_target="tpu_custom_call" | custom-call | flops 14495514624 | bytes 4194304 | tf_op jit(solution)/shard_map/attention/pallas_call | solution.py:237
  335.2 12.6 %convolution_convert_fusion = bf16[2048,2048]{1,0:T(8,128)(2,1)} fusion(bf16[2048,512]{1,0:T(8,128)(2,1)S(1)} %get-tuple-element.94, bf16[2048,384]{1,0:T(8,128)(2,1)S(1)} %get-tuple-element.22, bf16[2048,512]{1,0:T(8,128)(2,1)} %bitcast.49, bf16[2048,384]{1,0:T(8,128)(2,1)S(1)} %copy-done.14), kind=kOutput, calls=%fused_computation | convolution fusion | flops 7535067136 | bytes 15728640 | tf_op jit(solution)/shard_map/dot_general | solution.py:35
  347.8 14.6 %reshape.222 = bf16[4,512,4,512]{3,2,1,0:T(4,128)(2,1)} reshape(bf16[2048,2048]{1,0:T(8,128)(2,1)} %convolution_convert_fusion) | data formatting | bytes 16777216 | tf_op jit(solution)/shard_map/reshape | solution.py:424
  362.4 8.6 %copy.142 = bf16[4,4,512,512]{3,2,1,0:T(8,128)(2,1)} copy(bf16[4,4,512,512]{3,1,2,0:T(4,128)(2,1)} %bitcast.283) | data formatting | bytes 16777216 | tf_op jit(solution)/shard_map/transpose | solution.py:425
  371.1 10.9 %convolution_convert_fusion.1 = bf16[2048,2048]{1,0:T(8,128)(2,1)} fusion(bf16[2048,512]{1,0:T(8,128)(2,1)} %get-tuple-element.95, bf16[2048,128]{1,0:T(8,128)(2,1)S(1)} %get-tuple-element.21, bf16[2048,512]{1,0:T(8,128)(2,1)} %bitcast.293, bf16[2048,128]{1,0:T(8,128)(2,1)S(1)} %slice.211), kind=kOutput, calls=%fused_computation.1 | convolution fusion | flops 5383389184 | bytes 13631488 | tf_op jit(solution)/shard_map/dot_general | solution.py:35
  382.0 14.7 %reshape.220 = bf16[4,512,4,512]{3,2,1,0:T(4,128)(2,1)} reshape(bf16[2048,2048]{1,0:T(8,128)(2,1)} %convolution_convert_fusion.1) | data formatting | bytes 16777216 | tf_op jit(solution)/shard_map/reshape | solution.py:424
  396.7 8.6 %copy.141 = bf16[4,4,512,512]{3,2,1,0:T(8,128)(2,1)} copy(bf16[4,4,512,512]{3,1,2,0:T(4,128)(2,1)} %bitcast.284) | data formatting | bytes 16777216 | tf_op jit(solution)/shard_map/transpose | solution.py:425
  406.5 10.0 %fusion.13 = bf16[2048,512]{0,1:T(8,128)(2,1)} fusion(bf16[2048,512]{1,0:T(8,128)(2,1)} %get-tuple-element.95, bf16[2048,2048]{1,0:T(8,128)(2,1)} %bitcast.278), kind=kOutput, calls=%fused_computation.25 | convolution fusion | flops 4296015872 | bytes 12582912 | tf_op jit(solution)/shard_map/dot_general | solution.py:29
  416.5 4.7 reshape.235
  421.2 4.7 fusion.17
  426.0 7.0 %convolution_convert_fusion.4 = bf16[2048,384]{0,1:T(8,128)(2,1)S(1)} fusion(bf16[2048,2048]{1,0:T(8,128)(2,1)} %get-tuple-element.20, bf16[2048,384]{1,0:T(8,128)(2,1)S(1)} %get-tuple-element.22), kind=kOutput, calls=%fused_computation.24 | convolution fusion | flops 3222011904 | bytes 11534336 | tf_op jit(solution)/shard_map/dot_general | solution.py:29
  434.4 4.5 reshape.233
  438.9 3.0 constant_dynamic-slice_fusion.11
  442.7 3.3 collective-permute-start.13
  446.4 8.7 %convolution_convert_fusion.3 = bf16[2048,512]{1,0:T(8,128)(2,1)S(1)} fusion(bf16[2048,2048]{1,0:T(8,128)(2,1)} %get-tuple-element.20, bf16[2048,512]{1,0:T(8,128)(2,1)S(1)} %copy-done.26), kind=kOutput, calls=%fused_computation.22 | convolution fusion | flops 4296015872 | bytes 12582912 | tf_op jit(solution)/shard_map/dot_general | solution.py:29
  459.3 3.8 collective-permute-start.15
  479.4 3.2 collective-permute-start.23
  482.6 16.1 %collective-permute-start.17 = (bf16[2,256,512]{1,2,0:T(8,128)(2,1)}, bf16[2,256,512]{1,2,0:T(8,128)(2,1)S(1)}, u32[]{:S(2)}, u32[]{:S(2)}) collective-permute-start(bf16[2,256,512]{1,2,0:T(8,128)(2,1)} %bitcast.93), channel_id=1, source_target_pairs={{0,16},{8,24},{16,0},{24,8},{1,17},{9,25},{17,1},{25,9},{2,18},{10... | collective-permute-start | bytes 1572872 | tf_op jit(solution)/shard_map/ppermute | solution.py:46
  498.7 2.5 collective-permute-start.18
  502.8 13.8 %collective-permute-done.21 = bf16[2,256,512]{1,2,0:T(8,128)(2,1)} collective-permute-done((bf16[2,256,512]{1,2,0:T(8,128)(2,1)}, bf16[2,256,512]{1,2,0:T(8,128)(2,1)}, u32[]{:S(2)}, u32[]{:S(2)}) %collective-permute-start.21) | collective-permute-done | bytes 524320 | tf_op jit(solution)/shard_map/ppermute | solution.py:46
  517.5 14.2 %collective-permute-start.16 = (bf16[2,256,512]{1,2,0:T(8,128)(2,1)S(1)}, bf16[2,256,512]{1,2,0:T(8,128)(2,1)S(1)}, u32[]{:S(2)}, u32[]{:S(2)}) collective-permute-start(bf16[2,256,512]{1,2,0:T(8,128)(2,1)S(1)} %fusion.45), channel_id=1, source_target_pairs={{0,4},{4,0},{1,5},{5,1},{2,6},{6,2},{3,7},{7,3},{8,12},{12,8},{9,1... | collective-permute-start | bytes 1572872 | tf_op jit(solution)/shard_map/ppermute | solution.py:46
  534.2 27.8 %collective-permute-done.17 = bf16[2,256,512]{1,2,0:T(8,128)(2,1)S(1)} collective-permute-done((bf16[2,256,512]{1,2,0:T(8,128)(2,1)}, bf16[2,256,512]{1,2,0:T(8,128)(2,1)S(1)}, u32[]{:S(2)}, u32[]{:S(2)}) %collective-permute-start.17) | collective-permute-done | bytes 524320 | tf_op jit(solution)/shard_map/ppermute | solution.py:46
  561.9 6.8 collective-permute-done.19
  578.1 3.6 collective-permute-done.20
  585.1 2.9 copy.161
  593.9 55.2 %all-reduce.3 = (f32[512]{0:T(512)S(1)}, f32[512]{0:T(512)S(1)}) all-reduce(f32[512]{0:T(512)S(1)} %get-tuple-element.89, f32[512]{0:T(512)S(1)} %get-tuple-element.90), channel_id=1, replica_groups=mesh['s'=2,'g'=2,'h'=2,'m'=2,'c'=2] {'m','c'}, use_global_device_ids=true, to_apply=%region_5.6 | all-reduce | flops 1024 | bytes 8192 | tf_op jit(solution)/shard_map/psum | solution.py:447
  649.1 2.9 convert_reduce_fusion.2
  652.1 35.2 %all-reduce.2 = f32[8,640]{1,0:T(8,128)S(1)} all-reduce(f32[8,640]{1,0:T(8,128)S(1)} %concatenate.71), channel_id=6, replica_groups=mesh['s'=2,'g'=2,'h'=2,'m'=2,'c'=2] {'s','g','h'}, use_global_device_ids=true, to_apply=%region_11.12.clone | all-reduce | flops 5120 | bytes 40960
  (231 shorter events, 83.6 us)
Async XLA Ops:
  7.2 13.9 %copy-start.17 = (bf16[256,512]{1,0:T(8,128)(2,1)S(1)}, bf16[256,512]{1,0:T(8,128)(2,1)}, u32[]{:S(2)}) copy-start(bf16[256,512]{1,0:T(8,128)(2,1)} %param.22) | copy-start | bytes 786436
  7.2 14.0 %copy-start.18 = (bf16[256,512]{1,0:T(8,128)(2,1)S(1)}, bf16[256,512]{1,0:T(8,128)(2,1)}, u32[]{:S(2)}) copy-start(bf16[256,512]{1,0:T(8,128)(2,1)} %param.24) | copy-start | bytes 786436
  7.2 14.1 %copy-start.19 = (bf16[256,512]{1,0:T(8,128)(2,1)S(1)}, bf16[256,512]{1,0:T(8,128)(2,1)}, u32[]{:S(2)}) copy-start(bf16[256,512]{1,0:T(8,128)(2,1)} %param.26) | copy-start | bytes 786436
  7.2 186.0 %all-gather.7.cloned.1.call-start = ((), (), s32[]{:S(2)}) async-start(), calls=%async_computation.5 | async-start | bytes 8912896 | tf_op jit(solution)/shard_map/all_gather | solution.py:358
  7.9 219.3 %all-gather.5.cloned.1.call-start = ((), (), s32[]{:S(2)}) async-start(), calls=%async_computation.4 | async-start | bytes 9191424 | tf_op jit(solution)/shard_map/all_gather | solution.py:355
  13.4 5.7 collective-permute-start
  21.0 569.8 %reduce-scatter.5.cloned.1.call-start = ((), (), s32[]{:S(2)}) async-start(), calls=%async_computation.3 | async-start | bytes 8912896 | tf_op jit(solution)/shard_map/reduce_scatter | solution.py:426
  23.1 15.2 %collective-permute-start.1 = (bf16[256,2,512]{2,0,1:T(8,128)(2,1)}, bf16[256,2,512]{2,0,1:T(8,128)(2,1)}, u32[]{:S(2)}, u32[]{:S(2)}) collective-permute-start(bf16[256,2,512]{2,0,1:T(8,128)(2,1)} %dynamic-slice_bitcast_fusion), channel_id=1, source_target_pairs={{0,4},{4,0},{1,5},{5,1},{2,6},{6,2},{3,7},{7,3},{8,12},{12,8},{9,1... | collective-permute-start | bytes 1572872 | tf_op jit(solution)/shard_map/ppermute | solution.py:46
  26.6 22.9 %collective-permute-start.9 = (bf16[256,2,512]{2,0,1:T(8,128)(2,1)}, bf16[256,2,512]{2,0,1:T(8,128)(2,1)}, u32[]{:S(2)}, u32[]{:S(2)}) collective-permute-start(bf16[256,2,512]{2,0,1:T(8,128)(2,1)} %bitcast.40), channel_id=1, source_target_pairs={{0,4},{4,0},{1,5},{5,1},{2,6},{6,2},{3,7},{7,3},{8,12},{12,8},{9,1... | collective-permute-start | bytes 1572872 | tf_op jit(solution)/shard_map/ppermute | solution.py:46
  29.0 29.7 %collective-permute-start.5 = (bf16[256,2,512]{2,0,1:T(8,128)(2,1)}, bf16[256,2,512]{2,0,1:T(8,128)(2,1)}, u32[]{:S(2)}, u32[]{:S(2)}) collective-permute-start(bf16[256,2,512]{2,0,1:T(8,128)(2,1)} %bitcast.25), channel_id=1, source_target_pairs={{0,4},{4,0},{1,5},{5,1},{2,6},{6,2},{3,7},{7,3},{8,12},{12,8},{9,1... | collective-permute-start | bytes 1572872 | tf_op jit(solution)/shard_map/ppermute | solution.py:46
  39.5 102.6 %collective-permute-start.4 = (bf16[512,512]{1,0:T(8,128)(2,1)S(1)}, bf16[512,512]{1,0:T(8,128)(2,1)S(1)}, u32[]{:S(2)}, u32[]{:S(2)}) collective-permute-start(bf16[512,512]{1,0:T(8,128)(2,1)S(1)} %bitcast.315), channel_id=1, source_target_pairs={{0,24},{8,0},{16,8},{24,16},{1,25},{9,1},{17,9},{25,17},{2,26},{10... | collective-permute-start | bytes 1572872 | tf_op jit(solution)/shard_map/ppermute | solution.py:46
  43.5 41.1 %collective-permute-start.2 = (bf16[512,512]{1,0:T(8,128)(2,1)S(1)}, bf16[512,512]{1,0:T(8,128)(2,1)S(1)}, u32[]{:S(2)}, u32[]{:S(2)}) collective-permute-start(bf16[512,512]{1,0:T(8,128)(2,1)S(1)} %bitcast.316), channel_id=1, source_target_pairs={{0,8},{8,16},{16,24},{24,0},{1,9},{9,17},{17,25},{25,1},{2,10},{10... | collective-permute-start | bytes 1572872 | tf_op jit(solution)/shard_map/ppermute | solution.py:46
  60.0 82.1 %collective-permute-start.8 = (bf16[512,512]{1,0:T(8,128)(2,1)S(1)}, bf16[512,512]{1,0:T(8,128)(2,1)S(1)}, u32[]{:S(2)}, u32[]{:S(2)}) collective-permute-start(bf16[512,512]{1,0:T(8,128)(2,1)S(1)} %bitcast.311), channel_id=1, source_target_pairs={{0,24},{8,0},{16,8},{24,16},{1,25},{9,1},{17,9},{25,17},{2,26},{10... | collective-permute-start | bytes 1572872 | tf_op jit(solution)/shard_map/ppermute | solution.py:46
  63.7 43.4 %collective-permute-start.6 = (bf16[512,512]{1,0:T(8,128)(2,1)S(1)}, bf16[512,512]{1,0:T(8,128)(2,1)S(1)}, u32[]{:S(2)}, u32[]{:S(2)}) collective-permute-start(bf16[512,512]{1,0:T(8,128)(2,1)S(1)} %bitcast.312), channel_id=1, source_target_pairs={{0,8},{8,16},{16,24},{24,0},{1,9},{9,17},{17,25},{25,1},{2,10},{10... | collective-permute-start | bytes 1572872 | tf_op jit(solution)/shard_map/ppermute | solution.py:46
  63.7 66.1 %collective-permute-start.3 = (bf16[512,512]{1,0:T(8,128)(2,1)S(1)}, bf16[512,512]{1,0:T(8,128)(2,1)S(1)}, u32[]{:S(2)}, u32[]{:S(2)}) collective-permute-start(bf16[512,512]{1,0:T(8,128)(2,1)S(1)} %bitcast.299), channel_id=1, source_target_pairs={{0,16},{8,24},{16,0},{24,8},{1,17},{9,25},{17,1},{25,9},{2,18},{10... | collective-permute-start | bytes 1572872 | tf_op jit(solution)/shard_map/ppermute | solution.py:46
  84.6 57.4 %collective-permute-start.7 = (bf16[512,512]{1,0:T(8,128)(2,1)S(1)}, bf16[512,512]{1,0:T(8,128)(2,1)S(1)}, u32[]{:S(2)}, u32[]{:S(2)}) collective-permute-start(bf16[512,512]{1,0:T(8,128)(2,1)S(1)} %bitcast.297), channel_id=1, source_target_pairs={{0,16},{8,24},{16,0},{24,8},{1,17},{9,25},{17,1},{25,9},{2,18},{10... | collective-permute-start | bytes 1572872 | tf_op jit(solution)/shard_map/ppermute | solution.py:46
  107.2 85.3 %collective-permute-start.12 = (bf16[512,512]{1,0:T(8,128)(2,1)S(1)}, bf16[512,512]{1,0:T(8,128)(2,1)S(1)}, u32[]{:S(2)}, u32[]{:S(2)}) collective-permute-start(bf16[512,512]{1,0:T(8,128)(2,1)S(1)} %bitcast.309), channel_id=1, source_target_pairs={{0,24},{8,0},{16,8},{24,16},{1,25},{9,1},{17,9},{25,17},{2,26},{10... | collective-permute-start | bytes 1572872 | tf_op jit(solution)/shard_map/ppermute | solution.py:46
  129.8 42.3 %collective-permute-start.10 = (bf16[512,512]{1,0:T(8,128)(2,1)S(1)}, bf16[512,512]{1,0:T(8,128)(2,1)S(1)}, u32[]{:S(2)}, u32[]{:S(2)}) collective-permute-start(bf16[512,512]{1,0:T(8,128)(2,1)S(1)} %bitcast.310), channel_id=1, source_target_pairs={{0,8},{8,16},{16,24},{24,0},{1,9},{9,17},{17,25},{25,1},{2,10},{10... | collective-permute-start | bytes 1572872 | tf_op jit(solution)/shard_map/ppermute | solution.py:46
  142.0 49.6 %collective-permute-start.11 = (bf16[512,512]{1,0:T(8,128)(2,1)S(1)}, bf16[512,512]{1,0:T(8,128)(2,1)S(1)}, u32[]{:S(2)}, u32[]{:S(2)}) collective-permute-start(bf16[512,512]{1,0:T(8,128)(2,1)S(1)} %bitcast.295), channel_id=1, source_target_pairs={{0,16},{8,24},{16,0},{24,8},{1,17},{9,25},{17,1},{25,9},{2,18},{10... | collective-permute-start | bytes 1572872 | tf_op jit(solution)/shard_map/ppermute | solution.py:46
  142.2 73.5 %copy-start.9 = (bf16[4,512,512]{2,1,0:T(8,128)(2,1)}, bf16[4,512,512]{2,1,0:T(8,128)(2,1)S(1)}, u32[]{:S(2)}) copy-start(bf16[4,512,512]{2,1,0:T(8,128)(2,1)S(1)} %bitcast_dynamic-update-slice_fusion.3) | copy-start | bytes 6291460
  229.2 12.3 %copy-start.5 = (bf16[4,512,512]{2,1,0:T(8,128)(2,1)S(1)}, bf16[4,512,512]{2,1,0:T(8,128)(2,1)}, u32[]{:S(2)}) copy-start(bf16[4,512,512]{2,1,0:T(8,128)(2,1)} %copy-done.4) | copy-start | bytes 6291460
  229.2 22.3 %slice-start = ((s8[5242880]{0:T(1024)(128)(4,1)}), s8[4194304]{0:T(1024)(128)(4,1)S(1)}, s32[]{:S(2)}) async-start(s8[5242880]{0:T(1024)(128)(4,1)} %bitcast.320), calls=%async_computation.6 | async-start | bytes 8388608
  241.5 10.0 %copy-start = (f32[2048,128]{1,0:T(8,128)}, f32[2048,128]{1,0:T(8,128)S(1)}, u32[]{:S(2)}) copy-start(f32[2048,128]{1,0:T(8,128)S(1)} %get-tuple-element.23) | copy-start | bytes 3145732
  241.5 10.0 %slice-start.1 = ((s8[5242880]{0:T(1024)(128)(4,1)}), s8[1048576]{0:T(1024)(128)(4,1)S(1)}, s32[]{:S(2)}) async-start(s8[5242880]{0:T(1024)(128)(4,1)} %bitcast.320), calls=%async_computation.7 | async-start | bytes 2097152
  241.5 10.0 %copy-start.23 = (bf16[2048,2048]{1,0:T(8,128)(2,1)S(1)}, bf16[2048,2048]{1,0:T(8,128)(2,1)}, u32[]{:S(2)}) copy-start(bf16[2048,2048]{1,0:T(8,128)(2,1)} %get-tuple-element.20) | copy-start | bytes 25165828
  251.5 10.3 %copy-start.1 = (f32[2048,128]{1,0:T(8,128)S(1)}, f32[2048,128]{1,0:T(8,128)}, u32[]{:S(2)}) copy-start(f32[2048,128]{1,0:T(8,128)} %constant.260.clone.sine_ref) | copy-start | bytes 3145732
  251.5 10.3 %copy-start.2 = (f32[2048,128]{1,0:T(8,128)S(1)}, f32[2048,128]{1,0:T(8,128)}, u32[]{:S(2)}) copy-start(f32[2048,128]{1,0:T(8,128)} %constant.259.clone.cosine_ref) | copy-start | bytes 3145732
  261.8 73.4 %copy-start.25 = (bf16[2048,512]{1,0:T(8,128)(2,1)}, bf16[2048,512]{1,0:T(8,128)(2,1)S(1)}, u32[]{:S(2)}) copy-start(bf16[2048,512]{1,0:T(8,128)(2,1)S(1)} %get-tuple-element.94) | copy-start | bytes 6291460
  261.8 73.4 %copy-start.14 = (bf16[2048,384]{1,0:T(8,128)(2,1)S(1)}, bf16[2048,384]{1,0:T(8,128)(2,1)}, u32[]{:S(2)}) copy-start(bf16[2048,384]{1,0:T(8,128)(2,1)} %slice.206) | copy-start | bytes 4718596
  371.0 278.0 %reduce-scatter.3.cloned.1.call-start = ((), (), s32[]{:S(2)}) async-start(), calls=%async_computation.2 | async-start | bytes 8912896 | tf_op jit(solution)/shard_map/reduce_scatter | solution.py:426
  441.9 4.5 copy-start.26
  442.7 36.6 %collective-permute-start.13 = (bf16[2,256,512]{1,2,0:T(8,128)(2,1)}, bf16[2,256,512]{1,2,0:T(8,128)(2,1)}, u32[]{:S(2)}, u32[]{:S(2)}) collective-permute-start(bf16[2,256,512]{1,2,0:T(8,128)(2,1)} %bitcast.274), channel_id=1, source_target_pairs={{0,16},{8,24},{16,0},{24,8},{1,17},{9,25},{17,1},{25,9},{2,18},{10... | collective-permute-start | bytes 1572872 | tf_op jit(solution)/shard_map/ppermute | solution.py:46
  446.4 8.7 %copy-start.6 = (bf16[4,2,256,512]{2,1,0,3:T(2,128)(2,1)S(1)}, bf16[4,2,256,512]{2,1,0,3:T(2,128)(2,1)}, u32[]{:S(2)}) copy-start(bf16[4,2,256,512]{2,1,0,3:T(2,128)(2,1)} %reshape.235) | copy-start | bytes 6291460
  459.3 23.3 %collective-permute-start.14 = (bf16[2,256,512]{1,2,0:T(8,128)(2,1)}, bf16[2,256,512]{1,2,0:T(8,128)(2,1)}, u32[]{:S(2)}, u32[]{:S(2)}) collective-permute-start(bf16[2,256,512]{1,2,0:T(8,128)(2,1)} %bitcast.273), channel_id=1, source_target_pairs={{0,8},{8,16},{16,24},{24,0},{1,9},{9,17},{17,25},{25,1},{2,10},{10... | collective-permute-start | bytes 1572872 | tf_op jit(solution)/shard_map/ppermute | solution.py:46
  459.3 39.5 %collective-permute-start.15 = (bf16[2,256,512]{1,2,0:T(8,128)(2,1)}, bf16[2,256,512]{1,2,0:T(8,128)(2,1)}, u32[]{:S(2)}, u32[]{:S(2)}) collective-permute-start(bf16[2,256,512]{1,2,0:T(8,128)(2,1)} %bitcast.272), channel_id=1, source_target_pairs={{0,24},{8,0},{16,8},{24,16},{1,25},{9,1},{17,9},{25,17},{2,26},{10... | collective-permute-start | bytes 1572872 | tf_op jit(solution)/shard_map/ppermute | solution.py:46
  470.4 46.2 %collective-permute-start.21 = (bf16[2,256,512]{1,2,0:T(8,128)(2,1)}, bf16[2,256,512]{1,2,0:T(8,128)(2,1)}, u32[]{:S(2)}, u32[]{:S(2)}) collective-permute-start(bf16[2,256,512]{1,2,0:T(8,128)(2,1)} %bitcast.271), channel_id=1, source_target_pairs={{0,16},{8,24},{16,0},{24,8},{1,17},{9,25},{17,1},{25,9},{2,18},{10... | collective-permute-start | bytes 1572872 | tf_op jit(solution)/shard_map/ppermute | solution.py:46
  470.5 47.1 %collective-permute-start.22 = (bf16[2,256,512]{1,2,0:T(8,128)(2,1)}, bf16[2,256,512]{1,2,0:T(8,128)(2,1)}, u32[]{:S(2)}, u32[]{:S(2)}) collective-permute-start(bf16[2,256,512]{1,2,0:T(8,128)(2,1)} %bitcast.270), channel_id=1, source_target_pairs={{0,8},{8,16},{16,24},{24,0},{1,9},{9,17},{17,25},{25,1},{2,10},{10... | collective-permute-start | bytes 1572872 | tf_op jit(solution)/shard_map/ppermute | solution.py:46
  473.1 5.2 copy-start.12
  473.1 6.2 copy-start.16
  479.4 52.4 %collective-permute-start.23 = (bf16[2,256,512]{1,2,0:T(8,128)(2,1)S(1)}, bf16[2,256,512]{1,2,0:T(8,128)(2,1)S(1)}, u32[]{:S(2)}, u32[]{:S(2)}) collective-permute-start(bf16[2,256,512]{1,2,0:T(8,128)(2,1)S(1)} %bitcast.313), channel_id=1, source_target_pairs={{0,24},{8,0},{16,8},{24,16},{1,25},{9,1},{17,9},{25,17},{2,26},{10... | collective-permute-start | bytes 1572872 | tf_op jit(solution)/shard_map/ppermute | solution.py:46
  482.6 79.3 %collective-permute-start.17 = (bf16[2,256,512]{1,2,0:T(8,128)(2,1)}, bf16[2,256,512]{1,2,0:T(8,128)(2,1)S(1)}, u32[]{:S(2)}, u32[]{:S(2)}) collective-permute-start(bf16[2,256,512]{1,2,0:T(8,128)(2,1)} %bitcast.93), channel_id=1, source_target_pairs={{0,16},{8,24},{16,0},{24,8},{1,17},{9,25},{17,1},{25,9},{2,18},{10... | collective-permute-start | bytes 1572872 | tf_op jit(solution)/shard_map/ppermute | solution.py:46
  498.7 63.2 %collective-permute-start.18 = (bf16[2,256,512]{1,2,0:T(8,128)(2,1)}, bf16[2,256,512]{1,2,0:T(8,128)(2,1)S(1)}, u32[]{:S(2)}, u32[]{:S(2)}) collective-permute-start(bf16[2,256,512]{1,2,0:T(8,128)(2,1)} %bitcast.94), channel_id=1, source_target_pairs={{0,8},{8,16},{16,24},{24,0},{1,9},{9,17},{17,25},{25,1},{2,10},{10... | collective-permute-start | bytes 1572872 | tf_op jit(solution)/shard_map/ppermute | solution.py:46
  516.7 52.1 %collective-permute-start.19 = (bf16[2,256,512]{1,2,0:T(8,128)(2,1)}, bf16[2,256,512]{1,2,0:T(8,128)(2,1)S(1)}, u32[]{:S(2)}, u32[]{:S(2)}) collective-permute-start(bf16[2,256,512]{1,2,0:T(8,128)(2,1)} %bitcast.95), channel_id=1, source_target_pairs={{0,24},{8,0},{16,8},{24,16},{1,25},{9,1},{17,9},{25,17},{2,26},{10... | collective-permute-start | bytes 1572872 | tf_op jit(solution)/shard_map/ppermute | solution.py:46
  517.5 52.6 %collective-permute-start.16 = (bf16[2,256,512]{1,2,0:T(8,128)(2,1)S(1)}, bf16[2,256,512]{1,2,0:T(8,128)(2,1)S(1)}, u32[]{:S(2)}, u32[]{:S(2)}) collective-permute-start(bf16[2,256,512]{1,2,0:T(8,128)(2,1)S(1)} %fusion.45), channel_id=1, source_target_pairs={{0,4},{4,0},{1,5},{5,1},{2,6},{6,2},{3,7},{7,3},{8,12},{12,8},{9,1... | collective-permute-start | bytes 1572872 | tf_op jit(solution)/shard_map/ppermute | solution.py:46
  533.3 35.5 %copy-start.8 = (bf16[1,2,256,512]{2,3,1,0:T(8,128)(2,1)S(1)}, bf16[1,2,256,512]{2,3,1,0:T(8,128)(2,1)}, u32[]{:S(2)}) copy-start(bf16[1,2,256,512]{2,3,1,0:T(8,128)(2,1)} %copy.170) | copy-start | bytes 1572868
  534.1 53.9 %collective-permute-start.24 = (bf16[2,256,512]{1,2,0:T(8,128)(2,1)}, bf16[2,256,512]{1,2,0:T(8,128)(2,1)}, u32[]{:S(2)}, u32[]{:S(2)}) collective-permute-start(bf16[2,256,512]{1,2,0:T(8,128)(2,1)} %fusion.47), channel_id=1, source_target_pairs={{0,4},{4,0},{1,5},{5,1},{2,6},{6,2},{3,7},{7,3},{8,12},{12,8},{9,1... | collective-permute-start | bytes 1572872 | tf_op jit(solution)/shard_map/ppermute | solution.py:46
  570.1 11.6 %collective-permute-start.20 = (bf16[2,256,512]{1,2,0:T(8,128)(2,1)}, bf16[2,256,512]{1,2,0:T(8,128)(2,1)}, u32[]{:S(2)}, u32[]{:S(2)}) collective-permute-start(bf16[2,256,512]{1,2,0:T(8,128)(2,1)} %fusion.46), channel_id=1, source_target_pairs={{0,4},{4,0},{1,5},{5,1},{2,6},{6,2},{3,7},{7,3},{8,12},{12,8},{9,1... | collective-permute-start | bytes 1572872 | tf_op jit(solution)/shard_map/ppermute | solution.py:46
  589.4 59.7 %copy-start.10 = (bf16[512,512]{1,0:T(8,128)(2,1)S(1)}, bf16[512,512]{1,0:T(8,128)(2,1)}, u32[]{:S(2)}) copy-start(bf16[512,512]{1,0:T(8,128)(2,1)} %param.19) | copy-start | bytes 1572868
  (10 other events, 21.9 us)
Sparse Core Ops, SparseCore 0:
  9.6 108.8 all-gather.6
  120.7 83.2 all-gather.4
  371.2 135.8 reduce-scatter.4
  509.2 135.6 reduce-scatter.2

commit v2 on v1

v2 whole, which is shorter than its diff:
```python
from functools import partial
import math

import jax
import jax.numpy as jnp
import numpy as np
from jax import lax
from jax.experimental import pallas as pl
from jax.experimental.pallas import tpu as pltpu
from jax.sharding import Mesh, PartitionSpec as P

D = 2048
HEAD_DIM = 64
ROT = 32
EPSILON = 1e-05
VMEM_LIMIT = 56 * 2**20

WIDE = ("s", "g", "h")
LINE = ("s", "g")
NARROW = ("m", "c")
CUBE = ("g", "h", "m", "c")


def matmul(left_side, right_side):
    return jnp.dot(left_side, right_side, preferred_element_type=jnp.float32)


def contract_rows(left_side, right_side):
    return lax.dot_general(
        left_side, right_side, (((0,), (0,)), ((), ())), preferred_element_type=jnp.float32
    )


def contract_cols(left_side, right_side):
    return lax.dot_general(
        left_side, right_side, (((1,), (1,)), ((), ())), preferred_element_type=jnp.float32
    )


def pick(blocks, index, axis=0):
    return lax.dynamic_index_in_dim(blocks, index, axis, keepdims=False)


def shifted(value, axis, step):
    count = lax.axis_size(axis)
    return lax.ppermute(value, axis, [(source, (source + step) % count) for source in range(count)])


def in_order(mine, other, index):
    return (jnp.where(index == 0, mine, other), jnp.where(index == 0, other, mine))


def call(kernel, name, grid, in_specs, out_specs, out_shape, scratch=(), flops=0, nbytes=0):
    return pl.pallas_call(
        kernel,
        grid=grid,
        in_specs=in_specs,
        out_specs=out_specs,
        out_shape=out_shape,
        scratch_shapes=list(scratch),
        compiler_params=pltpu.CompilerParams(vmem_limit_bytes=VMEM_LIMIT),
        cost_estimate=pl.CostEstimate(flops=flops, bytes_accessed=nbytes, transcendentals=0),
        name=name,
    )


def whole(*shape):
    return pl.BlockSpec(shape, lambda i: (0,) * len(shape))


def band(rows, cols):
    return pl.BlockSpec((rows, cols), lambda i: (i, 0))


def block_band(rows, row_count, col_blocks, width):
    per = row_count // rows
    return pl.BlockSpec((1, col_blocks, rows, width), lambda i: (i // per, 0, i % per, 0))


ANY = pl.BlockSpec(memory_space=pl.ANY)
SCALARS = pl.BlockSpec(memory_space=pltpu.SMEM)


def struct(shape, dtype):
    return jax.ShapeDtypeStruct(shape, dtype)


def fill(pieces, starts_ref, target, cols, semaphores):
    copies = []
    for n, piece in enumerate(pieces):
        rows = piece.shape[0]
        start = pl.multiple_of(starts_ref[n], rows)
        copy = pltpu.make_async_copy(
            piece.at[:, cols], target.at[pl.ds(start, rows), :], semaphores.at[n]
        )
        copy.start()
        copies.append(copy)
    for copy in copies:
        copy.wait()


def rotary_tables(rows):
    lane = np.arange(2 * HEAD_DIM) % HEAD_DIM
    pair = (lane % (ROT // 2)).astype(np.float32)
    inverse = np.exp(pair * np.float32(-2.0 * math.log(10000.0) / ROT)).astype(np.float32)
    phase = np.arange(rows, dtype=np.float32)[:, None] * inverse[None, :]
    turned = (lane < ROT)[None, :]
    sign = np.where(lane < ROT // 2, -1.0, 1.0)[None, :]
    cosine = np.where(turned, np.cos(phase), 1.0).astype(np.float32)
    sine = np.where(turned, np.sin(phase) * sign, 0.0).astype(np.float32)
    return (cosine, sine)


def turn(values, cosine, sine):
    lane = lax.broadcasted_iota(jnp.int32, values.shape, 1) % HEAD_DIM
    width = values.shape[1]
    half = ROT // 2
    partner = jnp.where(
        lane < half, pltpu.roll(values, width - half, 1), pltpu.roll(values, half, 1)
    )
    return values * cosine + partner * sine


def norm_up_kernel(
    count, starts_ref, tokens_ref, gain_ref, shift_ref, bias_ref, *refs
):
    pieces = refs[:count]
    normed_ref, stats_ref, low_ref, slope_ref, weight, semaphores = refs[count:]

    @pl.when(pl.program_id(0) == 0)
    def _():
        fill(pieces, starts_ref, weight, slice(None), semaphores)

    parts = [tokens_ref[0, j].astype(jnp.float32) for j in range(tokens_ref.shape[1])]
    rows, width = parts[0].shape
    total = sum(jnp.sum(part, axis=1, keepdims=True) for part in parts)
    squares = sum(jnp.sum(part * part, axis=1, keepdims=True) for part in parts)
    mean = total / D
    inverse_std = lax.rsqrt(squares / D - mean * mean + EPSILON)
    up_input = bias_ref[...]
    for j, part in enumerate(parts):
        cols = slice(j * width, (j + 1) * width)
        standard = (part - mean) * inverse_std
        normed = (standard * gain_ref[:, cols] + shift_ref[:, cols]).astype(jnp.bfloat16)
        normed_ref[:, cols] = normed
        up_input = up_input + matmul(normed, weight[cols, :])
    stats_ref[...] = jnp.concatenate(
        [jnp.broadcast_to(mean, (rows, 64)), jnp.broadcast_to(inverse_std, (rows, 64))], axis=1
    )
    root = math.sqrt(2.0 / math.pi)
    square = up_input * up_input
    bend = jnp.tanh(root * (up_input + 0.044715 * square * up_input))
    half = 0.5 * (1.0 + bend)
    low_ref[...] = (up_input * half).astype(jnp.bfloat16)
    slope_ref[...] = half + 0.5 * up_input * (1.0 - bend * bend) * (
        root * (1.0 + 3 * 0.044715 * square)
    )


def norm_up(blocks, gain, shift, bias, weight, rows=256):
    row_blocks, col_blocks, row_count, width = blocks.shape
    pieces, starts = weight
    total, hidden = row_blocks * row_count, bias.shape[1]
    return call(
        partial(norm_up_kernel, len(pieces)),
        "norm_up",
        (total // rows,),
        [SCALARS, block_band(rows, row_count, col_blocks, width)]
        + [whole(1, D), whole(1, D), whole(1, hidden)]
        + [ANY] * len(pieces),
        [band(rows, D), band(rows, 128), band(rows, hidden), band(rows, hidden)],
        [
            struct((total, D), jnp.bfloat16),
            struct((total, 128), jnp.float32),
            struct((total, hidden), jnp.bfloat16),
            struct((total, hidden), jnp.float32),
        ],
        [pltpu.VMEM((D, hidden), jnp.bfloat16), pltpu.SemaphoreType.DMA((len(pieces),))],
        flops=6 * total * D * hidden,
        nbytes=6 * total * D,
    )(starts, blocks, gain, shift, bias, *pieces)


def heads_kernel(count, starts_ref, normed_ref, bias_ref, cosine_ref, sine_ref, *refs):
    pieces = refs[:count]
    heads_ref, weight, semaphores = refs[count:]

    @pl.when(pl.program_id(0) == 0)
    def _():
        fill(pieces, starts_ref, weight, slice(0, weight.shape[1]), semaphores)

    pre = matmul(normed_ref[...], weight[...]) + bias_ref[...]
    lanes = 2 * HEAD_DIM
    cosine, sine = cosine_ref[...], sine_ref[...]
    factor = 1.0 / math.sqrt(HEAD_DIM)
    heads_ref[:, :lanes] = (turn(pre[:, :lanes], cosine, sine) * factor).astype(jnp.bfloat16)
    heads_ref[:, lanes : 2 * lanes] = turn(pre[:, lanes : 2 * lanes], cosine, sine).astype(
        jnp.bfloat16
    )
    heads_ref[:, 2 * lanes :] = pre[:, 2 * lanes :].astype(jnp.bfloat16)


def project_heads(normed, bias, weight, rows=512):
    pieces, starts = weight
    total, width = normed.shape[0], bias.shape[1]
    cosine, sine = rotary_tables(total)
    lanes = 2 * HEAD_DIM
    return call(
        partial(heads_kernel, len(pieces)),
        "project_heads",
        (total // rows,),
        [SCALARS, band(rows, D), whole(1, width), band(rows, lanes), band(rows, lanes)]
        + [ANY] * len(pieces),
        band(rows, width),
        struct((total, width), jnp.bfloat16),
        [pltpu.VMEM((D, width), jnp.bfloat16), pltpu.SemaphoreType.DMA((len(pieces),))],
        flops=4 * total * D * width,
        nbytes=4 * total * D,
    )(starts, normed, bias, jnp.asarray(cosine), jnp.asarray(sine), *pieces)


def out_grad_kernel(count, col_start, starts_ref, cot_ref, *refs):
    pieces = refs[:count]
    out_ref, weight, semaphores = refs[count:]

    @pl.when(pl.program_id(0) == 0)
    def _():
        width = weight.shape[1]
        fill(pieces, starts_ref, weight, slice(col_start, col_start + width), semaphores)

    width = cot_ref.shape[3]
    out = 0.0
    for j in range(cot_ref.shape[1]):
        out = out + matmul(cot_ref[0, j], weight[j * width : (j + 1) * width, :])
    out_ref[...] = out.astype(jnp.bfloat16)


def attended_gradient(cot, weight, width, col_start, rows=512):
    row_blocks, col_blocks, row_count, block_width = cot.shape
    pieces, starts = weight
    total = row_blocks * row_count
    return call(
        partial(out_grad_kernel, len(pieces), col_start),
        "attended_gradient",
        (total // rows,),
        [SCALARS, block_band(rows, row_count, col_blocks, block_width)] + [ANY] * len(pieces),
        band(rows, width),
        struct((total, width), jnp.bfloat16),
        [pltpu.VMEM((D, width), jnp.bfloat16), pltpu.SemaphoreType.DMA((len(pieces),))],
        flops=8 * total * D * width,
        nbytes=4 * total * D,
    )(starts, cot, *pieces)


def up_grad_kernel(count, starts_ref, cot_ref, slope_ref, *refs):
    pieces = refs[:count]
    up_ref, sums_ref, weight, semaphores = refs[count:]

    @pl.when(pl.program_id(0) == 0)
    def _():
        fill(pieces, starts_ref, weight, slice(None), semaphores)
        sums_ref[...] = jnp.zeros_like(sums_ref)

    width = cot_ref.shape[3]
    up = 0.0
    for j in range(cot_ref.shape[1]):
        up = up + matmul(cot_ref[0, j], weight[j * width : (j + 1) * width, :])
    up = (up * slope_ref[...]).astype(jnp.bfloat16)
    up_ref[...] = up
    sums_ref[...] += jnp.sum(up.astype(jnp.float32), axis=0, keepdims=True)


def up_gradient(cot, slope, weight, rows=512):
    row_blocks, col_blocks, row_count, block_width = cot.shape
    pieces, starts = weight
    total, hidden = slope.shape
    return call(
        partial(up_grad_kernel, len(pieces)),
        "up_gradient",
        (total // rows,),
        [SCALARS, block_band(rows, row_count, col_blocks, block_width), band(rows, hidden)]
        + [ANY] * len(pieces),
        [band(rows, hidden), whole(1, hidden)],
        [struct((total, hidden), jnp.bfloat16), struct((1, hidden), jnp.float32)],
        [pltpu.VMEM((D, hidden), jnp.bfloat16), pltpu.SemaphoreType.DMA((len(pieces),))],
        flops=4 * total * D * hidden,
        nbytes=4 * total * D,
    )(starts, cot, slope, *pieces)


def rows_of(index, size):
    return pl.ds(pl.multiple_of(index * size, size), size)


def attention_kernel(
    blocks,
    block,
    qkv_ref,
    grad_ref,
    cosine_ref,
    sine_ref,
    attended_ref,
    pre_grad_ref,
    sums_ref,
    qt_ref,
    kt_ref,
    vt_ref,
    gt_ref,
    score_ref,
    slope_ref,
    k_total,
    v_total,
):
    i = pl.program_id(0)
    width = 2 * HEAD_DIM
    factor = 1.0 / math.sqrt(HEAD_DIM)
    heads = [slice(n * HEAD_DIM, (n + 1) * HEAD_DIM) for n in range(2)]
    chunk = 256
    chunks = qkv_ref.shape[0] // chunk

    @pl.when(i == 0)
    def _():
        def prepare(b, carry):
            rows = rows_of(b, chunk)
            for n, ref in enumerate((qt_ref, kt_ref, vt_ref)):
                ref[:, rows] = qkv_ref[rows, n * width : (n + 1) * width].T
            gt_ref[:, rows] = grad_ref[rows, :].T
            return carry

        lax.fori_loop(0, chunks, prepare, 0)
        k_total[...] = jnp.zeros_like(k_total)
        v_total[...] = jnp.zeros_like(v_total)
        sums_ref[...] = jnp.zeros_like(sums_ref)

    own = rows_of(i, block)
    causal = lax.broadcasted_iota(jnp.int32, (block, block), 0) <= lax.broadcasted_iota(
        jnp.int32, (block, block), 1
    )

    def fold(values, combine):
        return combine(values.reshape(block // 8, 8, block), axis=0)

    def score(j, best, diagonal):
        rows = rows_of(j, block)
        new = []
        for n, head in enumerate(heads):
            start = width + n * HEAD_DIM
            part = matmul(qkv_ref[rows, start : start + HEAD_DIM], qt_ref[head, own])
            if diagonal:
                part = jnp.where(causal, part, -1e30)
            score_ref[n, j] = part
            new.append(jnp.maximum(best[n], fold(part, jnp.max)))
        return tuple(new)

    low = jnp.full((8, block), -1e30, jnp.float32)
    best = lax.fori_loop(0, i, lambda j, b: score(j, b, False), (low, low))
    best = score(i, best, True)
    top = [jnp.max(value, axis=0, keepdims=True) for value in best]

    def weigh(j, carry):
        rows = rows_of(j, block)
        new = []
        for n, head in enumerate(heads):
            total, dots = carry[n]
            begin = 2 * width + n * HEAD_DIM
            weights = jnp.exp(score_ref[n, j] - top[n])
            slope = matmul(qkv_ref[rows, begin : begin + HEAD_DIM], gt_ref[head, own])
            score_ref[n, j] = weights
            slope_ref[n, j] = slope
            new.append((total + fold(weights, jnp.sum), dots + fold(weights * slope, jnp.sum)))
        return tuple(new)

    zero = jnp.zeros((8, block), jnp.float32)
    weighed = lax.fori_loop(0, i + 1, weigh, ((zero, zero), (zero, zero)))
    scales = [1.0 / jnp.sum(total, axis=0, keepdims=True) for total, _ in weighed]
    dots = [
        jnp.sum(dot, axis=0, keepdims=True) * scale for (_, dot), scale in zip(weighed, scales)
    ]

    def push(j, carry):
        rows = rows_of(j, block)
        new = []
        for n, head in enumerate(heads):
            out, q_grad = carry[n]
            probs = score_ref[n, j] * scales[n]
            low = probs.astype(jnp.bfloat16)
            score_grad = (probs * (slope_ref[n, j] - dots[n])).astype(jnp.bfloat16)
            k_total[rows, head] += matmul(score_grad, qkv_ref[own, head])
            v_total[rows, head] += matmul(low, grad_ref[own, head])
            out = out + matmul(vt_ref[head, rows], low)
            new.append((out, q_grad + matmul(kt_ref[head, rows], score_grad)))
        return tuple(new)

    zero = jnp.zeros((HEAD_DIM, block), jnp.float32)
    pushed = lax.fori_loop(0, i + 1, push, ((zero, zero), (zero, zero)))
    attended_ref[own, :] = jnp.concatenate([out for out, _ in pushed], axis=0).T.astype(
        jnp.bfloat16
    )
    q_grad = jnp.concatenate([grad for _, grad in pushed], axis=0).T * factor
    q_pre = turn(q_grad, cosine_ref[own, :], -sine_ref[own, :]).astype(jnp.bfloat16)
    pre_grad_ref[own, :width] = q_pre
    sums_ref[:, :width] += jnp.sum(q_pre.astype(jnp.float32), axis=0, keepdims=True)

    @pl.when(i == blocks - 1)
    def _():
        def finish(b, carry):
            rows = rows_of(b, chunk)
            k_pre = turn(k_total[rows, :], cosine_ref[rows, :], -sine_ref[rows, :])
            k_pre = k_pre.astype(jnp.bfloat16)
            v_pre = v_total[rows, :].astype(jnp.bfloat16)
            pre_grad_ref[rows, width : 2 * width] = k_pre
            pre_grad_ref[rows, 2 * width :] = v_pre
            both = jnp.concatenate([k_pre, v_pre], axis=1).astype(jnp.float32)
            return carry + jnp.sum(both, axis=0, keepdims=True)

        sums_ref[:, width:] = lax.fori_loop(
            0, chunks, finish, jnp.zeros((1, 2 * width), jnp.float32)
        )


def attention(qkv, out_grad, block=512):
    rows, width = qkv.shape[0], 2 * HEAD_DIM
    blocks = rows // block
    cosine, sine = rotary_tables(rows)
    return call(
        partial(attention_kernel, blocks, block),
        "attention",
        (blocks,),
        [whole(rows, 3 * width), whole(rows, width), whole(rows, width), whole(rows, width)],
        [whole(rows, width), whole(rows, 3 * width), whole(1, 3 * width)],
        [
            struct((rows, width), jnp.bfloat16),
            struct((rows, 3 * width), jnp.bfloat16),
            struct((1, 3 * width), jnp.float32),
        ],
        [pltpu.VMEM((width, rows), jnp.bfloat16)] * 4
        + [
            pltpu.VMEM((2, blocks, block, block), jnp.float32),
            pltpu.VMEM((2, blocks, block, block), jnp.float32),
            pltpu.VMEM((rows, width), jnp.float32),
            pltpu.VMEM((rows, width), jnp.float32),
        ],
        flops=28 * 10**9,
        nbytes=rows * width * 16,
    )(qkv, out_grad, jnp.asarray(cosine), jnp.asarray(sine))


def weight_grad_kernel(sources, place_ref, *refs):
    pairs = [refs[2 * n : 2 * n + 2] for n in range(sources)]
    outs = refs[2 * sources :]
    parts = []
    for left_ref, right_ref in pairs:
        if len(right_ref.shape) == 4:
            size = right_ref.shape[2]
            part = 0.0
            for b in range(right_ref.shape[0]):
                rows = slice(b * size, (b + 1) * size)
                part = part + contract_rows(left_ref[rows, :], right_ref[b, 0])
        else:
            part = contract_rows(left_ref[...], right_ref[...])
        parts.append(part.astype(jnp.bfloat16))
    for n, out_ref in enumerate(outs):

        @pl.when(pl.program_id(0) == n)
        def _(out_ref=out_ref):
            start = 0
            for part in parts:
                out_ref[start : start + part.shape[0], :] = part
                start += part.shape[0]


def weight_grad(pairs, place, count):
    cols = D // count
    rows = pairs[0][0].shape[0]
    height = sum(left.shape[1] for left, _ in pairs)

    def at(n, place_ref):
        return lax.rem(place_ref[0] + n, count)

    in_specs, operands = [], []
    for left, right in pairs:
        in_specs.append(pl.BlockSpec(left.shape, lambda n, p: (0, 0)))
        if right.ndim == 4:
            row_blocks, _, row_count, width = right.shape
            per = width // cols
            in_specs.append(
                pl.BlockSpec(
                    (row_blocks, 1, row_count, cols),
                    lambda n, p, per=per: (0, at(n, p) // per, 0, at(n, p) % per),
                )
            )
        else:
            in_specs.append(pl.BlockSpec((rows, cols), lambda n, p: (0, at(n, p))))
        operands += [left, right]
    return pl.pallas_call(
        partial(weight_grad_kernel, len(pairs)),
        grid_spec=pltpu.PrefetchScalarGridSpec(
            num_scalar_prefetch=1,
            grid=(count,),
            in_specs=in_specs,
            out_specs=[pl.BlockSpec((height, cols), lambda n, p: (0, 0))] * count,
        ),
        out_shape=[struct((height, cols), jnp.bfloat16)] * count,
        compiler_params=pltpu.CompilerParams(vmem_limit_bytes=VMEM_LIMIT),
        cost_estimate=pl.CostEstimate(
            flops=4 * rows * height * D, bytes_accessed=4 * rows * D, transcendentals=0
        ),
        name="weight_grad",
    )(place.reshape(1), *operands)


def partial_sum_kernel(counts, cols, *refs):
    sides = len(counts)
    starts = refs[:sides]
    lefts = refs[sides : 2 * sides]
    refs = refs[2 * sides :]
    pieces = []
    for count in counts:
        pieces.append(refs[:count])
        refs = refs[count:]
    out_ref, refs = refs[0], refs[1:]
    weights, semaphores = refs[:sides], refs[sides:]

    @pl.when(pl.program_id(0) == 0)
    def _():
        for n in range(sides):
            fill(pieces[n], starts[n], weights[n], slice(*cols[n]), semaphores[n])

    width = out_ref.shape[3]
    for j in range(out_ref.shape[1]):
        rows = slice(j * width, (j + 1) * width)
        out = 0.0
        for left, weight in zip(lefts, weights):
            out = out + contract_cols(left[...], weight[rows, :])
        out_ref[0, j] = out.astype(jnp.bfloat16)


def partial_sum(sides, row_count, width, name, rows=512):
    total = sides[0][0].shape[0]
    lefts = [left for left, _, _ in sides]
    counts = [len(weight[0]) for _, weight, _ in sides]
    cols = [(start, start + left.shape[1]) for left, _, start in sides]
    pieces = [piece for _, weight, _ in sides for piece in weight[0]]
    depth = sum(left.shape[1] for left in lefts)
    return call(
        partial(partial_sum_kernel, counts, cols),
        name,
        (total // rows,),
        [SCALARS] * len(sides)
        + [band(rows, left.shape[1]) for left in lefts]
        + [ANY] * len(pieces),
        block_band(rows, row_count, D // width, width),
        struct((total // row_count, D // width, row_count, width), jnp.bfloat16),
        [pltpu.VMEM((D, left.shape[1]), jnp.bfloat16) for left in lefts]
        + [pltpu.SemaphoreType.DMA((count,)) for count in counts],
        flops=4 * total * depth * D,
        nbytes=4 * total * D,
    )(*[weight[1] for _, weight, _ in sides], *lefts, *pieces)


def gather_line_first(shard):
    rows = shard.shape[0]
    own_g, own_h = lax.axis_index("g"), lax.axis_index("h")
    split = shard.reshape(rows, 2, 2, -1).transpose(1, 2, 0, 3)
    same, cross = pick(split, own_g), pick(split, 1 - own_g)
    count, place = lax.axis_size(LINE), lax.axis_index(LINE)
    steps = [step for step in range(1, count) if step != 1] + [1]
    arrived = [same] + [shifted(cross if step % 2 else same, LINE, step) for step in steps]
    mine = [pick(piece, own_h) for piece in arrived]
    other = shifted(jnp.stack([pick(piece, 1 - own_h) for piece in arrived]), "h", 1)
    places = [(place - step) % count for step in [0] + steps]
    pieces = mine + [other[n] for n in range(count)]
    starts = [(2 * p + own_h) * rows for p in places] + [(2 * p + 1 - own_h) * rows for p in places]
    return pieces, jnp.stack(starts).astype(jnp.int32)


def gather_side_first(shard):
    rows = shard.shape[0]
    own_g, own_h = lax.axis_index("g"), lax.axis_index("h")
    split = shard.reshape(rows, 2, 2, -1)
    mine = pick(split, own_h, 2)
    other = shifted(pick(split, 1 - own_h, 2), "h", 1)
    pair = in_order(mine, other, own_h)
    same = jnp.concatenate([pick(part, own_g, 1) for part in pair], axis=0)
    cross = jnp.concatenate([pick(part, 1 - own_g, 1) for part in pair], axis=0)
    count, place = lax.axis_size(LINE), lax.axis_index(LINE)
    steps = [step for step in range(1, count) if step != 1] + [1]
    pieces = [same] + [shifted(cross if step % 2 else same, LINE, step) for step in steps]
    starts = [(place - step) % count * 2 * rows for step in [0] + steps]
    return pieces, jnp.stack(starts).astype(jnp.int32)


def scatter(parts):
    count = len(parts)
    own_g, own_h = lax.axis_index("g"), lax.axis_index("h")
    height, cols = parts[0].shape
    steps = [step for step in range(1, count) if step != 1] + [1]
    arrived = {step: shifted(parts[step], LINE, step) for step in steps}
    same, cross = parts[0].astype(jnp.float32), 0.0
    for step in range(1, count):
        if step % 2:
            cross = cross + arrived[step].astype(jnp.float32)
        else:
            same = same + arrived[step].astype(jnp.float32)

    def half(index):
        return [
            lax.dynamic_slice_in_dim(part, index * (cols // 2), cols // 2, 1)
            for part in (same, cross)
        ]

    other = shifted(jnp.stack(half(1 - own_h)).astype(jnp.bfloat16), "h", 1).astype(jnp.float32)
    first, second = [in_order(part, other[n], own_h) for n, part in enumerate(half(own_h))]
    low = [jnp.where(own_g == 0, a, b) for a, b in zip(first, second)]
    high = [jnp.where(own_g == 0, b, a) for a, b in zip(first, second)]
    return jnp.stack(low + high)


def reduce_by_permutes(blocks):
    _, _, rows, cols = blocks.shape
    value = blocks.reshape(2, 2, 2, 2, rows, cols)
    for axis, position in (("c", 3), ("m", 2), ("h", 1), ("g", 0)):
        index = lax.axis_index(axis)
        arrived = shifted(pick(value, 1 - index, position), axis, 1)
        value = pick(value, index, position).astype(jnp.float32) + arrived.astype(jnp.float32)
        if axis != "g":
            value = value.astype(jnp.bfloat16)
    return value


def gather_vectors(packed, shared):
    for axis in ("h", "g"):
        packed = jnp.stack(in_order(packed, shifted(packed, axis, 1), lax.axis_index(axis)))
    sequences, own_s = lax.axis_size("s"), lax.axis_index("s")
    table = jnp.zeros((sequences,) + packed.shape, packed.dtype)
    table = lax.dynamic_update_index_in_dim(table, packed, own_s, 0)
    for step in range(1, sequences):
        table = lax.dynamic_update_index_in_dim(
            table, shifted(packed, "s", step), (own_s - step) % sequences, 0
        )
    table = table.reshape(4 * sequences, -1)
    wide = table[:, :shared]
    for axis in ("c", "m"):
        wide = jnp.stack(in_order(wide, shifted(wide, axis, 1), lax.axis_index(axis)))
    return table, wide.reshape(4, 4 * sequences, shared)


def body(
    tokens,
    cotangent,
    ln_gain,
    ln_shift,
    w_query,
    b_query,
    w_key,
    b_key,
    w_value,
    b_value,
    w_dense,
    b_dense,
    w_fc1,
    b_fc1,
    w_fc2,
    b_fc2,
):
    row_count, feature_count = tokens.shape
    own_g, own_h = lax.axis_index("g"), lax.axis_index("h")
    own_n = lax.axis_index(NARROW)
    quarter = 2 * own_g + own_h
    wide = lax.axis_size(WIDE)
    count, place = lax.axis_size(LINE), lax.axis_index(LINE)
    weight_rows = w_fc1.shape[0]
    lanes = w_query.shape[1] // 4

    token_blocks = lax.all_gather(tokens, CUBE, axis=0, tiled=False)
    token_blocks = token_blocks.reshape(4, 4, row_count, feature_count)
    cot = lax.all_gather(cotangent, CUBE, axis=0, tiled=False)
    cot = cot.reshape(4, 4, row_count, feature_count)

    up_weight = gather_line_first(w_fc1)
    attention_shard = jnp.concatenate(
        [part.reshape(weight_rows, 4, lanes) for part in (w_query, w_key, w_value, w_dense.T)],
        axis=2,
    )
    head_weight = gather_side_first(attention_shard.reshape(weight_rows, -1))
    down_weight = gather_side_first(w_fc2.T)

    vectors = (ln_gain, ln_shift, b_query, b_key, b_value, b_dense, b_fc2, b_fc1)
    lengths = [vector.shape[0] for vector in vectors]
    table, shared = gather_vectors(jnp.concatenate(vectors), 2 * lengths[0])
    shared = shared.astype(jnp.float32)
    gain = shared[:, :, : lengths[0]].reshape(1, D)
    shift = shared[:, :, lengths[0] :].reshape(1, D)
    table = table.astype(jnp.float32)
    local, start = [], 0
    for length in lengths:
        local.append(table[:, start : start + length].reshape(-1))
        start += length

    def quarter_of(vector):
        return pick(vector.reshape(4, -1), quarter)

    qkv_bias = jnp.concatenate([quarter_of(vector) for vector in local[2:5]]).reshape(1, -1)
    up_bias = quarter_of(local[7]).reshape(1, -1)
    own_gain, out_bias = local[0], local[5] + local[6]

    normed, stats, up_low, up_slope = norm_up(token_blocks, gain, shift, up_bias, up_weight)
    qkv = project_heads(normed, qkv_bias, head_weight)
    grad_down = weight_grad([(up_low, cot)], place, count)
    attended_grad = attended_gradient(cot, head_weight, lanes, 3 * lanes)
    up_grad, up_sums = up_gradient(cot, up_slope, down_weight)
    grad_up = weight_grad([(up_grad, normed)], place, count)
    attended, qkv_grad, qkv_sums = attention(qkv, attended_grad)
    normed_grad = partial_sum(
        [(qkv_grad, head_weight, 0), (up_grad, up_weight, 0)],
        row_count,
        feature_count,
        "normed_gradient",
    )
    grad_heads = weight_grad([(qkv_grad, normed), (attended, cot)], place, count)
    branch = partial_sum(
        [(attended, head_weight, 3 * lanes), (up_low, down_weight, 0)],
        row_count,
        feature_count,
        "branch_sum",
    )

    local_x = tokens.astype(jnp.float32)
    branch_sum = lax.psum_scatter(
        branch.reshape(16, row_count, feature_count), CUBE, scatter_dimension=0, tiled=False
    ).astype(jnp.float32)
    output = (local_x + branch_sum + out_bias).astype(jnp.bfloat16)

    hidden = up_low.shape[1]
    grad_down = scatter(grad_down).reshape(4 * hidden, weight_rows)
    grad_up = scatter(grad_up).reshape(4 * hidden, weight_rows).T
    grad_heads = scatter(grad_heads).reshape(4, 4, lanes, weight_rows)
    grad_query, grad_key, grad_value = (
        grad_heads[:, n].reshape(4 * lanes, weight_rows).T for n in range(3)
    )
    grad_dense = grad_heads[:, 3].reshape(4 * lanes, weight_rows)

    standard_grad = reduce_by_permutes(normed_grad)
    own_stats = pick(stats.reshape(4, row_count, 128), quarter)
    row_mean, inverse_std = own_stats[:, :1], own_stats[:, 64:65]
    standard = (local_x - row_mean) * inverse_std
    scaled_grad = standard_grad * own_gain
    row_sums = lax.psum(
        (jnp.sum(scaled_grad, axis=1), jnp.sum(scaled_grad * standard, axis=1)), NARROW
    )
    input_grad = (
        scaled_grad - row_sums[0][:, None] / D - standard * (row_sums[1][:, None] / D)
    ) * inverse_std + cotangent.astype(jnp.float32)

    def spread(vector):
        placed = jnp.zeros((4, vector.shape[0]), jnp.float32)
        placed = lax.dynamic_update_index_in_dim(placed, vector, quarter, 0)
        return placed.reshape(wide, -1)

    terms = [
        jnp.sum(standard_grad * standard, axis=0).reshape(wide, -1),
        jnp.sum(standard_grad, axis=0).reshape(wide, -1),
        spread(qkv_sums[0, :lanes]),
        spread(qkv_sums[0, lanes : 2 * lanes]),
        spread(qkv_sums[0, 2 * lanes :]),
        jnp.sum(cotangent.astype(jnp.float32), axis=0).reshape(wide, -1),
        spread(up_sums[0]),
    ]
    vector_sums = jnp.sum(lax.all_to_all(jnp.concatenate(terms, axis=1), WIDE, 0, 0), axis=0)
    vector_grads, start = [], 0
    for term in terms:
        vector_grads.append(vector_sums[start : start + term.shape[1]])
        start += term.shape[1]
    return (
        output,
        input_grad,
        vector_grads[0],
        vector_grads[1],
        grad_query,
        vector_grads[2],
        grad_key,
        vector_grads[3],
        grad_value,
        vector_grads[4],
        grad_dense,
        vector_grads[5],
        grad_up,
        vector_grads[6],
        grad_down,
        vector_grads[5],
    )


def solution(mesh):
    wide = mesh.shape["wide"]
    inner = Mesh(mesh.devices.reshape(wide // 4, 2, 2, 2, 2), ("s", "g", "h", "m", "c"))
    acts = P(WIDE, NARROW)
    vector = P(NARROW + WIDE)
    by_rows = P(WIDE, NARROW)
    by_cols = P(NARROW, WIDE)
    specs = (
        (acts, acts, vector, vector)
        + (by_rows, vector) * 3
        + (by_cols, vector, by_rows, vector, by_cols, vector)
    )
    return jax.shard_map(body, mesh=inner, in_specs=specs, out_specs=specs, check_vma=False)
```

time: 704 us -> 530 us (0.75)
  local copies, waits for them, and re-layouts: 139 us -> 41 us
  blocking collectives: 90.4 us -> 5.73 us
  matrix products: 83.2 us -> 0 us
  waiting for transfers between devices: 159 us -> 230 us
  Pallas kernels: 85.6 us -> 129 us
  other arithmetic: 25.8 us -> 15.3 us
    dot_general x9 -> x0, matrix products: 83.2 us -> none  [the longest x4 30.4 us: contract_rows(): lax.dot_general(left_side, right_side, (((0,), (0,)), ((), ())), preferre...]
    psum x1, blocking collectives: 55.2 us -> 5.73 us  [body(): lax.psum((jnp.sum(scaled_grad, axis=1), jnp.sum(scaled_grad * standard, a...]
    ppermute x25 -> x33, waiting for transfers between devices: 158 us -> 206 us  [shifted(): lax.ppermute(value, axis, [(source, (source + step) % count) for source i...]
    reshape x10 -> x6, local copies, waits for them, and re-layouts: 50.9 us -> 3.86 us  [the longest x1 1.81 us: body(): grad_up = scatter(grad_up).reshape(4 * hidden, weight_rows).T]
    pallas_call x2 -> x10, Pallas kernels: 85.6 us -> 129 us  [the longest x3 29.2 us: weight_grad(): pl.pallas_call(partial(weight_grad_kernel, len(pairs)), grid_spec=pltpu.P...]
    unnamed x1 -> x0, blocking collectives: 35.2 us -> none
    all_gather x2, waiting for transfers between devices: 0.02 us -> 23.3 us  [the longest x1 23.3 us: body(): cot = lax.all_gather(cotangent, CUBE, axis=0, tiled=False)]
    transpose x2 -> x0, local copies, waits for them, and re-layouts: 17.2 us -> none  [summed_blocks(): blocks = blocks.transpose(0, 2, 1, 3).reshape(16, row_count, feature_count)]
  transfers between devices with their start and end apart: 29 -> 37, of which waited for: 15 -> 16; matrix products, arithmetic and copies ran while one was open for 26% -> 9% of each run, Pallas kernels for 0% -> 22%
where the time goes in v2:
time: 530 us; the launch traced here: 528 us
  waiting for transfers between devices  230 us (43%)
  Pallas kernels  129 us (24%)
  starting transfers between devices  92.2 us (17%)
  local copies, waits for them, and re-layouts  41 us (8%)
  other arithmetic  15.3 us (3%)
  between operations  14.7 us (3%)
  blocking collectives  5.73 us (1%)
    ppermute x33, waiting for transfers between devices, shifted(): lax.ppermute(value, axis, [(source, (source + step) % count) for source i...  206 us
    ppermute x33, starting transfers between devices, shifted(): lax.ppermute(value, axis, [(source, (source + step) % count) for source i...  86.8 us
    pallas_call x3, Pallas kernels, weight_grad(): pl.pallas_call(partial(weight_grad_kernel, len(pairs)), grid_spec=pltpu.P...  29.2 us
    pallas_call x1, Pallas kernels, attention(): call(partial(attention_kernel, blocks, block), 'attention', (blocks,), [w...  28.2 us
    pallas_call x2, Pallas kernels, partial_sum(): call(partial(partial_sum_kernel, counts, cols), name, (total // rows,), [...  28 us
    all_gather x1, waiting for transfers between devices, body(): cot = lax.all_gather(cotangent, CUBE, axis=0, tiled=False)  23.3 us
    dynamic_slice x14, local copies, waits for them, and re-layouts, pick(): return lax.dynamic_index_in_dim(blocks, index, axis, keepdims=False)  18.8 us
    pallas_call x1, Pallas kernels, norm_up(): call(partial(norm_up_kernel, len(pieces)), 'norm_up', (total // rows,), [...  15.4 us
  transfers between devices with their start and end apart: 37, of which 16 were waited for; matrix products, arithmetic and copies ran while one was open for 9% of the time, Pallas kernels for 22%

profile of v2, /device:TPU:0, one launch (start us, length us, event | category | flops | bytes accessed | tf_op | source)
XLA Modules:
  0.0 528.5 jit_solution(578843498404337571)
XLA Ops:
  11.4 5.0 collective-permute-start.6
  24.3 3.5 collective-permute-start.1
  30.1 36.3 %collective-permute-done.1 = bf16[2,704]{1,0:T(2,128)(2,1)S(1)} collective-permute-done((bf16[2,704]{1,0:T(2,128)(2,1)S(1)}, bf16[2,704]{1,0:T(2,128)(2,1)S(1)}, u32[]{:S(2)}, u32[]{:S(2)}) %collective-permute-start.1) | collective-permute-done | bytes 2848 | tf_op jit(solution)/shard_map/ppermute | solution.py:46
  66.5 4.4 collective-permute-start.2
  74.6 3.0 collective-permute-done.4
  77.6 2.8 collective-permute-start.13
  81.9 1.8 constant_dynamic-slice_fusion.11
  83.6 1.8 constant_dynamic-slice_fusion.10
  87.4 5.7 %collective-permute-done.13 = bf16[256,2,512]{2,0,1:T(8,128)(2,1)S(1)} collective-permute-done((bf16[256,2,512]{2,0,1:T(8,128)(2,1)S(1)}, bf16[256,2,512]{2,0,1:T(8,128)(2,1)S(1)}, u32[]{:S(2)}, u32[]{:S(2)}) %collective-permute-start.13) | collective-permute-done | bytes 524320 | tf_op jit(solution)/shard_map/ppermute | solution.py:46
  93.5 2.1 collective-permute-start.15
  96.3 3.3 collective-permute-start.11
  99.7 14.8 %collective-permute-done.8 = bf16[4,256,512]{2,1,0:T(8,128)(2,1)S(1)} collective-permute-done((bf16[4,256,512]{2,1,0:T(8,128)(2,1)S(1)}, bf16[4,256,512]{2,1,0:T(8,128)(2,1)S(1)}, u32[]{:S(2)}, u32[]{:S(2)}) %collective-permute-start.8) | collective-permute-done | bytes 1048608 | tf_op jit(solution)/shard_map/ppermute | solution.py:46
  114.5 1.8 collective-permute-start.10
  117.3 15.4 %norm_up.1 = (bf16[2048,2048]{1,0:T(8,128)(2,1)}, f32[2048,128]{1,0:T(8,128)}, bf16[2048,512]{1,0:T(8,128)(2,1)}, f32[2048,512]{1,0:T(8,128)}) custom-call(s32[8]{0:T(128)} %stack.184.starts_ref.refs_1_, bf16[4,4,512,512]{3,2,1,0:T(8,128)(2,1)} %bitcast.295, f32[1,2048]{1,0:T(1,128)} %reshape.160.gain_ref, f32[1,2048]{1,0:T(1,128)} %reshape.161.shift_ref, ...), custom_call_target="tpu_custom_call" | custom-call | flops 12884901888 | bytes 25165824 | tf_op jit(solution)/shard_map/norm_up/pallas_call | solution.py:164
  132.8 43.6 %collective-permute-done.10.refs_1_.refs_5_ = bf16[512,512]{1,0:T(8,128)(2,1)} collective-permute-done((bf16[512,512]{1,0:T(8,128)(2,1)S(1)}, bf16[512,512]{1,0:T(8,128)(2,1)}, u32[]{:S(2)}, u32[]{:S(2)}) %collective-permute-start.10) | collective-permute-done | bytes 524320 | tf_op jit(solution)/shard_map/ppermute | solution.py:46
  176.4 3.5 collective-permute-start.14
  179.9 23.3 %all-gather.7.cloned.1.call-done = bf16[8192,512]{1,0:T(8,128)(2,1)} async-done(((bf16[512,512]{1,0:T(8,128)(2,1)}), bf16[8192,512]{1,0:T(8,128)(2,1)}) %all-gather.7.cloned.1.call-update) | async-done | bytes 8388624 | tf_op jit(solution)/shard_map/all_gather | solution.py:677
  203.2 7.5 %attended_gradient.1.grad_ref = bf16[2048,128]{1,0:T(8,128)(2,1)} custom-call(s32[4]{0:T(128)} %pad_add_fusion.starts_ref.refs_0_.refs_1_, bf16[4,4,512,512]{3,2,1,0:T(8,128)(2,1)} %bitcast.291, bf16[512,512]{1,0:T(8,128)(2,1)} %copy-done.5, bf16[512,512]{1,0:T(8,128)(2,1)} %collective-permute-done.10.refs_1_.refs_5_, ...), custom_call_target="tpu_custom_call" | custom-call | flops 4294967296 | bytes 16777216 | tf_op jit(solution)/shard_map/attended_gradient/pallas_call | solution.py:242
  210.7 10.4 %project_heads.1.qkv_ref = bf16[2048,384]{1,0:T(8,128)(2,1)} custom-call(s32[4]{0:T(128)} %pad_add_fusion.starts_ref.refs_0_.refs_1_, bf16[2048,2048]{1,0:T(8,128)(2,1)} %get-tuple-element.37.normed_ref.refs_1_, f32[1,384]{1,0:T(1,128)} %reshape.163.bias_ref, f32[2048,128]{1,0:T(8,128)} %constant.255.clone.cosine_ref, f32[2048,128]{1,0:T(8,128)} %constant.256.clone.sine_ref, ...), custom_call_target="tpu_custom_call" | custom-call | flops 6442450944 | bytes 16777216 | tf_op jit(solution)/shard_map/project_heads/pallas_call | solution.py:208
  221.1 28.2 %attention.1 = (bf16[2048,128]{1,0:T(8,128)(2,1)}, bf16[2048,384]{1,0:T(8,128)(2,1)}, f32[1,384]{1,0:T(1,128)}) custom-call(bf16[2048,384]{1,0:T(8,128)(2,1)} %project_heads.1.qkv_ref, bf16[2048,128]{1,0:T(8,128)(2,1)} %attended_gradient.1.grad_ref, f32[2048,128]{1,0:T(8,128)} %constant.255.clone.cosine_ref, f32[2048,128]{1,0:T(8,128)} %constant.256.clone.sine_ref), custom_call_target="tpu_custom_call" | custom-call | flops 28000000000 | bytes 4194304 | tf_op jit(solution)/shard_map/attention/pallas_call | solution.py:425
  250.4 12.6 %branch_sum.1 = bf16[4,4,512,512]{3,2,1,0:T(8,128)(2,1)} custom-call(s32[4]{0:T(128)} %pad_add_fusion.starts_ref.refs_0_.refs_1_, s32[4]{0:T(128)} %pad_add_fusion.starts_ref.refs_0_.refs_1_, bf16[2048,128]{1,0:T(8,128)(2,1)} %get-tuple-element.38.refs_2_, bf16[2048,512]{1,0:T(8,128)(2,1)} %get-tuple-element.39.refs_3_.refs_0_, bf16[512,512]{1,0:T(8,128)(2,1)} %copy-done.5, ...), custom_call_target="tpu_custom_call" | custom-call | flops 10737418240 | bytes 16777216 | tf_op jit(solution)/shard_map/branch_sum/pallas_call | solution.py:545
  263.1 10.5 %up_gradient.1 = (bf16[2048,512]{1,0:T(8,128)(2,1)}, f32[1,512]{1,0:T(1,128)}) custom-call(s32[4]{0:T(128)} %pad_add_fusion.starts_ref.refs_0_.refs_1_, bf16[4,4,512,512]{3,2,1,0:T(8,128)(2,1)} %bitcast.292, f32[2048,512]{1,0:T(8,128)} %get-tuple-element.41.slope_ref, bf16[512,512]{1,0:T(8,128)(2,1)} %copy-done.6, bf16[512,512]{1,0:T(8,128)(2,1)} %copy-done.29, ...), custom_call_target="tpu_custom_call" | custom-call | flops 8589934592 | bytes 16777216 | tf_op jit(solution)/shard_map/up_gradient/pallas_call | solution.py:277
  273.6 15.4 %normed_gradient.1 = bf16[4,4,512,512]{3,2,1,0:T(8,128)(2,1)} custom-call(s32[4]{0:T(128)} %pad_add_fusion.starts_ref.refs_0_.refs_1_, s32[8]{0:T(128)} %stack.184.starts_ref.refs_1_, bf16[2048,384]{1,0:T(8,128)(2,1)} %get-tuple-element.40.refs_2_.refs_0_, bf16[2048,512]{1,0:T(8,128)(2,1)} %get-tuple-element.42.refs_3_.refs_0_, bf16[512,512]{1,0:T(8,128)(2,1)} %copy-done.5, ...), custom_call_target="tpu_custom_call" | custom-call | flops 15032385536 | bytes 16777216 | tf_op jit(solution)/shard_map/normed_gradient/pallas_call | solution.py:545
  289.0 6.4 %constant_dynamic-slice_fusion.2 = (bf16[2,2,2,1,512,512]{5,4,3,2,1,0:T(8,128)(2,1)}, bf16[2,2,2,1,512,512]{5,4,3,2,1,0:T(8,128)(2,1)S(1)}) fusion(bf16[2,2,2,2,512,512]{5,4,3,2,1,0:T(8,128)(2,1)} %bitcast.259, s32[]{:T(128)S(6)} %select_n.340, s32[]{:T(128)S(6)} %select_n.341), kind=kLoop, calls=%fused_computation.110 | loop fusion | bytes 16777224 | tf_op jit(solution)/shard_map/jit(dynamic_index_in_dim)/dynamic_slice | solution.py:41
  295.4 2.4 copy.100
  298.2 9.3 %weight_grad.5 = (bf16[512,512]{1,0:T(8,128)(2,1)}, bf16[512,512]{1,0:T(8,128)(2,1)}, bf16[512,512]{1,0:T(8,128)(2,1)}, bf16[512,512]{1,0:T(8,128)(2,1)}) custom-call(s32[1]{0:T(128)} %bitcast.77.place_ref, bf16[2048,512]{1,0:T(8,128)(2,1)} %get-tuple-element.39.refs_3_.refs_0_, bf16[4,4,512,512]{3,2,1,0:T(8,128)(2,1)} %bitcast.293), custom_call_target="tpu_custom_call" | custom-call | flops 8589934592 | bytes 16777216 | tf_op jit(solution)/shard_map/weight_grad/pallas_call | solution.py:495
  308.9 2.4 collective-permute-start.31
  311.4 9.3 %weight_grad.4 = (bf16[512,512]{1,0:T(8,128)(2,1)}, bf16[512,512]{1,0:T(8,128)(2,1)}, bf16[512,512]{1,0:T(8,128)(2,1)}, bf16[512,512]{1,0:T(8,128)(2,1)}) custom-call(s32[1]{0:T(128)} %bitcast.77.place_ref, bf16[2048,512]{1,0:T(8,128)(2,1)} %get-tuple-element.42.refs_3_.refs_0_, bf16[2048,2048]{1,0:T(8,128)(2,1)} %get-tuple-element.37.normed_ref.refs_1_), custom_call_target="tpu_custom_call" | custom-call | flops 8589934592 | bytes 16777216 | tf_op jit(solution)/shard_map/weight_grad/pallas_call | solution.py:495
  320.6 10.6 %weight_grad.3 = (bf16[512,512]{1,0:T(8,128)(2,1)}, bf16[512,512]{1,0:T(8,128)(2,1)}, bf16[512,512]{1,0:T(8,128)(2,1)}, bf16[512,512]{1,0:T(8,128)(2,1)}) custom-call(s32[1]{0:T(128)} %bitcast.77.place_ref, bf16[2048,384]{1,0:T(8,128)(2,1)} %get-tuple-element.40.refs_2_.refs_0_, bf16[2048,2048]{1,0:T(8,128)(2,1)} %get-tuple-element.37.normed_ref.refs_1_, ...), custom_call_target="tpu_custom_call" | custom-call | flops 8589934592 | bytes 16777216 | tf_op jit(solution)/shard_map/weight_grad/pallas_call | solution.py:495
  331.3 2.9 collective-permute-start.25
  335.8 14.5 %collective-permute-done.31 = bf16[512,512]{1,0:T(8,128)(2,1)S(1)} collective-permute-done((bf16[512,512]{1,0:T(8,128)(2,1)}, bf16[512,512]{1,0:T(8,128)(2,1)S(1)}, u32[]{:S(2)}, u32[]{:S(2)}) %collective-permute-start.31) | collective-permute-done | bytes 524320 | tf_op jit(solution)/shard_map/ppermute | solution.py:46
  350.4 9.3 %collective-permute-done.29 = bf16[512,512]{1,0:T(8,128)(2,1)S(1)} collective-permute-done((bf16[512,512]{1,0:T(8,128)(2,1)}, bf16[512,512]{1,0:T(8,128)(2,1)S(1)}, u32[]{:S(2)}, u32[]{:S(2)}) %collective-permute-start.29) | collective-permute-done | bytes 524320 | tf_op jit(solution)/shard_map/ppermute | solution.py:46
  359.8 3.5 fusion
  363.5 30.9 %collective-permute-start.18 = (bf16[2,2,512,512]{3,2,0,1:T(8,128)(2,1)S(1)}, bf16[2,2,512,512]{3,2,0,1:T(8,128)(2,1)S(1)}, u32[]{:S(2)}, u32[]{:S(2)}) collective-permute-start(bf16[2,2,512,512]{3,2,0,1:T(8,128)(2,1)S(1)} %dynamic-slice_bitcast_fusion), channel_id=1, source_target_pairs={{0,2},{2,0},{1,3},{3,1},{4,6},{6,4},{5,7},{7,5},{8,10},{10,8},{9,1... | collective-permute-start | bytes 6291464 | tf_op jit(solution)/shard_map/ppermute | solution.py:46
  395.5 3.3 collective-permute-start.23
  398.8 9.5 %collective-permute-start.32 = (bf16[2,512,256]{2,1,0:T(8,128)(2,1)S(1)}, bf16[2,512,256]{2,1,0:T(8,128)(2,1)S(1)}, u32[]{:S(2)}, u32[]{:S(2)}) collective-permute-start(bf16[2,512,256]{2,1,0:T(8,128)(2,1)S(1)} %pad_maximum_fusion.11), channel_id=1, source_target_pairs={{0,4},{4,0},{1,5},{5,1},{2,6},{6,2},{3,7},{7,3},{8,12},{12,8},{9,1... | collective-permute-start | bytes 1572872 | tf_op jit(solution)/shard_map/ppermute | solution.py:46
  408.6 28.5 %collective-permute-done.21 = bf16[512,512]{1,0:T(8,128)(2,1)S(1)} collective-permute-done((bf16[512,512]{1,0:T(8,128)(2,1)}, bf16[512,512]{1,0:T(8,128)(2,1)S(1)}, u32[]{:S(2)}, u32[]{:S(2)}) %collective-permute-start.21) | collective-permute-done | bytes 524320 | tf_op jit(solution)/shard_map/ppermute | solution.py:46
  438.2 8.2 %collective-permute-done.23 = bf16[512,512]{1,0:T(8,128)(2,1)S(1)} collective-permute-done((bf16[512,512]{1,0:T(8,128)(2,1)S(1)}, bf16[512,512]{1,0:T(8,128)(2,1)S(1)}, u32[]{:S(2)}, u32[]{:S(2)}) %collective-permute-start.23) | collective-permute-done | bytes 524320 | tf_op jit(solution)/shard_map/ppermute | solution.py:46
  447.4 2.1 collective-permute-start.19
  450.4 11.2 %collective-permute-done.24 = bf16[2,512,256]{2,1,0:T(8,128)(2,1)S(1)} collective-permute-done((bf16[2,512,256]{2,1,0:T(8,128)(2,1)S(1)}, bf16[2,512,256]{2,1,0:T(8,128)(2,1)S(1)}, u32[]{:S(2)}, u32[]{:S(2)}) %collective-permute-start.24) | collective-permute-done | bytes 524320 | tf_op jit(solution)/shard_map/ppermute | solution.py:46
  463.7 19.6 %collective-permute-done.19 = bf16[2,512,512]{2,1,0:T(8,128)(2,1)S(1)} collective-permute-done((bf16[2,512,512]{2,1,0:T(8,128)(2,1)S(1)}, bf16[2,512,512]{2,1,0:T(8,128)(2,1)S(1)}, u32[]{:S(2)}, u32[]{:S(2)}) %collective-permute-start.19) | collective-permute-done | bytes 1048608 | tf_op jit(solution)/shard_map/ppermute | solution.py:46
  483.6 2.8 collective-permute-start.20
  489.1 8.4 %collective-permute-done.20 = bf16[512,512]{1,0:T(8,128)(2,1)S(1)} collective-permute-done((bf16[512,512]{1,0:T(8,128)(2,1)S(1)}, bf16[512,512]{1,0:T(8,128)(2,1)S(1)}, u32[]{:S(2)}, u32[]{:S(2)}) %collective-permute-start.20) | collective-permute-done | bytes 524320 | tf_op jit(solution)/shard_map/ppermute | solution.py:46
  498.3 5.7 %all-reduce = (f32[512]{0:T(512)S(1)}, f32[512]{0:T(512)S(1)}) all-reduce(f32[512]{0:T(512)S(1)} %get-tuple-element.59, f32[512]{0:T(512)S(1)} %get-tuple-element.60), channel_id=1, replica_groups=mesh['s'=2,'g'=2,'h'=2,'m'=2,'c'=2] {'m','c'}, use_global_device_ids=true, to_apply=%region_4.5 | all-reduce | flops 1024 | bytes 8192 | tf_op jit(solution)/shard_map/psum | solution.py:748
  504.0 2.8 convert_reduce_fusion
  507.6 5.3 all-to-all-start
  514.4 1.8 copy.86
  516.2 2.1 copy.90
  (234 shorter events, 44.3 us)
Async XLA Ops:
  7.2 110.2 %all-gather.5.cloned.1.call-start = ((), (), s32[]{:S(2)}) async-start(), calls=%async_computation.3 | async-start | bytes 8912896 | tf_op jit(solution)/shard_map/all_gather | solution.py:675
  7.9 195.3 %all-gather.7.cloned.1.call-start = ((), (), s32[]{:S(2)}) async-start(), calls=%async_computation.4 | async-start | bytes 8912896 | tf_op jit(solution)/shard_map/all_gather | solution.py:677
  8.7 495.3 %reduce-scatter.2.cloned.1.call-start = ((), (), s32[]{:S(2)}) async-start(), calls=%async_computation.2 | async-start | bytes 8912896 | tf_op jit(solution)/shard_map/reduce_scatter | solution.py:729
  10.4 10.1 %copy-start.12 = (bf16[256,512]{1,0:T(8,128)(2,1)S(1)}, bf16[256,512]{1,0:T(8,128)(2,1)}, u32[]{:S(2)}) copy-start(bf16[256,512]{1,0:T(8,128)(2,1)} %param.28) | copy-start | bytes 786436
  10.4 10.2 %copy-start.13 = (bf16[512,256]{1,0:T(8,128)(2,1)S(1)}, bf16[512,256]{1,0:T(8,128)(2,1)}, u32[]{:S(2)}) copy-start(bf16[512,256]{1,0:T(8,128)(2,1)} %param.30) | copy-start | bytes 786436
  11.4 70.4 %collective-permute-start.6 = (bf16[2,256,512]{2,1,0:T(8,128)(2,1)}, bf16[2,256,512]{2,1,0:T(8,128)(2,1)}, u32[]{:S(2)}, u32[]{:S(2)}) collective-permute-start(bf16[2,256,512]{2,1,0:T(8,128)(2,1)} %bitcast.29), channel_id=1, source_target_pairs={{0,24},{8,0},{16,8},{24,16},{1,25},{9,1},{17,9},{25,17},{2,26},{10... | collective-permute-start | bytes 1572872 | tf_op jit(solution)/shard_map/ppermute | solution.py:46
  16.5 67.1 %collective-permute-start.7 = (bf16[2,256,512]{2,1,0:T(8,128)(2,1)}, bf16[2,256,512]{2,1,0:T(8,128)(2,1)}, u32[]{:S(2)}, u32[]{:S(2)}) collective-permute-start(bf16[2,256,512]{2,1,0:T(8,128)(2,1)} %bitcast.29), channel_id=1, source_target_pairs={{0,8},{8,16},{16,24},{24,0},{1,9},{9,17},{17,25},{25,1},{2,10},{10... | collective-permute-start | bytes 1572872 | tf_op jit(solution)/shard_map/ppermute | solution.py:46
  17.5 67.9 %collective-permute-start.5 = (bf16[2,256,512]{2,1,0:T(8,128)(2,1)}, bf16[2,256,512]{2,1,0:T(8,128)(2,1)}, u32[]{:S(2)}, u32[]{:S(2)}) collective-permute-start(bf16[2,256,512]{2,1,0:T(8,128)(2,1)} %bitcast.26), channel_id=1, source_target_pairs={{0,16},{8,24},{16,0},{24,8},{1,17},{9,25},{17,1},{25,9},{2,18},{10... | collective-permute-start | bytes 1572872 | tf_op jit(solution)/shard_map/ppermute | solution.py:46
  18.7 5.6 %collective-permute-start = (bf16[704]{0:T(1024)(128)(2,1)S(1)}, bf16[704]{0:T(1024)(128)(2,1)S(1)}, u32[]{:S(2)}, u32[]{:S(2)}) collective-permute-start(bf16[704]{0:T(1024)(128)(2,1)S(1)} %concatenate.34), channel_id=1, source_target_pairs={{0,4},{4,0},{1,5},{5,1},{2,6},{6,2},{3,7},{7,3},{8,12},{12,8},{9,1... | collective-permute-start | bytes 4232 | tf_op jit(solution)/shard_map/ppermute | solution.py:46
  21.8 65.7 %collective-permute-start.9 = (bf16[256,2,512]{2,0,1:T(8,128)(2,1)}, bf16[256,2,512]{2,0,1:T(8,128)(2,1)S(1)}, u32[]{:S(2)}, u32[]{:S(2)}) collective-permute-start(bf16[256,2,512]{2,0,1:T(8,128)(2,1)} %bitcast.47), channel_id=1, source_target_pairs={{0,4},{4,0},{1,5},{5,1},{2,6},{6,2},{3,7},{7,3},{8,12},{12,8},{9,1... | collective-permute-start | bytes 1572872 | tf_op jit(solution)/shard_map/ppermute | solution.py:46
  24.3 42.1 %collective-permute-start.1 = (bf16[2,704]{1,0:T(2,128)(2,1)S(1)}, bf16[2,704]{1,0:T(2,128)(2,1)S(1)}, u32[]{:S(2)}, u32[]{:S(2)}) collective-permute-start(bf16[2,704]{1,0:T(2,128)(2,1)S(1)} %pad_maximum_fusion.15), channel_id=1, source_target_pairs={{0,8},{8,0},{1,9},{9,1},{2,10},{10,2},{3,11},{11,3},{4,12},{12,4},... | collective-permute-start | bytes 8456 | tf_op jit(solution)/shard_map/ppermute | solution.py:46
  66.5 6.1 %collective-permute-start.2 = (bf16[2,2,704]{2,1,0:T(2,128)(2,1)S(1)}, bf16[2,2,704]{2,1,0:T(2,128)(2,1)S(1)}, u32[]{:S(2)}, u32[]{:S(2)}) collective-permute-start(bf16[2,2,704]{2,1,0:T(2,128)(2,1)S(1)} %pad_maximum_fusion.13), channel_id=1, source_target_pairs={{0,16},{16,0},{1,17},{17,1},{2,18},{18,2},{3,19},{19,3},{4,20},{20... | collective-permute-start | bytes 16904 | tf_op jit(solution)/shard_map/ppermute | solution.py:46
  72.7 1.2 collective-permute-start.3
  73.9 3.7 collective-permute-start.4
  77.6 15.6 %collective-permute-start.13 = (bf16[256,2,512]{2,0,1:T(8,128)(2,1)S(1)}, bf16[256,2,512]{2,0,1:T(8,128)(2,1)S(1)}, u32[]{:S(2)}, u32[]{:S(2)}) collective-permute-start(bf16[256,2,512]{2,0,1:T(8,128)(2,1)S(1)} %bitcast.277), channel_id=1, source_target_pairs={{0,4},{4,0},{1,5},{5,1},{2,6},{6,2},{3,7},{7,3},{8,12},{12,8},{9,1... | collective-permute-start | bytes 1572872 | tf_op jit(solution)/shard_map/ppermute | solution.py:46
  87.3 27.2 %collective-permute-start.8 = (bf16[4,256,512]{2,1,0:T(8,128)(2,1)S(1)}, bf16[4,256,512]{2,1,0:T(8,128)(2,1)S(1)}, u32[]{:S(2)}, u32[]{:S(2)}) collective-permute-start(bf16[4,256,512]{2,1,0:T(8,128)(2,1)S(1)} %pad_maximum_fusion.3), channel_id=1, source_target_pairs={{0,4},{4,0},{1,5},{5,1},{2,6},{6,2},{3,7},{7,3},{8,12},{12,8},{9,1... | collective-permute-start | bytes 3145736 | tf_op jit(solution)/shard_map/ppermute | solution.py:46
  93.5 155.8 %collective-permute-start.15 = (bf16[512,512]{1,0:T(8,128)(2,1)S(1)}, bf16[512,512]{1,0:T(8,128)(2,1)S(1)}, u32[]{:S(2)}, u32[]{:S(2)}) collective-permute-start(bf16[512,512]{1,0:T(8,128)(2,1)S(1)} %pad_maximum_fusion.8), channel_id=1, source_target_pairs={{0,24},{8,0},{16,8},{24,16},{1,25},{9,1},{17,9},{25,17},{2,26},{10... | collective-permute-start | bytes 1572872 | tf_op jit(solution)/shard_map/ppermute | solution.py:46
  95.6 153.8 %collective-permute-start.16 = (bf16[512,512]{1,0:T(8,128)(2,1)S(1)}, bf16[512,512]{1,0:T(8,128)(2,1)S(1)}, u32[]{:S(2)}, u32[]{:S(2)}) collective-permute-start(bf16[512,512]{1,0:T(8,128)(2,1)S(1)} %pad_maximum_fusion.8), channel_id=1, source_target_pairs={{0,8},{8,16},{16,24},{24,0},{1,9},{9,17},{17,25},{25,1},{2,10},{10... | collective-permute-start | bytes 1572872 | tf_op jit(solution)/shard_map/ppermute | solution.py:46
  96.3 83.6 %collective-permute-start.11 = (bf16[512,512]{1,0:T(8,128)(2,1)S(1)}, bf16[512,512]{1,0:T(8,128)(2,1)}, u32[]{:S(2)}, u32[]{:S(2)}) collective-permute-start(bf16[512,512]{1,0:T(8,128)(2,1)S(1)} %pad_maximum_fusion.6), channel_id=1, source_target_pairs={{0,24},{8,0},{16,8},{24,16},{1,25},{9,1},{17,9},{25,17},{2,26},{10... | collective-permute-start | bytes 1572872 | tf_op jit(solution)/shard_map/ppermute | solution.py:46
  99.6 80.3 %collective-permute-start.12 = (bf16[512,512]{1,0:T(8,128)(2,1)S(1)}, bf16[512,512]{1,0:T(8,128)(2,1)}, u32[]{:S(2)}, u32[]{:S(2)}) collective-permute-start(bf16[512,512]{1,0:T(8,128)(2,1)S(1)} %pad_maximum_fusion.6), channel_id=1, source_target_pairs={{0,8},{8,16},{16,24},{24,0},{1,9},{9,17},{17,25},{25,1},{2,10},{10... | collective-permute-start | bytes 1572872 | tf_op jit(solution)/shard_map/ppermute | solution.py:46
  99.6 76.8 %copy-start.6 = (bf16[512,512]{1,0:T(8,128)(2,1)}, bf16[512,512]{1,0:T(8,128)(2,1)S(1)}, u32[]{:S(2)}) copy-start(bf16[512,512]{1,0:T(8,128)(2,1)S(1)} %pad_maximum_fusion.7.refs_8_.refs_0_) | copy-start | bytes 1572868
  99.7 33.1 %copy-start.5 = (bf16[512,512]{1,0:T(8,128)(2,1)}, bf16[512,512]{1,0:T(8,128)(2,1)S(1)}, u32[]{:S(2)}) copy-start(bf16[512,512]{1,0:T(8,128)(2,1)S(1)} %pad_maximum_fusion.5.refs_0_.refs_4_) | copy-start | bytes 1572868
  114.5 61.9 %collective-permute-start.10 = (bf16[512,512]{1,0:T(8,128)(2,1)S(1)}, bf16[512,512]{1,0:T(8,128)(2,1)}, u32[]{:S(2)}, u32[]{:S(2)}) collective-permute-start(bf16[512,512]{1,0:T(8,128)(2,1)S(1)} %pad_maximum_fusion.5.refs_0_.refs_4_), channel_id=1, source_target_pairs={{0,16},{8,24},{16,0},{24,8},{1,17},{9,25},{17,1},{25,9},{2,18},{10... | collective-permute-start | bytes 1572872 | tf_op jit(solution)/shard_map/ppermute | solution.py:46
  176.4 72.9 %collective-permute-start.14 = (bf16[512,512]{1,0:T(8,128)(2,1)S(1)}, bf16[512,512]{1,0:T(8,128)(2,1)S(1)}, u32[]{:S(2)}, u32[]{:S(2)}) collective-permute-start(bf16[512,512]{1,0:T(8,128)(2,1)S(1)} %pad_maximum_fusion.7.refs_8_.refs_0_), channel_id=1, source_target_pairs={{0,16},{8,24},{16,0},{24,8},{1,17},{9,25},{17,1},{25,9},{2,18},{10... | collective-permute-start | bytes 1572872 | tf_op jit(solution)/shard_map/ppermute | solution.py:46
  297.8 62.0 %collective-permute-start.17 = (bf16[2,2,2,512,512]{4,3,0,1,2:T(8,128)(2,1)}, bf16[2,2,2,512,512]{4,3,0,1,2:T(8,128)(2,1)}, u32[]{:S(2)}, u32[]{:S(2)}) collective-permute-start(bf16[2,2,2,512,512]{4,3,0,1,2:T(8,128)(2,1)} %bitcast.257), channel_id=1, source_target_pairs={{0,1},{1,0},{2,3},{3,2},{4,5},{5,4},{6,7},{7,6},{8,9},{9,8},{10,11... | collective-permute-start | bytes 12582920 | tf_op jit(solution)/shard_map/ppermute | solution.py:46
  307.5 28.2 %collective-permute-start.30 = (bf16[512,512]{1,0:T(8,128)(2,1)}, bf16[512,512]{1,0:T(8,128)(2,1)S(1)}, u32[]{:S(2)}, u32[]{:S(2)}) collective-permute-start(bf16[512,512]{1,0:T(8,128)(2,1)} %get-tuple-element.56), channel_id=1, source_target_pairs={{0,8},{8,16},{16,24},{24,0},{1,9},{9,17},{17,25},{25,1},{2,10},{10... | collective-permute-start | bytes 1572872 | tf_op jit(solution)/shard_map/ppermute | solution.py:46
  308.9 41.3 %collective-permute-start.31 = (bf16[512,512]{1,0:T(8,128)(2,1)}, bf16[512,512]{1,0:T(8,128)(2,1)S(1)}, u32[]{:S(2)}, u32[]{:S(2)}) collective-permute-start(bf16[512,512]{1,0:T(8,128)(2,1)} %get-tuple-element.57), channel_id=1, source_target_pairs={{0,24},{8,0},{16,8},{24,16},{1,25},{9,1},{17,9},{25,17},{2,26},{10... | collective-permute-start | bytes 1572872 | tf_op jit(solution)/shard_map/ppermute | solution.py:46
  320.6 14.7 %copy-start.14 = (f32[1,512]{1,0:T(1,128)S(1)}, f32[1,512]{1,0:T(1,128)}, u32[]{:S(2)}) copy-start(f32[1,512]{1,0:T(1,128)} %get-tuple-element.45) | copy-start | bytes 6148
  320.6 14.7 %copy-start.15 = (f32[1,384]{1,0:T(1,128)S(1)}, f32[1,384]{1,0:T(1,128)}, u32[]{:S(2)}) copy-start(f32[1,384]{1,0:T(1,128)} %get-tuple-element.44) | copy-start | bytes 4612
  331.2 28.4 %copy-start.9 = (bf16[512,512]{1,0:T(8,128)(2,1)S(1)}, bf16[512,512]{1,0:T(8,128)(2,1)}, u32[]{:S(2)}) copy-start(bf16[512,512]{1,0:T(8,128)(2,1)} %get-tuple-element.54) | copy-start | bytes 1572868
  331.2 28.4 %collective-permute-start.29 = (bf16[512,512]{1,0:T(8,128)(2,1)}, bf16[512,512]{1,0:T(8,128)(2,1)S(1)}, u32[]{:S(2)}, u32[]{:S(2)}) collective-permute-start(bf16[512,512]{1,0:T(8,128)(2,1)} %get-tuple-element.55), channel_id=1, source_target_pairs={{0,16},{8,24},{16,0},{24,8},{1,17},{9,25},{17,1},{25,9},{2,18},{10... | collective-permute-start | bytes 1572872 | tf_op jit(solution)/shard_map/ppermute | solution.py:46
  331.3 63.3 %collective-permute-start.25 = (bf16[512,512]{1,0:T(8,128)(2,1)}, bf16[512,512]{1,0:T(8,128)(2,1)S(1)}, u32[]{:S(2)}, u32[]{:S(2)}) collective-permute-start(bf16[512,512]{1,0:T(8,128)(2,1)} %get-tuple-element.51), channel_id=1, source_target_pairs={{0,16},{8,24},{16,0},{24,8},{1,17},{9,25},{17,1},{25,9},{2,18},{10... | collective-permute-start | bytes 1572872 | tf_op jit(solution)/shard_map/ppermute | solution.py:46
  335.8 59.1 %collective-permute-start.26 = (bf16[512,512]{1,0:T(8,128)(2,1)}, bf16[512,512]{1,0:T(8,128)(2,1)S(1)}, u32[]{:S(2)}, u32[]{:S(2)}) collective-permute-start(bf16[512,512]{1,0:T(8,128)(2,1)} %get-tuple-element.52), channel_id=1, source_target_pairs={{0,8},{8,16},{16,24},{24,0},{1,9},{9,17},{17,25},{25,1},{2,10},{10... | collective-permute-start | bytes 1572872 | tf_op jit(solution)/shard_map/ppermute | solution.py:46
  350.2 48.5 %collective-permute-start.27 = (bf16[512,512]{1,0:T(8,128)(2,1)}, bf16[512,512]{1,0:T(8,128)(2,1)S(1)}, u32[]{:S(2)}, u32[]{:S(2)}) collective-permute-start(bf16[512,512]{1,0:T(8,128)(2,1)} %get-tuple-element.53), channel_id=1, source_target_pairs={{0,24},{8,0},{16,8},{24,16},{1,25},{9,1},{17,9},{25,17},{2,26},{10... | collective-permute-start | bytes 1572872 | tf_op jit(solution)/shard_map/ppermute | solution.py:46
  359.6 77.5 %collective-permute-start.21 = (bf16[512,512]{1,0:T(8,128)(2,1)}, bf16[512,512]{1,0:T(8,128)(2,1)S(1)}, u32[]{:S(2)}, u32[]{:S(2)}) collective-permute-start(bf16[512,512]{1,0:T(8,128)(2,1)} %get-tuple-element.47), channel_id=1, source_target_pairs={{0,16},{8,24},{16,0},{24,8},{1,17},{9,25},{17,1},{25,9},{2,18},{10... | collective-permute-start | bytes 1572872 | tf_op jit(solution)/shard_map/ppermute | solution.py:46
  363.5 31.1 %copy-start.26 = (bf16[512,512]{1,0:T(8,128)(2,1)S(1)}, bf16[512,512]{1,0:T(8,128)(2,1)}, u32[]{:S(2)}) copy-start(bf16[512,512]{1,0:T(8,128)(2,1)} %get-tuple-element.48) | copy-start | bytes 1572868
  363.5 31.2 %copy-start.8 = (bf16[512,512]{1,0:T(8,128)(2,1)S(1)}, bf16[512,512]{1,0:T(8,128)(2,1)}, u32[]{:S(2)}) copy-start(bf16[512,512]{1,0:T(8,128)(2,1)} %get-tuple-element.50) | copy-start | bytes 1572868
  363.5 83.2 %collective-permute-start.18 = (bf16[2,2,512,512]{3,2,0,1:T(8,128)(2,1)S(1)}, bf16[2,2,512,512]{3,2,0,1:T(8,128)(2,1)S(1)}, u32[]{:S(2)}, u32[]{:S(2)}) collective-permute-start(bf16[2,2,512,512]{3,2,0,1:T(8,128)(2,1)S(1)} %dynamic-slice_bitcast_fusion), channel_id=1, source_target_pairs={{0,2},{2,0},{1,3},{3,1},{4,6},{6,4},{5,7},{7,5},{8,10},{10,8},{9,1... | collective-permute-start | bytes 6291464 | tf_op jit(solution)/shard_map/ppermute | solution.py:46
  394.6 43.6 %collective-permute-start.22 = (bf16[512,512]{1,0:T(8,128)(2,1)S(1)}, bf16[512,512]{1,0:T(8,128)(2,1)S(1)}, u32[]{:S(2)}, u32[]{:S(2)}) collective-permute-start(bf16[512,512]{1,0:T(8,128)(2,1)S(1)} %copy-done.26), channel_id=1, source_target_pairs={{0,8},{8,16},{16,24},{24,0},{1,9},{9,17},{17,25},{25,1},{2,10},{10... | collective-permute-start | bytes 1572872 | tf_op jit(solution)/shard_map/ppermute | solution.py:46
  394.8 43.1 %copy-start.7 = (bf16[512,512]{1,0:T(8,128)(2,1)S(1)}, bf16[512,512]{1,0:T(8,128)(2,1)}, u32[]{:S(2)}) copy-start(bf16[512,512]{1,0:T(8,128)(2,1)} %get-tuple-element.46) | copy-start | bytes 1572868
  395.5 50.9 %collective-permute-start.23 = (bf16[512,512]{1,0:T(8,128)(2,1)S(1)}, bf16[512,512]{1,0:T(8,128)(2,1)S(1)}, u32[]{:S(2)}, u32[]{:S(2)}) collective-permute-start(bf16[512,512]{1,0:T(8,128)(2,1)S(1)} %copy-done.25), channel_id=1, source_target_pairs={{0,24},{8,0},{16,8},{24,16},{1,25},{9,1},{17,9},{25,17},{2,26},{10... | collective-permute-start | bytes 1572872 | tf_op jit(solution)/shard_map/ppermute | solution.py:46
  398.8 50.7 %collective-permute-start.32 = (bf16[2,512,256]{2,1,0:T(8,128)(2,1)S(1)}, bf16[2,512,256]{2,1,0:T(8,128)(2,1)S(1)}, u32[]{:S(2)}, u32[]{:S(2)}) collective-permute-start(bf16[2,512,256]{2,1,0:T(8,128)(2,1)S(1)} %pad_maximum_fusion.11), channel_id=1, source_target_pairs={{0,4},{4,0},{1,5},{5,1},{2,6},{6,2},{3,7},{7,3},{8,12},{12,8},{9,1... | collective-permute-start | bytes 1572872 | tf_op jit(solution)/shard_map/ppermute | solution.py:46
  437.1 13.2 %collective-permute-start.28 = (bf16[2,512,256]{2,1,0:T(8,128)(2,1)S(1)}, bf16[2,512,256]{2,1,0:T(8,128)(2,1)S(1)}, u32[]{:S(2)}, u32[]{:S(2)}) collective-permute-start(bf16[2,512,256]{2,1,0:T(8,128)(2,1)S(1)} %pad_maximum_fusion.10), channel_id=1, source_target_pairs={{0,4},{4,0},{1,5},{5,1},{2,6},{6,2},{3,7},{7,3},{8,12},{12,8},{9,1... | collective-permute-start | bytes 1572872 | tf_op jit(solution)/shard_map/ppermute | solution.py:46
  446.6 14.9 %collective-permute-start.24 = (bf16[2,512,256]{2,1,0:T(8,128)(2,1)S(1)}, bf16[2,512,256]{2,1,0:T(8,128)(2,1)S(1)}, u32[]{:S(2)}, u32[]{:S(2)}) collective-permute-start(bf16[2,512,256]{2,1,0:T(8,128)(2,1)S(1)} %pad_maximum_fusion.9), channel_id=1, source_target_pairs={{0,4},{4,0},{1,5},{5,1},{2,6},{6,2},{3,7},{7,3},{8,12},{12,8},{9,1... | collective-permute-start | bytes 1572872 | tf_op jit(solution)/shard_map/ppermute | solution.py:46
  447.4 35.8 %collective-permute-start.19 = (bf16[2,512,512]{2,1,0:T(8,128)(2,1)S(1)}, bf16[2,512,512]{2,1,0:T(8,128)(2,1)S(1)}, u32[]{:S(2)}, u32[]{:S(2)}) collective-permute-start(bf16[2,512,512]{2,1,0:T(8,128)(2,1)S(1)} %dynamic-slice_bitcast_fusion.1), channel_id=1, source_target_pairs={{0,4},{4,0},{1,5},{5,1},{2,6},{6,2},{3,7},{7,3},{8,12},{12,8},{9,1... | collective-permute-start | bytes 3145736 | tf_op jit(solution)/shard_map/ppermute | solution.py:46
  483.6 13.9 %collective-permute-start.20 = (bf16[512,512]{1,0:T(8,128)(2,1)S(1)}, bf16[512,512]{1,0:T(8,128)(2,1)S(1)}, u32[]{:S(2)}, u32[]{:S(2)}) collective-permute-start(bf16[512,512]{1,0:T(8,128)(2,1)S(1)} %dynamic-slice_bitcast_fusion.2), channel_id=1, source_target_pairs={{0,8},{8,0},{1,9},{9,1},{2,10},{10,2},{3,11},{11,3},{4,12},{12,4},... | collective-permute-start | bytes 1572872 | tf_op jit(solution)/shard_map/ppermute | solution.py:46
  487.8 16.2 %copy-start.2 = (bf16[512,512]{1,0:T(8,128)(2,1)S(1)}, bf16[512,512]{1,0:T(8,128)(2,1)}, u32[]{:S(2)}) copy-start(bf16[512,512]{1,0:T(8,128)(2,1)} %param.21) | copy-start | bytes 1572868
  507.6 12.7 %all-to-all-start = ((f32[8,1,640]{2,1,0:T(1,128)}), f32[8,1,640]{2,1,0:T(1,128)S(1)}, u32[]{:S(2)}, u32[]{:S(2)}) async-start(f32[8,1,640]{2,1,0:T(1,128)} %all_to_all.6), calls=%async_computation.1 | async-start | bytes 40960 | tf_op jit(solution)/shard_map/all_to_all | solution.py:769
  (19 other events, 117.4 us)
Sparse Core Ops, SparseCore 0:
  9.6 80.6 all-gather.4
  91.9 111.2 all-gather.6
  263.2 147.9 reduce-scatter.1

commit v3 on v2

v3 whole, which is shorter than its diff:
```python
from functools import partial
import math

import jax
import jax.numpy as jnp
import numpy as np
from jax import lax
from jax.experimental import pallas as pl
from jax.experimental.pallas import tpu as pltpu
from jax.sharding import Mesh, PartitionSpec as P

D = 2048
HEAD_DIM = 64
ROT = 32
EPSILON = 1e-05
VMEM_LIMIT = 56 * 2**20
COST = 1

WIDE = ("s", "g", "h")
LINE = ("s", "g")
NARROW = ("m", "c")
CUBE = ("g", "h", "m", "c")


def matmul(left_side, right_side):
    return jnp.dot(left_side, right_side, preferred_element_type=jnp.float32)


def contract_rows(left_side, right_side):
    return lax.dot_general(
        left_side, right_side, (((0,), (0,)), ((), ())), preferred_element_type=jnp.float32
    )


def contract_cols(left_side, right_side):
    return lax.dot_general(
        left_side, right_side, (((1,), (1,)), ((), ())), preferred_element_type=jnp.float32
    )


def pick(blocks, index, axis=0):
    return lax.dynamic_index_in_dim(blocks, index, axis, keepdims=False)


def shifted(value, axis, step):
    count = lax.axis_size(axis)
    return lax.ppermute(value, axis, [(source, (source + step) % count) for source in range(count)])


def in_order(mine, other, index):
    return (jnp.where(index == 0, mine, other), jnp.where(index == 0, other, mine))


def call(
    kernel, name, grid, in_specs, out_specs, out_shape, scratch=(), flops=0, after=()
):
    skipped = len(after)

    def ordered(*refs):
        kernel(*refs[skipped:])

    run = pl.pallas_call(
        ordered,
        grid=grid,
        in_specs=[ANY] * skipped + list(in_specs),
        out_specs=out_specs,
        out_shape=out_shape,
        scratch_shapes=list(scratch),
        compiler_params=pltpu.CompilerParams(vmem_limit_bytes=VMEM_LIMIT),
        cost_estimate=pl.CostEstimate(flops=COST * flops // 1000, bytes_accessed=0, transcendentals=0),
        name=name,
    )
    return lambda *operands: run(*after, *operands)


def whole(*shape):
    return pl.BlockSpec(shape, lambda i: (0,) * len(shape))


def band(rows, cols):
    return pl.BlockSpec((rows, cols), lambda i: (i, 0))


ANY = pl.BlockSpec(memory_space=pl.ANY)
SCALARS = pl.BlockSpec(memory_space=pltpu.SMEM)


def struct(shape, dtype):
    return jax.ShapeDtypeStruct(shape, dtype)


def rotary_tables(rows):
    lane = np.arange(2 * HEAD_DIM) % HEAD_DIM
    pair = (lane % (ROT // 2)).astype(np.float32)
    inverse = np.exp(pair * np.float32(-2.0 * math.log(10000.0) / ROT)).astype(np.float32)
    phase = np.arange(rows, dtype=np.float32)[:, None] * inverse[None, :]
    turned = (lane < ROT)[None, :]
    sign = np.where(lane < ROT // 2, -1.0, 1.0)[None, :]
    cosine = np.where(turned, np.cos(phase), 1.0).astype(np.float32)
    sine = np.where(turned, np.sin(phase) * sign, 0.0).astype(np.float32)
    return (cosine, sine)


def turn(values, cosine, sine):
    lane = lax.broadcasted_iota(jnp.int32, values.shape, 1) % HEAD_DIM
    width = values.shape[1]
    half = ROT // 2
    partner = jnp.where(
        lane < half, pltpu.roll(values, width - half, 1), pltpu.roll(values, half, 1)
    )
    return values * cosine + partner * sine


def norm_up_kernel(
    tokens_ref, gain_ref, shift_ref, bias_ref, weight_ref, normed_ref, stats_ref, low_ref, slope_ref
):
    parts = [tokens_ref[0, j].astype(jnp.float32) for j in range(tokens_ref.shape[1])]
    rows, width = parts[0].shape
    total = sum(jnp.sum(part, axis=1, keepdims=True) for part in parts)
    squares = sum(jnp.sum(part * part, axis=1, keepdims=True) for part in parts)
    mean = total / D
    inverse_std = lax.rsqrt(squares / D - mean * mean + EPSILON)
    up_input = bias_ref[...]
    for j, part in enumerate(parts):
        cols = slice(j * width, (j + 1) * width)
        standard = (part - mean) * inverse_std
        normed = (standard * gain_ref[:, cols] + shift_ref[:, cols]).astype(jnp.bfloat16)
        normed_ref[:, cols] = normed
        up_input = up_input + matmul(normed, weight_rows_of(weight_ref, j * width, width))
    stats_ref[...] = jnp.concatenate(
        [jnp.broadcast_to(mean, (rows, 64)), jnp.broadcast_to(inverse_std, (rows, 64))], axis=1
    )
    root = math.sqrt(2.0 / math.pi)
    square = up_input * up_input
    bend = jnp.tanh(root * (up_input + 0.044715 * square * up_input))
    half = 0.5 * (1.0 + bend)
    low_ref[...] = (up_input * half).astype(jnp.bfloat16)
    slope_ref[...] = half + 0.5 * up_input * (1.0 - bend * bend) * (
        root * (1.0 + 3 * 0.044715 * square)
    )


class Weight:
    def __init__(self, array, rows, start, width):
        self.array, self.rows, self.width = array, rows, width
        self.spec = pl.BlockSpec(
            (array.shape[0], rows, width), lambda *_: (0, 0, start // width)
        )


def weight_rows_of(weight_ref, start, count):
    _, rows, width = weight_ref.shape
    return weight_ref[pl.ds(start // rows, count // rows)].reshape(count, width)


def norm_up(blocks, gain, shift, bias, weight, rows=256, after=()):
    row_blocks, col_blocks, row_count, width = blocks.shape
    total, hidden = row_blocks * row_count, bias.shape[1]
    per = row_count // rows
    spec = pl.BlockSpec((1, col_blocks, rows, width), lambda i: (i // per, 0, i % per, 0))
    return call(
        norm_up_kernel,
        "norm_up",
        (total // rows,),
        [spec]
        + [whole(1, D), whole(1, D), whole(1, hidden), weight.spec],
        [band(rows, D), band(rows, 128), band(rows, hidden), band(rows, hidden)],
        [
            struct((total, D), jnp.bfloat16),
            struct((total, 128), jnp.float32),
            struct((total, hidden), jnp.bfloat16),
            struct((total, hidden), jnp.float32),
        ],
        flops=6 * total * D * hidden,
        after=after,
    )(blocks, gain, shift, bias, weight.array)


def heads_kernel(normed_ref, bias_ref, cosine_ref, sine_ref, weight_ref, heads_ref):
    pre = matmul(normed_ref[...], weight_rows_of(weight_ref, 0, D)) + bias_ref[...]
    lanes = 2 * HEAD_DIM
    cosine, sine = cosine_ref[...], sine_ref[...]
    factor = 1.0 / math.sqrt(HEAD_DIM)
    heads_ref[:, :lanes] = (turn(pre[:, :lanes], cosine, sine) * factor).astype(jnp.bfloat16)
    heads_ref[:, lanes : 2 * lanes] = turn(pre[:, lanes : 2 * lanes], cosine, sine).astype(
        jnp.bfloat16
    )
    heads_ref[:, 2 * lanes :] = pre[:, 2 * lanes :].astype(jnp.bfloat16)


def project_heads(normed, bias, weight, rows=512, after=()):
    total, width = normed.shape[0], bias.shape[1]
    cosine, sine = rotary_tables(total)
    lanes = 2 * HEAD_DIM
    return call(
        heads_kernel,
        "project_heads",
        (total // rows,),
        [band(rows, D), whole(1, width), band(rows, lanes), band(rows, lanes)]
        + [weight.spec],
        band(rows, width),
        struct((total, width), jnp.bfloat16),
        flops=4 * total * D * width,
        after=after,
    )(normed, bias, jnp.asarray(cosine), jnp.asarray(sine), weight.array)


def cot_spec(cot, rows):
    row_count, width = cot.shape[-2:]
    per = row_count // rows
    return pl.BlockSpec(
        (2, 2, 1, 1, rows, width), lambda i: (0, 0, i // per % 2, i // per // 2, i % per, 0)
    )


def cot_product(cot_ref, weight_ref):
    width = cot_ref.shape[5]
    total = 0.0
    for j in range(4):
        part = cot_ref[j % 2, j // 2, 0, 0]
        total = total + matmul(part, weight_rows_of(weight_ref, j * width, width))
    return total


def out_grad_kernel(cot_ref, weight_ref, out_ref):
    out_ref[...] = cot_product(cot_ref, weight_ref).astype(jnp.bfloat16)


def attended_gradient(cot, weight, width, rows=512, after=()):
    total = 4 * cot.shape[4]
    return call(
        out_grad_kernel,
        "attended_gradient",
        (total // rows,),
        [cot_spec(cot, rows), weight.spec],
        band(rows, width),
        struct((total, width), jnp.bfloat16),
        flops=8 * total * D * width,
        after=after,
    )(cot, weight.array)


def up_grad_kernel(cot_ref, slope_ref, weight_ref, up_ref, sums_ref):
    @pl.when(pl.program_id(0) == 0)
    def _():
        sums_ref[...] = jnp.zeros_like(sums_ref)

    up = (cot_product(cot_ref, weight_ref) * slope_ref[...]).astype(jnp.bfloat16)
    up_ref[...] = up
    sums_ref[...] += jnp.sum(up.astype(jnp.float32), axis=0, keepdims=True)


def up_gradient(cot, slope, weight, rows=512, after=()):
    total, hidden = slope.shape
    return call(
        up_grad_kernel,
        "up_gradient",
        (total // rows,),
        [cot_spec(cot, rows), band(rows, hidden), weight.spec],
        [band(rows, hidden), whole(1, hidden)],
        [struct((total, hidden), jnp.bfloat16), struct((1, hidden), jnp.float32)],
        flops=4 * total * D * hidden,
        after=after,
    )(cot, slope, weight.array)


def rows_of(index, size):
    return pl.ds(pl.multiple_of(index * size, size), size)


def attention_kernel(
    blocks,
    block,
    qkv_ref,
    grad_ref,
    cosine_ref,
    sine_ref,
    attended_ref,
    pre_grad_ref,
    sums_ref,
    qt_ref,
    kt_ref,
    vt_ref,
    gt_ref,
    score_ref,
    slope_ref,
    k_total,
    v_total,
):
    i = pl.program_id(0)
    width = 2 * HEAD_DIM
    factor = 1.0 / math.sqrt(HEAD_DIM)
    heads = [slice(n * HEAD_DIM, (n + 1) * HEAD_DIM) for n in range(2)]
    chunk = 256
    chunks = qkv_ref.shape[0] // chunk

    @pl.when(i == 0)
    def _():
        def prepare(b, carry):
            rows = rows_of(b, chunk)
            for n, ref in enumerate((qt_ref, kt_ref, vt_ref)):
                ref[:, rows] = qkv_ref[rows, n * width : (n + 1) * width].T
            gt_ref[:, rows] = grad_ref[rows, :].T
            return carry

        lax.fori_loop(0, chunks, prepare, 0)
        k_total[...] = jnp.zeros_like(k_total)
        v_total[...] = jnp.zeros_like(v_total)
        sums_ref[...] = jnp.zeros_like(sums_ref)

    own = rows_of(i, block)
    causal = lax.broadcasted_iota(jnp.int32, (block, block), 0) <= lax.broadcasted_iota(
        jnp.int32, (block, block), 1
    )

    def fold(values, combine):
        return combine(values.reshape(block // 8, 8, block), axis=0)

    def score(j, best, diagonal):
        rows = rows_of(j, block)
        new = []
        for n, head in enumerate(heads):
            start = width + n * HEAD_DIM
            part = matmul(qkv_ref[rows, start : start + HEAD_DIM], qt_ref[head, own])
            if diagonal:
                part = jnp.where(causal, part, -1e30)
            score_ref[n, j] = part
            new.append(jnp.maximum(best[n], fold(part, jnp.max)))
        return tuple(new)

    low = jnp.full((8, block), -1e30, jnp.float32)
    best = lax.fori_loop(0, i, lambda j, b: score(j, b, False), (low, low))
    best = score(i, best, True)
    top = [jnp.max(value, axis=0, keepdims=True) for value in best]

    def weigh(j, carry):
        rows = rows_of(j, block)
        new = []
        for n, head in enumerate(heads):
            total, dots = carry[n]
            begin = 2 * width + n * HEAD_DIM
            weights = jnp.exp(score_ref[n, j] - top[n])
            slope = matmul(qkv_ref[rows, begin : begin + HEAD_DIM], gt_ref[head, own])
            score_ref[n, j] = weights
            slope_ref[n, j] = slope
            new.append((total + fold(weights, jnp.sum), dots + fold(weights * slope, jnp.sum)))
        return tuple(new)

    zero = jnp.zeros((8, block), jnp.float32)
    weighed = lax.fori_loop(0, i + 1, weigh, ((zero, zero), (zero, zero)))
    scales = [1.0 / jnp.sum(total, axis=0, keepdims=True) for total, _ in weighed]
    dots = [
        jnp.sum(dot, axis=0, keepdims=True) * scale for (_, dot), scale in zip(weighed, scales)
    ]

    def push(j, carry):
        rows = rows_of(j, block)
        new = []
        for n, head in enumerate(heads):
            out, q_grad = carry[n]
            probs = score_ref[n, j] * scales[n]
            low = probs.astype(jnp.bfloat16)
            score_grad = (probs * (slope_ref[n, j] - dots[n])).astype(jnp.bfloat16)
            k_total[rows, head] += matmul(score_grad, qkv_ref[own, head])
            v_total[rows, head] += matmul(low, grad_ref[own, head])
            out = out + matmul(vt_ref[head, rows], low)
            new.append((out, q_grad + matmul(kt_ref[head, rows], score_grad)))
        return tuple(new)

    zero = jnp.zeros((HEAD_DIM, block), jnp.float32)
    pushed = lax.fori_loop(0, i + 1, push, ((zero, zero), (zero, zero)))
    attended_ref[own, :] = jnp.concatenate([out for out, _ in pushed], axis=0).T.astype(
        jnp.bfloat16
    )
    q_grad = jnp.concatenate([grad for _, grad in pushed], axis=0).T * factor
    q_pre = turn(q_grad, cosine_ref[own, :], -sine_ref[own, :]).astype(jnp.bfloat16)
    pre_grad_ref[own, :width] = q_pre
    sums_ref[:, :width] += jnp.sum(q_pre.astype(jnp.float32), axis=0, keepdims=True)

    @pl.when(i == blocks - 1)
    def _():
        def finish(b, carry):
            rows = rows_of(b, chunk)
            k_pre = turn(k_total[rows, :], cosine_ref[rows, :], -sine_ref[rows, :])
            k_pre = k_pre.astype(jnp.bfloat16)
            v_pre = v_total[rows, :].astype(jnp.bfloat16)
            pre_grad_ref[rows, width : 2 * width] = k_pre
            pre_grad_ref[rows, 2 * width :] = v_pre
            both = jnp.concatenate([k_pre, v_pre], axis=1).astype(jnp.float32)
            return carry + jnp.sum(both, axis=0, keepdims=True)

        sums_ref[:, width:] = lax.fori_loop(
            0, chunks, finish, jnp.zeros((1, 2 * width), jnp.float32)
        )


def attention(qkv, out_grad, block=512, after=()):
    rows, width = qkv.shape[0], 2 * HEAD_DIM
    blocks = rows // block
    cosine, sine = rotary_tables(rows)
    return call(
        partial(attention_kernel, blocks, block),
        "attention",
        (blocks,),
        [whole(rows, 3 * width), whole(rows, width), whole(rows, width), whole(rows, width)],
        [whole(rows, width), whole(rows, 3 * width), whole(1, 3 * width)],
        [
            struct((rows, width), jnp.bfloat16),
            struct((rows, 3 * width), jnp.bfloat16),
            struct((1, 3 * width), jnp.float32),
        ],
        [pltpu.VMEM((width, rows), jnp.bfloat16)] * 4
        + [
            pltpu.VMEM((2, blocks, block, block), jnp.float32),
            pltpu.VMEM((2, blocks, block, block), jnp.float32),
            pltpu.VMEM((rows, width), jnp.float32),
            pltpu.VMEM((rows, width), jnp.float32),
        ],
        flops=28 * 10**9,
        after=after,
    )(qkv, out_grad, jnp.asarray(cosine), jnp.asarray(sine))


def weight_grad_kernel(riders, *refs):
    out_ref, refs = refs[-1], refs[:-1]
    if riders:
        height = out_ref.shape[1] - refs[0].shape[1]
        out_ref[:, height:, :] = refs[0][...]
        refs = refs[1:]
    cols = out_ref.shape[2]
    start = 0
    for left_ref, right_ref in zip(refs[::2], refs[1::2]):
        if len(right_ref.shape) == 6:
            size = right_ref.shape[4]
            part = 0.0
            for b in range(4):
                rows = slice(b * size, (b + 1) * size)
                part = part + contract_rows(left_ref[rows, :], right_ref[0, 0, b % 2, b // 2])
        else:
            part = contract_rows(left_ref[...], right_ref[...])
        part = part.astype(jnp.bfloat16)
        stop = start + part.shape[0]
        for n in range(out_ref.shape[0]):
            out_ref[n, start:stop, :] = part[:, n * cols : (n + 1) * cols]
        start = stop


def weight_grad(pairs, parts, rider=None, after=()):
    cols = D // parts
    per = parts // 4
    rows = pairs[0][0].shape[0]
    height = sum(left.shape[1] for left, _ in pairs)
    in_specs, operands = [], []
    if rider is not None:
        in_specs.append(pl.BlockSpec((per,) + rider.shape[1:], lambda i: (i, 0, 0)))
        operands.append(rider)
        height += rider.shape[1]
    for left, right in pairs:
        in_specs.append(whole(*left.shape))
        if right.ndim == 6:
            in_specs.append(
                pl.BlockSpec(
                    (1, 1, 2, 2, right.shape[4], D // 4), lambda i: (i % 2, i // 2, 0, 0, 0, 0)
                )
            )
        else:
            in_specs.append(pl.BlockSpec((rows, D // 4), lambda i: (0, i)))
        operands += [left, right]
    return call(
        partial(weight_grad_kernel, rider is not None),
        "weight_grad",
        (4,),
        in_specs,
        pl.BlockSpec((per, height, cols), lambda i: (i, 0, 0)),
        struct((parts, height, cols), jnp.bfloat16),
        flops=4 * rows * height * D,
        after=after,
    )(*operands)


def partial_sum_kernel(sides, core_ref, *refs):
    lefts, weights, outs = refs[:sides], refs[sides : 2 * sides], refs[2 * sides :]
    width = outs[0].shape[3]
    for m in range(2):
        for core, out_ref in zip((core_ref[0], 1 - core_ref[0]), outs):
            start = (2 * m + core) * width
            out = 0.0
            for left, weight in zip(lefts, weights):
                out = out + contract_cols(left[...], weight_rows_of(weight, start, width))
            out_ref[m, 0] = out.astype(jnp.bfloat16)


def partial_sum(sides, core, row_count, width, name, rows=512, after=()):
    total = sides[0][0].shape[0]
    per = row_count // rows
    lefts = [left for left, _ in sides]
    depth = sum(left.shape[1] for left in lefts)
    spec = pl.BlockSpec((2, 1, rows, width), lambda i: (0, i // per, i % per, 0))
    shape = struct((2, total // row_count, row_count, width), jnp.bfloat16)
    return call(
        partial(partial_sum_kernel, len(sides)),
        name,
        (total // rows,),
        [SCALARS]
        + [band(rows, left.shape[1]) for left in lefts]
        + [
            weight.spec for _, weight in sides
        ],
        [spec, spec],
        [shape, shape],
        flops=4 * total * depth * D,
        after=after,
    )(core, *lefts, *[weight.array for _, weight in sides])


def switch_specs(count, block):
    zeros = (0,) * (len(block) - 1)
    return [
        pl.BlockSpec(block, lambda k, j, p: (j + k * (count - 1 - j),) + zeros),
        pl.BlockSpec(block, lambda k, j, p: (j * k,) + zeros),
    ]


def prefetch_call(kernel, name, index, grid, in_specs, out_specs, out_shape, after=()):
    skipped = len(after)

    def ordered(index_ref, *refs):
        kernel(index_ref, *refs[skipped:])

    run = pl.pallas_call(
        ordered,
        grid_spec=pltpu.PrefetchScalarGridSpec(
            num_scalar_prefetch=1,
            grid=grid,
            in_specs=[ANY] * skipped + list(in_specs),
            out_specs=out_specs,
        ),
        out_shape=out_shape,
        compiler_params=pltpu.CompilerParams(vmem_limit_bytes=VMEM_LIMIT),
        cost_estimate=pl.CostEstimate(flops=0, bytes_accessed=0, transcendentals=0),
        name=name,
    )
    return lambda *operands: run(index.astype(jnp.int32).reshape(1), *after, *operands)


def column_specs(shards, turned, block):
    specs, width = [], 0
    for flip, shard in zip(turned, shards):
        height, cols = shard.shape
        if flip:
            specs.append(pl.BlockSpec((height // 4, cols), lambda *at: (block(*at), 0)))
            rows, width = cols, width + height // 4
        else:
            specs.append(pl.BlockSpec((height, cols // 4), lambda *at: (0, block(*at))))
            rows, width = height, width + cols // 4
    return specs, rows, width


def write_columns(turned, refs, store):
    start = 0
    for flip, ref in zip(turned, refs):
        part = ref[...].T if flip else ref[...]
        store(slice(start, start + part.shape[1]), part)
        start += part.shape[1]


def pack_kernel(turned, rows, riders, *refs):
    out_ref, refs = refs[-1], refs[:-1]
    if riders:
        rider, refs = refs[0][...], refs[1:]

    def store(cols, part):
        for n in range(out_ref.shape[0]):
            out_ref[n, 0, :rows, cols] = part

    write_columns(turned, refs, store)
    if riders:
        for n in range(out_ref.shape[0]):
            out_ref[n, 0, rows:, :] = rider


def gathered(shards, turned, rider=None, after=()):
    wide = lax.axis_size(WIDE)
    specs, rows, width = column_specs(shards, turned, lambda i: i)
    height = rows
    if rider is not None:
        specs = [whole(*rider.shape)] + specs
        shards = [rider] + shards
        height += rider.shape[0]
    blocks = call(
        partial(pack_kernel, turned, rows, rider is not None),
        "pack",
        (4,),
        specs,
        pl.BlockSpec((wide // 4, 1, height, width), lambda i: (0, i, 0, 0)),
        struct((wide // 4, 4, height, width), jnp.bfloat16),
    )(*shards)
    blocks = lax.optimization_barrier((blocks, *after))[0]
    return lax.all_to_all(blocks.reshape(wide, height, width), WIDE, 0, 0)


def unpack_kernel(turned, arrived_ref, *outs):
    total = arrived_ref[0, 0].astype(jnp.float32)
    for n in range(1, arrived_ref.shape[0]):
        total = total + arrived_ref[n, 0].astype(jnp.float32)
    start = 0
    for flip, out_ref in zip(turned, outs):
        height = out_ref.shape[0] if flip else out_ref.shape[1]
        part = total[start : start + height]
        out_ref[...] = part if flip else part.T
        start += height


def scatter_columns(grad, heights, turned, after=()):
    sequences = lax.axis_size("s")
    _, height, rows = grad.shape
    arrived = lax.all_to_all(grad, WIDE, 0, 0)
    riders = arrived[:, sum(heights) :]
    arrived = arrived.reshape(sequences, 4, height, rows)
    height = sum(heights)
    specs, shapes = [], []
    for flip, part in zip(turned, heights):
        if flip:
            specs.append(pl.BlockSpec((part, rows), lambda i: (i, 0)))
            shapes.append(struct((4 * part, rows), jnp.float32))
        else:
            specs.append(pl.BlockSpec((rows, part), lambda i: (0, i)))
            shapes.append(struct((rows, 4 * part), jnp.float32))
    shards = call(
        partial(unpack_kernel, turned),
        "unpack",
        (4,),
        [pl.BlockSpec((sequences, 1, height, rows), lambda i: (0, i, 0, 0))],
        specs,
        shapes,
        after=after,
    )(arrived)
    return shards, riders


def fold_kernel(index_ref, mine_ref, arrived_ref, keep_ref, send_ref):
    total = mine_ref[0, 0, 0].astype(jnp.float32) + arrived_ref[0, 0, 0].astype(jnp.float32)
    total = total.astype(jnp.bfloat16)

    @pl.when(pl.program_id(0) == 0)
    def _():
        keep_ref[0] = total

    @pl.when(pl.program_id(0) == 1)
    def _():
        send_ref[0] = total


def folded(mine, arrived, axes, axis, after=()):
    position = axes.index(axis)
    high, low = 2**position, 2 ** (len(axes) - 1 - position)
    rows, cols = mine.shape[-2:]
    spec = pl.BlockSpec(
        (1, 1, 1, rows, cols),
        lambda k, j, p: (j // low, lax.rem(k + p[0], 2), lax.rem(j, low), 0, 0),
    )
    shape = (high, 2, low, rows, cols)
    count = high * low
    return prefetch_call(
        fold_kernel,
        "fold",
        lax.axis_index(axis),
        (2, count),
        [spec, spec],
        switch_specs(count, (1, rows, cols)),
        [struct((count, rows, cols), jnp.bfloat16)] * 2,
        after=after,
    )(mine.reshape(shape), arrived.reshape(shape))


def join_kernel(index_ref, mine_ref, other_ref, out_ref):
    @pl.when(pl.program_id(0) == 0)
    def _():
        out_ref[0, 0] = mine_ref[0]

    @pl.when(pl.program_id(0) == 1)
    def _():
        out_ref[0, 0] = other_ref[0]


def joined(mine, axis, after=()):
    other = shifted(mine, axis, 1)
    rows, cols = mine.shape[-2:]
    count = mine.size // (rows * cols)
    out = prefetch_call(
        join_kernel,
        "join",
        lax.axis_index(axis),
        (2, count),
        switch_specs(count, (1, rows, cols)),
        pl.BlockSpec((1, 1, rows, cols), lambda k, j, p: (lax.rem(k + p[0], 2), j, 0, 0)),
        struct((2, count, rows, cols), mine.dtype),
        after=after,
    )(mine.reshape(count, rows, cols), other.reshape(count, rows, cols))
    return out.reshape((2,) + mine.shape)


def gather_narrow(value):
    for axis in ("c", "m"):
        other = shifted(value, axis, 1)
        value = jnp.stack(in_order(value, other, lax.axis_index(axis)))
    return value.reshape((4,) + value.shape[2:])


def summed_along_wide(value):
    for axis in ("h", "g"):
        value = value + shifted(value, axis, 1)
    total = value
    for step in range(1, lax.axis_size("s")):
        total = total + shifted(value, "s", step)
    return total


def body(
    tokens,
    cotangent,
    ln_gain,
    ln_shift,
    w_query,
    b_query,
    w_key,
    b_key,
    w_value,
    b_value,
    w_dense,
    b_dense,
    w_fc1,
    b_fc1,
    w_fc2,
    b_fc2,
):
    row_count, feature_count = tokens.shape
    own_g, own_h = lax.axis_index("g"), lax.axis_index("h")
    own_n = lax.axis_index(NARROW)
    quarter = 2 * own_g + own_h
    wide = lax.axis_size(WIDE)
    weight_rows = w_fc1.shape[0]
    lanes = w_query.shape[1] // 4

    core = lax.axis_index("c").astype(jnp.int32).reshape(1)

    vectors = (ln_gain, ln_shift, b_query, b_key, b_value, b_dense, b_fc2, b_fc1)
    lengths = [vector.shape[0] for vector in vectors]
    hidden = w_fc1.shape[1] // 4
    width = 4 * lanes + hidden
    packed = jnp.concatenate(vectors)
    packed = jnp.pad(packed, (0, 16 * width - packed.shape[0])).reshape(16, width)

    tokens_full = lax.all_gather(tokens, CUBE, axis=0, tiled=False)
    tokens_full = tokens_full.reshape(4, 4, row_count, feature_count)
    cot = joined(cotangent, "g")
    arrived = gathered(
        [w_query, w_key, w_value, w_dense, w_fc1],
        [False, False, False, True, False],
        packed,
        after=[cot],
    )
    cot = joined(joined(cot, "h"), "m")
    cot = lax.all_gather(cot, "c", axis=0, tiled=False)
    down_weight = Weight(gathered([w_fc2], [True]), weight_rows, 0, hidden)
    qkv_weight = Weight(arrived, weight_rows, 0, 3 * lanes)
    dense_weight = Weight(arrived, weight_rows, 3 * lanes, lanes)
    up_weight = Weight(arrived, weight_rows, 4 * lanes, hidden)

    here = arrived[:, weight_rows:].reshape(wide, 16 * width)
    local, start = [], 0
    for length in lengths:
        local.append(here[:, start : start + length].astype(jnp.float32).reshape(-1))
        start += length
    shared = gather_narrow(here[:, : 2 * lengths[0]].astype(jnp.float32))
    gain = shared[:, :, : lengths[0]].reshape(1, D)
    shift = shared[:, :, lengths[0] :].reshape(1, D)

    def quarter_of(vector):
        return pick(vector.reshape(4, -1), quarter)

    qkv_bias = jnp.concatenate([quarter_of(vector) for vector in local[2:5]]).reshape(1, -1)
    up_bias = quarter_of(local[7]).reshape(1, -1)
    own_gain, out_bias = local[0], local[5] + local[6]

    normed, stats, up_low, up_slope = norm_up(tokens_full, gain, shift, up_bias, up_weight)
    qkv = project_heads(normed, qkv_bias, qkv_weight)
    attended_grad = attended_gradient(cot, dense_weight, lanes, after=[qkv])
    grad_down = weight_grad([(up_low, cot)], wide, after=[attended_grad])
    attended, qkv_grad, qkv_sums = attention(qkv, attended_grad, after=[grad_down])
    up_grad, up_sums = up_gradient(cot, up_slope, down_weight, after=[attended])
    normed_grad = partial_sum(
        [(qkv_grad, qkv_weight), (up_grad, up_weight)],
        core,
        row_count,
        feature_count,
        "normed_gradient",
    )
    grad_up = weight_grad([(up_grad, normed)], wide, after=normed_grad[:1])
    branch = partial_sum(
        [(attended, dense_weight), (up_low, down_weight)],
        core,
        row_count,
        feature_count,
        "branch_sum",
        after=[grad_up],
    )
    first = folded(normed_grad[0], shifted(normed_grad[1], "c", 1), "mgh", "m", after=branch[:1])
    second = folded(branch[0], shifted(branch[1], "c", 1), "mgh", "h", after=first[:1])
    def spread(vector):
        placed = jnp.zeros((4, vector.shape[0]), jnp.float32)
        placed = lax.dynamic_update_index_in_dim(placed, vector, quarter, 0)
        return placed.reshape(wide, -1)

    terms = [
        spread(qkv_sums[0, :lanes]),
        spread(qkv_sums[0, lanes : 2 * lanes]),
        spread(qkv_sums[0, 2 * lanes :]),
        jnp.sum(cotangent.astype(jnp.float32), axis=0).reshape(wide, -1),
        spread(up_sums[0]),
    ]
    rider = jnp.concatenate(terms, axis=1).astype(jnp.bfloat16)
    early_count = rider.shape[1]
    rider = jnp.pad(rider, ((0, 0), (0, 16 * weight_rows - early_count)))
    grad_heads = weight_grad(
        [(qkv_grad, normed), (attended, cot)],
        wide,
        rider.reshape(wide, 16, weight_rows),
        after=second[:1],
    )
    (grad_down,), _ = scatter_columns(grad_down, [hidden], [True], after=[grad_heads])
    first = folded(first[0], shifted(first[1], "m", 1), "gh", "h", after=[grad_down])
    second = folded(second[0], shifted(second[1], "h", 1), "mg", "m", after=first[:1])
    (grad_up,), _ = scatter_columns(grad_up, [hidden], [False], after=second[:1])
    first = folded(first[0], shifted(first[1], "h", 1), "g", "g", after=[grad_up])
    second = folded(second[0], shifted(second[1], "m", 1), "g", "g", after=first[:1])
    (grad_query, grad_key, grad_value, grad_dense), riders = scatter_columns(
        grad_heads, [lanes] * 4, [False, False, False, True]
    )
    early = jnp.sum(riders.astype(jnp.float32), axis=0).reshape(-1)[:early_count]

    def last(keep, send):
        return keep[0].astype(jnp.float32) + shifted(send[0], "g", 1).astype(jnp.float32)

    local_x = tokens.astype(jnp.float32)
    standard_grad = last(*first)
    output = (local_x + last(*second) + out_bias).astype(jnp.bfloat16)
    own_stats = pick(stats.reshape(4, row_count, 128), quarter)
    row_mean, inverse_std = own_stats[:, :1], own_stats[:, 64:65]
    standard = (local_x - row_mean) * inverse_std
    scaled_grad = standard_grad * own_gain
    row_sums = lax.psum(
        (jnp.sum(scaled_grad, axis=1), jnp.sum(scaled_grad * standard, axis=1)), NARROW
    )
    input_grad = (
        scaled_grad - row_sums[0][:, None] / D - standard * (row_sums[1][:, None] / D)
    ) * inverse_std + cotangent.astype(jnp.float32)

    own_terms = [jnp.sum(standard_grad * standard, axis=0), jnp.sum(standard_grad, axis=0)]
    own_terms = [term.reshape(wide, -1) for term in own_terms]
    late = summed_along_wide(jnp.concatenate(own_terms, axis=1))
    terms = own_terms + terms
    vector_sums = jnp.concatenate([pick(late, lax.axis_index(WIDE)), early])
    vector_grads, start = [], 0
    for term in terms:
        vector_grads.append(vector_sums[start : start + term.shape[1]])
        start += term.shape[1]
    return (
        output,
        input_grad,
        vector_grads[0],
        vector_grads[1],
        grad_query,
        vector_grads[2],
        grad_key,
        vector_grads[3],
        grad_value,
        vector_grads[4],
        grad_dense,
        vector_grads[5],
        grad_up,
        vector_grads[6],
        grad_down,
        vector_grads[5],
    )


def solution(mesh):
    wide = mesh.shape["wide"]
    inner = Mesh(mesh.devices.reshape(wide // 4, 2, 2, 2, 2), ("s", "g", "h", "m", "c"))
    acts = P(WIDE, NARROW)
    vector = P(NARROW + WIDE)
    by_rows = P(WIDE, NARROW)
    by_cols = P(NARROW, WIDE)
    specs = (
        (acts, acts, vector, vector)
        + (by_rows, vector) * 3
        + (by_cols, vector, by_rows, vector, by_cols, vector)
    )
    return jax.shard_map(body, mesh=inner, in_specs=specs, out_specs=specs, check_vma=False)
```

time: 530 us -> 483 us (0.911)
  Pallas kernels: 129 us -> 186 us
  waiting for transfers between devices: 230 us -> 185 us
  starting transfers between devices: 92.2 us -> 66 us
  local copies, waits for them, and re-layouts: 41 us -> 17.2 us
  other arithmetic: 15.3 us -> 5.46 us
    pallas_call x10 -> x24, Pallas kernels: 129 us -> 186 us  [the longest x15 141 us: call(): return lambda *operands: run(*after, *operands)]
    ppermute x33 -> x16, starting transfers between devices: 86.8 us -> 40.7 us  [shifted(): lax.ppermute(value, axis, [(source, (source + step) % count) for source i...]
    ppermute x33 -> x16, waiting for transfers between devices: 206 us -> 167 us  [shifted(): lax.ppermute(value, axis, [(source, (source + step) % count) for source i...]
    all_gather x2, waiting for transfers between devices: 23.3 us -> 0.01 us  [the longest x1 0.01 us: body(): tokens_full = lax.all_gather(tokens, CUBE, axis=0, tiled=False)]
    all_to_all x1 -> x5, starting transfers between devices: 5.26 us -> 25.3 us  [the longest x3 15.5 us: scatter_columns(): arrived = lax.all_to_all(grad, WIDE, 0, 0)]
    all_to_all x1 -> x5, waiting for transfers between devices: 0.01 us -> 17.1 us  [the longest x3 16.8 us: scatter_columns(): arrived = lax.all_to_all(grad, WIDE, 0, 0)]
    dynamic_slice x14 -> x4, local copies, waits for them, and re-layouts: 18.8 us -> 2.4 us  [pick(): return lax.dynamic_index_in_dim(blocks, index, axis, keepdims=False)]
    another operation x19 -> x3, local copies, waits for them, and re-layouts: 6.14 us -> 0.01 us  [the longest x3 4.08 us: body(): grad_heads[:, n].reshape(4 * lanes, weight_rows)]
  transfers between devices with their start and end apart: 37 -> 23, of which waited for: 16 -> 11; matrix products, arithmetic and copies ran while one was open for 9% -> 3% of each run, Pallas kernels for 22% -> 38%
where the time goes in v3:
time: 483 us; the launch traced here: 481 us
  Pallas kernels  186 us (39%)
  waiting for transfers between devices  185 us (38%)
  starting transfers between devices  66 us (14%)
  local copies, waits for them, and re-layouts  17.2 us (4%)
  between operations  14.3 us (3%)
  blocking collectives  6.04 us (1%)
  other arithmetic  5.46 us (1%)
    ppermute x16, waiting for transfers between devices, shifted(): lax.ppermute(value, axis, [(source, (source + step) % count) for source i...  167 us
    pallas_call x15, Pallas kernels, call(): return lambda *operands: run(*after, *operands)  141 us
    pallas_call x9, Pallas kernels, prefetch_call(): run(index.astype(jnp.int32).reshape(1), *after, *operands)  45.6 us
    ppermute x16, starting transfers between devices, shifted(): lax.ppermute(value, axis, [(source, (source + step) % count) for source i...  40.7 us
    all_to_all x3, waiting for transfers between devices, scatter_columns(): arrived = lax.all_to_all(grad, WIDE, 0, 0)  16.8 us
    all_to_all x3, starting transfers between devices, scatter_columns(): arrived = lax.all_to_all(grad, WIDE, 0, 0)  15.5 us
    all_to_all x2, starting transfers between devices, gathered(): return lax.all_to_all(blocks.reshape(wide, height, width), WIDE, 0, 0)  9.74 us
  transfers between devices with their start and end apart: 23, of which 11 were waited for; matrix products, arithmetic and copies ran while one was open for 3% of the time, Pallas kernels for 38%

profile of v3, /device:TPU:0, one launch (start us, length us, event | category | flops | bytes accessed | tf_op | source)
XLA Modules:
  0.0 480.5 jit_solution(9320396919179915533)
XLA Ops:
  8.0 3.1 collective-permute-start
  11.1 16.2 %collective-permute-done = bf16[512,512]{1,0:T(8,128)(2,1)S(1)} collective-permute-done((bf16[512,512]{1,0:T(8,128)(2,1)}, bf16[512,512]{1,0:T(8,128)(2,1)S(1)}, u32[]{:S(2)}, u32[]{:S(2)}) %collective-permute-start) | collective-permute-done | bytes 524320 | tf_op jit(solution)/shard_map/ppermute | solution.py:47
  28.1 2.2 join.3
  32.5 4.7 pack.2
  37.2 5.7 %all-to-all-start = ((bf16[8,272,1024]{2,1,0:T(8,128)(2,1)}), bf16[8,272,1024]{2,1,0:T(8,128)(2,1)}, u32[]{:S(2)}, u32[]{:S(2)}) async-start(bf16[8,272,1024]{2,1,0:T(8,128)(2,1)} %bitcast.74), calls=%async_computation | async-start | bytes 8912896 | tf_op jit(solution)/shard_map/all_to_all | solution.py:599
  43.0 44.9 %collective-permute-done.3.refs_1_ = bf16[2,512,512]{2,1,0:T(8,128)(2,1)S(1)} collective-permute-done((bf16[2,512,512]{2,1,0:T(8,128)(2,1)}, bf16[2,512,512]{2,1,0:T(8,128)(2,1)S(1)}, u32[]{:S(2)}, u32[]{:S(2)}) %collective-permute-start.3) | collective-permute-done | bytes 1048608 | tf_op jit(solution)/shard_map/ppermute | solution.py:47
  88.8 4.1 join.4
  92.9 22.0 %collective-permute-start.4 = (bf16[2,2,512,512]{3,2,1,0:T(8,128)(2,1)}, bf16[2,2,512,512]{3,2,1,0:T(8,128)(2,1)S(1)}, u32[]{:S(2)}, u32[]{:S(2)}) collective-permute-start(bf16[2,2,512,512]{3,2,1,0:T(8,128)(2,1)} %join.4), channel_id=1, source_target_pairs={{0,2},{2,0},{1,3},{3,1},{4,6},{6,4},{5,7},{7,5},{8,10},{10,8},{9,1... | collective-permute-start | bytes 6291464 | tf_op jit(solution)/shard_map/ppermute | solution.py:47
  114.9 48.6 %collective-permute-done.4 = bf16[2,2,512,512]{3,2,1,0:T(8,128)(2,1)S(1)} collective-permute-done((bf16[2,2,512,512]{3,2,1,0:T(8,128)(2,1)}, bf16[2,2,512,512]{3,2,1,0:T(8,128)(2,1)S(1)}, u32[]{:S(2)}, u32[]{:S(2)}) %collective-permute-start.4) | collective-permute-done | bytes 2097184 | tf_op jit(solution)/shard_map/ppermute | solution.py:47
  164.7 7.2 %join.5 = bf16[2,4,512,512]{3,2,1,0:T(8,128)(2,1)} custom-call(s32[1]{0:T(128)} %bitcast.1.index_ref, bf16[4,512,512]{2,1,0:T(8,128)(2,1)} %bitcast.83, bf16[4,512,512]{2,1,0:T(8,128)(2,1)} %bitcast.90), custom_call_target="tpu_custom_call" | custom-call | tf_op jit(solution)/shard_map/join/pallas_call | solution.py:543
  171.9 3.8 pack.3
  175.7 4.0 all-to-all-start.1
  183.0 2.8 collective-permute-done.2
  187.3 14.4 %norm_up.1 = (bf16[2048,2048]{1,0:T(8,128)(2,1)}, f32[2048,128]{1,0:T(8,128)}, bf16[2048,512]{1,0:T(8,128)(2,1)}, f32[2048,512]{1,0:T(8,128)}) custom-call(bf16[4,4,512,512]{3,2,1,0:T(8,128)(2,1)} %bitcast.79, f32[1,2048]{1,0:T(1,128)} %reshape.208.refs_1_, f32[1,2048]{1,0:T(1,128)} %reshape.209.refs_2_, f32[1,512]{1,0:T(1,128)} %constant_dynamic-slice_fusion.5.refs_3_, ...), custom_call_target="tpu_custom_call" | custom-call | flops 12884901 | tf_op jit(solution)/shard_map/norm_up/pallas_call | solution.py:73
  201.7 9.4 %project_heads.1.refs_0_.refs_1_ = bf16[2048,384]{1,0:T(8,128)(2,1)} custom-call(bf16[2048,2048]{1,0:T(8,128)(2,1)} %get-tuple-element.47.refs_0_.refs_2_.refs_3_, f32[1,384]{1,0:T(1,128)} %reshape.210.refs_1_, f32[2048,128]{1,0:T(8,128)} %constant.71.clone.refs_2_.refs_3_, f32[2048,128]{1,0:T(8,128)} %constant.72.clone.refs_3_.refs_4_, ...), custom_call_target="tpu_custom_call" | custom-call | flops 6442450 | tf_op jit(solution)/shard_map/project_heads/pallas_call | solution.py:73
  211.0 6.4 %attended_gradient.1.refs_0_.refs_2_ = bf16[2048,128]{1,0:T(8,128)(2,1)} custom-call(bf16[2048,384]{1,0:T(8,128)(2,1)} %project_heads.1.refs_0_.refs_1_, bf16[2,2,2,2,512,512]{5,4,3,2,1,0:T(8,128)(2,1)} %all-gather.4.cloned.1.call-done.refs_1_.refs_2_.refs_5_, bf16[8,272,1024]{2,1,0:T(8,128)(2,1)} %all-to-all-done.refs_4_.refs_2_.refs_3_), custom_call_target="tpu_custom_call" | custom-call | flops 4294967 | tf_op jit(solution)/shard_map/attended_gradient/pallas_call | solution.py:73
  217.4 8.8 %weight_grad.3.refs_0_ = bf16[8,512,256]{2,1,0:T(8,128)(2,1)} custom-call(bf16[2048,128]{1,0:T(8,128)(2,1)} %attended_gradient.1.refs_0_.refs_2_, bf16[2048,512]{1,0:T(8,128)(2,1)} %get-tuple-element.48.refs_1_.refs_3_, bf16[2,2,2,2,512,512]{5,4,3,2,1,0:T(8,128)(2,1)} %all-gather.4.cloned.1.call-done.refs_1_.refs_2_.refs_5_), custom_call_target="tpu_custom_call" | custom-call | flops 8589934 | tf_op jit(solution)/shard_map/weight_grad/pallas_call | solution.py:73
  227.8 5.7 %all-to-all-start.2 = ((bf16[8,512,256]{2,1,0:T(8,128)(2,1)}), bf16[8,512,256]{2,1,0:T(8,128)(2,1)}, u32[]{:S(2)}, u32[]{:S(2)}) async-start(bf16[8,512,256]{2,1,0:T(8,128)(2,1)} %weight_grad.3.refs_0_), calls=%async_computation.2 | async-start | bytes 4194304 | tf_op jit(solution)/shard_map/all_to_all | solution.py:617
  233.5 28.2 %attention.1 = (bf16[2048,128]{1,0:T(8,128)(2,1)}, bf16[2048,384]{1,0:T(8,128)(2,1)}, f32[1,384]{1,0:T(1,128)}) custom-call(bf16[8,512,256]{2,1,0:T(8,128)(2,1)} %weight_grad.3.refs_0_, bf16[2048,384]{1,0:T(8,128)(2,1)} %project_heads.1.refs_0_.refs_1_, bf16[2048,128]{1,0:T(8,128)(2,1)} %attended_gradient.1.refs_0_.refs_2_, ...), custom_call_target="tpu_custom_call" | custom-call | flops 28000000 | tf_op jit(solution)/shard_map/attention/pallas_call | solution.py:73
  261.7 9.4 %up_gradient.1 = (bf16[2048,512]{1,0:T(8,128)(2,1)}, f32[1,512]{1,0:T(1,128)}) custom-call(bf16[2048,128]{1,0:T(8,128)(2,1)} %get-tuple-element.50.refs_0_.refs_2_.refs_4_, bf16[2,2,2,2,512,512]{5,4,3,2,1,0:T(8,128)(2,1)} %all-gather.4.cloned.1.call-done.refs_1_.refs_2_.refs_5_, f32[2048,512]{1,0:T(8,128)} %get-tuple-element.51.refs_2_, ...), custom_call_target="tpu_custom_call" | custom-call | flops 8589934 | tf_op jit(solution)/shard_map/up_gradient/pallas_call | solution.py:73
  271.1 13.5 %normed_gradient.1 = (bf16[2,4,512,512]{3,2,1,0:T(8,128)(2,1)}, bf16[2,4,512,512]{3,2,1,0:T(8,128)(2,1)}) custom-call(s32[1]{0:T(128)} %bitcast.3.refs_0_.refs_1_, bf16[2048,384]{1,0:T(8,128)(2,1)} %get-tuple-element.49.refs_1_.refs_2_, bf16[2048,512]{1,0:T(8,128)(2,1)} %get-tuple-element.52.refs_2_.refs_1_, ...), custom_call_target="tpu_custom_call" | custom-call | flops 15032385 | tf_op jit(solution)/shard_map/normed_gradient/pallas_call | solution.py:73
  284.6 8.8 %weight_grad.4.refs_0_ = bf16[8,512,256]{2,1,0:T(8,128)(2,1)} custom-call(bf16[2,4,512,512]{3,2,1,0:T(8,128)(2,1)} %get-tuple-element.53.refs_0_, bf16[2048,512]{1,0:T(8,128)(2,1)} %get-tuple-element.52.refs_2_.refs_1_, bf16[2048,2048]{1,0:T(8,128)(2,1)} %get-tuple-element.47.refs_0_.refs_2_.refs_3_), custom_call_target="tpu_custom_call" | custom-call | flops 8589934 | tf_op jit(solution)/shard_map/weight_grad/pallas_call | solution.py:73
  293.4 10.8 %branch_sum.1 = (bf16[2,4,512,512]{3,2,1,0:T(8,128)(2,1)}, bf16[2,4,512,512]{3,2,1,0:T(8,128)(2,1)}) custom-call(bf16[8,512,256]{2,1,0:T(8,128)(2,1)} %weight_grad.4.refs_0_, s32[1]{0:T(128)} %bitcast.3.refs_0_.refs_1_, bf16[2048,128]{1,0:T(8,128)(2,1)} %get-tuple-element.50.refs_0_.refs_2_.refs_4_, bf16[2048,512]{1,0:T(8,128)(2,1)} %get-tuple-element.48.refs_1_.refs_3_, ...), custom_call_target="tpu_custom_call" | custom-call | flops 10737418 | tf_op jit(solution)/shard_map/branch_sum/pallas_call | solution.py:73
  304.7 6.0 %all-to-all-start.3 = ((bf16[8,512,256]{2,1,0:T(8,128)(2,1)}), bf16[8,512,256]{2,1,0:T(8,128)(2,1)S(1)}, u32[]{:S(2)}, u32[]{:S(2)}) async-start(bf16[8,512,256]{2,1,0:T(8,128)(2,1)} %weight_grad.4.refs_0_), calls=%async_computation.3 | async-start | bytes 4194304 | tf_op jit(solution)/shard_map/all_to_all | solution.py:617
  310.7 8.4 %fold.6 = (bf16[4,512,512]{2,1,0:T(8,128)(2,1)}, bf16[4,512,512]{2,1,0:T(8,128)(2,1)}) custom-call(s32[1]{0:T(128)} %bitcast.1.index_ref, bf16[2,4,512,512]{3,2,1,0:T(8,128)(2,1)} %get-tuple-element.54.refs_0_, bf16[1,2,4,512,512]{4,3,2,1,0:T(8,128)(2,1)} %bitcast.77, bf16[1,2,4,512,512]{4,3,2,1,0:T(8,128)(2,1)} %bitcast.22.refs_2_), custom_call_target="tpu_custom_call" | custom-call | tf_op jit(solution)/shard_map/fold/pallas_call | solution.py:543
  319.4 8.6 %fold.7 = (bf16[4,512,512]{2,1,0:T(8,128)(2,1)}, bf16[4,512,512]{2,1,0:T(8,128)(2,1)}) custom-call(s32[1]{0:T(128)} %bitcast.2.index_ref, bf16[4,512,512]{2,1,0:T(8,128)(2,1)} %get-tuple-element.56.refs_0_, bf16[4,2,1,512,512]{4,3,2,1,0:T(8,128)(2,1)} %bitcast.76, bf16[4,2,1,512,512]{4,3,2,1,0:T(8,128)(2,1)} %bitcast.24.refs_2_), custom_call_target="tpu_custom_call" | custom-call | tf_op jit(solution)/shard_map/fold/pallas_call | solution.py:543
  328.0 2.0 collective-permute-start.8
  331.4 11.0 %weight_grad.5.refs_0_ = bf16[8,528,256]{2,1,0:T(8,128)(2,1)} custom-call(bf16[4,512,512]{2,1,0:T(8,128)(2,1)} %get-tuple-element.58.refs_0_, bf16[8,16,256]{2,1,0:T(8,128)(2,1)} %bitcast.98, bf16[2048,384]{1,0:T(8,128)(2,1)} %get-tuple-element.49.refs_1_.refs_2_, bf16[2048,2048]{1,0:T(8,128)(2,1)} %get-tuple-element.47.refs_0_.refs_2_.refs_3_, ...), custom_call_target="tpu_custom_call" | custom-call | flops 8858370 | tf_op jit(solution)/shard_map/weight_grad/pallas_call | solution.py:73
  342.3 16.8 %all-to-all-done.3 = bf16[8,512,256]{2,1,0:T(8,128)(2,1)S(1)} async-done(((bf16[8,512,256]{2,1,0:T(8,128)(2,1)}), bf16[8,512,256]{2,1,0:T(8,128)(2,1)S(1)}, u32[]{:S(2)}, u32[]{:S(2)}) %all-to-all-start.3) | async-done | bytes 2097184 | tf_op jit(solution)/shard_map/all_to_all | solution.py:617
  360.5 3.8 all-to-all-start.4
  364.3 3.8 unpack.3.refs_0_
  368.2 4.8 fold.8
  373.0 1.8 collective-permute-start.9
  374.8 28.7 %collective-permute-done.8 = bf16[4,512,512]{2,1,0:T(8,128)(2,1)} collective-permute-done((bf16[4,512,512]{2,1,0:T(8,128)(2,1)}, bf16[4,512,512]{2,1,0:T(8,128)(2,1)}, u32[]{:S(2)}, u32[]{:S(2)}) %collective-permute-start.8) | collective-permute-done | bytes 2097184 | tf_op jit(solution)/shard_map/ppermute | solution.py:47
  403.5 4.8 %fold.9 = (bf16[2,512,512]{2,1,0:T(8,128)(2,1)}, bf16[2,512,512]{2,1,0:T(8,128)(2,1)}) custom-call(s32[1]{0:T(128)} %bitcast.1.index_ref, bf16[2,512,512]{2,1,0:T(8,128)(2,1)} %get-tuple-element.62.refs_0_, bf16[1,2,2,512,512]{4,3,2,1,0:T(8,128)(2,1)} %bitcast.84, bf16[1,2,2,512,512]{4,3,2,1,0:T(8,128)(2,1)} %bitcast.29.refs_2_), custom_call_target="tpu_custom_call" | custom-call | tf_op jit(solution)/shard_map/fold/pallas_call | solution.py:543
  409.4 4.1 unpack.4.refs_0_
  413.5 16.8 %collective-permute-done.9 = bf16[2,512,512]{2,1,0:T(8,128)(2,1)} collective-permute-done((bf16[2,512,512]{2,1,0:T(8,128)(2,1)}, bf16[2,512,512]{2,1,0:T(8,128)(2,1)}, u32[]{:S(2)}, u32[]{:S(2)}) %collective-permute-start.9) | collective-permute-done | bytes 1048608 | tf_op jit(solution)/shard_map/ppermute | solution.py:47
  430.2 2.7 fold.10
  433.0 3.7 collective-permute-start.12
  439.5 2.8 fold.11
  442.3 7.5 %collective-permute-done.12 = bf16[512,512]{1,0:T(8,128)(2,1)} collective-permute-done((bf16[512,512]{1,0:T(8,128)(2,1)}, bf16[512,512]{1,0:T(8,128)(2,1)}, u32[]{:S(2)}, u32[]{:S(2)}) %collective-permute-start.12) | collective-permute-done | bytes 524320 | tf_op jit(solution)/shard_map/ppermute | solution.py:47
  449.8 1.7 fusion.10
  451.7 6.0 %all-reduce.2 = (f32[512]{0:T(512)S(1)}, f32[512]{0:T(512)S(1)}) all-reduce(f32[512]{0:T(512)S(1)} %get-tuple-element.77, f32[512]{0:T(512)S(1)} %get-tuple-element.78), channel_id=1, replica_groups=mesh['s'=2,'g'=2,'h'=2,'m'=2,'c'=2] {'m','c'}, use_global_device_ids=true, to_apply=%region_4.5 | all-reduce | flops 1024 | bytes 8192 | tf_op jit(solution)/shard_map/psum | solution.py:852
  457.8 2.0 collective-permute-start.14
  459.9 1.6 collective-permute-done.14
  461.5 2.6 collective-permute-start.15
  464.0 3.3 fusion.9
  469.3 3.9 unpack.5
  (131 shorter events, 22.6 us)
Async XLA Ops:
  7.2 24.5 %copy-start.17 = (bf16[64]{0:T(256)(128)(2,1)S(1)}, bf16[64]{0:T(256)(128)(2,1)}, u32[]{:S(2)}) copy-start(bf16[64]{0:T(256)(128)(2,1)} %param.35) | copy-start | bytes 388
  7.2 24.5 %copy-start.18 = (bf16[256]{0:T(256)(128)(2,1)S(1)}, bf16[256]{0:T(256)(128)(2,1)}, u32[]{:S(2)}) copy-start(bf16[256]{0:T(256)(128)(2,1)} %param.33) | copy-start | bytes 1540
  7.2 24.5 %copy-start.16 = (bf16[64]{0:T(256)(128)(2,1)S(1)}, bf16[64]{0:T(256)(128)(2,1)}, u32[]{:S(2)}) copy-start(bf16[64]{0:T(256)(128)(2,1)} %param.31) | copy-start | bytes 388
  7.2 24.5 %copy-start.15 = (bf16[64]{0:T(256)(128)(2,1)S(1)}, bf16[64]{0:T(256)(128)(2,1)}, u32[]{:S(2)}) copy-start(bf16[64]{0:T(256)(128)(2,1)} %param.29) | copy-start | bytes 388
  7.2 24.5 %copy-start.14 = (bf16[64]{0:T(256)(128)(2,1)S(1)}, bf16[64]{0:T(256)(128)(2,1)}, u32[]{:S(2)}) copy-start(bf16[64]{0:T(256)(128)(2,1)} %param.27) | copy-start | bytes 388
  7.2 24.5 %copy-start.13 = (bf16[64]{0:T(256)(128)(2,1)S(1)}, bf16[64]{0:T(256)(128)(2,1)}, u32[]{:S(2)}) copy-start(bf16[64]{0:T(256)(128)(2,1)} %param.25) | copy-start | bytes 388
  7.2 24.5 %copy-start.12 = (bf16[64]{0:T(256)(128)(2,1)S(1)}, bf16[64]{0:T(256)(128)(2,1)}, u32[]{:S(2)}) copy-start(bf16[64]{0:T(256)(128)(2,1)} %param.23) | copy-start | bytes 388
  7.3 24.5 %copy-start.11 = (bf16[64]{0:T(256)(128)(2,1)S(1)}, bf16[64]{0:T(256)(128)(2,1)}, u32[]{:S(2)}) copy-start(bf16[64]{0:T(256)(128)(2,1)} %param.22) | copy-start | bytes 388
  7.3 180.0 %all-gather.6.cloned.1.call-start = ((), (), s32[]{:S(2)}) async-start(), calls=%async_computation.6 | async-start | bytes 8912896 | tf_op jit(solution)/shard_map/all_gather | solution.py:754
  8.0 19.3 %collective-permute-start = (bf16[512,512]{1,0:T(8,128)(2,1)}, bf16[512,512]{1,0:T(8,128)(2,1)S(1)}, u32[]{:S(2)}, u32[]{:S(2)}) collective-permute-start(bf16[512,512]{1,0:T(8,128)(2,1)} %param.21), channel_id=1, source_target_pairs={{0,8},{8,0},{1,9},{9,1},{2,10},{10,2},{3,11},{11,3},{4,12},{12,4},... | collective-permute-start | bytes 1572872 | tf_op jit(solution)/shard_map/ppermute | solution.py:47
  27.3 0.8 copy-start.8
  30.3 57.5 %collective-permute-start.3 = (bf16[2,512,512]{2,1,0:T(8,128)(2,1)}, bf16[2,512,512]{2,1,0:T(8,128)(2,1)S(1)}, u32[]{:S(2)}, u32[]{:S(2)}) collective-permute-start(bf16[2,512,512]{2,1,0:T(8,128)(2,1)} %bitcast.86), channel_id=1, source_target_pairs={{0,4},{4,0},{1,5},{5,1},{2,6},{6,2},{3,7},{7,3},{8,12},{12,8},{9,1... | collective-permute-start | bytes 3145736 | tf_op jit(solution)/shard_map/ppermute | solution.py:47
  37.2 138.5 %all-to-all-start = ((bf16[8,272,1024]{2,1,0:T(8,128)(2,1)}), bf16[8,272,1024]{2,1,0:T(8,128)(2,1)}, u32[]{:S(2)}, u32[]{:S(2)}) async-start(bf16[8,272,1024]{2,1,0:T(8,128)(2,1)} %bitcast.74), calls=%async_computation | async-start | bytes 8912896 | tf_op jit(solution)/shard_map/all_to_all | solution.py:599
  42.9 168.1 %all-gather.4.cloned.1.call-start = ((), (), s32[]{:S(2)}) async-start(), calls=%async_computation.5 | async-start | bytes 12582912 | tf_op jit(solution)/shard_map/all_gather | solution.py:764
  87.8 1.0 copy-start.7
  92.9 70.5 %collective-permute-start.4 = (bf16[2,2,512,512]{3,2,1,0:T(8,128)(2,1)}, bf16[2,2,512,512]{3,2,1,0:T(8,128)(2,1)S(1)}, u32[]{:S(2)}, u32[]{:S(2)}) collective-permute-start(bf16[2,2,512,512]{3,2,1,0:T(8,128)(2,1)} %join.4), channel_id=1, source_target_pairs={{0,2},{2,0},{1,3},{3,1},{4,6},{6,4},{5,7},{7,5},{8,10},{10,8},{9,1... | collective-permute-start | bytes 6291464 | tf_op jit(solution)/shard_map/ppermute | solution.py:47
  163.4 1.3 copy-start.6
  175.7 50.8 %all-to-all-start.1 = ((bf16[8,256,512]{2,1,0:T(8,128)(2,1)}), bf16[8,256,512]{2,1,0:T(8,128)(2,1)S(1)}, u32[]{:S(2)}, u32[]{:S(2)}) async-start(bf16[8,256,512]{2,1,0:T(8,128)(2,1)} %bitcast.81), calls=%async_computation.1 | async-start | bytes 4194304 | tf_op jit(solution)/shard_map/all_to_all | solution.py:599
  180.9 1.2 collective-permute-start.1
  182.2 3.7 collective-permute-start.2
  226.5 1.3 copy-start
  227.8 76.9 %all-to-all-start.2 = ((bf16[8,512,256]{2,1,0:T(8,128)(2,1)}), bf16[8,512,256]{2,1,0:T(8,128)(2,1)}, u32[]{:S(2)}, u32[]{:S(2)}) async-start(bf16[8,512,256]{2,1,0:T(8,128)(2,1)} %weight_grad.3.refs_0_), calls=%async_computation.2 | async-start | bytes 4194304 | tf_op jit(solution)/shard_map/all_to_all | solution.py:617
  284.6 26.1 %collective-permute-start.5 = (bf16[2,4,512,512]{3,2,1,0:T(8,128)(2,1)}, bf16[2,4,512,512]{3,2,1,0:T(8,128)(2,1)}, u32[]{:S(2)}, u32[]{:S(2)}) collective-permute-start(bf16[2,4,512,512]{3,2,1,0:T(8,128)(2,1)} %get-tuple-element.55), channel_id=1, source_target_pairs={{0,1},{1,0},{2,3},{3,2},{4,5},{5,4},{6,7},{7,6},{8,9},{9,8},{10,11... | collective-permute-start | bytes 12582920 | tf_op jit(solution)/shard_map/ppermute | solution.py:47
  304.2 15.2 %collective-permute-start.6 = (bf16[2,4,512,512]{3,2,1,0:T(8,128)(2,1)}, bf16[2,4,512,512]{3,2,1,0:T(8,128)(2,1)}, u32[]{:S(2)}, u32[]{:S(2)}) collective-permute-start(bf16[2,4,512,512]{3,2,1,0:T(8,128)(2,1)} %get-tuple-element.57), channel_id=1, source_target_pairs={{0,1},{1,0},{2,3},{3,2},{4,5},{5,4},{6,7},{7,6},{8,9},{9,8},{10,11... | collective-permute-start | bytes 12582920 | tf_op jit(solution)/shard_map/ppermute | solution.py:47
  304.7 54.4 %all-to-all-start.3 = ((bf16[8,512,256]{2,1,0:T(8,128)(2,1)}), bf16[8,512,256]{2,1,0:T(8,128)(2,1)S(1)}, u32[]{:S(2)}, u32[]{:S(2)}) async-start(bf16[8,512,256]{2,1,0:T(8,128)(2,1)} %weight_grad.4.refs_0_), calls=%async_computation.3 | async-start | bytes 4194304 | tf_op jit(solution)/shard_map/all_to_all | solution.py:617
  319.1 49.1 %collective-permute-start.7 = (bf16[4,512,512]{2,1,0:T(8,128)(2,1)}, bf16[4,512,512]{2,1,0:T(8,128)(2,1)}, u32[]{:S(2)}, u32[]{:S(2)}) collective-permute-start(bf16[4,512,512]{2,1,0:T(8,128)(2,1)} %get-tuple-element.61), channel_id=1, source_target_pairs={{0,2},{2,0},{1,3},{3,1},{4,6},{6,4},{5,7},{7,5},{8,10},{10,8},{9,1... | collective-permute-start | bytes 6291464 | tf_op jit(solution)/shard_map/ppermute | solution.py:47
  319.4 10.6 %copy-start.3 = (bf16[512,512]{1,0:T(8,128)(2,1)S(1)}, bf16[512,512]{1,0:T(8,128)(2,1)}, u32[]{:S(2)}) copy-start(bf16[512,512]{1,0:T(8,128)(2,1)} %param.21) | copy-start | bytes 1572868
  319.4 10.8 %copy-start.9 = (f32[1,512]{1,0:T(1,128)S(1)}, f32[1,512]{1,0:T(1,128)}, u32[]{:S(2)}) copy-start(f32[1,512]{1,0:T(1,128)} %get-tuple-element.60) | copy-start | bytes 6148
  319.4 10.8 %copy-start.10 = (f32[1,384]{1,0:T(1,128)S(1)}, f32[1,384]{1,0:T(1,128)}, u32[]{:S(2)}) copy-start(f32[1,384]{1,0:T(1,128)} %get-tuple-element.59) | copy-start | bytes 4612
  328.0 75.5 %collective-permute-start.8 = (bf16[4,512,512]{2,1,0:T(8,128)(2,1)}, bf16[4,512,512]{2,1,0:T(8,128)(2,1)}, u32[]{:S(2)}, u32[]{:S(2)}) collective-permute-start(bf16[4,512,512]{2,1,0:T(8,128)(2,1)} %get-tuple-element.63), channel_id=1, source_target_pairs={{0,4},{4,0},{1,5},{5,1},{2,6},{6,2},{3,7},{7,3},{8,12},{12,8},{9,1... | collective-permute-start | bytes 6291464 | tf_op jit(solution)/shard_map/ppermute | solution.py:47
  359.2 1.3 copy-start.2
  360.5 107.4 %all-to-all-start.4 = ((bf16[8,528,256]{2,1,0:T(8,128)(2,1)}), bf16[8,528,256]{2,1,0:T(8,128)(2,1)S(1)}, u32[]{:S(2)}, u32[]{:S(2)}) async-start(bf16[8,528,256]{2,1,0:T(8,128)(2,1)} %weight_grad.5.refs_0_), calls=%async_computation.4 | async-start | bytes 4325376 | tf_op jit(solution)/shard_map/all_to_all | solution.py:617
  373.0 57.3 %collective-permute-start.9 = (bf16[2,512,512]{2,1,0:T(8,128)(2,1)}, bf16[2,512,512]{2,1,0:T(8,128)(2,1)}, u32[]{:S(2)}, u32[]{:S(2)}) collective-permute-start(bf16[2,512,512]{2,1,0:T(8,128)(2,1)} %get-tuple-element.65), channel_id=1, source_target_pairs={{0,4},{4,0},{1,5},{5,1},{2,6},{6,2},{3,7},{7,3},{8,12},{12,8},{9,1... | collective-permute-start | bytes 3145736 | tf_op jit(solution)/shard_map/ppermute | solution.py:47
  408.3 31.2 %collective-permute-start.10 = (bf16[2,512,512]{2,1,0:T(8,128)(2,1)}, bf16[2,512,512]{2,1,0:T(8,128)(2,1)}, u32[]{:S(2)}, u32[]{:S(2)}) collective-permute-start(bf16[2,512,512]{2,1,0:T(8,128)(2,1)} %get-tuple-element.67), channel_id=1, source_target_pairs={{0,2},{2,0},{1,3},{3,1},{4,6},{6,4},{5,7},{7,5},{8,10},{10,8},{9,1... | collective-permute-start | bytes 3145736 | tf_op jit(solution)/shard_map/ppermute | solution.py:47
  433.0 16.8 %copy-start.4 = (bf16[512,512]{1,0:T(8,128)(2,1)S(1)}, bf16[512,512]{1,0:T(8,128)(2,1)}, u32[]{:S(2)}) copy-start(bf16[512,512]{1,0:T(8,128)(2,1)} %param.20) | copy-start | bytes 1572868
  433.0 16.8 %collective-permute-start.12 = (bf16[512,512]{1,0:T(8,128)(2,1)}, bf16[512,512]{1,0:T(8,128)(2,1)}, u32[]{:S(2)}, u32[]{:S(2)}) collective-permute-start(bf16[512,512]{1,0:T(8,128)(2,1)} %bitcast.109), channel_id=1, source_target_pairs={{0,8},{8,0},{1,9},{9,1},{2,10},{10,2},{3,11},{11,3},{4,12},{12,4},... | collective-permute-start | bytes 1572872 | tf_op jit(solution)/shard_map/ppermute | solution.py:47
  438.7 11.1 %copy-start.5 = (bf16[1,512,512]{2,1,0:T(8,128)(2,1)S(1)}, bf16[1,512,512]{2,1,0:T(8,128)(2,1)}, u32[]{:S(2)}) copy-start(bf16[1,512,512]{2,1,0:T(8,128)(2,1)} %get-tuple-element.66.refs_0_) | copy-start | bytes 1572868
  442.3 21.8 %collective-permute-start.11 = (bf16[512,512]{1,0:T(8,128)(2,1)}, bf16[512,512]{1,0:T(8,128)(2,1)}, u32[]{:S(2)}, u32[]{:S(2)}) collective-permute-start(bf16[512,512]{1,0:T(8,128)(2,1)} %bitcast.108), channel_id=1, source_target_pairs={{0,8},{8,0},{1,9},{9,1},{2,10},{10,2},{3,11},{11,3},{4,12},{12,4},... | collective-permute-start | bytes 1572872 | tf_op jit(solution)/shard_map/ppermute | solution.py:47
  451.7 6.0 %collective-permute-start.13 = (f32[8,128]{1,0:T(8,128)S(1)}, f32[8,128]{1,0:T(8,128)S(1)}, u32[]{:S(2)}, u32[]{:S(2)}) collective-permute-start(f32[8,128]{1,0:T(8,128)S(1)} %pad_maximum_fusion.2), channel_id=1, source_target_pairs={{0,4},{4,0},{1,5},{5,1},{2,6},{6,2},{3,7},{7,3},{8,12},{12,8},{9,1... | collective-permute-start | bytes 12296 | tf_op jit(solution)/shard_map/ppermute | solution.py:47
  457.8 3.6 collective-permute-start.14
  461.5 5.8 %collective-permute-start.15 = (f32[8,128]{1,0:T(8,128)S(1)}, f32[8,128]{1,0:T(8,128)S(1)}, u32[]{:S(2)}, u32[]{:S(2)}) collective-permute-start(f32[8,128]{1,0:T(8,128)S(1)} %add.85), channel_id=1, source_target_pairs={{0,16},{16,0},{1,17},{17,1},{2,18},{18,2},{3,19},{19,3},{4,20},{20... | collective-permute-start | bytes 12296 | tf_op jit(solution)/shard_map/ppermute | solution.py:47
  467.9 1.4 copy-start.1
  469.1 4.6 copy-start.19
Sparse Core Ops, SparseCore 0:
  9.7 124.1 all-gather.5
  172.0 18.4 all-gather.3

commit v4 on v3

--- a/solution.py
+++ b/solution.py
@@ -144,7 +144,8 @@
     def __init__(self, array, rows, start, width):
         self.array, self.rows, self.width = array, rows, width
         self.spec = pl.BlockSpec(
-            (array.shape[0], rows, width), lambda *_: (0, 0, start // width)
+            array.shape[:-2] + (rows, width),
+            lambda *_: (0,) * (len(array.shape) - 1) + (start // width,),
         )
 
 
@@ -209,80 +210,166 @@
     row_count, width = cot.shape[-2:]
     per = row_count // rows
     return pl.BlockSpec(
-        (2, 2, 1, 1, rows, width), lambda i: (0, 0, i // per % 2, i // per // 2, i % per, 0)
-    )
-
-
-def cot_product(cot_ref, weight_ref):
-    width = cot_ref.shape[5]
-    total = 0.0
-    for j in range(4):
-        part = cot_ref[j % 2, j // 2, 0, 0]
-        total = total + matmul(part, weight_rows_of(weight_ref, j * width, width))
-    return total
-
-
-def out_grad_kernel(cot_ref, weight_ref, out_ref):
-    out_ref[...] = cot_product(cot_ref, weight_ref).astype(jnp.bfloat16)
-
-
-def attended_gradient(cot, weight, width, rows=512, after=()):
-    total = 4 * cot.shape[4]
-    return call(
-        out_grad_kernel,
-        "attended_gradient",
-        (total // rows,),
-        [cot_spec(cot, rows), weight.spec],
-        band(rows, width),
-        struct((total, width), jnp.bfloat16),
-        flops=8 * total * D * width,
-        after=after,
-    )(cot, weight.array)
-
-
-def up_grad_kernel(cot_ref, slope_ref, weight_ref, up_ref, sums_ref):
+        (1, 4, 1, rows, width), lambda i: (i // per % 2, 0, i // per // 2, i % per, 0)
+    )
+
+
+def back_kernel(
+    cot_ref, slope_ref, dense_ref, down_ref, attended_ref, up_ref, sums_ref
+):
     @pl.when(pl.program_id(0) == 0)
     def _():
         sums_ref[...] = jnp.zeros_like(sums_ref)
 
-    up = (cot_product(cot_ref, weight_ref) * slope_ref[...]).astype(jnp.bfloat16)
+    width = cot_ref.shape[4]
+    attended, up = 0.0, 0.0
+    for j in range(4):
+        part = cot_ref[0, j, 0]
+        attended = attended + matmul(part, weight_rows_of(dense_ref, j * width, width))
+        up = up + matmul(part, weight_rows_of(down_ref, j * width, width))
+    attended_ref[...] = attended.astype(jnp.bfloat16)
+    up = (up * slope_ref[...]).astype(jnp.bfloat16)
     up_ref[...] = up
     sums_ref[...] += jnp.sum(up.astype(jnp.float32), axis=0, keepdims=True)
 
 
-def up_gradient(cot, slope, weight, rows=512, after=()):
+def back_through(cot, slope, dense, down, rows=512, after=()):
     total, hidden = slope.shape
+    lanes = dense.width
     return call(
-        up_grad_kernel,
-        "up_gradient",
+        back_kernel,
+        "back_through",
         (total // rows,),
-        [cot_spec(cot, rows), band(rows, hidden), weight.spec],
-        [band(rows, hidden), whole(1, hidden)],
-        [struct((total, hidden), jnp.bfloat16), struct((1, hidden), jnp.float32)],
-        flops=4 * total * D * hidden,
-        after=after,
-    )(cot, slope, weight.array)
+        [cot_spec(cot, rows), band(rows, hidden), dense.spec, down.spec],
+        [band(rows, lanes), band(rows, hidden), whole(1, hidden)],
+        [
+            struct((total, lanes), jnp.bfloat16),
+            struct((total, hidden), jnp.bfloat16),
+            struct((1, hidden), jnp.float32),
+        ],
+        flops=4 * total * D * (hidden + lanes),
+        after=after,
+    )(cot, slope, dense.array, down.array)
 
 
 def rows_of(index, size):
     return pl.ds(pl.multiple_of(index * size, size), size)
 
 
-def attention_kernel(
+HEADS_HERE = [slice(n * HEAD_DIM, (n + 1) * HEAD_DIM) for n in range(2)]
+
+
+def turned_into(ref, source_ref, cols):
+    chunk = 256
+
+    def one(b, carry):
+        rows = rows_of(b, chunk)
+        ref[:, rows] = source_ref[rows, cols].T
+        return carry
+
+    lax.fori_loop(0, source_ref.shape[0] // chunk, one, 0)
+
+
+def causal_block(block):
+    return lax.broadcasted_iota(jnp.int32, (block, block), 0) <= lax.broadcasted_iota(
+        jnp.int32, (block, block), 1
+    )
+
+
+def fold_rows(values, combine):
+    rows, cols = values.shape
+    return combine(values.reshape(rows // 8, 8, cols), axis=0)
+
+
+def attention_kernel(block, qkv_ref, attended_ref, log_sums_ref, qt_ref, vt_ref, score_ref):
+    i = pl.program_id(0)
+    width = 2 * HEAD_DIM
+
+    @pl.when(i == 0)
+    def _():
+        turned_into(qt_ref, qkv_ref, slice(0, width))
+        turned_into(vt_ref, qkv_ref, slice(2 * width, 3 * width))
+        log_sums_ref[...] = jnp.zeros_like(log_sums_ref)
+
+    own = rows_of(i, block)
+    causal = causal_block(block)
+
+    def score(j, best, diagonal):
+        rows = rows_of(j, block)
+        new = []
+        for n, head in enumerate(HEADS_HERE):
+            start = width + n * HEAD_DIM
+            part = matmul(qkv_ref[rows, start : start + HEAD_DIM], qt_ref[head, own])
+            if diagonal:
+                part = jnp.where(causal, part, -1e30)
+            score_ref[n, j] = part
+            new.append(jnp.maximum(best[n], fold_rows(part, jnp.max)))
+        return tuple(new)
+
+    low = jnp.full((8, block), -1e30, jnp.float32)
+    best = lax.fori_loop(0, i, lambda j, b: score(j, b, False), (low, low))
+    best = score(i, best, True)
+    top = [jnp.max(value, axis=0, keepdims=True) for value in best]
+
+    def weigh(j, carry):
+        new = []
+        for n in range(2):
+            weights = jnp.exp(score_ref[n, j] - top[n])
+            score_ref[n, j] = weights
+            new.append(carry[n] + fold_rows(weights, jnp.sum))
+        return tuple(new)
+
+    zero = jnp.zeros((8, block), jnp.float32)
+    totals = lax.fori_loop(0, i + 1, weigh, (zero, zero))
+    totals = [jnp.sum(total, axis=0, keepdims=True) for total in totals]
+    scales = [1.0 / total for total in totals]
+    for n in range(2):
+        log_sums_ref[n : n + 1, own] = top[n] + jnp.log(totals[n])
+
+    def push(j, carry):
+        rows = rows_of(j, block)
+        new = []
+        for n, head in enumerate(HEADS_HERE):
+            probs = (score_ref[n, j] * scales[n]).astype(jnp.bfloat16)
+            new.append(carry[n] + matmul(vt_ref[head, rows], probs))
+        return tuple(new)
+
+    zero = jnp.zeros((HEAD_DIM, block), jnp.float32)
+    out = lax.fori_loop(0, i + 1, push, (zero, zero))
+    attended_ref[own, :] = jnp.concatenate(out, axis=0).T.astype(jnp.bfloat16)
+
+
+def attention(qkv, block=512, after=()):
+    rows, width = qkv.shape[0], 2 * HEAD_DIM
+    blocks = rows // block
+    return call(
+        partial(attention_kernel, block),
+        "attention",
+        (blocks,),
+        [whole(rows, 3 * width)],
+        [whole(rows, width), whole(8, rows)],
+        [struct((rows, width), jnp.bfloat16), struct((8, rows), jnp.float32)],
+        [pltpu.VMEM((width, rows), jnp.bfloat16)] * 2
+        + [pltpu.VMEM((2, blocks, block, block), jnp.float32)],
+        flops=10 * 10**9,
+        after=after,
+    )(qkv)
+
+
+def attention_back_kernel(
     blocks,
     block,
     qkv_ref,
     grad_ref,
+    log_sums_ref,
     cosine_ref,
     sine_ref,
-    attended_ref,
     pre_grad_ref,
     sums_ref,
     qt_ref,
     kt_ref,
-    vt_ref,
     gt_ref,
-    score_ref,
+    prob_ref,
     slope_ref,
     k_total,
     v_total,
@@ -290,89 +377,56 @@
     i = pl.program_id(0)
     width = 2 * HEAD_DIM
     factor = 1.0 / math.sqrt(HEAD_DIM)
-    heads = [slice(n * HEAD_DIM, (n + 1) * HEAD_DIM) for n in range(2)]
     chunk = 256
-    chunks = qkv_ref.shape[0] // chunk
 
     @pl.when(i == 0)
     def _():
-        def prepare(b, carry):
-            rows = rows_of(b, chunk)
-            for n, ref in enumerate((qt_ref, kt_ref, vt_ref)):
-                ref[:, rows] = qkv_ref[rows, n * width : (n + 1) * width].T
-            gt_ref[:, rows] = grad_ref[rows, :].T
-            return carry
-
-        lax.fori_loop(0, chunks, prepare, 0)
+        turned_into(qt_ref, qkv_ref, slice(0, width))
+        turned_into(kt_ref, qkv_ref, slice(width, 2 * width))
+        turned_into(gt_ref, grad_ref, slice(0, width))
         k_total[...] = jnp.zeros_like(k_total)
         v_total[...] = jnp.zeros_like(v_total)
         sums_ref[...] = jnp.zeros_like(sums_ref)
 
     own = rows_of(i, block)
-    causal = lax.broadcasted_iota(jnp.int32, (block, block), 0) <= lax.broadcasted_iota(
-        jnp.int32, (block, block), 1
-    )
-
-    def fold(values, combine):
-        return combine(values.reshape(block // 8, 8, block), axis=0)
-
-    def score(j, best, diagonal):
+    causal = causal_block(block)
+    log_sums = [log_sums_ref[n : n + 1, own] for n in range(2)]
+
+    def weigh(j, carry, diagonal):
         rows = rows_of(j, block)
         new = []
-        for n, head in enumerate(heads):
+        for n, head in enumerate(HEADS_HERE):
             start = width + n * HEAD_DIM
-            part = matmul(qkv_ref[rows, start : start + HEAD_DIM], qt_ref[head, own])
+            scores = matmul(qkv_ref[rows, start : start + HEAD_DIM], qt_ref[head, own])
+            probs = jnp.exp(scores - log_sums[n])
             if diagonal:
-                part = jnp.where(causal, part, -1e30)
-            score_ref[n, j] = part
-            new.append(jnp.maximum(best[n], fold(part, jnp.max)))
+                probs = jnp.where(causal, probs, 0.0)
+            start += width
+            slope = matmul(qkv_ref[rows, start : start + HEAD_DIM], gt_ref[head, own])
+            prob_ref[n, j] = probs
+            slope_ref[n, j] = slope
+            new.append(carry[n] + fold_rows(probs * slope, jnp.sum))
         return tuple(new)
 
-    low = jnp.full((8, block), -1e30, jnp.float32)
-    best = lax.fori_loop(0, i, lambda j, b: score(j, b, False), (low, low))
-    best = score(i, best, True)
-    top = [jnp.max(value, axis=0, keepdims=True) for value in best]
-
-    def weigh(j, carry):
-        rows = rows_of(j, block)
-        new = []
-        for n, head in enumerate(heads):
-            total, dots = carry[n]
-            begin = 2 * width + n * HEAD_DIM
-            weights = jnp.exp(score_ref[n, j] - top[n])
-            slope = matmul(qkv_ref[rows, begin : begin + HEAD_DIM], gt_ref[head, own])
-            score_ref[n, j] = weights
-            slope_ref[n, j] = slope
-            new.append((total + fold(weights, jnp.sum), dots + fold(weights * slope, jnp.sum)))
-        return tuple(new)
-
     zero = jnp.zeros((8, block), jnp.float32)
-    weighed = lax.fori_loop(0, i + 1, weigh, ((zero, zero), (zero, zero)))
-    scales = [1.0 / jnp.sum(total, axis=0, keepdims=True) for total, _ in weighed]
-    dots = [
-        jnp.sum(dot, axis=0, keepdims=True) * scale for (_, dot), scale in zip(weighed, scales)
-    ]
+    dots = lax.fori_loop(0, i, lambda j, c: weigh(j, c, False), (zero, zero))
+    dots = weigh(i, dots, True)
+    dots = [jnp.sum(dot, axis=0, keepdims=True) for dot in dots]
 
     def push(j, carry):
         rows = rows_of(j, block)
         new = []
-        for n, head in enumerate(heads):
-            out, q_grad = carry[n]
-            probs = score_ref[n, j] * scales[n]
-            low = probs.astype(jnp.bfloat16)
+        for n, head in enumerate(HEADS_HERE):
+            probs = prob_ref[n, j]
             score_grad = (probs * (slope_ref[n, j] - dots[n])).astype(jnp.bfloat16)
             k_total[rows, head] += matmul(score_grad, qkv_ref[own, head])
-            v_total[rows, head] += matmul(low, grad_ref[own, head])
-            out = out + matmul(vt_ref[head, rows], low)
-            new.append((out, q_grad + matmul(kt_ref[head, rows], score_grad)))
+            v_total[rows, head] += matmul(probs.astype(jnp.bfloat16), grad_ref[own, head])
+            new.append(carry[n] + matmul(kt_ref[head, rows], score_grad))
         return tuple(new)
 
     zero = jnp.zeros((HEAD_DIM, block), jnp.float32)
-    pushed = lax.fori_loop(0, i + 1, push, ((zero, zero), (zero, zero)))
-    attended_ref[own, :] = jnp.concatenate([out for out, _ in pushed], axis=0).T.astype(
-        jnp.bfloat16
-    )
-    q_grad = jnp.concatenate([grad for _, grad in pushed], axis=0).T * factor
+    q_grad = lax.fori_loop(0, i + 1, push, (zero, zero))
+    q_grad = jnp.concatenate(q_grad, axis=0).T * factor
     q_pre = turn(q_grad, cosine_ref[own, :], -sine_ref[own, :]).astype(jnp.bfloat16)
     pre_grad_ref[own, :width] = q_pre
     sums_ref[:, :width] += jnp.sum(q_pre.astype(jnp.float32), axis=0, keepdims=True)
@@ -390,35 +444,28 @@
             return carry + jnp.sum(both, axis=0, keepdims=True)
 
         sums_ref[:, width:] = lax.fori_loop(
-            0, chunks, finish, jnp.zeros((1, 2 * width), jnp.float32)
+            0, qkv_ref.shape[0] // chunk, finish, jnp.zeros((1, 2 * width), jnp.float32)
         )
 
 
-def attention(qkv, out_grad, block=512, after=()):
+def attention_back(qkv, out_grad, log_sums, block=512, after=()):
     rows, width = qkv.shape[0], 2 * HEAD_DIM
     blocks = rows // block
     cosine, sine = rotary_tables(rows)
     return call(
-        partial(attention_kernel, blocks, block),
-        "attention",
+        partial(attention_back_kernel, blocks, block),
+        "attention_back",
         (blocks,),
-        [whole(rows, 3 * width), whole(rows, width), whole(rows, width), whole(rows, width)],
-        [whole(rows, width), whole(rows, 3 * width), whole(1, 3 * width)],
-        [
-            struct((rows, width), jnp.bfloat16),
-            struct((rows, 3 * width), jnp.bfloat16),
-            struct((1, 3 * width), jnp.float32),
-        ],
-        [pltpu.VMEM((width, rows), jnp.bfloat16)] * 4
-        + [
-            pltpu.VMEM((2, blocks, block, block), jnp.float32),
-            pltpu.VMEM((2, blocks, block, block), jnp.float32),
-            pltpu.VMEM((rows, width), jnp.float32),
-            pltpu.VMEM((rows, width), jnp.float32),
-        ],
-        flops=28 * 10**9,
-        after=after,
-    )(qkv, out_grad, jnp.asarray(cosine), jnp.asarray(sine))
+        [whole(rows, 3 * width), whole(rows, width), whole(8, rows)]
+        + [whole(rows, width), whole(rows, width)],
+        [whole(rows, 3 * width), whole(1, 3 * width)],
+        [struct((rows, 3 * width), jnp.bfloat16), struct((1, 3 * width), jnp.float32)],
+        [pltpu.VMEM((width, rows), jnp.bfloat16)] * 3
+        + [pltpu.VMEM((2, blocks, block, block), jnp.float32)] * 2
+        + [pltpu.VMEM((rows, width), jnp.float32)] * 2,
+        flops=20 * 10**9,
+        after=after,
+    )(qkv, out_grad, log_sums, jnp.asarray(cosine), jnp.asarray(sine))
 
 
 def weight_grad_kernel(riders, *refs):
@@ -430,12 +477,12 @@
     cols = out_ref.shape[2]
     start = 0
     for left_ref, right_ref in zip(refs[::2], refs[1::2]):
-        if len(right_ref.shape) == 6:
-            size = right_ref.shape[4]
+        if len(right_ref.shape) == 5:
+            size = right_ref.shape[3]
             part = 0.0
             for b in range(4):
                 rows = slice(b * size, (b + 1) * size)
-                part = part + contract_rows(left_ref[rows, :], right_ref[0, 0, b % 2, b // 2])
+                part = part + contract_rows(left_ref[rows, :], right_ref[b % 2, 0, b // 2])
         else:
             part = contract_rows(left_ref[...], right_ref[...])
         part = part.astype(jnp.bfloat16)
@@ -457,11 +504,9 @@
         height += rider.shape[1]
     for left, right in pairs:
         in_specs.append(whole(*left.shape))
-        if right.ndim == 6:
+        if right.ndim == 5:
             in_specs.append(
-                pl.BlockSpec(
-                    (1, 1, 2, 2, right.shape[4], D // 4), lambda i: (i % 2, i // 2, 0, 0, 0, 0)
-                )
+                pl.BlockSpec((2, 1, 2, right.shape[3], D // 4), lambda i: (0, i, 0, 0, 0))
             )
         else:
             in_specs.append(pl.BlockSpec((rows, D // 4), lambda i: (0, i)))
@@ -478,39 +523,45 @@
     )(*operands)
 
 
-def partial_sum_kernel(sides, core_ref, *refs):
-    lefts, weights, outs = refs[:sides], refs[sides : 2 * sides], refs[2 * sides :]
-    width = outs[0].shape[3]
-    for m in range(2):
-        for core, out_ref in zip((core_ref[0], 1 - core_ref[0]), outs):
-            start = (2 * m + core) * width
-            out = 0.0
-            for left, weight in zip(lefts, weights):
-                out = out + contract_cols(left[...], weight_rows_of(weight, start, width))
-            out_ref[m, 0] = out.astype(jnp.bfloat16)
-
-
-def partial_sum(sides, core, row_count, width, name, rows=512, after=()):
+def partial_sum_kernel(sides, halves, index_ref, *refs):
+    lefts, refs = refs[: 2 * sides], refs[2 * sides :]
+    weights, others, outs = refs[:sides], refs[sides : 2 * sides], refs[2 * sides :]
+    rows, width = outs[0].shape[1:]
+    own_m, core = index_ref[0], index_ref[1]
+    for n_m, m in enumerate((own_m, 1 - own_m)):
+        out = 0.0
+        for n in range(sides):
+            weight = weight_rows_of(weights[n], (2 * m + core) * width, width)
+            out = out + contract_cols(lefts[n][...], weight)
+            other = others[n][m].reshape(width, weight.shape[1])
+            out = out + contract_cols(lefts[sides + n][...], other)
+        out = out.astype(jnp.bfloat16)
+        for half in range(halves):
+            outs[2 * half + n_m][0] = out[half * rows : (half + 1) * rows]
+
+
+def partial_sum(sides, row_count, width, name, halves, after=()):
     total = sides[0][0].shape[0]
-    per = row_count // rows
-    lefts = [left for left, _ in sides]
+    rows = row_count // halves
+    lefts = [side[0] for side in sides] + [side[1] for side in sides]
+    weights = [side[2] for side in sides]
+    others = [side[3] for side in sides]
     depth = sum(left.shape[1] for left in lefts)
-    spec = pl.BlockSpec((2, 1, rows, width), lambda i: (0, i // per, i % per, 0))
-    shape = struct((2, total // row_count, row_count, width), jnp.bfloat16)
+    outs = 2 * halves
+    index = jnp.stack([lax.axis_index("m"), lax.axis_index("c")]).astype(jnp.int32)
     return call(
-        partial(partial_sum_kernel, len(sides)),
+        partial(partial_sum_kernel, len(sides), halves),
         name,
-        (total // rows,),
+        (total // row_count,),
         [SCALARS]
-        + [band(rows, left.shape[1]) for left in lefts]
-        + [
-            weight.spec for _, weight in sides
-        ],
-        [spec, spec],
-        [shape, shape],
-        flops=4 * total * depth * D,
-        after=after,
-    )(core, *lefts, *[weight.array for _, weight in sides])
+        + [band(row_count, left.shape[1]) for left in lefts]
+        + [weight.spec for weight in weights]
+        + [other.spec for other in others],
+        [pl.BlockSpec((1, rows, width), lambda i: (i, 0, 0))] * outs,
+        [struct((total // row_count, rows, width), jnp.bfloat16)] * outs,
+        flops=2 * total * depth * D,
+        after=after,
+    )(index, *lefts, *[weight.array for weight in weights], *[other.array for other in others])
 
 
 def switch_specs(count, block):
@@ -579,7 +630,7 @@
             out_ref[n, 0, rows:, :] = rider
 
 
-def gathered(shards, turned, rider=None, after=()):
+def packed(shards, turned, rider=None):
     wide = lax.axis_size(WIDE)
     specs, rows, width = column_specs(shards, turned, lambda i: i)
     height = rows
@@ -595,8 +646,12 @@
         pl.BlockSpec((wide // 4, 1, height, width), lambda i: (0, i, 0, 0)),
         struct((wide // 4, 4, height, width), jnp.bfloat16),
     )(*shards)
+    return blocks.reshape(wide, height, width)
+
+
+def exchanged(blocks, after=()):
     blocks = lax.optimization_barrier((blocks, *after))[0]
-    return lax.all_to_all(blocks.reshape(wide, height, width), WIDE, 0, 0)
+    return lax.all_to_all(blocks, WIDE, 0, 0)
 
 
 def unpack_kernel(turned, arrived_ref, *outs):
@@ -638,66 +693,76 @@
     return shards, riders
 
 
-def fold_kernel(index_ref, mine_ref, arrived_ref, keep_ref, send_ref):
-    total = mine_ref[0, 0, 0].astype(jnp.float32) + arrived_ref[0, 0, 0].astype(jnp.float32)
-    total = total.astype(jnp.bfloat16)
-
-    @pl.when(pl.program_id(0) == 0)
-    def _():
-        keep_ref[0] = total
-
-    @pl.when(pl.program_id(0) == 1)
-    def _():
-        send_ref[0] = total
+def fold_kernel(index_ref, mine_keep, mine_send, arrived_keep, arrived_send, keep_ref, send_ref):
+    keep_ref[...] = mine_keep[...] + arrived_keep[...]
+    send_ref[...] = mine_send[...] + arrived_send[...]
 
 
 def folded(mine, arrived, axes, axis, after=()):
     position = axes.index(axis)
     high, low = 2**position, 2 ** (len(axes) - 1 - position)
     rows, cols = mine.shape[-2:]
-    spec = pl.BlockSpec(
-        (1, 1, 1, rows, cols),
-        lambda k, j, p: (j // low, lax.rem(k + p[0], 2), lax.rem(j, low), 0, 0),
-    )
-    shape = (high, 2, low, rows, cols)
-    count = high * low
-    return prefetch_call(
+    shape = (high, 2, low * rows, cols)
+    steps = 2 if low > 1 else 1
+    block = low * rows // steps
+    halves = [
+        pl.BlockSpec((high, None, block, cols), lambda j, p: (0, p[0], j, 0)),
+        pl.BlockSpec((high, None, block, cols), lambda j, p: (0, 1 - p[0], j, 0)),
+    ]
+    out = pl.BlockSpec((high, block, cols), lambda j, p: (0, j, 0))
+    mine, arrived = mine.reshape(shape), arrived.reshape(shape)
+    keep, send = prefetch_call(
         fold_kernel,
         "fold",
         lax.axis_index(axis),
-        (2, count),
-        [spec, spec],
-        switch_specs(count, (1, rows, cols)),
-        [struct((count, rows, cols), jnp.bfloat16)] * 2,
-        after=after,
-    )(mine.reshape(shape), arrived.reshape(shape))
+        (steps,),
+        halves * 2,
+        [out, out],
+        [struct((high, low * rows, cols), jnp.bfloat16)] * 2,
+        after=after,
+    )(mine, mine, arrived, arrived)
+    return [part.reshape(high * low, rows, cols) for part in (keep, send)]
 
 
 def join_kernel(index_ref, mine_ref, other_ref, out_ref):
-    @pl.when(pl.program_id(0) == 0)
-    def _():
-        out_ref[0, 0] = mine_ref[0]
-
-    @pl.when(pl.program_id(0) == 1)
-    def _():
-        out_ref[0, 0] = other_ref[0]
+    out_ref[index_ref[0]] = mine_ref[...]
+    out_ref[1 - index_ref[0]] = other_ref[...]
 
 
 def joined(mine, axis, after=()):
     other = shifted(mine, axis, 1)
-    rows, cols = mine.shape[-2:]
-    count = mine.size // (rows * cols)
+    rows, cols = mine.size // mine.shape[-1] // 2, mine.shape[-1]
+    spec = pl.BlockSpec((rows, cols), lambda j, p: (j, 0))
     out = prefetch_call(
         join_kernel,
         "join",
         lax.axis_index(axis),
-        (2, count),
-        switch_specs(count, (1, rows, cols)),
-        pl.BlockSpec((1, 1, rows, cols), lambda k, j, p: (lax.rem(k + p[0], 2), j, 0, 0)),
-        struct((2, count, rows, cols), mine.dtype),
-        after=after,
-    )(mine.reshape(count, rows, cols), other.reshape(count, rows, cols))
+        (2,),
+        [spec, spec],
+        pl.BlockSpec((2, rows, cols), lambda j, p: (0, j, 0)),
+        struct((2, 2 * rows, cols), mine.dtype),
+        after=after,
+    )(mine.reshape(2 * rows, cols), other.reshape(2 * rows, cols))
     return out.reshape((2,) + mine.shape)
+
+
+def finish_kernel(tokens_ref, keep_ref, arrived_ref, bias_ref, out_ref):
+    total = tokens_ref[...].astype(jnp.float32) + keep_ref[...].astype(jnp.float32)
+    total = total + arrived_ref[...].astype(jnp.float32) + bias_ref[...]
+    out_ref[...] = total.astype(jnp.bfloat16)
+
+
+def finished(tokens, keep, arrived, bias, after=()):
+    spec = whole(*tokens.shape)
+    return call(
+        finish_kernel,
+        "finish",
+        (1,),
+        [spec, spec, spec, whole(*bias.shape)],
+        spec,
+        struct(tokens.shape, tokens.dtype),
+        after=after,
+    )(tokens, keep, arrived, bias)
 
 
 def gather_narrow(value):
@@ -742,32 +807,38 @@
     weight_rows = w_fc1.shape[0]
     lanes = w_query.shape[1] // 4
 
-    core = lax.axis_index("c").astype(jnp.int32).reshape(1)
-
     vectors = (ln_gain, ln_shift, b_query, b_key, b_value, b_dense, b_fc2, b_fc1)
     lengths = [vector.shape[0] for vector in vectors]
     hidden = w_fc1.shape[1] // 4
-    width = 4 * lanes + hidden
-    packed = jnp.concatenate(vectors)
-    packed = jnp.pad(packed, (0, 16 * width - packed.shape[0])).reshape(16, width)
+    rider = jnp.concatenate(vectors)
+    rider = jnp.pad(rider, (0, 16 * hidden - rider.shape[0])).reshape(16, hidden)
 
     tokens_full = lax.all_gather(tokens, CUBE, axis=0, tiled=False)
     tokens_full = tokens_full.reshape(4, 4, row_count, feature_count)
-    cot = joined(cotangent, "g")
-    arrived = gathered(
-        [w_query, w_key, w_value, w_dense, w_fc1],
-        [False, False, False, True, False],
-        packed,
-        after=[cot],
-    )
-    cot = joined(joined(cot, "h"), "m")
-    cot = lax.all_gather(cot, "c", axis=0, tiled=False)
-    down_weight = Weight(gathered([w_fc2], [True]), weight_rows, 0, hidden)
-    qkv_weight = Weight(arrived, weight_rows, 0, 3 * lanes)
-    dense_weight = Weight(arrived, weight_rows, 3 * lanes, lanes)
-    up_weight = Weight(arrived, weight_rows, 4 * lanes, hidden)
-
-    here = arrived[:, weight_rows:].reshape(wide, 16 * width)
+    up_blocks = packed([w_fc1], [False], rider)
+    head_blocks = packed([w_query, w_key, w_value, w_dense], [False, False, False, True])
+    cot = joined(cotangent, "g", after=[up_blocks, head_blocks])
+    arrived = exchanged(up_blocks, after=[cot])
+    cot = lax.all_gather(cot, ("h", "m", "c"), axis=0, tiled=False)
+    cot = cot.reshape(2, 4, 2, row_count, feature_count)
+    head_arrived = exchanged(head_blocks)
+    down_arrived = exchanged(packed([w_fc2], [True]))
+    up_weight = Weight(arrived, weight_rows, 0, hidden)
+    qkv_weight = Weight(head_arrived, weight_rows, 0, 3 * lanes)
+    dense_weight = Weight(head_arrived, weight_rows, 3 * lanes, lanes)
+    down_weight = Weight(down_arrived, weight_rows, 0, hidden)
+
+    def from_other_core(array):
+        split = array[:, :weight_rows].reshape(2, 2, wide // 4, weight_rows, -1)
+        return shifted(pick(split, 1 - lax.axis_index("c"), 1), "c", 1)
+
+    up_other = Weight(from_other_core(arrived), weight_rows, 0, hidden)
+    head_other = from_other_core(head_arrived)
+    qkv_other = Weight(head_other, weight_rows, 0, 3 * lanes)
+    dense_other = Weight(head_other, weight_rows, 3 * lanes, lanes)
+    down_other = Weight(from_other_core(down_arrived), weight_rows, 0, hidden)
+
+    here = arrived[:, weight_rows:].reshape(wide, 16 * hidden)
     local, start = [], 0
     for length in lengths:
         local.append(here[:, start : start + length].astype(jnp.float32).reshape(-1))
@@ -783,30 +854,29 @@
     up_bias = quarter_of(local[7]).reshape(1, -1)
     own_gain, out_bias = local[0], local[5] + local[6]
 
-    normed, stats, up_low, up_slope = norm_up(tokens_full, gain, shift, up_bias, up_weight)
+    normed, stats, up_low, up_slope = norm_up(
+        tokens_full, gain, shift, up_bias, up_weight, after=[up_other.array]
+    )
     qkv = project_heads(normed, qkv_bias, qkv_weight)
-    attended_grad = attended_gradient(cot, dense_weight, lanes, after=[qkv])
-    grad_down = weight_grad([(up_low, cot)], wide, after=[attended_grad])
-    attended, qkv_grad, qkv_sums = attention(qkv, attended_grad, after=[grad_down])
-    up_grad, up_sums = up_gradient(cot, up_slope, down_weight, after=[attended])
-    normed_grad = partial_sum(
-        [(qkv_grad, qkv_weight), (up_grad, up_weight)],
-        core,
-        row_count,
-        feature_count,
-        "normed_gradient",
-    )
-    grad_up = weight_grad([(up_grad, normed)], wide, after=normed_grad[:1])
+    attended, log_sums = attention(qkv)
+    grad_down = weight_grad([(up_low, cot)], wide, after=[attended])
+    attended_grad, up_grad, up_sums = back_through(
+        cot, up_slope, dense_weight, down_weight, after=[grad_down]
+    )
     branch = partial_sum(
-        [(attended, dense_weight), (up_low, down_weight)],
-        core,
+        [
+            (attended, shifted(attended, "c", 1), dense_weight, dense_other),
+            (up_low, shifted(up_low, "c", 1), down_weight, down_other),
+        ],
         row_count,
         feature_count,
         "branch_sum",
-        after=[grad_up],
-    )
-    first = folded(normed_grad[0], shifted(normed_grad[1], "c", 1), "mgh", "m", after=branch[:1])
-    second = folded(branch[0], shifted(branch[1], "c", 1), "mgh", "h", after=first[:1])
+        1,
+        after=[up_grad],
+    )
+    qkv_grad, qkv_sums = attention_back(qkv, attended_grad, log_sums, after=branch[:1])
+    qkv_grad_other = shifted(qkv_grad, "c", 1)
+
     def spread(vector):
         placed = jnp.zeros((4, vector.shape[0]), jnp.float32)
         placed = lax.dynamic_update_index_in_dim(placed, vector, quarter, 0)
@@ -822,36 +892,60 @@
     rider = jnp.concatenate(terms, axis=1).astype(jnp.bfloat16)
     early_count = rider.shape[1]
     rider = jnp.pad(rider, ((0, 0), (0, 16 * weight_rows - early_count)))
-    grad_heads = weight_grad(
-        [(qkv_grad, normed), (attended, cot)],
+    grad_rest = weight_grad(
+        [(up_grad, normed), (qkv_grad, normed), (attended, cot)],
         wide,
         rider.reshape(wide, 16, weight_rows),
+    )
+    second = folded(branch[0], shifted(branch[1], "m", 1), "gh", "h", after=[grad_rest, qkv_grad_other])
+    grad_rest = lax.optimization_barrier((grad_rest, second[0]))[0]
+    normed_grad = partial_sum(
+        [
+            (qkv_grad, qkv_grad_other, qkv_weight, qkv_other),
+            (up_grad, shifted(up_grad, "c", 1), up_weight, up_other),
+        ],
+        row_count,
+        feature_count,
+        "normed_gradient",
+        2,
         after=second[:1],
     )
-    (grad_down,), _ = scatter_columns(grad_down, [hidden], [True], after=[grad_heads])
-    first = folded(first[0], shifted(first[1], "m", 1), "gh", "h", after=[grad_down])
-    second = folded(second[0], shifted(second[1], "h", 1), "mg", "m", after=first[:1])
-    (grad_up,), _ = scatter_columns(grad_up, [hidden], [False], after=second[:1])
-    first = folded(first[0], shifted(first[1], "h", 1), "g", "g", after=[grad_up])
-    second = folded(second[0], shifted(second[1], "m", 1), "g", "g", after=first[:1])
-    (grad_query, grad_key, grad_value, grad_dense), riders = scatter_columns(
-        grad_heads, [lanes] * 4, [False, False, False, True]
+
+    (grad_down,), _ = scatter_columns(grad_down, [hidden], [True], after=normed_grad[:1])
+    first = [normed_grad[:2], normed_grad[2:]]
+    first[0] = folded(first[0][0], shifted(first[0][1], "m", 1), "gh", "h", after=[grad_down])
+    second = folded(second[0], shifted(second[1], "h", 1), "g", "g", after=first[0][:1])
+    first[1] = folded(first[1][0], shifted(first[1][1], "m", 1), "gh", "h", after=second[:1])
+    first[0] = folded(first[0][0], shifted(first[0][1], "h", 1), "g", "g", after=first[1][:1])
+    first[1] = folded(first[1][0], shifted(first[1][1], "h", 1), "g", "g", after=first[0][:1])
+    output = finished(
+        tokens,
+        second[0][0],
+        shifted(second[1][0], "g", 1),
+        out_bias.reshape(1, -1),
+        after=first[1][:1],
+    )
+    (grad_up, grad_query, grad_key, grad_value, grad_dense), riders = scatter_columns(
+        grad_rest,
+        [hidden] + [lanes] * 4,
+        [False, False, False, False, True],
+        after=[output],
     )
     early = jnp.sum(riders.astype(jnp.float32), axis=0).reshape(-1)[:early_count]
 
     def last(keep, send):
-        return keep[0].astype(jnp.float32) + shifted(send[0], "g", 1).astype(jnp.float32)
+        arrived = lax.optimization_barrier((shifted(send[0], "g", 1), grad_dense))[0]
+        return keep[0].astype(jnp.float32) + arrived.astype(jnp.float32)
 
     local_x = tokens.astype(jnp.float32)
-    standard_grad = last(*first)
-    output = (local_x + last(*second) + out_bias).astype(jnp.bfloat16)
+    standard_grad = jnp.concatenate([last(*part) for part in first], axis=0)
     own_stats = pick(stats.reshape(4, row_count, 128), quarter)
     row_mean, inverse_std = own_stats[:, :1], own_stats[:, 64:65]
     standard = (local_x - row_mean) * inverse_std
     scaled_grad = standard_grad * own_gain
-    row_sums = lax.psum(
-        (jnp.sum(scaled_grad, axis=1), jnp.sum(scaled_grad * standard, axis=1)), NARROW
-    )
+    row_sums = jnp.stack([jnp.sum(scaled_grad, axis=1), jnp.sum(scaled_grad * standard, axis=1)])
+    for axis in ("c", "m"):
+        row_sums = row_sums + shifted(row_sums, axis, 1)
     input_grad = (
         scaled_grad - row_sums[0][:, None] / D - standard * (row_sums[1][:, None] / D)
     ) * inverse_std + cotangent.astype(jnp.float32)

time: 483 us -> 440 us (0.911)
  Pallas kernels: 186 us -> 162 us
  starting transfers between devices: 66 us -> 50.7 us
  local copies, waits for them, and re-layouts: 17.2 us -> 31.8 us
  waiting for transfers between devices: 185 us -> 175 us
  blocking collectives: 6.04 us -> 0 us
    all_to_all x2 -> x3, waiting for transfers between devices: 0.29 us -> 96.5 us  [exchanged(): return lax.all_to_all(blocks, WIDE, 0, 0)]
    ppermute x16 -> x24, waiting for transfers between devices: 167 us -> 77.6 us  [shifted(): lax.ppermute(value, axis, [(source, (source + step) % count) for source i...]
    pallas_call x9 -> x7, Pallas kernels: 45.6 us -> 17.3 us  [prefetch_call(): run(index.astype(jnp.int32).reshape(1), *after, *operands)]
    ppermute x16 -> x24, starting transfers between devices: 40.7 us -> 20 us  [shifted(): lax.ppermute(value, axis, [(source, (source + step) % count) for source i...]
    all_to_all x3 -> x2, waiting for transfers between devices: 16.8 us -> 0.01 us  [scatter_columns(): arrived = lax.all_to_all(grad, WIDE, 0, 0)]
    all_to_all x2 -> x3, starting transfers between devices: 9.74 us -> 18.4 us  [exchanged(): return lax.all_to_all(blocks, WIDE, 0, 0)]
    unnamed x46 -> x56, local copies, waits for them, and re-layouts: 8.27 us -> 14.6 us
    psum x1 -> x0, blocking collectives: 6.04 us -> none  [body(): lax.psum((jnp.sum(scaled_grad, axis=1), jnp.sum(scaled_grad * standard, a...]
  transfers between devices with their start and end apart: 23 -> 31, of which waited for: 11 -> 15; matrix products, arithmetic and copies ran while one was open for 3% -> 5% of each run, Pallas kernels for 38% -> 37%
where the time goes in v4:
time: 440 us; the launch traced here: 438 us
  waiting for transfers between devices  175 us (40%)
  Pallas kernels  162 us (37%)
  starting transfers between devices  50.7 us (12%)
  local copies, waits for them, and re-layouts  31.8 us (7%)
  between operations  14.5 us (3%)
    pallas_call x15, Pallas kernels, call(): return lambda *operands: run(*after, *operands)  145 us
    all_to_all x3, waiting for transfers between devices, exchanged(): return lax.all_to_all(blocks, WIDE, 0, 0)  96.5 us
    ppermute x24, waiting for transfers between devices, shifted(): lax.ppermute(value, axis, [(source, (source + step) % count) for source i...  77.6 us
    ppermute x24, starting transfers between devices, shifted(): lax.ppermute(value, axis, [(source, (source + step) % count) for source i...  20 us
    all_to_all x3, starting transfers between devices, exchanged(): return lax.all_to_all(blocks, WIDE, 0, 0)  18.4 us
    pallas_call x7, Pallas kernels, prefetch_call(): run(index.astype(jnp.int32).reshape(1), *after, *operands)  17.3 us
    unnamed x56, local copies, waits for them, and re-layouts  14.6 us
    all_to_all x2, starting transfers between devices, scatter_columns(): arrived = lax.all_to_all(grad, WIDE, 0, 0)  12.3 us
  transfers between devices with their start and end apart: 31, of which 15 were waited for; matrix products, arithmetic and copies ran while one was open for 5% of the time, Pallas kernels for 37%

profile of v4, /device:TPU:0, one launch (start us, length us, event | category | flops | bytes accessed | tf_op | source)
XLA Modules:
  0.0 437.7 jit_solution(5556350130435784853)
XLA Ops:
  8.0 3.1 collective-permute-start
  11.1 5.4 %concatenate.16 = bf16[704]{0:T(1024)(128)(2,1)S(1)} concatenate(bf16[64]{0:T(256)(128)(2,1)} %param.22, bf16[64]{0:T(256)(128)(2,1)} %param.23, bf16[64]{0:T(256)(128)(2,1)} %param.25, bf16[64]{0:T(256)(128)(2,1)} %param.27, bf16[64]{0:T(256)(128)(2,1)} %param.29, bf16[64]{0:T(256)(128)(2,1)} %param.31, bf16[64]{0:T(256)(128)(2,1)} %param.35, bf16[256]{0:T(256)(128)(2,1)} %param.33), dimensions={0} | concatenate | bytes 2816 | tf_op jit(solution)/shard_map/concatenate | solution.py:813
  17.1 3.6 pack.3
  20.7 3.8 pack.4
  24.5 2.8 collective-permute-done.refs_3_
  28.1 2.1 join.1
  30.2 6.6 %all-to-all-start.1 = ((bf16[8,256,512]{2,1,0:T(8,128)(2,1)}), bf16[8,256,512]{2,1,0:T(8,128)(2,1)S(1)}, u32[]{:S(2)}, u32[]{:S(2)}) async-start(bf16[8,256,512]{2,1,0:T(8,128)(2,1)} %bitcast.97), calls=%async_computation.1 | async-start | bytes 4194304 | tf_op jit(solution)/shard_map/all_to_all | solution.py:654
  36.8 53.2 %all-to-all-done.1.refs_4_.refs_3_.refs_6_ = bf16[8,256,512]{2,1,0:T(8,128)(2,1)S(1)} async-done(((bf16[8,256,512]{2,1,0:T(8,128)(2,1)}), bf16[8,256,512]{2,1,0:T(8,128)(2,1)S(1)}, u32[]{:S(2)}, u32[]{:S(2)}) %all-to-all-start.1) | async-done | bytes 2097184 | tf_op jit(solution)/shard_map/all_to_all | solution.py:654
  91.3 7.3 %all-to-all-start = ((bf16[8,272,512]{2,1,0:T(8,128)(2,1)}), bf16[8,272,512]{2,1,0:T(8,128)(2,1)}, u32[]{:S(2)}, u32[]{:S(2)}) async-start(bf16[8,272,512]{2,1,0:T(8,128)(2,1)} %bitcast.95), calls=%async_computation | async-start | bytes 4456448 | tf_op jit(solution)/shard_map/all_to_all | solution.py:654
  98.6 3.8 pack.5
  102.4 43.3 %all-to-all-done.refs_5_.refs_7_ = bf16[8,272,512]{2,1,0:T(8,128)(2,1)} async-done(((bf16[8,272,512]{2,1,0:T(8,128)(2,1)}), bf16[8,272,512]{2,1,0:T(8,128)(2,1)}, u32[]{:S(2)}, u32[]{:S(2)}) %all-to-all-start) | async-done | bytes 2228256 | tf_op jit(solution)/shard_map/all_to_all | solution.py:654
  145.7 4.4 %all-to-all-start.2 = ((bf16[8,256,512]{2,1,0:T(8,128)(2,1)}), bf16[8,256,512]{2,1,0:T(8,128)(2,1)}, u32[]{:S(2)}, u32[]{:S(2)}) async-start(bf16[8,256,512]{2,1,0:T(8,128)(2,1)} %bitcast.105), calls=%async_computation.2 | async-start | bytes 4194304 | tf_op jit(solution)/shard_map/all_to_all | solution.py:654
  151.2 1.8 slice.129
  154.5 3.2 collective-permute-done.3
  160.1 14.4 %norm_up.1 = (bf16[2048,2048]{1,0:T(8,128)(2,1)}, f32[2048,128]{1,0:T(8,128)}, bf16[2048,512]{1,0:T(8,128)(2,1)}, f32[2048,512]{1,0:T(8,128)}) custom-call(bf16[2,2,256,512]{3,2,1,0:T(8,128)(2,1)} %copy-done.7, bf16[4,4,512,512]{3,2,1,0:T(8,128)(2,1)} %bitcast.104, f32[1,2048]{1,0:T(1,128)} %reshape.219.refs_2_, f32[1,2048]{1,0:T(1,128)} %reshape.220.refs_3_, ...), custom_call_target="tpu_custom_call" | custom-call | flops 12884901 | tf_op jit(solution)/shard_map/norm_up/pallas_call | solution.py:73
  175.3 9.4 %project_heads.1.refs_0_.refs_1_ = bf16[2048,384]{1,0:T(8,128)(2,1)} custom-call(bf16[2048,2048]{1,0:T(8,128)(2,1)} %get-tuple-element.55.refs_0_.refs_2_.refs_4_, f32[1,384]{1,0:T(1,128)} %reshape.221.refs_1_, f32[2048,128]{1,0:T(8,128)} %constant.83.clone.refs_2_.refs_4_, f32[2048,128]{1,0:T(8,128)} %constant.84.clone.refs_3_.refs_5_, ...), custom_call_target="tpu_custom_call" | custom-call | flops 6442450 | tf_op jit(solution)/shard_map/project_heads/pallas_call | solution.py:73
  184.7 14.3 %attention.1 = (bf16[2048,128]{1,0:T(8,128)(2,1)}, f32[8,2048]{1,0:T(8,128)}) custom-call(bf16[2048,384]{1,0:T(8,128)(2,1)} %project_heads.1.refs_0_.refs_1_), custom_call_target="tpu_custom_call" | custom-call | flops 10000000 | tf_op jit(solution)/shard_map/attention/pallas_call | solution.py:73
  199.1 8.7 %weight_grad.2.refs_0_ = bf16[8,512,256]{2,1,0:T(8,128)(2,1)} custom-call(bf16[2048,128]{1,0:T(8,128)(2,1)} %get-tuple-element.56.refs_0_.refs_2_.refs_5_, bf16[2048,512]{1,0:T(8,128)(2,1)} %get-tuple-element.57.refs_1_.refs_3_, bf16[2,4,2,512,512]{4,3,2,1,0:T(8,128)(2,1)} %bitcast.90), custom_call_target="tpu_custom_call" | custom-call | flops 8589934 | tf_op jit(solution)/shard_map/weight_grad/pallas_call | solution.py:73
  207.8 6.1 %all-to-all-start.3 = ((bf16[8,512,256]{2,1,0:T(8,128)(2,1)}), bf16[8,512,256]{2,1,0:T(8,128)(2,1)}, u32[]{:S(2)}, u32[]{:S(2)}) async-start(bf16[8,512,256]{2,1,0:T(8,128)(2,1)} %weight_grad.2.refs_0_), calls=%async_computation.3 | async-start | bytes 4194304 | tf_op jit(solution)/shard_map/all_to_all | solution.py:672
  217.0 11.2 %back_through.1 = (bf16[2048,128]{1,0:T(8,128)(2,1)}, bf16[2048,512]{1,0:T(8,128)(2,1)}, f32[1,512]{1,0:T(1,128)}) custom-call(bf16[8,512,256]{2,1,0:T(8,128)(2,1)} %weight_grad.2.refs_0_, bf16[2,4,2,512,512]{4,3,2,1,0:T(8,128)(2,1)} %bitcast.91, f32[2048,512]{1,0:T(8,128)} %get-tuple-element.58.refs_2_, bf16[8,256,512]{2,1,0:T(8,128)(2,1)} %copy-done, ...), custom_call_target="tpu_custom_call" | custom-call | flops 10737418 | tf_op jit(solution)/shard_map/back_through/pallas_call | solution.py:73
  229.7 10.8 %branch_sum.1 = (bf16[4,512,512]{2,1,0:T(8,128)(2,1)}, bf16[4,512,512]{2,1,0:T(8,128)(2,1)}) custom-call(bf16[2048,512]{1,0:T(8,128)(2,1)} %get-tuple-element.59.refs_0_.refs_1_.refs_3_, s32[2]{0:T(128)} %pad_add_fusion.refs_1_, bf16[2048,128]{1,0:T(8,128)(2,1)} %get-tuple-element.56.refs_0_.refs_2_.refs_5_, ...), custom_call_target="tpu_custom_call" | custom-call | flops 10737418 | tf_op jit(solution)/shard_map/branch_sum/pallas_call | solution.py:73
  240.6 24.0 %attention_back.1 = (bf16[2048,384]{1,0:T(8,128)(2,1)}, f32[1,384]{1,0:T(1,128)}) custom-call(bf16[4,512,512]{2,1,0:T(8,128)(2,1)} %get-tuple-element.60.refs_0_, bf16[2048,384]{1,0:T(8,128)(2,1)} %project_heads.1.refs_0_.refs_1_, bf16[2048,128]{1,0:T(8,128)(2,1)} %get-tuple-element.61.refs_2_, f32[8,2048]{1,0:T(8,128)} %get-tuple-element.62.refs_3_, ...), custom_call_target="tpu_custom_call" | custom-call | flops 20000000 | tf_op jit(solution)/shard_map/attention_back/pallas_call | solution.py:73
  266.7 15.6 %weight_grad.3.refs_0_ = bf16[8,1040,256]{2,1,0:T(8,128)(2,1)} custom-call(bf16[8,16,256]{2,1,0:T(8,128)(2,1)} %bitcast.127, bf16[2048,512]{1,0:T(8,128)(2,1)} %get-tuple-element.59.refs_0_.refs_1_.refs_3_, bf16[2048,2048]{1,0:T(8,128)(2,1)} %get-tuple-element.55.refs_0_.refs_2_.refs_4_, bf16[2048,384]{1,0:T(8,128)(2,1)} %get-tuple-element.65.refs_3_.refs_2_, ...), custom_call_target="tpu_custom_call" | custom-call | flops 17448304 | tf_op jit(solution)/shard_map/weight_grad/pallas_call | solution.py:73
  282.3 6.0 %collective-permute-done.9 = bf16[4,512,512]{2,1,0:T(8,128)(2,1)S(1)} collective-permute-done((bf16[4,512,512]{2,1,0:T(8,128)(2,1)}, bf16[4,512,512]{2,1,0:T(8,128)(2,1)S(1)}, u32[]{:S(2)}, u32[]{:S(2)}) %collective-permute-start.9) | collective-permute-done | bytes 2097184 | tf_op jit(solution)/shard_map/ppermute | solution.py:47
  289.7 3.6 fold.6
  293.3 6.1 %all-to-all-start.4 = ((bf16[8,1040,256]{2,1,0:T(8,128)(2,1)}), bf16[8,1040,256]{2,1,0:T(8,128)(2,1)}, u32[]{:S(2)}, u32[]{:S(2)}) async-start(bf16[8,1040,256]{2,1,0:T(8,128)(2,1)} %weight_grad.3.refs_0_), calls=%async_computation.4 | async-start | bytes 8519680 | tf_op jit(solution)/shard_map/all_to_all | solution.py:672
  299.5 4.1 collective-permute-done.10.refs_5_
  305.0 13.7 %normed_gradient.1 = (bf16[4,256,512]{2,1,0:T(8,128)(2,1)}, bf16[4,256,512]{2,1,0:T(8,128)(2,1)}, bf16[4,256,512]{2,1,0:T(8,128)(2,1)}, bf16[4,256,512]{2,1,0:T(8,128)(2,1)}) custom-call(bf16[2,512,512]{2,1,0:T(8,128)(2,1)} %get-tuple-element.67.refs_0_, s32[2]{0:T(128)} %pad_add_fusion.refs_1_, bf16[2048,384]{1,0:T(8,128)(2,1)} %get-tuple-element.65.refs_3_.refs_2_, ...), custom_call_target="tpu_custom_call" | custom-call | flops 15032385 | tf_op jit(solution)/shard_map/normed_gradient/pallas_call | solution.py:73
  319.0 2.0 collective-permute-start.12
  321.0 1.7 collective-permute-start.13
  322.7 3.8 unpack.2.refs_0_
  326.6 18.4 %collective-permute-done.11 = bf16[4,256,512]{2,1,0:T(8,128)(2,1)S(1)} collective-permute-done((bf16[4,256,512]{2,1,0:T(8,128)(2,1)}, bf16[4,256,512]{2,1,0:T(8,128)(2,1)S(1)}, u32[]{:S(2)}, u32[]{:S(2)}) %collective-permute-start.11) | collective-permute-done | bytes 1048608 | tf_op jit(solution)/shard_map/ppermute | solution.py:47
  345.9 2.5 fold.7
  348.4 2.0 collective-permute-start.14
  350.4 20.1 %collective-permute-done.12 = bf16[2,512,512]{2,1,0:T(8,128)(2,1)S(1)} collective-permute-done((bf16[2,512,512]{2,1,0:T(8,128)(2,1)S(1)}, bf16[2,512,512]{2,1,0:T(8,128)(2,1)S(1)}, u32[]{:S(2)}, u32[]{:S(2)}) %collective-permute-start.12) | collective-permute-done | bytes 1048608 | tf_op jit(solution)/shard_map/ppermute | solution.py:47
  371.5 2.5 fold.8
  375.0 2.5 fold.9
  377.5 2.1 collective-permute-start.16
  382.5 2.0 fold.10
  384.5 8.4 %collective-permute-done.15 = bf16[2,256,512]{2,1,0:T(8,128)(2,1)S(1)} collective-permute-done((bf16[2,256,512]{2,1,0:T(8,128)(2,1)}, bf16[2,256,512]{2,1,0:T(8,128)(2,1)S(1)}, u32[]{:S(2)}, u32[]{:S(2)}) %collective-permute-start.15) | collective-permute-done | bytes 524320 | tf_op jit(solution)/shard_map/ppermute | solution.py:47
  393.7 2.0 fold.11
  395.7 2.1 collective-permute-start.18
  399.0 6.0 %collective-permute-done.16.refs_3_ = bf16[512,512]{1,0:T(8,128)(2,1)S(1)} collective-permute-done((bf16[512,512]{1,0:T(8,128)(2,1)}, bf16[512,512]{1,0:T(8,128)(2,1)S(1)}, u32[]{:S(2)}, u32[]{:S(2)}) %collective-permute-start.16) | collective-permute-done | bytes 524320 | tf_op jit(solution)/shard_map/ppermute | solution.py:47
  405.8 2.4 finish.1.refs_0_
  408.2 5.1 %unpack.3 = (f32[256,2048]{1,0:T(8,128)}, f32[256,512]{1,0:T(8,128)}, f32[256,512]{1,0:T(8,128)}, f32[256,512]{1,0:T(8,128)}, f32[512,256]{1,0:T(8,128)}) custom-call(bf16[512,512]{1,0:T(8,128)(2,1)} %finish.1.refs_0_, bf16[2,4,1040,256]{3,2,1,0:T(8,128)(2,1)} %bitcast.40.refs_1_), custom_call_target="tpu_custom_call" | custom-call | tf_op jit(solution)/shard_map/unpack/pallas_call | solution.py:73
  413.3 2.9 collective-permute-done.17
  418.1 2.6 collective-permute-done.21
  424.4 3.8 collective-permute-start.23
  (164 shorter events, 35.8 us)
Async XLA Ops:
  7.2 151.9 %all-gather.5.cloned.1.call-start = ((), (), s32[]{:S(2)}) async-start(), calls=%async_computation.5 | async-start | bytes 8912896 | tf_op jit(solution)/shard_map/all_gather | solution.py:816
  7.9 191.1 %all-gather.7.cloned.1.call-start = ((), (), s32[]{:S(2)}) async-start(), calls=%async_computation.6 | async-start | bytes 9437184 | tf_op jit(solution)/shard_map/all_gather | solution.py:822
  8.0 19.3 %collective-permute-start = (bf16[512,512]{1,0:T(8,128)(2,1)}, bf16[512,512]{1,0:T(8,128)(2,1)S(1)}, u32[]{:S(2)}, u32[]{:S(2)}) collective-permute-start(bf16[512,512]{1,0:T(8,128)(2,1)} %refs_2_.4), channel_id=1, source_target_pairs={{0,8},{8,0},{1,9},{9,1},{2,10},{10,2},{3,11},{11,3},{4,12},{12,4},... | collective-permute-start | bytes 1572872 | tf_op jit(solution)/shard_map/ppermute | solution.py:47
  30.2 59.8 %all-to-all-start.1 = ((bf16[8,256,512]{2,1,0:T(8,128)(2,1)}), bf16[8,256,512]{2,1,0:T(8,128)(2,1)S(1)}, u32[]{:S(2)}, u32[]{:S(2)}) async-start(bf16[8,256,512]{2,1,0:T(8,128)(2,1)} %bitcast.97), calls=%async_computation.1 | async-start | bytes 4194304 | tf_op jit(solution)/shard_map/all_to_all | solution.py:654
  90.0 1.3 copy-start
  91.3 54.3 %all-to-all-start = ((bf16[8,272,512]{2,1,0:T(8,128)(2,1)}), bf16[8,272,512]{2,1,0:T(8,128)(2,1)}, u32[]{:S(2)}, u32[]{:S(2)}) async-start(bf16[8,272,512]{2,1,0:T(8,128)(2,1)} %bitcast.95), calls=%async_computation | async-start | bytes 4456448 | tf_op jit(solution)/shard_map/all_to_all | solution.py:654
  145.7 62.1 %all-to-all-start.2 = ((bf16[8,256,512]{2,1,0:T(8,128)(2,1)}), bf16[8,256,512]{2,1,0:T(8,128)(2,1)}, u32[]{:S(2)}, u32[]{:S(2)}) async-start(bf16[8,256,512]{2,1,0:T(8,128)(2,1)} %bitcast.105), calls=%async_computation.2 | async-start | bytes 4194304 | tf_op jit(solution)/shard_map/all_to_all | solution.py:654
  151.1 2.6 collective-permute-start.2
  153.1 6.0 %collective-permute-start.1 = (bf16[2,2,256,512]{3,2,1,0:T(8,128)(2,1)S(1)}, bf16[2,2,256,512]{3,2,1,0:T(8,128)(2,1)S(1)}, u32[]{:S(2)}, u32[]{:S(2)}) collective-permute-start(bf16[2,2,256,512]{3,2,1,0:T(8,128)(2,1)S(1)} %dynamic-slice_bitcast_fusion.2), channel_id=1, source_target_pairs={{0,1},{1,0},{2,3},{3,2},{4,5},{5,4},{6,7},{7,6},{8,9},{9,8},{10,11... | collective-permute-start | bytes 3145736 | tf_op jit(solution)/shard_map/ppermute | solution.py:47
  153.8 3.9 collective-permute-start.3
  174.4 53.9 %collective-permute-start.5 = (bf16[2048,512]{1,0:T(8,128)(2,1)}, bf16[2048,512]{1,0:T(8,128)(2,1)}, u32[]{:S(2)}, u32[]{:S(2)}) collective-permute-start(bf16[2048,512]{1,0:T(8,128)(2,1)} %get-tuple-element.57.refs_1_.refs_3_), channel_id=1, source_target_pairs={{0,1},{1,0},{2,3},{3,2},{4,5},{5,4},{6,7},{7,6},{8,9},{9,8},{10,11... | collective-permute-start | bytes 6291464 | tf_op jit(solution)/shard_map/ppermute | solution.py:47
  207.8 6.2 %copy-start.1 = (bf16[8,256,512]{2,1,0:T(8,128)(2,1)S(1)}, bf16[8,256,512]{2,1,0:T(8,128)(2,1)}, u32[]{:S(2)}) copy-start(bf16[8,256,512]{2,1,0:T(8,128)(2,1)} %copy-done) | copy-start | bytes 6291460
  207.8 85.5 %all-to-all-start.3 = ((bf16[8,512,256]{2,1,0:T(8,128)(2,1)}), bf16[8,512,256]{2,1,0:T(8,128)(2,1)}, u32[]{:S(2)}, u32[]{:S(2)}) async-start(bf16[8,512,256]{2,1,0:T(8,128)(2,1)} %weight_grad.2.refs_0_), calls=%async_computation.3 | async-start | bytes 4194304 | tf_op jit(solution)/shard_map/all_to_all | solution.py:672
  214.0 2.0 copy-start.5
  214.1 14.2 %collective-permute-start.6 = (bf16[2,2,256,512]{3,2,1,0:T(8,128)(2,1)S(1)}, bf16[2,2,256,512]{3,2,1,0:T(8,128)(2,1)S(1)}, u32[]{:S(2)}, u32[]{:S(2)}) collective-permute-start(bf16[2,2,256,512]{3,2,1,0:T(8,128)(2,1)S(1)} %dynamic-slice_bitcast_fusion.1), channel_id=1, source_target_pairs={{0,1},{1,0},{2,3},{3,2},{4,5},{5,4},{6,7},{7,6},{8,9},{9,8},{10,11... | collective-permute-start | bytes 3145736 | tf_op jit(solution)/shard_map/ppermute | solution.py:47
  215.8 12.4 %collective-permute-start.7 = (bf16[2,2,256,512]{3,2,1,0:T(8,128)(2,1)S(1)}, bf16[2,2,256,512]{3,2,1,0:T(8,128)(2,1)S(1)}, u32[]{:S(2)}, u32[]{:S(2)}) collective-permute-start(bf16[2,2,256,512]{3,2,1,0:T(8,128)(2,1)S(1)} %dynamic-slice_bitcast_fusion), channel_id=1, source_target_pairs={{0,1},{1,0},{2,3},{3,2},{4,5},{5,4},{6,7},{7,6},{8,9},{9,8},{10,11... | collective-permute-start | bytes 3145736 | tf_op jit(solution)/shard_map/ppermute | solution.py:47
  216.0 12.3 %collective-permute-start.4 = (bf16[2048,128]{1,0:T(8,128)(2,1)S(1)}, bf16[2048,128]{1,0:T(8,128)(2,1)S(1)}, u32[]{:S(2)}, u32[]{:S(2)}) collective-permute-start(bf16[2048,128]{1,0:T(8,128)(2,1)S(1)} %copy-done.5), channel_id=1, source_target_pairs={{0,1},{1,0},{2,3},{3,2},{4,5},{5,4},{6,7},{7,6},{8,9},{9,8},{10,11... | collective-permute-start | bytes 1572872 | tf_op jit(solution)/shard_map/ppermute | solution.py:47
  228.2 1.0 copy-start.11
  228.3 1.3 copy-start.16
  228.3 1.4 copy-start.20
  240.5 47.8 %collective-permute-start.9 = (bf16[4,512,512]{2,1,0:T(8,128)(2,1)}, bf16[4,512,512]{2,1,0:T(8,128)(2,1)S(1)}, u32[]{:S(2)}, u32[]{:S(2)}) collective-permute-start(bf16[4,512,512]{2,1,0:T(8,128)(2,1)} %get-tuple-element.66), channel_id=1, source_target_pairs={{0,2},{2,0},{1,3},{3,1},{4,6},{6,4},{5,7},{7,5},{8,10},{10,8},{9,1... | collective-permute-start | bytes 6291464 | tf_op jit(solution)/shard_map/ppermute | solution.py:47
  240.5 24.1 %copy-start.6 = (bf16[512,512]{1,0:T(8,128)(2,1)S(1)}, bf16[512,512]{1,0:T(8,128)(2,1)}, u32[]{:S(2)}) copy-start(bf16[512,512]{1,0:T(8,128)(2,1)} %refs_2_.4) | copy-start | bytes 1572868
  240.5 24.3 %copy-start.21 = (f32[1,512]{1,0:T(1,128)S(1)}, f32[1,512]{1,0:T(1,128)}, u32[]{:S(2)}) copy-start(f32[1,512]{1,0:T(1,128)} %get-tuple-element.64) | copy-start | bytes 6148
  264.5 17.8 %collective-permute-start.8 = (bf16[2048,384]{1,0:T(8,128)(2,1)}, bf16[2048,384]{1,0:T(8,128)(2,1)}, u32[]{:S(2)}, u32[]{:S(2)}) collective-permute-start(bf16[2048,384]{1,0:T(8,128)(2,1)} %get-tuple-element.65.refs_3_.refs_2_), channel_id=1, source_target_pairs={{0,1},{1,0},{2,3},{3,2},{4,5},{5,4},{6,7},{7,6},{8,9},{9,8},{10,11... | collective-permute-start | bytes 4718600 | tf_op jit(solution)/shard_map/ppermute | solution.py:47
  288.4 1.3 copy-start.4
  293.3 6.1 %copy-start.2 = (bf16[2048,512]{1,0:T(8,128)(2,1)S(1)}, bf16[2048,512]{1,0:T(8,128)(2,1)}, u32[]{:S(2)}) copy-start(bf16[2048,512]{1,0:T(8,128)(2,1)} %get-tuple-element.59.refs_0_.refs_1_.refs_3_) | copy-start | bytes 6291460
  293.3 114.9 %all-to-all-start.4 = ((bf16[8,1040,256]{2,1,0:T(8,128)(2,1)}), bf16[8,1040,256]{2,1,0:T(8,128)(2,1)}, u32[]{:S(2)}, u32[]{:S(2)}) async-start(bf16[8,1040,256]{2,1,0:T(8,128)(2,1)} %weight_grad.3.refs_0_), calls=%async_computation.4 | async-start | bytes 8519680 | tf_op jit(solution)/shard_map/all_to_all | solution.py:672
  299.4 19.6 %copy-start.23 = (bf16[2,512,512]{2,1,0:T(8,128)(2,1)S(1)}, bf16[2,512,512]{2,1,0:T(8,128)(2,1)}, u32[]{:S(2)}) copy-start(bf16[2,512,512]{2,1,0:T(8,128)(2,1)} %get-tuple-element.71) | copy-start | bytes 3145732
  299.4 4.2 collective-permute-start.10
  303.6 1.3 copy-start.13
  318.6 26.3 %collective-permute-start.11 = (bf16[4,256,512]{2,1,0:T(8,128)(2,1)}, bf16[4,256,512]{2,1,0:T(8,128)(2,1)S(1)}, u32[]{:S(2)}, u32[]{:S(2)}) collective-permute-start(bf16[4,256,512]{2,1,0:T(8,128)(2,1)} %get-tuple-element.69), channel_id=1, source_target_pairs={{0,2},{2,0},{1,3},{3,1},{4,6},{6,4},{5,7},{7,5},{8,10},{10,8},{9,1... | collective-permute-start | bytes 3145736 | tf_op jit(solution)/shard_map/ppermute | solution.py:47
  319.0 51.5 %collective-permute-start.12 = (bf16[2,512,512]{2,1,0:T(8,128)(2,1)S(1)}, bf16[2,512,512]{2,1,0:T(8,128)(2,1)S(1)}, u32[]{:S(2)}, u32[]{:S(2)}) collective-permute-start(bf16[2,512,512]{2,1,0:T(8,128)(2,1)S(1)} %copy-done.23), channel_id=1, source_target_pairs={{0,4},{4,0},{1,5},{5,1},{2,6},{6,2},{3,7},{7,3},{8,12},{12,8},{9,1... | collective-permute-start | bytes 3145736 | tf_op jit(solution)/shard_map/ppermute | solution.py:47
  321.0 53.0 %collective-permute-start.13 = (bf16[4,256,512]{2,1,0:T(8,128)(2,1)}, bf16[4,256,512]{2,1,0:T(8,128)(2,1)S(1)}, u32[]{:S(2)}, u32[]{:S(2)}) collective-permute-start(bf16[4,256,512]{2,1,0:T(8,128)(2,1)} %get-tuple-element.74), channel_id=1, source_target_pairs={{0,2},{2,0},{1,3},{3,1},{4,6},{6,4},{5,7},{7,5},{8,10},{10,8},{9,1... | collective-permute-start | bytes 3145736 | tf_op jit(solution)/shard_map/ppermute | solution.py:47
  348.4 33.3 %collective-permute-start.14 = (bf16[2,256,512]{2,1,0:T(8,128)(2,1)}, bf16[2,256,512]{2,1,0:T(8,128)(2,1)S(1)}, u32[]{:S(2)}, u32[]{:S(2)}) collective-permute-start(bf16[2,256,512]{2,1,0:T(8,128)(2,1)} %get-tuple-element.76), channel_id=1, source_target_pairs={{0,4},{4,0},{1,5},{5,1},{2,6},{6,2},{3,7},{7,3},{8,12},{12,8},{9,1... | collective-permute-start | bytes 1572872 | tf_op jit(solution)/shard_map/ppermute | solution.py:47
  377.5 15.4 %collective-permute-start.15 = (bf16[2,256,512]{2,1,0:T(8,128)(2,1)}, bf16[2,256,512]{2,1,0:T(8,128)(2,1)S(1)}, u32[]{:S(2)}, u32[]{:S(2)}) collective-permute-start(bf16[2,256,512]{2,1,0:T(8,128)(2,1)} %get-tuple-element.78), channel_id=1, source_target_pairs={{0,4},{4,0},{1,5},{5,1},{2,6},{6,2},{3,7},{7,3},{8,12},{12,8},{9,1... | collective-permute-start | bytes 1572872 | tf_op jit(solution)/shard_map/ppermute | solution.py:47
  377.5 27.5 %collective-permute-start.16 = (bf16[512,512]{1,0:T(8,128)(2,1)}, bf16[512,512]{1,0:T(8,128)(2,1)S(1)}, u32[]{:S(2)}, u32[]{:S(2)}) collective-permute-start(bf16[512,512]{1,0:T(8,128)(2,1)} %bitcast.37), channel_id=1, source_target_pairs={{0,8},{8,0},{1,9},{9,1},{2,10},{10,2},{3,11},{11,3},{4,12},{12,4},... | collective-permute-start | bytes 1572872 | tf_op jit(solution)/shard_map/ppermute | solution.py:47
  384.5 13.3 %copy-start.24 = (bf16[1,256,512]{2,1,0:T(8,128)(2,1)S(1)}, bf16[1,256,512]{2,1,0:T(8,128)(2,1)}, u32[]{:S(2)}) copy-start(bf16[1,256,512]{2,1,0:T(8,128)(2,1)} %get-tuple-element.81) | copy-start | bytes 786436
  395.7 17.5 %collective-permute-start.18 = (bf16[256,512]{1,0:T(8,128)(2,1)}, bf16[256,512]{1,0:T(8,128)(2,1)S(1)}, u32[]{:S(2)}, u32[]{:S(2)}) collective-permute-start(bf16[256,512]{1,0:T(8,128)(2,1)} %bitcast.151), channel_id=1, source_target_pairs={{0,8},{8,0},{1,9},{9,1},{2,10},{10,2},{3,11},{11,3},{4,12},{12,4},... | collective-permute-start | bytes 786440 | tf_op jit(solution)/shard_map/ppermute | solution.py:47
  397.8 18.3 %collective-permute-start.17 = (bf16[256,512]{1,0:T(8,128)(2,1)S(1)}, bf16[256,512]{1,0:T(8,128)(2,1)S(1)}, u32[]{:S(2)}, u32[]{:S(2)}) collective-permute-start(bf16[256,512]{1,0:T(8,128)(2,1)S(1)} %bitcast.150), channel_id=1, source_target_pairs={{0,8},{8,0},{1,9},{9,1},{2,10},{10,2},{3,11},{11,3},{4,12},{12,4},... | collective-permute-start | bytes 786440 | tf_op jit(solution)/shard_map/ppermute | solution.py:47
  408.2 8.0 %copy-start.15 = (bf16[1,256,512]{2,1,0:T(8,128)(2,1)S(1)}, bf16[1,256,512]{2,1,0:T(8,128)(2,1)}, u32[]{:S(2)}) copy-start(bf16[1,256,512]{2,1,0:T(8,128)(2,1)} %get-tuple-element.77.refs_0_) | copy-start | bytes 786436
  408.2 8.0 %copy-start.17 = (bf16[1,256,512]{2,1,0:T(8,128)(2,1)S(1)}, bf16[1,256,512]{2,1,0:T(8,128)(2,1)}, u32[]{:S(2)}) copy-start(bf16[1,256,512]{2,1,0:T(8,128)(2,1)} %get-tuple-element.79.refs_0_) | copy-start | bytes 786436
  413.3 3.1 copy-start.3
  417.1 3.6 collective-permute-start.21
  417.1 3.7 collective-permute-start.19
  420.8 3.6 collective-permute-start.22
  420.8 7.3 %collective-permute-start.20 = (f32[2,512]{1,0:T(2,128)S(1)}, f32[2,512]{1,0:T(2,128)S(1)}, u32[]{:S(2)}, u32[]{:S(2)}) collective-permute-start(f32[2,512]{1,0:T(2,128)S(1)} %fusion.3), channel_id=1, source_target_pairs={{0,2},{2,0},{1,3},{3,1},{4,6},{6,4},{5,7},{7,5},{8,10},{10,8},{9,1... | collective-permute-start | bytes 12296 | tf_op jit(solution)/shard_map/ppermute | solution.py:47
  422.1 8.8 %copy-start.22 = (f32[64]{0:T(128)}, f32[64]{0:T(128)S(1)}, u32[]{:S(2)}) copy-start(f32[64]{0:T(128)S(1)} %get-tuple-element.155) | copy-start | bytes 772
  424.4 5.4 %collective-permute-start.23 = (f32[8,128]{1,0:T(8,128)S(1)}, f32[8,128]{1,0:T(8,128)S(1)}, u32[]{:S(2)}, u32[]{:S(2)}) collective-permute-start(f32[8,128]{1,0:T(8,128)S(1)} %add.86), channel_id=1, source_target_pairs={{0,16},{16,0},{1,17},{17,1},{2,18},{18,2},{3,19},{19,3},{4,20},{20... | collective-permute-start | bytes 12296 | tf_op jit(solution)/shard_map/ppermute | solution.py:47
  (8 other events, 7.1 us)
Sparse Core Ops, SparseCore 0:
  9.6 88.2 all-gather.4
  99.8 96.3 all-gather.6

commit v5 on v4

--- a/solution.py
+++ b/solution.py
@@ -17,6 +17,7 @@
 COST = 1
 
 WIDE = ("s", "g", "h")
+LINE = ("s", "g")
 LINE = ("s", "g")
 NARROW = ("m", "c")
 CUBE = ("g", "h", "m", "c")
@@ -523,11 +524,12 @@
     )(*operands)
 
 
-def partial_sum_kernel(sides, halves, index_ref, *refs):
+def partial_sum_kernel(sides, axes, index_ref, *refs):
     lefts, refs = refs[: 2 * sides], refs[2 * sides :]
     weights, others, outs = refs[:sides], refs[sides : 2 * sides], refs[2 * sides :]
-    rows, width = outs[0].shape[1:]
-    own_m, core = index_ref[0], index_ref[1]
+    rows, width = outs[0].shape[-2:]
+    own_m, own_h, core = index_ref[0], index_ref[1], index_ref[2]
+    here = lax.rem(pl.program_id(0), 2) == own_h
     for n_m, m in enumerate((own_m, 1 - own_m)):
         out = 0.0
         for n in range(sides):
@@ -536,29 +538,45 @@
             other = others[n][m].reshape(width, weight.shape[1])
             out = out + contract_cols(lefts[sides + n][...], other)
         out = out.astype(jnp.bfloat16)
-        for half in range(halves):
-            outs[2 * half + n_m][0] = out[half * rows : (half + 1) * rows]
-
-
-def partial_sum(sides, row_count, width, name, halves, after=()):
+        for half, axis in enumerate(axes):
+            part = out[half * rows : (half + 1) * rows]
+            if axis == "m":
+                outs[2 * half + n_m][0] = part
+                continue
+            for n_h, mine in enumerate((here, jnp.logical_not(here))):
+
+                @pl.when(mine)
+                def _(out_ref=outs[2 * half + n_h], m=m, part=part):
+                    out_ref[0, m] = part
+
+
+def partial_sum(sides, row_count, width, name, axes, after=()):
     total = sides[0][0].shape[0]
-    rows = row_count // halves
+    rows = row_count // len(axes)
+    blocks = total // row_count
     lefts = [side[0] for side in sides] + [side[1] for side in sides]
     weights = [side[2] for side in sides]
     others = [side[3] for side in sides]
     depth = sum(left.shape[1] for left in lefts)
-    outs = 2 * halves
-    index = jnp.stack([lax.axis_index("m"), lax.axis_index("c")]).astype(jnp.int32)
+    specs, shapes = [], []
+    for axis in axes:
+        if axis == "m":
+            specs += [pl.BlockSpec((1, rows, width), lambda i: (i, 0, 0))] * 2
+            shapes += [struct((blocks, rows, width), jnp.bfloat16)] * 2
+        else:
+            specs += [pl.BlockSpec((1, 2, rows, width), lambda i: (i // 2, 0, 0, 0))] * 2
+            shapes += [struct((blocks // 2, 2, rows, width), jnp.bfloat16)] * 2
+    index = jnp.stack([lax.axis_index(axis) for axis in "mhc"]).astype(jnp.int32)
     return call(
-        partial(partial_sum_kernel, len(sides), halves),
+        partial(partial_sum_kernel, len(sides), axes),
         name,
-        (total // row_count,),
+        (blocks,),
         [SCALARS]
         + [band(row_count, left.shape[1]) for left in lefts]
         + [weight.spec for weight in weights]
         + [other.spec for other in others],
-        [pl.BlockSpec((1, rows, width), lambda i: (i, 0, 0))] * outs,
-        [struct((total // row_count, rows, width), jnp.bfloat16)] * outs,
+        specs,
+        shapes,
         flops=2 * total * depth * D,
         after=after,
     )(index, *lefts, *[weight.array for weight in weights], *[other.array for other in others])
@@ -652,6 +670,68 @@
 def exchanged(blocks, after=()):
     blocks = lax.optimization_barrier((blocks, *after))[0]
     return lax.all_to_all(blocks, WIDE, 0, 0)
+
+
+def sides_kernel(turned, index_ref, *refs):
+    for out_ref, blocks in zip(refs[-2:], (refs[:-2][::2], refs[:-2][1::2])):
+
+        def store(cols, part, out_ref=out_ref):
+            out_ref[0, :, cols] = part
+
+        write_columns(turned, blocks, store)
+
+
+def packed_sides(shards, turned):
+    specs, operands, width = [], [], 0
+    for flip, shard in zip(turned, shards):
+        height, cols = shard.shape
+        if flip:
+            rows, width = cols, width + height // 4
+            shape, at = (height // 4, cols), lambda block: (block, 0)
+        else:
+            rows, width = height, width + cols // 4
+            shape, at = (height, cols // 4), lambda block: (0, block)
+        specs.append(pl.BlockSpec(shape, lambda j, p, at=at: at(2 * j + p[0])))
+        specs.append(pl.BlockSpec(shape, lambda j, p, at=at: at(2 * j + 1 - p[0])))
+        operands += [shard, shard]
+    return prefetch_call(
+        partial(sides_kernel, turned),
+        "pack",
+        lax.axis_index("h"),
+        (2,),
+        specs,
+        [pl.BlockSpec((1, rows, width), lambda j, p: (j, 0, 0))] * 2,
+        [struct((2, rows, width), jnp.bfloat16)] * 2,
+    )(*operands)
+
+
+def spread_kernel(index_ref, mine_ref, other_ref, out_ref):
+    for n in range(out_ref.shape[0]):
+        out_ref[n, 0, index_ref[0]] = mine_ref[0]
+        out_ref[n, 0, 1 - index_ref[0]] = other_ref[0]
+
+
+def spread_sides(sides, after=()):
+    mine, send = sides
+    sequences = lax.axis_size("s")
+    _, rows, width = mine.shape
+    spec = pl.BlockSpec((1, rows, width), lambda j, p: (j, 0, 0))
+    blocks = prefetch_call(
+        spread_kernel,
+        "spread",
+        lax.axis_index("h"),
+        (2,),
+        [spec, spec],
+        pl.BlockSpec((sequences, 1, 2, rows, width), lambda j, p: (0, j, 0, 0, 0)),
+        struct((sequences, 2, 2, rows, width), jnp.bfloat16),
+        after=after,
+    )(mine, shifted(send, "h", 1))
+    return blocks.reshape(2 * sequences, 2 * rows, width)
+
+
+def exchanged_along_line(blocks):
+    count, rows, width = blocks.shape
+    return lax.all_to_all(blocks, LINE, 0, 0).reshape(2 * count, rows // 2, width)
 
 
 def unpack_kernel(turned, arrived_ref, *outs):
@@ -746,23 +826,28 @@
     return out.reshape((2,) + mine.shape)
 
 
-def finish_kernel(tokens_ref, keep_ref, arrived_ref, bias_ref, out_ref):
-    total = tokens_ref[...].astype(jnp.float32) + keep_ref[...].astype(jnp.float32)
-    total = total + arrived_ref[...].astype(jnp.float32) + bias_ref[...]
-    out_ref[...] = total.astype(jnp.bfloat16)
+def finish_kernel(tokens_ref, *refs):
+    bias_ref, out_ref = refs[-2:]
+    parts = len(refs) // 2 - 1
+    rows = refs[0].shape[0]
+    for n, (keep_ref, arrived_ref) in enumerate(zip(refs[:parts], refs[parts : 2 * parts])):
+        at = slice(n * rows, (n + 1) * rows)
+        total = tokens_ref[at, :].astype(jnp.float32) + keep_ref[...].astype(jnp.float32)
+        total = total + arrived_ref[...].astype(jnp.float32) + bias_ref[...]
+        out_ref[at, :] = total.astype(jnp.bfloat16)
 
 
 def finished(tokens, keep, arrived, bias, after=()):
-    spec = whole(*tokens.shape)
+    operands = [tokens, *keep, *arrived, bias]
     return call(
         finish_kernel,
         "finish",
         (1,),
-        [spec, spec, spec, whole(*bias.shape)],
-        spec,
+        [whole(*operand.shape) for operand in operands],
+        whole(*tokens.shape),
         struct(tokens.shape, tokens.dtype),
         after=after,
-    )(tokens, keep, arrived, bias)
+    )(*operands)
 
 
 def gather_narrow(value):
@@ -772,12 +857,10 @@
     return value.reshape((4,) + value.shape[2:])
 
 
-def summed_along_wide(value):
-    for axis in ("h", "g"):
-        value = value + shifted(value, axis, 1)
+def summed(value, axis):
     total = value
-    for step in range(1, lax.axis_size("s")):
-        total = total + shifted(value, "s", step)
+    for step in range(1, lax.axis_size(axis)):
+        total = total + shifted(value, axis, step)
     return total
 
 
@@ -816,17 +899,19 @@
     tokens_full = lax.all_gather(tokens, CUBE, axis=0, tiled=False)
     tokens_full = tokens_full.reshape(4, 4, row_count, feature_count)
     up_blocks = packed([w_fc1], [False], rider)
-    head_blocks = packed([w_query, w_key, w_value, w_dense], [False, False, False, True])
-    cot = joined(cotangent, "g", after=[up_blocks, head_blocks])
+    head_sides = packed_sides(
+        [w_query, w_key, w_value, w_dense], [False, False, False, True]
+    )
+    down_sides = packed_sides([w_fc2], [True])
+    cot = joined(cotangent, "g", after=[up_blocks, head_sides[0], down_sides[0]])
     arrived = exchanged(up_blocks, after=[cot])
     cot = lax.all_gather(cot, ("h", "m", "c"), axis=0, tiled=False)
     cot = cot.reshape(2, 4, 2, row_count, feature_count)
-    head_arrived = exchanged(head_blocks)
-    down_arrived = exchanged(packed([w_fc2], [True]))
+    head_blocks = spread_sides(head_sides, after=[arrived])
+    head_arrived = exchanged_along_line(head_blocks)
     up_weight = Weight(arrived, weight_rows, 0, hidden)
     qkv_weight = Weight(head_arrived, weight_rows, 0, 3 * lanes)
     dense_weight = Weight(head_arrived, weight_rows, 3 * lanes, lanes)
-    down_weight = Weight(down_arrived, weight_rows, 0, hidden)
 
     def from_other_core(array):
         split = array[:, :weight_rows].reshape(2, 2, wide // 4, weight_rows, -1)
@@ -836,7 +921,6 @@
     head_other = from_other_core(head_arrived)
     qkv_other = Weight(head_other, weight_rows, 0, 3 * lanes)
     dense_other = Weight(head_other, weight_rows, 3 * lanes, lanes)
-    down_other = Weight(from_other_core(down_arrived), weight_rows, 0, hidden)
 
     here = arrived[:, weight_rows:].reshape(wide, 16 * hidden)
     local, start = [], 0
@@ -857,12 +941,32 @@
     normed, stats, up_low, up_slope = norm_up(
         tokens_full, gain, shift, up_bias, up_weight, after=[up_other.array]
     )
+    down_blocks = spread_sides(down_sides, after=[normed])
+    down_arrived = exchanged_along_line(down_blocks)
+    down_weight = Weight(down_arrived, weight_rows, 0, hidden)
+    down_other = Weight(from_other_core(down_arrived), weight_rows, 0, hidden)
     qkv = project_heads(normed, qkv_bias, qkv_weight)
     attended, log_sums = attention(qkv)
     grad_down = weight_grad([(up_low, cot)], wide, after=[attended])
     attended_grad, up_grad, up_sums = back_through(
         cot, up_slope, dense_weight, down_weight, after=[grad_down]
     )
+    qkv_grad, qkv_sums = attention_back(qkv, attended_grad, log_sums)
+    qkv_grad_other = shifted(qkv_grad, "c", 1)
+
+    grad_up = weight_grad([(up_grad, normed)], wide, after=[qkv_grad])
+    normed_grad = partial_sum(
+        [
+            (qkv_grad, qkv_grad_other, qkv_weight, qkv_other),
+            (up_grad, shifted(up_grad, "c", 1), up_weight, up_other),
+        ],
+        row_count,
+        feature_count,
+        "normed_gradient",
+        "mh",
+        after=[grad_up],
+    )
+
     branch = partial_sum(
         [
             (attended, shifted(attended, "c", 1), dense_weight, dense_other),
@@ -871,12 +975,9 @@
         row_count,
         feature_count,
         "branch_sum",
-        1,
-        after=[up_grad],
-    )
-    qkv_grad, qkv_sums = attention_back(qkv, attended_grad, log_sums, after=branch[:1])
-    qkv_grad_other = shifted(qkv_grad, "c", 1)
-
+        "mm",
+        after=normed_grad[:1],
+    )
     def spread(vector):
         placed = jnp.zeros((4, vector.shape[0]), jnp.float32)
         placed = lax.dynamic_update_index_in_dim(placed, vector, quarter, 0)
@@ -892,49 +993,28 @@
     rider = jnp.concatenate(terms, axis=1).astype(jnp.bfloat16)
     early_count = rider.shape[1]
     rider = jnp.pad(rider, ((0, 0), (0, 16 * weight_rows - early_count)))
-    grad_rest = weight_grad(
-        [(up_grad, normed), (qkv_grad, normed), (attended, cot)],
+    grad_heads = weight_grad(
+        [(qkv_grad, normed), (attended, cot)],
         wide,
         rider.reshape(wide, 16, weight_rows),
-    )
-    second = folded(branch[0], shifted(branch[1], "m", 1), "gh", "h", after=[grad_rest, qkv_grad_other])
-    grad_rest = lax.optimization_barrier((grad_rest, second[0]))[0]
-    normed_grad = partial_sum(
-        [
-            (qkv_grad, qkv_grad_other, qkv_weight, qkv_other),
-            (up_grad, shifted(up_grad, "c", 1), up_weight, up_other),
-        ],
-        row_count,
-        feature_count,
-        "normed_gradient",
-        2,
-        after=second[:1],
-    )
-
-    (grad_down,), _ = scatter_columns(grad_down, [hidden], [True], after=normed_grad[:1])
+        after=branch[:1],
+    )
     first = [normed_grad[:2], normed_grad[2:]]
-    first[0] = folded(first[0][0], shifted(first[0][1], "m", 1), "gh", "h", after=[grad_down])
-    second = folded(second[0], shifted(second[1], "h", 1), "g", "g", after=first[0][:1])
-    first[1] = folded(first[1][0], shifted(first[1][1], "m", 1), "gh", "h", after=second[:1])
-    first[0] = folded(first[0][0], shifted(first[0][1], "h", 1), "g", "g", after=first[1][:1])
-    first[1] = folded(first[1][0], shifted(first[1][1], "h", 1), "g", "g", after=first[0][:1])
-    output = finished(
-        tokens,
-        second[0][0],
-        shifted(second[1][0], "g", 1),
-        out_bias.reshape(1, -1),
-        after=first[1][:1],
-    )
-    (grad_up, grad_query, grad_key, grad_value, grad_dense), riders = scatter_columns(
-        grad_rest,
-        [hidden] + [lanes] * 4,
-        [False, False, False, False, True],
-        after=[output],
-    )
-    early = jnp.sum(riders.astype(jnp.float32), axis=0).reshape(-1)[:early_count]
+    second = [branch[:2], branch[2:]]
+
+    def fold(part, arrived, axes, after):
+        return folded(part[0], shifted(part[1], arrived, 1), axes, axes[-1], after=[after])
+
+    first[0] = fold(first[0], "m", "gh", grad_heads)
+    (grad_down,), _ = scatter_columns(grad_down, [hidden], [True], after=first[0][:1])
+    first[1] = fold(first[1], "h", "gm", grad_down)
+    second[0] = fold(second[0], "m", "gh", first[1][0])
+    first[0] = fold(first[0], "h", "g", second[0][0])
+    first[1] = fold(first[1], "m", "g", first[0][0])
+    (grad_up,), _ = scatter_columns(grad_up, [hidden], [False], after=first[1][:1])
 
     def last(keep, send):
-        arrived = lax.optimization_barrier((shifted(send[0], "g", 1), grad_dense))[0]
+        arrived = lax.optimization_barrier((shifted(send[0], "g", 1), grad_up))[0]
         return keep[0].astype(jnp.float32) + arrived.astype(jnp.float32)
 
     local_x = tokens.astype(jnp.float32)
@@ -952,7 +1032,22 @@
 
     own_terms = [jnp.sum(standard_grad * standard, axis=0), jnp.sum(standard_grad, axis=0)]
     own_terms = [term.reshape(wide, -1) for term in own_terms]
-    late = summed_along_wide(jnp.concatenate(own_terms, axis=1))
+    late = summed(jnp.concatenate(own_terms, axis=1), "h")
+    late = summed(summed(late, "g"), "s")
+    second[1] = fold(second[1], "m", "gh", standard_grad)
+    second[0] = fold(second[0], "h", "g", second[1][0])
+    second[1] = fold(second[1], "h", "g", second[0][0])
+    (grad_query, grad_key, grad_value, grad_dense), riders = scatter_columns(
+        grad_heads, [lanes] * 4, [False, False, False, True], after=second[1][:1]
+    )
+    early = jnp.sum(riders.astype(jnp.float32), axis=0).reshape(-1)[:early_count]
+    output = finished(
+        tokens,
+        [part[0][0] for part in second],
+        [shifted(part[1][0], "g", 1) for part in second],
+        out_bias.reshape(1, -1),
+        after=[grad_dense],
+    )
     terms = own_terms + terms
     vector_sums = jnp.concatenate([pick(late, lax.axis_index(WIDE)), early])
     vector_grads, start = [], 0

time: 440 us -> 424 us (0.964)
  waiting for transfers between devices: 175 us -> 141 us
  Pallas kernels: 162 us -> 175 us
    all_to_all x3 -> x1, waiting for transfers between devices: 96.5 us -> 24.5 us  [exchanged(): return lax.all_to_all(blocks, WIDE, 0, 0)]
    all_to_all x0 -> x2, waiting for transfers between devices: none -> 27 us  [exchanged_along_line(): lax.all_to_all(blocks, LINE, 0, 0).reshape(2 * count, rows // 2, width)]
    pallas_call x7 -> x13, Pallas kernels: 17.3 us -> 29.9 us  [prefetch_call(): run(index.astype(jnp.int32).reshape(1), *after, *operands)]
    all_to_all x3 -> x1, starting transfers between devices: 18.4 us -> 6.76 us  [exchanged(): return lax.all_to_all(blocks, WIDE, 0, 0)]
    all_to_all x0 -> x2, starting transfers between devices: none -> 9.01 us  [exchanged_along_line(): lax.all_to_all(blocks, LINE, 0, 0).reshape(2 * count, rows // 2, width)]
    ppermute x24 -> x29, waiting for transfers between devices: 77.6 us -> 85.8 us  [shifted(): lax.ppermute(value, axis, [(source, (source + step) % count) for source i...]
    ppermute x24 -> x29, starting transfers between devices: 20 us -> 24.6 us  [shifted(): lax.ppermute(value, axis, [(source, (source + step) % count) for source i...]
    unnamed x56 -> x64, local copies, waits for them, and re-layouts: 14.6 us -> 12.4 us
  transfers between devices with their start and end apart: 31 -> 37, of which waited for: 15 -> 19; matrix products, arithmetic and copies ran while one was open for 5% -> 6% of each run, Pallas kernels for 37% -> 41%
where the time goes in v5:
time: 424 us; the launch traced here: 422 us
  Pallas kernels  175 us (41%)
  waiting for transfers between devices  141 us (33%)
  starting transfers between devices  54.7 us (13%)
  local copies, waits for them, and re-layouts  30.7 us (7%)
  between operations  14.3 us (3%)
  other arithmetic  6.46 us (2%)
    pallas_call x15, Pallas kernels, call(): return lambda *operands: run(*after, *operands)  145 us
    ppermute x29, waiting for transfers between devices, shifted(): lax.ppermute(value, axis, [(source, (source + step) % count) for source i...  85.8 us
    pallas_call x13, Pallas kernels, prefetch_call(): run(index.astype(jnp.int32).reshape(1), *after, *operands)  29.9 us
    all_to_all x2, waiting for transfers between devices, exchanged_along_line(): lax.all_to_all(blocks, LINE, 0, 0).reshape(2 * count, rows // 2, width)  27 us
    ppermute x29, starting transfers between devices, shifted(): lax.ppermute(value, axis, [(source, (source + step) % count) for source i...  24.6 us
    all_to_all x1, waiting for transfers between devices, exchanged(): return lax.all_to_all(blocks, WIDE, 0, 0)  24.5 us
    all_to_all x3, starting transfers between devices, scatter_columns(): arrived = lax.all_to_all(grad, WIDE, 0, 0)  14.2 us
    unnamed x64, local copies, waits for them, and re-layouts  12.4 us
  transfers between devices with their start and end apart: 37, of which 19 were waited for; matrix products, arithmetic and copies ran while one was open for 6% of the time, Pallas kernels for 41%

profile of v5, /device:TPU:0, one launch (start us, length us, event | category | flops | bytes accessed | tf_op | source)
XLA Modules:
  0.0 421.9 jit_solution(14378592327901515799)
XLA Ops:
  8.0 3.1 collective-permute-start
  11.1 5.4 %concatenate.16 = bf16[704]{0:T(1024)(128)(2,1)S(1)} concatenate(bf16[64]{0:T(256)(128)(2,1)} %param.22, bf16[64]{0:T(256)(128)(2,1)} %param.23, bf16[64]{0:T(256)(128)(2,1)} %param.25, bf16[64]{0:T(256)(128)(2,1)} %param.27, bf16[64]{0:T(256)(128)(2,1)} %param.29, bf16[64]{0:T(256)(128)(2,1)} %param.31, bf16[64]{0:T(256)(128)(2,1)} %param.35, bf16[256]{0:T(256)(128)(2,1)} %param.33), dimensions={0} | concatenate | bytes 2816 | tf_op jit(solution)/shard_map/concatenate | solution.py:896
  17.1 3.6 pack.3
  20.7 2.2 pack.5
  22.9 2.2 pack.4
  25.1 2.2 collective-permute-done.refs_4_
  30.2 6.8 %all-to-all-start = ((bf16[8,272,512]{2,1,0:T(8,128)(2,1)}), bf16[8,272,512]{2,1,0:T(8,128)(2,1)S(1)}, u32[]{:S(2)}, u32[]{:S(2)}) async-start(bf16[8,272,512]{2,1,0:T(8,128)(2,1)} %bitcast.103), calls=%async_computation | async-start | bytes 4456448 | tf_op jit(solution)/shard_map/all_to_all | solution.py:672
  39.0 29.4 %collective-permute-done.4.refs_2_ = bf16[2,256,512]{2,1,0:T(8,128)(2,1)S(1)} collective-permute-done((bf16[2,256,512]{2,1,0:T(8,128)(2,1)S(1)}, bf16[2,256,512]{2,1,0:T(8,128)(2,1)S(1)}, u32[]{:S(2)}, u32[]{:S(2)}) %collective-permute-start.4) | collective-permute-done | bytes 524320 | tf_op jit(solution)/shard_map/ppermute | solution.py:48
  68.4 24.5 %all-to-all-done.refs_5_.refs_0_.refs_7_ = bf16[8,272,512]{2,1,0:T(8,128)(2,1)S(1)} async-done(((bf16[8,272,512]{2,1,0:T(8,128)(2,1)}), bf16[8,272,512]{2,1,0:T(8,128)(2,1)S(1)}, u32[]{:S(2)}, u32[]{:S(2)}) %all-to-all-start) | async-done | bytes 2228256 | tf_op jit(solution)/shard_map/all_to_all | solution.py:672
  94.3 2.4 spread.2
  96.7 4.5 %all-to-all-start.1 = ((bf16[4,512,512]{2,1,0:T(8,128)(2,1)}), bf16[4,512,512]{2,1,0:T(8,128)(2,1)S(1)}, u32[]{:S(2)}, u32[]{:S(2)}) async-start(bf16[4,512,512]{2,1,0:T(8,128)(2,1)} %bitcast.110), calls=%async_computation.1 | async-start | bytes 4194304 | tf_op jit(solution)/shard_map/all_to_all | solution.py:734
  101.3 3.4 collective-permute-start.5
  110.5 3.1 collective-permute-done.3
  116.0 14.3 %norm_up.1 = (bf16[2048,2048]{1,0:T(8,128)(2,1)}, f32[2048,128]{1,0:T(8,128)}, bf16[2048,512]{1,0:T(8,128)(2,1)}, f32[2048,512]{1,0:T(8,128)}) custom-call(bf16[2,2,256,512]{3,2,1,0:T(8,128)(2,1)} %copy-done.9, bf16[4,4,512,512]{3,2,1,0:T(8,128)(2,1)} %bitcast.109, f32[1,2048]{1,0:T(1,128)} %reshape.236.refs_2_, f32[1,2048]{1,0:T(1,128)} %reshape.237.refs_3_, ...), custom_call_target="tpu_custom_call" | custom-call | flops 12884901 | tf_op jit(solution)/shard_map/norm_up/pallas_call | solution.py:74
  130.3 2.6 spread.3
  132.9 12.7 %all-to-all-done.1 = bf16[4,512,512]{2,1,0:T(8,128)(2,1)S(1)} async-done(((bf16[4,512,512]{2,1,0:T(8,128)(2,1)}), bf16[4,512,512]{2,1,0:T(8,128)(2,1)S(1)}, u32[]{:S(2)}, u32[]{:S(2)}) %all-to-all-start.1) | async-done | bytes 2097184 | tf_op jit(solution)/shard_map/all_to_all | solution.py:734
  147.0 4.5 %all-to-all-start.2 = ((bf16[4,512,512]{2,1,0:T(8,128)(2,1)}), bf16[4,512,512]{2,1,0:T(8,128)(2,1)}, u32[]{:S(2)}, u32[]{:S(2)}) async-start(bf16[4,512,512]{2,1,0:T(8,128)(2,1)} %bitcast.111), calls=%async_computation.2 | async-start | bytes 4194304 | tf_op jit(solution)/shard_map/all_to_all | solution.py:734
  152.4 9.4 %project_heads.1.refs_0_ = bf16[2048,384]{1,0:T(8,128)(2,1)} custom-call(bf16[2048,2048]{1,0:T(8,128)(2,1)} %get-tuple-element.65.refs_0_.refs_2_.refs_3_, f32[1,384]{1,0:T(1,128)} %reshape.238.refs_1_, f32[2048,128]{1,0:T(8,128)} %constant.83.clone.refs_2_.refs_3_, f32[2048,128]{1,0:T(8,128)} %constant.84.clone.refs_3_.refs_4_, bf16[8,256,512]{2,1,0:T(8,128)(2,1)} %bitcast.96), custom_call_target="tpu_custom_call" | custom-call | flops 6442450 | tf_op jit(solution)/shard_map/project_heads/pallas_call | solution.py:74
  161.8 14.3 %attention.1 = (bf16[2048,128]{1,0:T(8,128)(2,1)}, f32[8,2048]{1,0:T(8,128)}) custom-call(bf16[2048,384]{1,0:T(8,128)(2,1)} %project_heads.1.refs_0_), custom_call_target="tpu_custom_call" | custom-call | flops 10000000 | tf_op jit(solution)/shard_map/attention/pallas_call | solution.py:74
  176.1 8.8 %weight_grad.3.refs_0_ = bf16[8,512,256]{2,1,0:T(8,128)(2,1)} custom-call(bf16[2048,128]{1,0:T(8,128)(2,1)} %get-tuple-element.67.refs_0_.refs_2_.refs_4_, bf16[2048,512]{1,0:T(8,128)(2,1)} %get-tuple-element.68.refs_1_.refs_3_, bf16[2,4,2,512,512]{4,3,2,1,0:T(8,128)(2,1)} %bitcast.93), custom_call_target="tpu_custom_call" | custom-call | flops 8589934 | tf_op jit(solution)/shard_map/weight_grad/pallas_call | solution.py:74
  184.9 14.3 %all-to-all-done.2 = bf16[4,512,512]{2,1,0:T(8,128)(2,1)} async-done(((bf16[4,512,512]{2,1,0:T(8,128)(2,1)}), bf16[4,512,512]{2,1,0:T(8,128)(2,1)}, u32[]{:S(2)}, u32[]{:S(2)}) %all-to-all-start.2) | async-done | bytes 2097184 | tf_op jit(solution)/shard_map/all_to_all | solution.py:734
  199.2 5.2 %all-to-all-start.3 = ((bf16[8,512,256]{2,1,0:T(8,128)(2,1)}), bf16[8,512,256]{2,1,0:T(8,128)(2,1)}, u32[]{:S(2)}, u32[]{:S(2)}) async-start(bf16[8,512,256]{2,1,0:T(8,128)(2,1)} %weight_grad.3.refs_0_), calls=%async_computation.3 | async-start | bytes 4194304 | tf_op jit(solution)/shard_map/all_to_all | solution.py:752
  204.4 11.2 %back_through.1 = (bf16[2048,128]{1,0:T(8,128)(2,1)}, bf16[2048,512]{1,0:T(8,128)(2,1)}, f32[1,512]{1,0:T(1,128)}) custom-call(bf16[8,512,256]{2,1,0:T(8,128)(2,1)} %weight_grad.3.refs_0_, bf16[2,4,2,512,512]{4,3,2,1,0:T(8,128)(2,1)} %bitcast.94, f32[2048,512]{1,0:T(8,128)} %get-tuple-element.69.refs_2_, bf16[8,256,512]{2,1,0:T(8,128)(2,1)} %bitcast.97, ...), custom_call_target="tpu_custom_call" | custom-call | flops 10737418 | tf_op jit(solution)/shard_map/back_through/pallas_call | solution.py:74
  215.7 23.9 %attention_back.1 = (bf16[2048,384]{1,0:T(8,128)(2,1)}, f32[1,384]{1,0:T(1,128)}) custom-call(bf16[2048,384]{1,0:T(8,128)(2,1)} %project_heads.1.refs_0_, bf16[2048,128]{1,0:T(8,128)(2,1)} %get-tuple-element.71.refs_1_, f32[8,2048]{1,0:T(8,128)} %get-tuple-element.72.refs_2_, f32[2048,128]{1,0:T(8,128)} %constant.83.clone.refs_2_.refs_3_, ...), custom_call_target="tpu_custom_call" | custom-call | flops 20000000 | tf_op jit(solution)/shard_map/attention_back/pallas_call | solution.py:74
  239.5 8.8 %weight_grad.4.refs_0_ = bf16[8,512,256]{2,1,0:T(8,128)(2,1)} custom-call(bf16[2048,384]{1,0:T(8,128)(2,1)} %get-tuple-element.73.refs_0_.refs_2_, bf16[2048,512]{1,0:T(8,128)(2,1)} %get-tuple-element.74.refs_1_.refs_3_, bf16[2048,2048]{1,0:T(8,128)(2,1)} %get-tuple-element.65.refs_0_.refs_2_.refs_3_), custom_call_target="tpu_custom_call" | custom-call | flops 8589934 | tf_op jit(solution)/shard_map/weight_grad/pallas_call | solution.py:74
  248.3 3.0 all-to-all-done.3
  251.3 4.4 %all-to-all-start.4 = ((bf16[8,512,256]{2,1,0:T(8,128)(2,1)}), bf16[8,512,256]{2,1,0:T(8,128)(2,1)}, u32[]{:S(2)}, u32[]{:S(2)}) async-start(bf16[8,512,256]{2,1,0:T(8,128)(2,1)} %weight_grad.4.refs_0_), calls=%async_computation.4 | async-start | bytes 4194304 | tf_op jit(solution)/shard_map/all_to_all | solution.py:752
  256.9 2.3 dynamic-slice_bitcast_fusion
  259.8 5.3 %collective-permute-done.8.refs_8_ = bf16[2,2,256,512]{3,2,1,0:T(8,128)(2,1)S(1)} collective-permute-done((bf16[2,2,256,512]{3,2,1,0:T(8,128)(2,1)S(1)}, bf16[2,2,256,512]{3,2,1,0:T(8,128)(2,1)S(1)}, u32[]{:S(2)}, u32[]{:S(2)}) %collective-permute-start.8) | collective-permute-done | bytes 1048608 | tf_op jit(solution)/shard_map/ppermute | solution.py:48
  267.4 15.0 %normed_gradient.1 = (bf16[4,256,512]{2,1,0:T(8,128)(2,1)}, bf16[4,256,512]{2,1,0:T(8,128)(2,1)}, bf16[2,2,256,512]{3,2,1,0:T(8,128)(2,1)}, bf16[2,2,256,512]{3,2,1,0:T(8,128)(2,1)}) custom-call(bf16[8,512,256]{2,1,0:T(8,128)(2,1)} %weight_grad.4.refs_0_, s32[3]{0:T(128)} %pad_add_fusion.refs_1_, bf16[2048,384]{1,0:T(8,128)(2,1)} %get-tuple-element.73.refs_0_.refs_2_, ...), custom_call_target="tpu_custom_call" | custom-call | flops 15032385 | tf_op jit(solution)/shard_map/normed_gradient/pallas_call | solution.py:74
  286.4 10.9 %branch_sum.1 = (bf16[4,256,512]{2,1,0:T(8,128)(2,1)}, bf16[4,256,512]{2,1,0:T(8,128)(2,1)}, bf16[4,256,512]{2,1,0:T(8,128)(2,1)}, bf16[4,256,512]{2,1,0:T(8,128)(2,1)}) custom-call(bf16[4,256,512]{2,1,0:T(8,128)(2,1)} %get-tuple-element.75.refs_0_, s32[3]{0:T(128)} %pad_add_fusion.refs_1_, bf16[2048,128]{1,0:T(8,128)(2,1)} %get-tuple-element.67.refs_0_.refs_2_.refs_4_, ...), custom_call_target="tpu_custom_call" | custom-call | flops 10737418 | tf_op jit(solution)/shard_map/branch_sum/pallas_call | solution.py:74
  300.4 10.3 %weight_grad.5.refs_0_ = bf16[8,528,256]{2,1,0:T(8,128)(2,1)} custom-call(bf16[4,256,512]{2,1,0:T(8,128)(2,1)} %get-tuple-element.76.refs_0_, bf16[8,16,256]{2,1,0:T(8,128)(2,1)} %bitcast.129, bf16[2048,384]{1,0:T(8,128)(2,1)} %get-tuple-element.73.refs_0_.refs_2_, bf16[2048,2048]{1,0:T(8,128)(2,1)} %get-tuple-element.65.refs_0_.refs_2_.refs_3_, ...), custom_call_target="tpu_custom_call" | custom-call | flops 8858370 | tf_op jit(solution)/shard_map/weight_grad/pallas_call | solution.py:74
  310.7 4.6 %all-to-all-start.5 = ((bf16[8,528,256]{2,1,0:T(8,128)(2,1)}), bf16[8,528,256]{2,1,0:T(8,128)(2,1)S(1)}, u32[]{:S(2)}, u32[]{:S(2)}) async-start(bf16[8,528,256]{2,1,0:T(8,128)(2,1)} %weight_grad.5.refs_0_), calls=%async_computation.5 | async-start | bytes 4325376 | tf_op jit(solution)/shard_map/all_to_all | solution.py:752
  315.3 2.5 fold.8
  319.9 3.8 unpack.3.refs_0_
  323.7 2.5 fold.9
  326.7 4.5 %collective-permute-done.14 = bf16[4,256,512]{2,1,0:T(8,128)(2,1)S(1)} collective-permute-done((bf16[4,256,512]{2,1,0:T(8,128)(2,1)}, bf16[4,256,512]{2,1,0:T(8,128)(2,1)S(1)}, u32[]{:S(2)}, u32[]{:S(2)}) %collective-permute-start.14) | collective-permute-done | bytes 1048608 | tf_op jit(solution)/shard_map/ppermute | solution.py:48
  332.1 2.6 fold.10
  334.7 17.1 %collective-permute-done.15 = bf16[2,256,512]{2,1,0:T(8,128)(2,1)} collective-permute-done((bf16[2,256,512]{2,1,0:T(8,128)(2,1)}, bf16[2,256,512]{2,1,0:T(8,128)(2,1)}, u32[]{:S(2)}, u32[]{:S(2)}) %collective-permute-start.15) | collective-permute-done | bytes 524320 | tf_op jit(solution)/shard_map/ppermute | solution.py:48
  359.6 4.2 unpack.4
  363.7 6.6 %collective-permute-done.18 = bf16[256,512]{1,0:T(8,128)(2,1)S(1)} collective-permute-done((bf16[256,512]{1,0:T(8,128)(2,1)}, bf16[256,512]{1,0:T(8,128)(2,1)S(1)}, u32[]{:S(2)}, u32[]{:S(2)}) %collective-permute-start.18) | collective-permute-done | bytes 262176 | tf_op jit(solution)/shard_map/ppermute | solution.py:48
  370.3 5.6 %collective-permute-done.16 = bf16[256,512]{1,0:T(8,128)(2,1)} collective-permute-done((bf16[256,512]{1,0:T(8,128)(2,1)S(1)}, bf16[256,512]{1,0:T(8,128)(2,1)}, u32[]{:S(2)}, u32[]{:S(2)}) %collective-permute-start.16) | collective-permute-done | bytes 262176 | tf_op jit(solution)/shard_map/ppermute | solution.py:48
  380.2 2.2 collective-permute-done.26
  383.5 2.9 multiply_add_fusion
  386.3 2.5 fold.13
  396.9 5.1 %collective-permute-done.21 = bf16[2,256,512]{2,1,0:T(8,128)(2,1)S(1)} collective-permute-done((bf16[2,256,512]{2,1,0:T(8,128)(2,1)}, bf16[2,256,512]{2,1,0:T(8,128)(2,1)S(1)}, u32[]{:S(2)}, u32[]{:S(2)}) %collective-permute-start.21) | collective-permute-done | bytes 524320 | tf_op jit(solution)/shard_map/ppermute | solution.py:48
  407.2 3.9 unpack.5
  412.2 2.4 finish.1
  (191 shorter events, 60.4 us)
Async XLA Ops:
  7.2 107.9 %all-gather.5.cloned.1.call-start = ((), (), s32[]{:S(2)}) async-start(), calls=%async_computation.6 | async-start | bytes 8912896 | tf_op jit(solution)/shard_map/all_gather | solution.py:899
  7.9 168.2 %all-gather.7.cloned.1.call-start = ((), (), s32[]{:S(2)}) async-start(), calls=%async_computation.7 | async-start | bytes 9437184 | tf_op jit(solution)/shard_map/all_gather | solution.py:908
  8.0 19.3 %collective-permute-start = (bf16[512,512]{1,0:T(8,128)(2,1)}, bf16[512,512]{1,0:T(8,128)(2,1)S(1)}, u32[]{:S(2)}, u32[]{:S(2)}) collective-permute-start(bf16[512,512]{1,0:T(8,128)(2,1)} %refs_3_.5), channel_id=1, source_target_pairs={{0,8},{8,0},{1,9},{9,1},{2,10},{10,2},{3,11},{11,3},{4,12},{12,4},... | collective-permute-start | bytes 1572872 | tf_op jit(solution)/shard_map/ppermute | solution.py:48
  30.2 62.7 %all-to-all-start = ((bf16[8,272,512]{2,1,0:T(8,128)(2,1)}), bf16[8,272,512]{2,1,0:T(8,128)(2,1)S(1)}, u32[]{:S(2)}, u32[]{:S(2)}) async-start(bf16[8,272,512]{2,1,0:T(8,128)(2,1)} %bitcast.103), calls=%async_computation | async-start | bytes 4456448 | tf_op jit(solution)/shard_map/all_to_all | solution.py:672
  37.0 31.4 %collective-permute-start.4 = (bf16[2,256,512]{2,1,0:T(8,128)(2,1)S(1)}, bf16[2,256,512]{2,1,0:T(8,128)(2,1)S(1)}, u32[]{:S(2)}, u32[]{:S(2)}) collective-permute-start(bf16[2,256,512]{2,1,0:T(8,128)(2,1)S(1)} %copy-done.27), channel_id=1, source_target_pairs={{0,4},{4,0},{1,5},{5,1},{2,6},{6,2},{3,7},{7,3},{8,12},{12,8},{9,1... | collective-permute-start | bytes 1572872 | tf_op jit(solution)/shard_map/ppermute | solution.py:48
  68.4 24.5 %copy-start.20 = (bf16[2,256,512]{2,1,0:T(8,128)(2,1)}, bf16[2,256,512]{2,1,0:T(8,128)(2,1)S(1)}, u32[]{:S(2)}) copy-start(bf16[2,256,512]{2,1,0:T(8,128)(2,1)S(1)} %collective-permute-done.4.refs_2_) | copy-start | bytes 1572868
  96.7 48.9 %all-to-all-start.1 = ((bf16[4,512,512]{2,1,0:T(8,128)(2,1)}), bf16[4,512,512]{2,1,0:T(8,128)(2,1)S(1)}, u32[]{:S(2)}, u32[]{:S(2)}) async-start(bf16[4,512,512]{2,1,0:T(8,128)(2,1)} %bitcast.110), calls=%async_computation.1 | async-start | bytes 4194304 | tf_op jit(solution)/shard_map/all_to_all | solution.py:734
  101.3 29.0 %collective-permute-start.5 = (bf16[2,256,512]{2,1,0:T(8,128)(2,1)}, bf16[2,256,512]{2,1,0:T(8,128)(2,1)}, u32[]{:S(2)}, u32[]{:S(2)}) collective-permute-start(bf16[2,256,512]{2,1,0:T(8,128)(2,1)} %get-tuple-element.70), channel_id=1, source_target_pairs={{0,4},{4,0},{1,5},{5,1},{2,6},{6,2},{3,7},{7,3},{8,12},{12,8},{9,1... | collective-permute-start | bytes 1572872 | tf_op jit(solution)/shard_map/ppermute | solution.py:48
  107.3 7.8 %collective-permute-start.1 = (bf16[2,2,256,512]{3,2,1,0:T(8,128)(2,1)}, bf16[2,2,256,512]{3,2,1,0:T(8,128)(2,1)S(1)}, u32[]{:S(2)}, u32[]{:S(2)}) collective-permute-start(bf16[2,2,256,512]{3,2,1,0:T(8,128)(2,1)} %dynamic-slice_bitcast_fusion.2), channel_id=1, source_target_pairs={{0,1},{1,0},{2,3},{3,2},{4,5},{5,4},{6,7},{7,6},{8,9},{9,8},{10,11... | collective-permute-start | bytes 3145736 | tf_op jit(solution)/shard_map/ppermute | solution.py:48
  107.4 44.1 %copy-start.23 = (bf16[1,8,16,512]{3,1,2,0:T(8,128)(2,1)}, bf16[1,8,16,512]{3,1,2,0:T(8,128)(2,1)S(1)}, u32[]{:S(2)}) copy-start(bf16[1,8,16,512]{3,1,2,0:T(8,128)(2,1)S(1)} %copy.42) | copy-start | bytes 393220
  107.4 2.5 collective-permute-start.2
  109.9 3.7 collective-permute-start.3
  147.0 52.2 %all-to-all-start.2 = ((bf16[4,512,512]{2,1,0:T(8,128)(2,1)}), bf16[4,512,512]{2,1,0:T(8,128)(2,1)}, u32[]{:S(2)}, u32[]{:S(2)}) async-start(bf16[4,512,512]{2,1,0:T(8,128)(2,1)} %bitcast.111), calls=%async_computation.2 | async-start | bytes 4194304 | tf_op jit(solution)/shard_map/all_to_all | solution.py:734
  199.2 52.1 %all-to-all-start.3 = ((bf16[8,512,256]{2,1,0:T(8,128)(2,1)}), bf16[8,512,256]{2,1,0:T(8,128)(2,1)}, u32[]{:S(2)}, u32[]{:S(2)}) async-start(bf16[8,512,256]{2,1,0:T(8,128)(2,1)} %weight_grad.3.refs_0_), calls=%async_computation.3 | async-start | bytes 4194304 | tf_op jit(solution)/shard_map/all_to_all | solution.py:752
  248.3 8.0 %copy-start.1 = (bf16[4,512,512]{2,1,0:T(8,128)(2,1)S(1)}, bf16[4,512,512]{2,1,0:T(8,128)(2,1)}, u32[]{:S(2)}) copy-start(bf16[4,512,512]{2,1,0:T(8,128)(2,1)} %copy-done) | copy-start | bytes 6291460
  251.3 59.4 %all-to-all-start.4 = ((bf16[8,512,256]{2,1,0:T(8,128)(2,1)}), bf16[8,512,256]{2,1,0:T(8,128)(2,1)}, u32[]{:S(2)}, u32[]{:S(2)}) async-start(bf16[8,512,256]{2,1,0:T(8,128)(2,1)} %weight_grad.4.refs_0_), calls=%async_computation.4 | async-start | bytes 4194304 | tf_op jit(solution)/shard_map/all_to_all | solution.py:752
  255.7 10.2 %collective-permute-start.7 = (bf16[2048,512]{1,0:T(8,128)(2,1)}, bf16[2048,512]{1,0:T(8,128)(2,1)S(1)}, u32[]{:S(2)}, u32[]{:S(2)}) collective-permute-start(bf16[2048,512]{1,0:T(8,128)(2,1)} %get-tuple-element.74.refs_1_.refs_3_), channel_id=1, source_target_pairs={{0,1},{1,0},{2,3},{3,2},{4,5},{5,4},{6,7},{7,6},{8,9},{9,8},{10,11... | collective-permute-start | bytes 6291464 | tf_op jit(solution)/shard_map/ppermute | solution.py:48
  255.7 10.1 %collective-permute-start.6 = (bf16[2048,384]{1,0:T(8,128)(2,1)}, bf16[2048,384]{1,0:T(8,128)(2,1)}, u32[]{:S(2)}, u32[]{:S(2)}) collective-permute-start(bf16[2048,384]{1,0:T(8,128)(2,1)} %get-tuple-element.73.refs_0_.refs_2_), channel_id=1, source_target_pairs={{0,1},{1,0},{2,3},{3,2},{4,5},{5,4},{6,7},{7,6},{8,9},{9,8},{10,11... | collective-permute-start | bytes 4718600 | tf_op jit(solution)/shard_map/ppermute | solution.py:48
  256.2 28.3 %collective-permute-start.10 = (bf16[2048,512]{1,0:T(8,128)(2,1)}, bf16[2048,512]{1,0:T(8,128)(2,1)S(1)}, u32[]{:S(2)}, u32[]{:S(2)}) collective-permute-start(bf16[2048,512]{1,0:T(8,128)(2,1)} %get-tuple-element.68.refs_1_.refs_3_), channel_id=1, source_target_pairs={{0,1},{1,0},{2,3},{3,2},{4,5},{5,4},{6,7},{7,6},{8,9},{9,8},{10,11... | collective-permute-start | bytes 6291464 | tf_op jit(solution)/shard_map/ppermute | solution.py:48
  256.3 8.8 %copy-start.6 = (bf16[2048,128]{1,0:T(8,128)(2,1)S(1)}, bf16[2048,128]{1,0:T(8,128)(2,1)}, u32[]{:S(2)}) copy-start(bf16[2048,128]{1,0:T(8,128)(2,1)} %get-tuple-element.67.refs_0_.refs_2_.refs_4_) | copy-start | bytes 1572868
  256.4 8.7 %collective-permute-start.8 = (bf16[2,2,256,512]{3,2,1,0:T(8,128)(2,1)S(1)}, bf16[2,2,256,512]{3,2,1,0:T(8,128)(2,1)S(1)}, u32[]{:S(2)}, u32[]{:S(2)}) collective-permute-start(bf16[2,2,256,512]{3,2,1,0:T(8,128)(2,1)S(1)} %dynamic-slice_bitcast_fusion.1), channel_id=1, source_target_pairs={{0,1},{1,0},{2,3},{3,2},{4,5},{5,4},{6,7},{7,6},{8,9},{9,8},{10,11... | collective-permute-start | bytes 3145736 | tf_op jit(solution)/shard_map/ppermute | solution.py:48
  259.2 25.3 %collective-permute-start.11 = (bf16[2,2,256,512]{3,2,1,0:T(8,128)(2,1)}, bf16[2,2,256,512]{3,2,1,0:T(8,128)(2,1)S(1)}, u32[]{:S(2)}, u32[]{:S(2)}) collective-permute-start(bf16[2,2,256,512]{3,2,1,0:T(8,128)(2,1)} %dynamic-slice_bitcast_fusion), channel_id=1, source_target_pairs={{0,1},{1,0},{2,3},{3,2},{4,5},{5,4},{6,7},{7,6},{8,9},{9,8},{10,11... | collective-permute-start | bytes 3145736 | tf_op jit(solution)/shard_map/ppermute | solution.py:48
  265.1 19.4 %collective-permute-start.9 = (bf16[2048,128]{1,0:T(8,128)(2,1)S(1)}, bf16[2048,128]{1,0:T(8,128)(2,1)S(1)}, u32[]{:S(2)}, u32[]{:S(2)}) collective-permute-start(bf16[2048,128]{1,0:T(8,128)(2,1)S(1)} %copy-done.6), channel_id=1, source_target_pairs={{0,1},{1,0},{2,3},{3,2},{4,5},{5,4},{6,7},{7,6},{8,9},{9,8},{10,11... | collective-permute-start | bytes 1572872 | tf_op jit(solution)/shard_map/ppermute | solution.py:48
  282.4 32.9 %collective-permute-start.12 = (bf16[4,256,512]{2,1,0:T(8,128)(2,1)}, bf16[4,256,512]{2,1,0:T(8,128)(2,1)}, u32[]{:S(2)}, u32[]{:S(2)}) collective-permute-start(bf16[4,256,512]{2,1,0:T(8,128)(2,1)} %get-tuple-element.79), channel_id=1, source_target_pairs={{0,2},{2,0},{1,3},{3,1},{4,6},{6,4},{5,7},{7,5},{8,10},{10,8},{9,1... | collective-permute-start | bytes 3145736 | tf_op jit(solution)/shard_map/ppermute | solution.py:48
  282.9 40.8 %collective-permute-start.13 = (bf16[2,2,256,512]{3,2,1,0:T(8,128)(2,1)}, bf16[2,2,256,512]{3,2,1,0:T(8,128)(2,1)}, u32[]{:S(2)}, u32[]{:S(2)}) collective-permute-start(bf16[2,2,256,512]{3,2,1,0:T(8,128)(2,1)} %get-tuple-element.82), channel_id=1, source_target_pairs={{0,4},{4,0},{1,5},{5,1},{2,6},{6,2},{3,7},{7,3},{8,12},{12,8},{9,1... | collective-permute-start | bytes 3145736 | tf_op jit(solution)/shard_map/ppermute | solution.py:48
  286.4 12.7 %copy-start.8 = (bf16[512,512]{1,0:T(8,128)(2,1)S(1)}, bf16[512,512]{1,0:T(8,128)(2,1)}, u32[]{:S(2)}) copy-start(bf16[512,512]{1,0:T(8,128)(2,1)} %refs_3_.5) | copy-start | bytes 1572868
  286.4 12.9 %copy-start.25 = (f32[1,384]{1,0:T(1,128)S(1)}, f32[1,384]{1,0:T(1,128)}, u32[]{:S(2)}) copy-start(f32[1,384]{1,0:T(1,128)} %get-tuple-element.77) | copy-start | bytes 4612
  286.4 13.3 %copy-start.24 = (f32[1,512]{1,0:T(1,128)S(1)}, f32[1,512]{1,0:T(1,128)}, u32[]{:S(2)}) copy-start(f32[1,512]{1,0:T(1,128)} %get-tuple-element.78) | copy-start | bytes 6148
  297.3 33.9 %collective-permute-start.14 = (bf16[4,256,512]{2,1,0:T(8,128)(2,1)}, bf16[4,256,512]{2,1,0:T(8,128)(2,1)S(1)}, u32[]{:S(2)}, u32[]{:S(2)}) collective-permute-start(bf16[4,256,512]{2,1,0:T(8,128)(2,1)} %get-tuple-element.84), channel_id=1, source_target_pairs={{0,2},{2,0},{1,3},{3,1},{4,6},{6,4},{5,7},{7,5},{8,10},{10,8},{9,1... | collective-permute-start | bytes 3145736 | tf_op jit(solution)/shard_map/ppermute | solution.py:48
  310.7 95.2 %all-to-all-start.5 = ((bf16[8,528,256]{2,1,0:T(8,128)(2,1)}), bf16[8,528,256]{2,1,0:T(8,128)(2,1)S(1)}, u32[]{:S(2)}, u32[]{:S(2)}) async-start(bf16[8,528,256]{2,1,0:T(8,128)(2,1)} %weight_grad.5.refs_0_), calls=%async_computation.5 | async-start | bytes 4325376 | tf_op jit(solution)/shard_map/all_to_all | solution.py:752
  317.9 34.0 %collective-permute-start.15 = (bf16[2,256,512]{2,1,0:T(8,128)(2,1)}, bf16[2,256,512]{2,1,0:T(8,128)(2,1)}, u32[]{:S(2)}, u32[]{:S(2)}) collective-permute-start(bf16[2,256,512]{2,1,0:T(8,128)(2,1)} %get-tuple-element.86), channel_id=1, source_target_pairs={{0,4},{4,0},{1,5},{5,1},{2,6},{6,2},{3,7},{7,3},{8,12},{12,8},{9,1... | collective-permute-start | bytes 1572872 | tf_op jit(solution)/shard_map/ppermute | solution.py:48
  326.2 27.6 %collective-permute-start.17 = (bf16[2,256,512]{2,1,0:T(8,128)(2,1)}, bf16[2,256,512]{2,1,0:T(8,128)(2,1)}, u32[]{:S(2)}, u32[]{:S(2)}) collective-permute-start(bf16[2,256,512]{2,1,0:T(8,128)(2,1)} %get-tuple-element.89), channel_id=1, source_target_pairs={{0,2},{2,0},{1,3},{3,1},{4,6},{6,4},{5,7},{7,5},{8,10},{10,8},{9,1... | collective-permute-start | bytes 1572872 | tf_op jit(solution)/shard_map/ppermute | solution.py:48
  355.9 14.4 %collective-permute-start.18 = (bf16[256,512]{1,0:T(8,128)(2,1)}, bf16[256,512]{1,0:T(8,128)(2,1)S(1)}, u32[]{:S(2)}, u32[]{:S(2)}) collective-permute-start(bf16[256,512]{1,0:T(8,128)(2,1)} %bitcast.155), channel_id=1, source_target_pairs={{0,8},{8,0},{1,9},{9,1},{2,10},{10,2},{3,11},{11,3},{4,12},{12,4},... | collective-permute-start | bytes 786440 | tf_op jit(solution)/shard_map/ppermute | solution.py:48
  355.9 20.1 %collective-permute-start.16 = (bf16[256,512]{1,0:T(8,128)(2,1)S(1)}, bf16[256,512]{1,0:T(8,128)(2,1)}, u32[]{:S(2)}, u32[]{:S(2)}) collective-permute-start(bf16[256,512]{1,0:T(8,128)(2,1)S(1)} %bitcast.153), channel_id=1, source_target_pairs={{0,8},{8,0},{1,9},{9,1},{2,10},{10,2},{3,11},{11,3},{4,12},{12,4},... | collective-permute-start | bytes 786440 | tf_op jit(solution)/shard_map/ppermute | solution.py:48
  359.0 27.3 %collective-permute-start.19 = (bf16[4,256,512]{2,1,0:T(8,128)(2,1)}, bf16[4,256,512]{2,1,0:T(8,128)(2,1)}, u32[]{:S(2)}, u32[]{:S(2)}) collective-permute-start(bf16[4,256,512]{2,1,0:T(8,128)(2,1)} %get-tuple-element.95), channel_id=1, source_target_pairs={{0,2},{2,0},{1,3},{3,1},{4,6},{6,4},{5,7},{7,5},{8,10},{10,8},{9,1... | collective-permute-start | bytes 3145736 | tf_op jit(solution)/shard_map/ppermute | solution.py:48
  359.5 33.4 %collective-permute-start.20 = (bf16[2,256,512]{2,1,0:T(8,128)(2,1)}, bf16[2,256,512]{2,1,0:T(8,128)(2,1)}, u32[]{:S(2)}, u32[]{:S(2)}) collective-permute-start(bf16[2,256,512]{2,1,0:T(8,128)(2,1)} %get-tuple-element.97), channel_id=1, source_target_pairs={{0,4},{4,0},{1,5},{5,1},{2,6},{6,2},{3,7},{7,3},{8,12},{12,8},{9,1... | collective-permute-start | bytes 1572872 | tf_op jit(solution)/shard_map/ppermute | solution.py:48
  359.6 16.4 %copy-start.17 = (bf16[1,256,512]{2,1,0:T(8,128)(2,1)S(1)}, bf16[1,256,512]{2,1,0:T(8,128)(2,1)}, u32[]{:S(2)}) copy-start(bf16[1,256,512]{2,1,0:T(8,128)(2,1)} %get-tuple-element.90.refs_0_) | copy-start | bytes 786436
  359.6 16.5 %copy-start.16 = (bf16[1,256,512]{2,1,0:T(8,128)(2,1)S(1)}, bf16[1,256,512]{2,1,0:T(8,128)(2,1)}, u32[]{:S(2)}) copy-start(bf16[1,256,512]{2,1,0:T(8,128)(2,1)} %get-tuple-element.87.refs_0_) | copy-start | bytes 786436
  363.7 14.2 %copy-start.5 = (bf16[512,512]{1,0:T(8,128)(2,1)S(1)}, bf16[512,512]{1,0:T(8,128)(2,1)}, u32[]{:S(2)}) copy-start(bf16[512,512]{1,0:T(8,128)(2,1)} %refs_1_.7) | copy-start | bytes 1572868
  378.5 1.2 collective-permute-start.24
  378.8 3.6 collective-permute-start.26
  379.8 3.7 collective-permute-start.25
  382.5 7.5 %collective-permute-start.27 = (f32[8,128]{1,0:T(8,128)S(1)}, f32[8,128]{1,0:T(8,128)S(1)}, u32[]{:S(2)}, u32[]{:S(2)}) collective-permute-start(f32[8,128]{1,0:T(8,128)S(1)} %fusion.10), channel_id=1, source_target_pairs={{0,8},{8,0},{1,9},{9,1},{2,10},{10,2},{3,11},{11,3},{4,12},{12,4},... | collective-permute-start | bytes 12296 | tf_op jit(solution)/shard_map/ppermute | solution.py:48
  388.9 13.2 %collective-permute-start.21 = (bf16[2,256,512]{2,1,0:T(8,128)(2,1)}, bf16[2,256,512]{2,1,0:T(8,128)(2,1)S(1)}, u32[]{:S(2)}, u32[]{:S(2)}) collective-permute-start(bf16[2,256,512]{2,1,0:T(8,128)(2,1)} %get-tuple-element.99), channel_id=1, source_target_pairs={{0,4},{4,0},{1,5},{5,1},{2,6},{6,2},{3,7},{7,3},{8,12},{12,8},{9,1... | collective-permute-start | bytes 1572872 | tf_op jit(solution)/shard_map/ppermute | solution.py:48
  390.0 6.3 %collective-permute-start.28 = (f32[8,128]{1,0:T(8,128)S(1)}, f32[8,128]{1,0:T(8,128)S(1)}, u32[]{:S(2)}, u32[]{:S(2)}) collective-permute-start(f32[8,128]{1,0:T(8,128)S(1)} %add.86), channel_id=1, source_target_pairs={{0,16},{16,0},{1,17},{17,1},{2,18},{18,2},{3,19},{19,3},{4,20},{20... | collective-permute-start | bytes 12296 | tf_op jit(solution)/shard_map/ppermute | solution.py:48
  395.0 16.2 %collective-permute-start.22 = (bf16[256,512]{1,0:T(8,128)(2,1)}, bf16[256,512]{1,0:T(8,128)(2,1)S(1)}, u32[]{:S(2)}, u32[]{:S(2)}) collective-permute-start(bf16[256,512]{1,0:T(8,128)(2,1)} %bitcast.152), channel_id=1, source_target_pairs={{0,8},{8,0},{1,9},{9,1},{2,10},{10,2},{3,11},{11,3},{4,12},{12,4},... | collective-permute-start | bytes 786440 | tf_op jit(solution)/shard_map/ppermute | solution.py:48
  404.9 6.6 %collective-permute-start.23 = (bf16[256,512]{1,0:T(8,128)(2,1)}, bf16[256,512]{1,0:T(8,128)(2,1)S(1)}, u32[]{:S(2)}, u32[]{:S(2)}) collective-permute-start(bf16[256,512]{1,0:T(8,128)(2,1)} %bitcast.154), channel_id=1, source_target_pairs={{0,8},{8,0},{1,9},{9,1},{2,10},{10,2},{3,11},{11,3},{4,12},{12,4},... | collective-permute-start | bytes 786440 | tf_op jit(solution)/shard_map/ppermute | solution.py:48
  407.2 7.4 %copy-start.26 = (f32[64]{0:T(128)}, f32[64]{0:T(128)S(1)}, u32[]{:S(2)}) copy-start(f32[64]{0:T(128)S(1)} %get-tuple-element.173) | copy-start | bytes 772
  (19 other events, 29.1 us)
Sparse Core Ops, SparseCore 0:
  9.6 90.3 all-gather.4
  101.9 54.8 all-gather.6

commit v6 on v5

--- a/solution.py
+++ b/solution.py
@@ -773,6 +773,72 @@
     return shards, riders
 
 
+def side_sums_kernel(index_ref, arrived_ref, keep_ref, send_ref):
+    for out_ref, side in ((keep_ref, index_ref[0]), (send_ref, 1 - index_ref[0])):
+        total = arrived_ref[0, 0, side].astype(jnp.float32)
+        for n in range(1, arrived_ref.shape[0]):
+            total = total + arrived_ref[n, 0, side].astype(jnp.float32)
+        out_ref[0] = total.astype(out_ref.dtype)
+
+
+def unpack_sides_kernel(turned, index_ref, keep_ref, other_ref, *outs):
+    def write(total):
+        start = 0
+        for flip, out_ref in zip(turned, outs):
+            height = out_ref.shape[0] if flip else out_ref.shape[1]
+            part = total[start : start + height]
+            out_ref[...] = part if flip else part.T
+            start += height
+
+    @pl.when(pl.program_id(1) == 0)
+    def _():
+        write(keep_ref[0])
+
+    @pl.when(pl.program_id(1) == 1)
+    def _():
+        write(other_ref[0].astype(jnp.float32))
+
+
+def scatter_along_line(grad, heights, turned, after=(), late_after=()):
+    sequences, side = lax.axis_size("s"), lax.axis_index("h")
+    wide, height, rows = grad.shape
+    arrived = lax.all_to_all(grad.reshape(wide // 2, 2 * height, rows), LINE, 0, 0)
+    band_of = pl.BlockSpec((1, height, rows), lambda j, p: (j, 0, 0))
+    keep, send = prefetch_call(
+        side_sums_kernel,
+        "side_sums",
+        side,
+        (2,),
+        [pl.BlockSpec((sequences, 1, 2, height, rows), lambda j, p: (0, j, 0, 0, 0))],
+        [band_of, band_of],
+        [struct((2, height, rows), jnp.float32), struct((2, height, rows), jnp.bfloat16)],
+        after=after,
+    )(arrived.reshape(sequences, 2, 2, height, rows))
+    other = shifted(send, "h", 1)
+    riders = keep[:, sum(heights) :] + other[:, sum(heights) :].astype(jnp.float32)
+    specs, shapes = [], []
+    block = lambda j, n, p: 2 * j + p[0] + n - 2 * n * p[0]
+    for flip, part in zip(turned, heights):
+        if flip:
+            specs.append(pl.BlockSpec((part, rows), lambda j, n, p: (block(j, n, p), 0)))
+            shapes.append(struct((4 * part, rows), jnp.float32))
+        else:
+            specs.append(pl.BlockSpec((rows, part), lambda j, n, p: (0, block(j, n, p))))
+            shapes.append(struct((rows, 4 * part), jnp.float32))
+    part_of = pl.BlockSpec((1, sum(heights), rows), lambda j, n, p: (j, 0, 0))
+    shards = prefetch_call(
+        partial(unpack_sides_kernel, turned),
+        "unpack",
+        side,
+        (2, 2),
+        [part_of, part_of],
+        specs,
+        shapes,
+        after=late_after,
+    )(keep, other)
+    return shards, riders
+
+
 def fold_kernel(index_ref, mine_keep, mine_send, arrived_keep, arrived_send, keep_ref, send_ref):
     keep_ref[...] = mine_keep[...] + arrived_keep[...]
     send_ref[...] = mine_send[...] + arrived_send[...]
@@ -944,8 +1010,7 @@
     down_blocks = spread_sides(down_sides, after=[normed])
     down_arrived = exchanged_along_line(down_blocks)
     down_weight = Weight(down_arrived, weight_rows, 0, hidden)
-    down_other = Weight(from_other_core(down_arrived), weight_rows, 0, hidden)
-    qkv = project_heads(normed, qkv_bias, qkv_weight)
+    qkv = project_heads(normed, qkv_bias, qkv_weight, after=[head_other])
     attended, log_sums = attention(qkv)
     grad_down = weight_grad([(up_low, cot)], wide, after=[attended])
     attended_grad, up_grad, up_sums = back_through(
@@ -955,10 +1020,12 @@
     qkv_grad_other = shifted(qkv_grad, "c", 1)
 
     grad_up = weight_grad([(up_grad, normed)], wide, after=[qkv_grad])
+    up_grad_other = shifted(up_grad, "c", 1)
+    grad_up = lax.optimization_barrier((grad_up, qkv_grad_other, up_grad_other))[0]
     normed_grad = partial_sum(
         [
             (qkv_grad, qkv_grad_other, qkv_weight, qkv_other),
-            (up_grad, shifted(up_grad, "c", 1), up_weight, up_other),
+            (up_grad, up_grad_other, up_weight, up_other),
         ],
         row_count,
         feature_count,
@@ -967,6 +1034,8 @@
         after=[grad_up],
     )
 
+    down_other = lax.optimization_barrier((down_arrived, normed_grad[0]))[0]
+    down_other = Weight(from_other_core(down_other), weight_rows, 0, hidden)
     branch = partial_sum(
         [
             (attended, shifted(attended, "c", 1), dense_weight, dense_other),
@@ -1002,13 +1071,16 @@
     first = [normed_grad[:2], normed_grad[2:]]
     second = [branch[:2], branch[2:]]
 
-    def fold(part, arrived, axes, after):
-        return folded(part[0], shifted(part[1], arrived, 1), axes, axes[-1], after=[after])
+    def fold(part, arrived, axes, after, axis=None):
+        other = shifted(part[1], arrived, 1)
+        return folded(part[0], other, axes, axis or axes[-1], after=[after])
 
     first[0] = fold(first[0], "m", "gh", grad_heads)
     (grad_down,), _ = scatter_columns(grad_down, [hidden], [True], after=first[0][:1])
     first[1] = fold(first[1], "h", "gm", grad_down)
     second[0] = fold(second[0], "m", "gh", first[1][0])
+    later = lax.optimization_barrier((branch[3], first[1][0]))[0]
+    second[1] = [branch[2], later]
     first[0] = fold(first[0], "h", "g", second[0][0])
     first[1] = fold(first[1], "m", "g", first[0][0])
     (grad_up,), _ = scatter_columns(grad_up, [hidden], [False], after=first[1][:1])
@@ -1034,17 +1106,21 @@
     own_terms = [term.reshape(wide, -1) for term in own_terms]
     late = summed(jnp.concatenate(own_terms, axis=1), "h")
     late = summed(summed(late, "g"), "s")
-    second[1] = fold(second[1], "m", "gh", standard_grad)
+    second[1] = fold(second[1], "m", "gh", standard_grad, "g")
     second[0] = fold(second[0], "h", "g", second[1][0])
-    second[1] = fold(second[1], "h", "g", second[0][0])
-    (grad_query, grad_key, grad_value, grad_dense), riders = scatter_columns(
-        grad_heads, [lanes] * 4, [False, False, False, True], after=second[1][:1]
+    second[1] = fold(second[1], "g", "h", second[0][0])
+    (grad_query, grad_key, grad_value, grad_dense), riders = scatter_along_line(
+        grad_heads,
+        [lanes] * 4,
+        [False, False, False, True],
+        after=[standard_grad],
+        late_after=second[1][:1],
     )
     early = jnp.sum(riders.astype(jnp.float32), axis=0).reshape(-1)[:early_count]
     output = finished(
         tokens,
         [part[0][0] for part in second],
-        [shifted(part[1][0], "g", 1) for part in second],
+        [shifted(part[1][0], axis, 1) for part, axis in zip(second, "gh")],
         out_bias.reshape(1, -1),
         after=[grad_dense],
     )

time: 424 us -> 414 us (0.976)
  waiting for transfers between devices: 141 us -> 125 us
    ppermute x29 -> x30, waiting for transfers between devices: 85.8 us -> 71.5 us  [shifted(): lax.ppermute(value, axis, [(source, (source + step) % count) for source i...]
    pallas_call x13 -> x15, Pallas kernels: 29.9 us -> 36 us  [prefetch_call(): run(index.astype(jnp.int32).reshape(1), *after, *operands)]
    all_to_all x3 -> x2, starting transfers between devices: 14.2 us -> 9.54 us  [scatter_columns(): arrived = lax.all_to_all(grad, WIDE, 0, 0)]
    ppermute x29 -> x30, starting transfers between devices: 24.6 us -> 29.2 us  [shifted(): lax.ppermute(value, axis, [(source, (source + step) % count) for source i...]
    pallas_call x15 -> x14, Pallas kernels: 145 us -> 141 us  [call(): return lambda *operands: run(*after, *operands)]
    unnamed x64 -> x66, local copies, waits for them, and re-layouts: 12.4 us -> 13.1 us
  transfers between devices with their start and end apart: 37 -> 38, of which waited for: 19 -> 18; matrix products, arithmetic and copies ran while one was open for 6% -> 6% of each run, Pallas kernels for 41% -> 42%
where the time goes in v6:
time: 414 us; the launch traced here: 412 us
  Pallas kernels  177 us (43%)
  waiting for transfers between devices  125 us (30%)
  starting transfers between devices  58.4 us (14%)
  local copies, waits for them, and re-layouts  30.4 us (7%)
  between operations  14.4 us (3%)
  other arithmetic  7.22 us (2%)
    pallas_call x14, Pallas kernels, call(): return lambda *operands: run(*after, *operands)  141 us
    ppermute x30, waiting for transfers between devices, shifted(): lax.ppermute(value, axis, [(source, (source + step) % count) for source i...  71.5 us
    pallas_call x15, Pallas kernels, prefetch_call(): run(index.astype(jnp.int32).reshape(1), *after, *operands)  36 us
    ppermute x30, starting transfers between devices, shifted(): lax.ppermute(value, axis, [(source, (source + step) % count) for source i...  29.2 us
    all_to_all x1, waiting for transfers between devices, exchanged(): return lax.all_to_all(blocks, WIDE, 0, 0)  24.5 us
    all_to_all x2, waiting for transfers between devices, exchanged_along_line(): lax.all_to_all(blocks, LINE, 0, 0).reshape(2 * count, rows // 2, width)  24.2 us
    unnamed x66, local copies, waits for them, and re-layouts  13.1 us
    all_to_all x2, starting transfers between devices, scatter_columns(): arrived = lax.all_to_all(grad, WIDE, 0, 0)  9.54 us
  transfers between devices with their start and end apart: 38, of which 18 were waited for; matrix products, arithmetic and copies ran while one was open for 6% of the time, Pallas kernels for 42%

profile of v6, /device:TPU:0, one launch (start us, length us, event | category | flops | bytes accessed | tf_op | source)
XLA Modules:
  0.0 412.0 jit_solution(11477238074500698016)
XLA Ops:
  8.0 3.1 collective-permute-start
  11.1 5.4 %concatenate.16 = bf16[704]{0:T(1024)(128)(2,1)S(1)} concatenate(bf16[64]{0:T(256)(128)(2,1)} %param.22, bf16[64]{0:T(256)(128)(2,1)} %param.23, bf16[64]{0:T(256)(128)(2,1)} %param.25, bf16[64]{0:T(256)(128)(2,1)} %param.27, bf16[64]{0:T(256)(128)(2,1)} %param.29, bf16[64]{0:T(256)(128)(2,1)} %param.31, bf16[64]{0:T(256)(128)(2,1)} %param.35, bf16[256]{0:T(256)(128)(2,1)} %param.33), dimensions={0} | concatenate | bytes 2816 | tf_op jit(solution)/shard_map/concatenate | solution.py:962
  17.1 3.6 pack.3
  20.7 2.2 pack.5
  22.9 2.2 pack.4
  25.1 2.2 collective-permute-done.refs_4_
  28.1 2.1 join.1
  30.2 6.8 %all-to-all-start = ((bf16[8,272,512]{2,1,0:T(8,128)(2,1)}), bf16[8,272,512]{2,1,0:T(8,128)(2,1)S(1)}, u32[]{:S(2)}, u32[]{:S(2)}) async-start(bf16[8,272,512]{2,1,0:T(8,128)(2,1)} %bitcast.108), calls=%async_computation | async-start | bytes 4456448 | tf_op jit(solution)/shard_map/all_to_all | solution.py:672
  39.0 29.4 %collective-permute-done.1.refs_2_ = bf16[2,256,512]{2,1,0:T(8,128)(2,1)S(1)} collective-permute-done((bf16[2,256,512]{2,1,0:T(8,128)(2,1)S(1)}, bf16[2,256,512]{2,1,0:T(8,128)(2,1)S(1)}, u32[]{:S(2)}, u32[]{:S(2)}) %collective-permute-start.1) | collective-permute-done | bytes 524320 | tf_op jit(solution)/shard_map/ppermute | solution.py:48
  68.4 24.5 %all-to-all-done.refs_0_.refs_5_.refs_7_ = bf16[8,272,512]{2,1,0:T(8,128)(2,1)S(1)} async-done(((bf16[8,272,512]{2,1,0:T(8,128)(2,1)}), bf16[8,272,512]{2,1,0:T(8,128)(2,1)S(1)}, u32[]{:S(2)}, u32[]{:S(2)}) %all-to-all-start) | async-done | bytes 2228256 | tf_op jit(solution)/shard_map/all_to_all | solution.py:672
  94.2 2.4 spread.2
  96.7 4.6 %all-to-all-start.1 = ((bf16[4,512,512]{2,1,0:T(8,128)(2,1)}), bf16[4,512,512]{2,1,0:T(8,128)(2,1)S(1)}, u32[]{:S(2)}, u32[]{:S(2)}) async-start(bf16[4,512,512]{2,1,0:T(8,128)(2,1)} %bitcast.116), calls=%async_computation.1 | async-start | bytes 4194304 | tf_op jit(solution)/shard_map/all_to_all | solution.py:734
  101.2 3.4 collective-permute-start.6
  110.5 3.1 collective-permute-done.5
  116.0 14.3 %norm_up.1 = (bf16[2048,2048]{1,0:T(8,128)(2,1)}, f32[2048,128]{1,0:T(8,128)}, bf16[2048,512]{1,0:T(8,128)(2,1)}, f32[2048,512]{1,0:T(8,128)}) custom-call(bf16[2,2,256,512]{3,2,1,0:T(8,128)(2,1)} %copy-done.10, bf16[4,4,512,512]{3,2,1,0:T(8,128)(2,1)} %bitcast.115, f32[1,2048]{1,0:T(1,128)} %reshape.248.refs_2_, f32[1,2048]{1,0:T(1,128)} %reshape.249.refs_3_, ...), custom_call_target="tpu_custom_call" | custom-call | flops 12884901 | tf_op jit(solution)/shard_map/norm_up/pallas_call | solution.py:74
  130.3 2.6 spread.3
  132.9 12.7 %all-to-all-done.1 = bf16[4,512,512]{2,1,0:T(8,128)(2,1)S(1)} async-done(((bf16[4,512,512]{2,1,0:T(8,128)(2,1)}), bf16[4,512,512]{2,1,0:T(8,128)(2,1)S(1)}, u32[]{:S(2)}, u32[]{:S(2)}) %all-to-all-start.1) | async-done | bytes 2097184 | tf_op jit(solution)/shard_map/all_to_all | solution.py:734
  145.6 4.5 %all-to-all-start.2 = ((bf16[4,512,512]{2,1,0:T(8,128)(2,1)}), bf16[4,512,512]{2,1,0:T(8,128)(2,1)}, u32[]{:S(2)}, u32[]{:S(2)}) async-start(bf16[4,512,512]{2,1,0:T(8,128)(2,1)} %bitcast.117), calls=%async_computation.2 | async-start | bytes 4194304 | tf_op jit(solution)/shard_map/all_to_all | solution.py:734
  153.9 9.4 %project_heads.1.refs_0_ = bf16[2048,384]{1,0:T(8,128)(2,1)} custom-call(bf16[2,2,256,512]{3,2,1,0:T(8,128)(2,1)} %copy-done.3, bf16[2048,2048]{1,0:T(8,128)(2,1)} %get-tuple-element.71.refs_1_.refs_0_.refs_2_.refs_3_, f32[1,384]{1,0:T(1,128)} %reshape.250.refs_2_, f32[2048,128]{1,0:T(8,128)} %constant.83.clone.refs_3_, f32[2048,128]{1,0:T(8,128)} %constant.84.clone.refs_4_, ...), custom_call_target="tpu_custom_call" | custom-call | flops 6442450 | tf_op jit(solution)/shard_map/project_heads/pallas_call | solution.py:74
  163.3 14.3 %attention.1 = (bf16[2048,128]{1,0:T(8,128)(2,1)}, f32[8,2048]{1,0:T(8,128)}) custom-call(bf16[2048,384]{1,0:T(8,128)(2,1)} %project_heads.1.refs_0_), custom_call_target="tpu_custom_call" | custom-call | flops 10000000 | tf_op jit(solution)/shard_map/attention/pallas_call | solution.py:74
  177.6 8.8 %weight_grad.3.refs_0_ = bf16[8,512,256]{2,1,0:T(8,128)(2,1)} custom-call(bf16[2048,128]{1,0:T(8,128)(2,1)} %get-tuple-element.72.refs_0_.refs_2_.refs_4_, bf16[2048,512]{1,0:T(8,128)(2,1)} %get-tuple-element.73.refs_1_.refs_3_, bf16[2,4,2,512,512]{4,3,2,1,0:T(8,128)(2,1)} %bitcast.98), custom_call_target="tpu_custom_call" | custom-call | flops 8589934 | tf_op jit(solution)/shard_map/weight_grad/pallas_call | solution.py:74
  186.4 11.5 %all-to-all-done.2 = bf16[4,512,512]{2,1,0:T(8,128)(2,1)} async-done(((bf16[4,512,512]{2,1,0:T(8,128)(2,1)}), bf16[4,512,512]{2,1,0:T(8,128)(2,1)}, u32[]{:S(2)}, u32[]{:S(2)}) %all-to-all-start.2) | async-done | bytes 2097184 | tf_op jit(solution)/shard_map/all_to_all | solution.py:734
  197.9 5.2 %all-to-all-start.3 = ((bf16[8,512,256]{2,1,0:T(8,128)(2,1)}), bf16[8,512,256]{2,1,0:T(8,128)(2,1)}, u32[]{:S(2)}, u32[]{:S(2)}) async-start(bf16[8,512,256]{2,1,0:T(8,128)(2,1)} %weight_grad.3.refs_0_), calls=%async_computation.3 | async-start | bytes 4194304 | tf_op jit(solution)/shard_map/all_to_all | solution.py:752
  203.1 11.2 %back_through.1 = (bf16[2048,128]{1,0:T(8,128)(2,1)}, bf16[2048,512]{1,0:T(8,128)(2,1)}, f32[1,512]{1,0:T(1,128)}) custom-call(bf16[8,512,256]{2,1,0:T(8,128)(2,1)} %weight_grad.3.refs_0_, bf16[2,4,2,512,512]{4,3,2,1,0:T(8,128)(2,1)} %bitcast.99, f32[2048,512]{1,0:T(8,128)} %get-tuple-element.74.refs_2_, bf16[8,256,512]{2,1,0:T(8,128)(2,1)} %bitcast.103, ...), custom_call_target="tpu_custom_call" | custom-call | flops 10737418 | tf_op jit(solution)/shard_map/back_through/pallas_call | solution.py:74
  214.3 23.9 %attention_back.1 = (bf16[2048,384]{1,0:T(8,128)(2,1)}, f32[1,384]{1,0:T(1,128)}) custom-call(bf16[2048,384]{1,0:T(8,128)(2,1)} %project_heads.1.refs_0_, bf16[2048,128]{1,0:T(8,128)(2,1)} %get-tuple-element.76.refs_1_, f32[8,2048]{1,0:T(8,128)} %get-tuple-element.77.refs_2_, f32[2048,128]{1,0:T(8,128)} %constant.83.clone.refs_3_, ...), custom_call_target="tpu_custom_call" | custom-call | flops 20000000 | tf_op jit(solution)/shard_map/attention_back/pallas_call | solution.py:74
  238.7 8.8 %weight_grad.4.refs_0_ = bf16[8,512,256]{2,1,0:T(8,128)(2,1)} custom-call(bf16[2048,384]{1,0:T(8,128)(2,1)} %get-tuple-element.78.refs_0_.refs_2_, bf16[2048,512]{1,0:T(8,128)(2,1)} %get-tuple-element.79.refs_1_.refs_3_, bf16[2048,2048]{1,0:T(8,128)(2,1)} %get-tuple-element.71.refs_1_.refs_0_.refs_2_.refs_3_), custom_call_target="tpu_custom_call" | custom-call | flops 8589934 | tf_op jit(solution)/shard_map/weight_grad/pallas_call | solution.py:74
  247.5 2.4 all-to-all-done.3
  250.0 4.3 %all-to-all-start.4 = ((bf16[8,512,256]{2,1,0:T(8,128)(2,1)}), bf16[8,512,256]{2,1,0:T(8,128)(2,1)}, u32[]{:S(2)}, u32[]{:S(2)}) async-start(bf16[8,512,256]{2,1,0:T(8,128)(2,1)} %weight_grad.4.refs_0_), calls=%async_computation.4 | async-start | bytes 4194304 | tf_op jit(solution)/shard_map/all_to_all | solution.py:752
  255.0 15.0 %normed_gradient.1 = (bf16[4,256,512]{2,1,0:T(8,128)(2,1)}, bf16[4,256,512]{2,1,0:T(8,128)(2,1)}, bf16[2,2,256,512]{3,2,1,0:T(8,128)(2,1)}, bf16[2,2,256,512]{3,2,1,0:T(8,128)(2,1)}) custom-call(bf16[8,512,256]{2,1,0:T(8,128)(2,1)} %weight_grad.4.refs_0_, s32[3]{0:T(128)} %pad_add_fusion.refs_1_, bf16[2048,384]{1,0:T(8,128)(2,1)} %get-tuple-element.78.refs_0_.refs_2_, ...), custom_call_target="tpu_custom_call" | custom-call | flops 15032385 | tf_op jit(solution)/shard_map/normed_gradient/pallas_call | solution.py:74
  277.4 10.9 %branch_sum.1 = (bf16[4,256,512]{2,1,0:T(8,128)(2,1)}, bf16[4,256,512]{2,1,0:T(8,128)(2,1)}, bf16[4,256,512]{2,1,0:T(8,128)(2,1)}, bf16[4,256,512]{2,1,0:T(8,128)(2,1)}) custom-call(bf16[4,256,512]{2,1,0:T(8,128)(2,1)} %get-tuple-element.81.refs_0_, s32[3]{0:T(128)} %pad_add_fusion.refs_1_, bf16[2048,128]{1,0:T(8,128)(2,1)} %get-tuple-element.72.refs_0_.refs_2_.refs_4_, ...), custom_call_target="tpu_custom_call" | custom-call | flops 10737418 | tf_op jit(solution)/shard_map/branch_sum/pallas_call | solution.py:74
  290.7 10.2 %weight_grad.5.refs_0_ = bf16[8,528,256]{2,1,0:T(8,128)(2,1)} custom-call(bf16[4,256,512]{2,1,0:T(8,128)(2,1)} %get-tuple-element.83.refs_0_, bf16[8,16,256]{2,1,0:T(8,128)(2,1)} %bitcast.138, bf16[2048,384]{1,0:T(8,128)(2,1)} %get-tuple-element.78.refs_0_.refs_2_, bf16[2048,2048]{1,0:T(8,128)(2,1)} %get-tuple-element.71.refs_1_.refs_0_.refs_2_.refs_3_, ...), custom_call_target="tpu_custom_call" | custom-call | flops 8858370 | tf_op jit(solution)/shard_map/weight_grad/pallas_call | solution.py:74
  302.3 3.8 all-to-all-start.5
  306.1 2.5 fold.8
  310.1 3.8 unpack.3.refs_0_
  314.0 2.5 fold.9
  317.4 3.4 collective-permute-done.14
  320.8 2.5 fold.10
  326.1 5.3 %collective-permute-done.17 = bf16[2,256,512]{2,1,0:T(8,128)(2,1)S(1)} collective-permute-done((bf16[2,256,512]{2,1,0:T(8,128)(2,1)}, bf16[2,256,512]{2,1,0:T(8,128)(2,1)S(1)}, u32[]{:S(2)}, u32[]{:S(2)}) %collective-permute-start.17) | collective-permute-done | bytes 524320 | tf_op jit(solution)/shard_map/ppermute | solution.py:48
  339.6 4.2 %unpack.4 = f32[256,2048]{1,0:T(8,128)} custom-call(bf16[1,256,512]{2,1,0:T(8,128)(2,1)} %get-tuple-element.97.refs_0_, bf16[2,4,512,256]{3,2,1,0:T(8,128)(2,1)} %bitcast.36.refs_1_), custom_call_target="tpu_custom_call" | custom-call | tf_op jit(solution)/shard_map/unpack/pallas_call | solution.py:74
  343.8 4.2 %collective-permute-done.18 = bf16[256,512]{1,0:T(8,128)(2,1)S(1)} collective-permute-done((bf16[256,512]{1,0:T(8,128)(2,1)}, bf16[256,512]{1,0:T(8,128)(2,1)S(1)}, u32[]{:S(2)}, u32[]{:S(2)}) %collective-permute-start.18) | collective-permute-done | bytes 262176 | tf_op jit(solution)/shard_map/ppermute | solution.py:48
  348.0 10.7 %collective-permute-done.16 = bf16[256,512]{1,0:T(8,128)(2,1)} collective-permute-done((bf16[256,512]{1,0:T(8,128)(2,1)S(1)}, bf16[256,512]{1,0:T(8,128)(2,1)}, u32[]{:S(2)}, u32[]{:S(2)}) %collective-permute-start.16) | collective-permute-done | bytes 262176 | tf_op jit(solution)/shard_map/ppermute | solution.py:48
  367.0 2.9 multiply_add_fusion
  369.9 2.4 fold.13
  372.5 3.8 collective-permute-start.29
  377.6 2.5 side_sums.1
  389.8 5.8 %collective-permute-done.22.refs_2_ = bf16[2,528,256]{2,1,0:T(8,128)(2,1)S(1)} collective-permute-done((bf16[2,528,256]{2,1,0:T(8,128)(2,1)}, bf16[2,528,256]{2,1,0:T(8,128)(2,1)S(1)}, u32[]{:S(2)}, u32[]{:S(2)}) %collective-permute-start.22) | collective-permute-done | bytes 540704 | tf_op jit(solution)/shard_map/ppermute | solution.py:48
  397.5 4.0 unpack.5
  402.3 2.4 finish.1
  (196 shorter events, 66.0 us)
Async XLA Ops:
  7.2 107.8 %all-gather.5.cloned.1.call-start = ((), (), s32[]{:S(2)}) async-start(), calls=%async_computation.6 | async-start | bytes 8912896 | tf_op jit(solution)/shard_map/all_gather | solution.py:965
  7.9 169.7 %all-gather.7.cloned.1.call-start = ((), (), s32[]{:S(2)}) async-start(), calls=%async_computation.7 | async-start | bytes 9437184 | tf_op jit(solution)/shard_map/all_gather | solution.py:974
  8.0 19.3 %collective-permute-start = (bf16[512,512]{1,0:T(8,128)(2,1)}, bf16[512,512]{1,0:T(8,128)(2,1)S(1)}, u32[]{:S(2)}, u32[]{:S(2)}) collective-permute-start(bf16[512,512]{1,0:T(8,128)(2,1)} %refs_3_.5), channel_id=1, source_target_pairs={{0,8},{8,0},{1,9},{9,1},{2,10},{10,2},{3,11},{11,3},{4,12},{12,4},... | collective-permute-start | bytes 1572872 | tf_op jit(solution)/shard_map/ppermute | solution.py:48
  30.2 62.7 %all-to-all-start = ((bf16[8,272,512]{2,1,0:T(8,128)(2,1)}), bf16[8,272,512]{2,1,0:T(8,128)(2,1)S(1)}, u32[]{:S(2)}, u32[]{:S(2)}) async-start(bf16[8,272,512]{2,1,0:T(8,128)(2,1)} %bitcast.108), calls=%async_computation | async-start | bytes 4456448 | tf_op jit(solution)/shard_map/all_to_all | solution.py:672
  37.0 31.4 %collective-permute-start.1 = (bf16[2,256,512]{2,1,0:T(8,128)(2,1)S(1)}, bf16[2,256,512]{2,1,0:T(8,128)(2,1)S(1)}, u32[]{:S(2)}, u32[]{:S(2)}) collective-permute-start(bf16[2,256,512]{2,1,0:T(8,128)(2,1)S(1)} %copy-done.28), channel_id=1, source_target_pairs={{0,4},{4,0},{1,5},{5,1},{2,6},{6,2},{3,7},{7,3},{8,12},{12,8},{9,1... | collective-permute-start | bytes 1572872 | tf_op jit(solution)/shard_map/ppermute | solution.py:48
  68.4 24.5 %copy-start.21 = (bf16[2,256,512]{2,1,0:T(8,128)(2,1)}, bf16[2,256,512]{2,1,0:T(8,128)(2,1)S(1)}, u32[]{:S(2)}) copy-start(bf16[2,256,512]{2,1,0:T(8,128)(2,1)S(1)} %collective-permute-done.1.refs_2_) | copy-start | bytes 1572868
  96.7 48.9 %all-to-all-start.1 = ((bf16[4,512,512]{2,1,0:T(8,128)(2,1)}), bf16[4,512,512]{2,1,0:T(8,128)(2,1)S(1)}, u32[]{:S(2)}, u32[]{:S(2)}) async-start(bf16[4,512,512]{2,1,0:T(8,128)(2,1)} %bitcast.116), calls=%async_computation.1 | async-start | bytes 4194304 | tf_op jit(solution)/shard_map/all_to_all | solution.py:734
  101.2 29.1 %collective-permute-start.6 = (bf16[2,256,512]{2,1,0:T(8,128)(2,1)}, bf16[2,256,512]{2,1,0:T(8,128)(2,1)}, u32[]{:S(2)}, u32[]{:S(2)}) collective-permute-start(bf16[2,256,512]{2,1,0:T(8,128)(2,1)} %get-tuple-element.75), channel_id=1, source_target_pairs={{0,4},{4,0},{1,5},{5,1},{2,6},{6,2},{3,7},{7,3},{8,12},{12,8},{9,1... | collective-permute-start | bytes 1572872 | tf_op jit(solution)/shard_map/ppermute | solution.py:48
  107.2 7.8 %collective-permute-start.3 = (bf16[2,2,256,512]{3,2,1,0:T(8,128)(2,1)}, bf16[2,2,256,512]{3,2,1,0:T(8,128)(2,1)S(1)}, u32[]{:S(2)}, u32[]{:S(2)}) collective-permute-start(bf16[2,2,256,512]{3,2,1,0:T(8,128)(2,1)} %dynamic-slice_bitcast_fusion.1), channel_id=1, source_target_pairs={{0,1},{1,0},{2,3},{3,2},{4,5},{5,4},{6,7},{7,6},{8,9},{9,8},{10,11... | collective-permute-start | bytes 3145736 | tf_op jit(solution)/shard_map/ppermute | solution.py:48
  107.3 42.9 %copy-start.24 = (bf16[1,8,16,512]{3,1,2,0:T(8,128)(2,1)}, bf16[1,8,16,512]{3,1,2,0:T(8,128)(2,1)S(1)}, u32[]{:S(2)}) copy-start(bf16[1,8,16,512]{3,1,2,0:T(8,128)(2,1)S(1)} %copy.46) | copy-start | bytes 393220
  107.4 2.5 collective-permute-start.4
  109.9 3.7 collective-permute-start.5
  145.6 52.2 %all-to-all-start.2 = ((bf16[4,512,512]{2,1,0:T(8,128)(2,1)}), bf16[4,512,512]{2,1,0:T(8,128)(2,1)}, u32[]{:S(2)}, u32[]{:S(2)}) async-start(bf16[4,512,512]{2,1,0:T(8,128)(2,1)} %bitcast.117), calls=%async_computation.2 | async-start | bytes 4194304 | tf_op jit(solution)/shard_map/all_to_all | solution.py:734
  150.2 2.7 collective-permute-start.2
  197.9 52.1 %all-to-all-start.3 = ((bf16[8,512,256]{2,1,0:T(8,128)(2,1)}), bf16[8,512,256]{2,1,0:T(8,128)(2,1)}, u32[]{:S(2)}, u32[]{:S(2)}) async-start(bf16[8,512,256]{2,1,0:T(8,128)(2,1)} %weight_grad.3.refs_0_), calls=%async_computation.3 | async-start | bytes 4194304 | tf_op jit(solution)/shard_map/all_to_all | solution.py:752
  214.3 33.2 %collective-permute-start.8 = (bf16[2048,512]{1,0:T(8,128)(2,1)}, bf16[2048,512]{1,0:T(8,128)(2,1)}, u32[]{:S(2)}, u32[]{:S(2)}) collective-permute-start(bf16[2048,512]{1,0:T(8,128)(2,1)} %get-tuple-element.79.refs_1_.refs_3_), channel_id=1, source_target_pairs={{0,1},{1,0},{2,3},{3,2},{4,5},{5,4},{6,7},{7,6},{8,9},{9,8},{10,11... | collective-permute-start | bytes 6291464 | tf_op jit(solution)/shard_map/ppermute | solution.py:48
  238.3 9.2 %collective-permute-start.7 = (bf16[2048,384]{1,0:T(8,128)(2,1)}, bf16[2048,384]{1,0:T(8,128)(2,1)}, u32[]{:S(2)}, u32[]{:S(2)}) collective-permute-start(bf16[2048,384]{1,0:T(8,128)(2,1)} %get-tuple-element.78.refs_0_.refs_2_), channel_id=1, source_target_pairs={{0,1},{1,0},{2,3},{3,2},{4,5},{5,4},{6,7},{7,6},{8,9},{9,8},{10,11... | collective-permute-start | bytes 4718600 | tf_op jit(solution)/shard_map/ppermute | solution.py:48
  250.0 52.3 %all-to-all-start.4 = ((bf16[8,512,256]{2,1,0:T(8,128)(2,1)}), bf16[8,512,256]{2,1,0:T(8,128)(2,1)}, u32[]{:S(2)}, u32[]{:S(2)}) async-start(bf16[8,512,256]{2,1,0:T(8,128)(2,1)} %weight_grad.4.refs_0_), calls=%async_computation.4 | async-start | bytes 4194304 | tf_op jit(solution)/shard_map/all_to_all | solution.py:752
  254.3 20.6 %collective-permute-start.10 = (bf16[2048,512]{1,0:T(8,128)(2,1)S(1)}, bf16[2048,512]{1,0:T(8,128)(2,1)S(1)}, u32[]{:S(2)}, u32[]{:S(2)}) collective-permute-start(bf16[2048,512]{1,0:T(8,128)(2,1)S(1)} %copy-done.5), channel_id=1, source_target_pairs={{0,1},{1,0},{2,3},{3,2},{4,5},{5,4},{6,7},{7,6},{8,9},{9,8},{10,11... | collective-permute-start | bytes 6291464 | tf_op jit(solution)/shard_map/ppermute | solution.py:48
  271.4 3.6 collective-permute-start.11
  271.9 3.0 collective-permute-start.9
  272.0 34.1 %collective-permute-start.12 = (bf16[4,256,512]{2,1,0:T(8,128)(2,1)}, bf16[4,256,512]{2,1,0:T(8,128)(2,1)}, u32[]{:S(2)}, u32[]{:S(2)}) collective-permute-start(bf16[4,256,512]{2,1,0:T(8,128)(2,1)} %get-tuple-element.86), channel_id=1, source_target_pairs={{0,2},{2,0},{1,3},{3,1},{4,6},{6,4},{5,7},{7,5},{8,10},{10,8},{9,1... | collective-permute-start | bytes 3145736 | tf_op jit(solution)/shard_map/ppermute | solution.py:48
  272.4 16.9 %copy-start.9 = (bf16[512,512]{1,0:T(8,128)(2,1)S(1)}, bf16[512,512]{1,0:T(8,128)(2,1)}, u32[]{:S(2)}) copy-start(bf16[512,512]{1,0:T(8,128)(2,1)} %refs_3_.5) | copy-start | bytes 1572868
  272.4 17.1 %copy-start.26 = (f32[1,384]{1,0:T(1,128)S(1)}, f32[1,384]{1,0:T(1,128)}, u32[]{:S(2)}) copy-start(f32[1,384]{1,0:T(1,128)} %get-tuple-element.84) | copy-start | bytes 4612
  272.4 17.5 %copy-start.25 = (f32[1,512]{1,0:T(1,128)S(1)}, f32[1,512]{1,0:T(1,128)}, u32[]{:S(2)}) copy-start(f32[1,512]{1,0:T(1,128)} %get-tuple-element.85) | copy-start | bytes 6148
  272.4 41.6 %collective-permute-start.13 = (bf16[2,2,256,512]{3,2,1,0:T(8,128)(2,1)}, bf16[2,2,256,512]{3,2,1,0:T(8,128)(2,1)}, u32[]{:S(2)}, u32[]{:S(2)}) collective-permute-start(bf16[2,2,256,512]{3,2,1,0:T(8,128)(2,1)} %get-tuple-element.89), channel_id=1, source_target_pairs={{0,4},{4,0},{1,5},{5,1},{2,6},{6,2},{3,7},{7,3},{8,12},{12,8},{9,1... | collective-permute-start | bytes 3145736 | tf_op jit(solution)/shard_map/ppermute | solution.py:48
  288.3 32.5 %collective-permute-start.14 = (bf16[4,256,512]{2,1,0:T(8,128)(2,1)}, bf16[4,256,512]{2,1,0:T(8,128)(2,1)}, u32[]{:S(2)}, u32[]{:S(2)}) collective-permute-start(bf16[4,256,512]{2,1,0:T(8,128)(2,1)} %get-tuple-element.91), channel_id=1, source_target_pairs={{0,2},{2,0},{1,3},{3,1},{4,6},{6,4},{5,7},{7,5},{8,10},{10,8},{9,1... | collective-permute-start | bytes 3145736 | tf_op jit(solution)/shard_map/ppermute | solution.py:48
  302.3 74.0 %all-to-all-start.5 = ((bf16[4,1056,256]{2,1,0:T(8,128)(2,1)}), bf16[4,1056,256]{2,1,0:T(8,128)(2,1)S(1)}, u32[]{:S(2)}, u32[]{:S(2)}) async-start(bf16[4,1056,256]{2,1,0:T(8,128)(2,1)} %bitcast.109), calls=%async_computation.5 | async-start | bytes 4325376 | tf_op jit(solution)/shard_map/all_to_all | solution.py:805
  308.7 14.6 %collective-permute-start.15 = (bf16[2,256,512]{2,1,0:T(8,128)(2,1)}, bf16[2,256,512]{2,1,0:T(8,128)(2,1)S(1)}, u32[]{:S(2)}, u32[]{:S(2)}) collective-permute-start(bf16[2,256,512]{2,1,0:T(8,128)(2,1)} %get-tuple-element.93), channel_id=1, source_target_pairs={{0,4},{4,0},{1,5},{5,1},{2,6},{6,2},{3,7},{7,3},{8,12},{12,8},{9,1... | collective-permute-start | bytes 1572872 | tf_op jit(solution)/shard_map/ppermute | solution.py:48
  316.5 14.9 %collective-permute-start.17 = (bf16[2,256,512]{2,1,0:T(8,128)(2,1)}, bf16[2,256,512]{2,1,0:T(8,128)(2,1)S(1)}, u32[]{:S(2)}, u32[]{:S(2)}) collective-permute-start(bf16[2,256,512]{2,1,0:T(8,128)(2,1)} %get-tuple-element.96), channel_id=1, source_target_pairs={{0,2},{2,0},{1,3},{3,1},{4,6},{6,4},{5,7},{7,5},{8,10},{10,8},{9,1... | collective-permute-start | bytes 1572872 | tf_op jit(solution)/shard_map/ppermute | solution.py:48
  326.1 10.0 %copy-start.29 = (bf16[1,256,512]{2,1,0:T(8,128)(2,1)S(1)}, bf16[1,256,512]{2,1,0:T(8,128)(2,1)}, u32[]{:S(2)}) copy-start(bf16[1,256,512]{2,1,0:T(8,128)(2,1)} %get-tuple-element.95) | copy-start | bytes 786436
  334.2 13.7 %collective-permute-start.18 = (bf16[256,512]{1,0:T(8,128)(2,1)}, bf16[256,512]{1,0:T(8,128)(2,1)S(1)}, u32[]{:S(2)}, u32[]{:S(2)}) collective-permute-start(bf16[256,512]{1,0:T(8,128)(2,1)} %bitcast.165), channel_id=1, source_target_pairs={{0,8},{8,0},{1,9},{9,1},{2,10},{10,2},{3,11},{11,3},{4,12},{12,4},... | collective-permute-start | bytes 786440 | tf_op jit(solution)/shard_map/ppermute | solution.py:48
  336.0 22.6 %collective-permute-start.16 = (bf16[256,512]{1,0:T(8,128)(2,1)S(1)}, bf16[256,512]{1,0:T(8,128)(2,1)}, u32[]{:S(2)}, u32[]{:S(2)}) collective-permute-start(bf16[256,512]{1,0:T(8,128)(2,1)S(1)} %bitcast.163), channel_id=1, source_target_pairs={{0,8},{8,0},{1,9},{9,1},{2,10},{10,2},{3,11},{11,3},{4,12},{12,4},... | collective-permute-start | bytes 786440 | tf_op jit(solution)/shard_map/ppermute | solution.py:48
  337.4 32.5 %collective-permute-start.19 = (bf16[4,256,512]{2,1,0:T(8,128)(2,1)}, bf16[4,256,512]{2,1,0:T(8,128)(2,1)}, u32[]{:S(2)}, u32[]{:S(2)}) collective-permute-start(bf16[4,256,512]{2,1,0:T(8,128)(2,1)} %get-tuple-element.103), channel_id=1, source_target_pairs={{0,2},{2,0},{1,3},{3,1},{4,6},{6,4},{5,7},{7,5},{8,10},{10,8},{9,1... | collective-permute-start | bytes 3145736 | tf_op jit(solution)/shard_map/ppermute | solution.py:48
  337.8 44.6 %collective-permute-start.20 = (bf16[2,256,512]{2,1,0:T(8,128)(2,1)}, bf16[2,256,512]{2,1,0:T(8,128)(2,1)}, u32[]{:S(2)}, u32[]{:S(2)}) collective-permute-start(bf16[2,256,512]{2,1,0:T(8,128)(2,1)} %get-tuple-element.105), channel_id=1, source_target_pairs={{0,4},{4,0},{1,5},{5,1},{2,6},{6,2},{3,7},{7,3},{8,12},{12,8},{9,1... | collective-permute-start | bytes 1572872 | tf_op jit(solution)/shard_map/ppermute | solution.py:48
  339.6 19.0 %copy-start.17 = (bf16[1,256,512]{2,1,0:T(8,128)(2,1)S(1)}, bf16[1,256,512]{2,1,0:T(8,128)(2,1)}, u32[]{:S(2)}) copy-start(bf16[1,256,512]{2,1,0:T(8,128)(2,1)} %get-tuple-element.97.refs_0_) | copy-start | bytes 786436
  339.6 19.1 %copy-start.16 = (bf16[1,256,512]{2,1,0:T(8,128)(2,1)S(1)}, bf16[1,256,512]{2,1,0:T(8,128)(2,1)}, u32[]{:S(2)}) copy-start(bf16[1,256,512]{2,1,0:T(8,128)(2,1)} %get-tuple-element.94.refs_0_) | copy-start | bytes 786436
  343.8 16.8 %copy-start.6 = (bf16[512,512]{1,0:T(8,128)(2,1)S(1)}, bf16[512,512]{1,0:T(8,128)(2,1)}, u32[]{:S(2)}) copy-start(bf16[512,512]{1,0:T(8,128)(2,1)} %refs_1_.7) | copy-start | bytes 1572868
  361.2 2.0 collective-permute-start.25
  361.5 3.6 collective-permute-start.27
  363.3 3.7 collective-permute-start.26
  365.2 7.3 %collective-permute-start.28 = (f32[8,128]{1,0:T(8,128)S(1)}, f32[8,128]{1,0:T(8,128)S(1)}, u32[]{:S(2)}, u32[]{:S(2)}) collective-permute-start(f32[8,128]{1,0:T(8,128)S(1)} %fusion.10), channel_id=1, source_target_pairs={{0,8},{8,0},{1,9},{9,1},{2,10},{10,2},{3,11},{11,3},{4,12},{12,4},... | collective-permute-start | bytes 12296 | tf_op jit(solution)/shard_map/ppermute | solution.py:48
  372.2 13.9 %collective-permute-start.21 = (bf16[2,256,512]{2,1,0:T(8,128)(2,1)}, bf16[2,256,512]{2,1,0:T(8,128)(2,1)S(1)}, u32[]{:S(2)}, u32[]{:S(2)}) collective-permute-start(bf16[2,256,512]{2,1,0:T(8,128)(2,1)} %bitcast.161), channel_id=1, source_target_pairs={{0,8},{8,0},{1,9},{9,1},{2,10},{10,2},{3,11},{11,3},{4,12},{12,4},... | collective-permute-start | bytes 1572872 | tf_op jit(solution)/shard_map/ppermute | solution.py:48
  372.5 13.0 %collective-permute-start.29 = (f32[8,128]{1,0:T(8,128)S(1)}, f32[8,128]{1,0:T(8,128)S(1)}, u32[]{:S(2)}, u32[]{:S(2)}) collective-permute-start(f32[8,128]{1,0:T(8,128)S(1)} %add.89), channel_id=1, source_target_pairs={{0,16},{16,0},{1,17},{17,1},{2,18},{18,2},{3,19},{19,3},{4,20},{20... | collective-permute-start | bytes 12296 | tf_op jit(solution)/shard_map/ppermute | solution.py:48
  380.2 15.4 %collective-permute-start.22 = (bf16[2,528,256]{2,1,0:T(8,128)(2,1)}, bf16[2,528,256]{2,1,0:T(8,128)(2,1)S(1)}, u32[]{:S(2)}, u32[]{:S(2)}) collective-permute-start(bf16[2,528,256]{2,1,0:T(8,128)(2,1)} %get-tuple-element.110), channel_id=1, source_target_pairs={{0,4},{4,0},{1,5},{5,1},{2,6},{6,2},{3,7},{7,3},{8,12},{12,8},{9,1... | collective-permute-start | bytes 1622024 | tf_op jit(solution)/shard_map/ppermute | solution.py:48
  384.5 17.1 %collective-permute-start.23 = (bf16[256,512]{1,0:T(8,128)(2,1)}, bf16[256,512]{1,0:T(8,128)(2,1)S(1)}, u32[]{:S(2)}, u32[]{:S(2)}) collective-permute-start(bf16[256,512]{1,0:T(8,128)(2,1)} %bitcast.162), channel_id=1, source_target_pairs={{0,8},{8,0},{1,9},{9,1},{2,10},{10,2},{3,11},{11,3},{4,12},{12,4},... | collective-permute-start | bytes 786440 | tf_op jit(solution)/shard_map/ppermute | solution.py:48
  389.0 12.5 %collective-permute-start.24 = (bf16[256,512]{1,0:T(8,128)(2,1)}, bf16[256,512]{1,0:T(8,128)(2,1)S(1)}, u32[]{:S(2)}, u32[]{:S(2)}) collective-permute-start(bf16[256,512]{1,0:T(8,128)(2,1)} %bitcast.164), channel_id=1, source_target_pairs={{0,4},{4,0},{1,5},{5,1},{2,6},{6,2},{3,7},{7,3},{8,12},{12,8},{9,1... | collective-permute-start | bytes 786440 | tf_op jit(solution)/shard_map/ppermute | solution.py:48
  397.5 7.2 %copy-start.27 = (f32[64]{0:T(128)}, f32[64]{0:T(128)S(1)}, u32[]{:S(2)}) copy-start(f32[64]{0:T(128)S(1)} %get-tuple-element.183) | copy-start | bytes 772
  (21 other events, 39.4 us)
Sparse Core Ops, SparseCore 0:
  9.6 90.3 all-gather.4
  101.9 54.8 all-gather.6

commit v7 on v6

--- a/solution.py
+++ b/solution.py
@@ -215,42 +215,55 @@
     )
 
 
-def back_kernel(
-    cot_ref, slope_ref, dense_ref, down_ref, attended_ref, up_ref, sums_ref
-):
+def cot_product(cot_ref, weight_ref):
+    width = cot_ref.shape[4]
+    total = 0.0
+    for j in range(4):
+        part = cot_ref[0, j, 0]
+        total = total + matmul(part, weight_rows_of(weight_ref, j * width, width))
+    return total
+
+
+def out_grad_kernel(cot_ref, weight_ref, out_ref):
+    out_ref[...] = cot_product(cot_ref, weight_ref).astype(jnp.bfloat16)
+
+
+def attended_gradient(cot, weight, width, rows=512, after=()):
+    total = 4 * cot.shape[3]
+    return call(
+        out_grad_kernel,
+        "attended_gradient",
+        (total // rows,),
+        [cot_spec(cot, rows), weight.spec],
+        band(rows, width),
+        struct((total, width), jnp.bfloat16),
+        flops=8 * total * D * width,
+        after=after,
+    )(cot, weight.array)
+
+
+def up_grad_kernel(cot_ref, slope_ref, weight_ref, up_ref, sums_ref):
     @pl.when(pl.program_id(0) == 0)
     def _():
         sums_ref[...] = jnp.zeros_like(sums_ref)
 
-    width = cot_ref.shape[4]
-    attended, up = 0.0, 0.0
-    for j in range(4):
-        part = cot_ref[0, j, 0]
-        attended = attended + matmul(part, weight_rows_of(dense_ref, j * width, width))
-        up = up + matmul(part, weight_rows_of(down_ref, j * width, width))
-    attended_ref[...] = attended.astype(jnp.bfloat16)
-    up = (up * slope_ref[...]).astype(jnp.bfloat16)
+    up = (cot_product(cot_ref, weight_ref) * slope_ref[...]).astype(jnp.bfloat16)
     up_ref[...] = up
     sums_ref[...] += jnp.sum(up.astype(jnp.float32), axis=0, keepdims=True)
 
 
-def back_through(cot, slope, dense, down, rows=512, after=()):
+def up_gradient(cot, slope, weight, rows=512, after=()):
     total, hidden = slope.shape
-    lanes = dense.width
     return call(
-        back_kernel,
-        "back_through",
+        up_grad_kernel,
+        "up_gradient",
         (total // rows,),
-        [cot_spec(cot, rows), band(rows, hidden), dense.spec, down.spec],
-        [band(rows, lanes), band(rows, hidden), whole(1, hidden)],
-        [
-            struct((total, lanes), jnp.bfloat16),
-            struct((total, hidden), jnp.bfloat16),
-            struct((1, hidden), jnp.float32),
-        ],
-        flops=4 * total * D * (hidden + lanes),
-        after=after,
-    )(cot, slope, dense.array, down.array)
+        [cot_spec(cot, rows), band(rows, hidden), weight.spec],
+        [band(rows, hidden), whole(1, hidden)],
+        [struct((total, hidden), jnp.bfloat16), struct((1, hidden), jnp.float32)],
+        flops=4 * total * D * hidden,
+        after=after,
+    )(cot, slope, weight.array)
 
 
 def rows_of(index, size):
@@ -875,8 +888,7 @@
     out_ref[1 - index_ref[0]] = other_ref[...]
 
 
-def joined(mine, axis, after=()):
-    other = shifted(mine, axis, 1)
+def joined(mine, other, axis, after=()):
     rows, cols = mine.size // mine.shape[-1] // 2, mine.shape[-1]
     spec = pl.BlockSpec((rows, cols), lambda j, p: (j, 0))
     out = prefetch_call(
@@ -969,8 +981,9 @@
         [w_query, w_key, w_value, w_dense], [False, False, False, True]
     )
     down_sides = packed_sides([w_fc2], [True])
-    cot = joined(cotangent, "g", after=[up_blocks, head_sides[0], down_sides[0]])
-    arrived = exchanged(up_blocks, after=[cot])
+    other = shifted(cotangent, "g", 1)
+    arrived = exchanged(up_blocks, after=[other])
+    cot = joined(cotangent, other, "g", after=[up_blocks, head_sides[0], down_sides[0]])
     cot = lax.all_gather(cot, ("h", "m", "c"), axis=0, tiled=False)
     cot = cot.reshape(2, 4, 2, row_count, feature_count)
     head_blocks = spread_sides(head_sides, after=[arrived])
@@ -1013,10 +1026,10 @@
     qkv = project_heads(normed, qkv_bias, qkv_weight, after=[head_other])
     attended, log_sums = attention(qkv)
     grad_down = weight_grad([(up_low, cot)], wide, after=[attended])
-    attended_grad, up_grad, up_sums = back_through(
-        cot, up_slope, dense_weight, down_weight, after=[grad_down]
-    )
-    qkv_grad, qkv_sums = attention_back(qkv, attended_grad, log_sums)
+    attended_grad = attended_gradient(cot, dense_weight, lanes, after=[grad_down])
+    grad_down = lax.optimization_barrier((grad_down, attended_grad))[0]
+    up_grad, up_sums = up_gradient(cot, up_slope, down_weight, after=[attended_grad])
+    qkv_grad, qkv_sums = attention_back(qkv, attended_grad, log_sums, after=[up_grad])
     qkv_grad_other = shifted(qkv_grad, "c", 1)
 
     grad_up = weight_grad([(up_grad, normed)], wide, after=[qkv_grad])

time: 414 us -> 411 us (level)
  waiting for transfers between devices: 125 us -> 109 us
  starting transfers between devices: 58.4 us -> 64.7 us
    ppermute x30, waiting for transfers between devices: 71.5 us -> 59.9 us  [shifted(): lax.ppermute(value, axis, [(source, (source + step) % count) for source i...]
    ppermute x30, starting transfers between devices: 29.2 us -> 34.9 us  [shifted(): lax.ppermute(value, axis, [(source, (source + step) % count) for source i...]
    all_to_all x2, waiting for transfers between devices: 24.2 us -> 19.4 us  [exchanged_along_line(): lax.all_to_all(blocks, LINE, 0, 0).reshape(2 * count, rows // 2, width)]
    pallas_call x14 -> x15, Pallas kernels: 141 us -> 145 us  [call(): return lambda *operands: run(*after, *operands)]
    unnamed x66 -> x60, local copies, waits for them, and re-layouts: 13.1 us -> 13.2 us
  transfers between devices with their start and end apart: 38 -> 38, of which waited for: 18 -> 17; matrix products, arithmetic and copies ran while one was open for 6% -> 6% of each run, Pallas kernels for 42% -> 44%
where the time goes in v7:
time: 411 us; the launch traced here: 409 us
  Pallas kernels  181 us (44%)
  waiting for transfers between devices  109 us (27%)
  starting transfers between devices  64.7 us (16%)
  local copies, waits for them, and re-layouts  30.5 us (7%)
  between operations  14.4 us (4%)
  other arithmetic  9.02 us (2%)
    pallas_call x15, Pallas kernels, call(): return lambda *operands: run(*after, *operands)  145 us
    ppermute x30, waiting for transfers between devices, shifted(): lax.ppermute(value, axis, [(source, (source + step) % count) for source i...  59.9 us
    pallas_call x15, Pallas kernels, prefetch_call(): run(index.astype(jnp.int32).reshape(1), *after, *operands)  36 us
    ppermute x30, starting transfers between devices, shifted(): lax.ppermute(value, axis, [(source, (source + step) % count) for source i...  34.9 us
    all_to_all x1, waiting for transfers between devices, exchanged(): return lax.all_to_all(blocks, WIDE, 0, 0)  24.5 us
    all_to_all x2, waiting for transfers between devices, exchanged_along_line(): lax.all_to_all(blocks, LINE, 0, 0).reshape(2 * count, rows // 2, width)  19.4 us
    unnamed x60, local copies, waits for them, and re-layouts  13.2 us
    all_to_all x2, starting transfers between devices, scatter_columns(): arrived = lax.all_to_all(grad, WIDE, 0, 0)  9.57 us
  transfers between devices with their start and end apart: 38, of which 17 were waited for; matrix products, arithmetic and copies ran while one was open for 6% of the time, Pallas kernels for 44%

profile of v7, /device:TPU:0, one launch (start us, length us, event | category | flops | bytes accessed | tf_op | source)
XLA Modules:
  0.0 408.8 jit_solution(4982989786167180300)
XLA Ops:
  8.0 3.1 collective-permute-start
  11.1 5.4 %concatenate.16 = bf16[704]{0:T(1024)(128)(2,1)S(1)} concatenate(bf16[64]{0:T(256)(128)(2,1)} %param.22, bf16[64]{0:T(256)(128)(2,1)} %param.23, bf16[64]{0:T(256)(128)(2,1)} %param.25, bf16[64]{0:T(256)(128)(2,1)} %param.27, bf16[64]{0:T(256)(128)(2,1)} %param.29, bf16[64]{0:T(256)(128)(2,1)} %param.31, bf16[64]{0:T(256)(128)(2,1)} %param.35, bf16[256]{0:T(256)(128)(2,1)} %param.33), dimensions={0} | concatenate | bytes 2816 | tf_op jit(solution)/shard_map/concatenate | solution.py:974
  17.1 2.2 pack.5
  19.3 3.6 pack.3
  22.9 2.2 pack.4
  25.1 2.2 collective-permute-done.refs_4_
  30.2 6.8 %all-to-all-start = ((bf16[8,272,512]{2,1,0:T(8,128)(2,1)}), bf16[8,272,512]{2,1,0:T(8,128)(2,1)S(1)}, u32[]{:S(2)}, u32[]{:S(2)}) async-start(bf16[8,272,512]{2,1,0:T(8,128)(2,1)} %bitcast.109), calls=%async_computation | async-start | bytes 4456448 | tf_op jit(solution)/shard_map/all_to_all | solution.py:685
  39.0 29.4 %collective-permute-done.1.refs_2_ = bf16[2,256,512]{2,1,0:T(8,128)(2,1)S(1)} collective-permute-done((bf16[2,256,512]{2,1,0:T(8,128)(2,1)S(1)}, bf16[2,256,512]{2,1,0:T(8,128)(2,1)S(1)}, u32[]{:S(2)}, u32[]{:S(2)}) %collective-permute-start.1) | collective-permute-done | bytes 524320 | tf_op jit(solution)/shard_map/ppermute | solution.py:48
  68.4 24.5 %all-to-all-done.refs_0_.refs_5_.refs_7_ = bf16[8,272,512]{2,1,0:T(8,128)(2,1)S(1)} async-done(((bf16[8,272,512]{2,1,0:T(8,128)(2,1)}), bf16[8,272,512]{2,1,0:T(8,128)(2,1)S(1)}, u32[]{:S(2)}, u32[]{:S(2)}) %all-to-all-start) | async-done | bytes 2228256 | tf_op jit(solution)/shard_map/all_to_all | solution.py:685
  94.3 2.4 spread.2
  96.7 4.6 %all-to-all-start.1 = ((bf16[4,512,512]{2,1,0:T(8,128)(2,1)}), bf16[4,512,512]{2,1,0:T(8,128)(2,1)S(1)}, u32[]{:S(2)}, u32[]{:S(2)}) async-start(bf16[4,512,512]{2,1,0:T(8,128)(2,1)} %bitcast.117), calls=%async_computation.1 | async-start | bytes 4194304 | tf_op jit(solution)/shard_map/all_to_all | solution.py:747
  101.2 3.4 collective-permute-start.6
  109.1 3.0 collective-permute-done.5
  114.6 14.3 %norm_up.1 = (bf16[2048,2048]{1,0:T(8,128)(2,1)}, f32[2048,128]{1,0:T(8,128)}, bf16[2048,512]{1,0:T(8,128)(2,1)}, f32[2048,512]{1,0:T(8,128)}) custom-call(bf16[2,2,256,512]{3,2,1,0:T(8,128)(2,1)} %copy-done.8, bf16[4,4,512,512]{3,2,1,0:T(8,128)(2,1)} %bitcast.116, f32[1,2048]{1,0:T(1,128)} %reshape.248.refs_2_, f32[1,2048]{1,0:T(1,128)} %reshape.249.refs_3_, ...), custom_call_target="tpu_custom_call" | custom-call | flops 12884901 | tf_op jit(solution)/shard_map/norm_up/pallas_call | solution.py:74
  128.9 2.5 spread.3
  131.4 14.2 %all-to-all-done.1 = bf16[4,512,512]{2,1,0:T(8,128)(2,1)S(1)} async-done(((bf16[4,512,512]{2,1,0:T(8,128)(2,1)}), bf16[4,512,512]{2,1,0:T(8,128)(2,1)S(1)}, u32[]{:S(2)}, u32[]{:S(2)}) %all-to-all-start.1) | async-done | bytes 2097184 | tf_op jit(solution)/shard_map/all_to_all | solution.py:747
  145.6 4.4 %all-to-all-start.2 = ((bf16[4,512,512]{2,1,0:T(8,128)(2,1)}), bf16[4,512,512]{2,1,0:T(8,128)(2,1)}, u32[]{:S(2)}, u32[]{:S(2)}) async-start(bf16[4,512,512]{2,1,0:T(8,128)(2,1)} %bitcast.118), calls=%async_computation.2 | async-start | bytes 4194304 | tf_op jit(solution)/shard_map/all_to_all | solution.py:747
  153.9 9.4 %project_heads.1.refs_0_.refs_1_ = bf16[2048,384]{1,0:T(8,128)(2,1)} custom-call(bf16[2,2,256,512]{3,2,1,0:T(8,128)(2,1)} %copy-done.2, bf16[2048,2048]{1,0:T(8,128)(2,1)} %get-tuple-element.70.refs_1_.refs_0_.refs_2_.refs_3_, f32[1,384]{1,0:T(1,128)} %reshape.250.refs_2_, f32[2048,128]{1,0:T(8,128)} %constant.83.clone.refs_3_.refs_4_, ...), custom_call_target="tpu_custom_call" | custom-call | flops 6442450 | tf_op jit(solution)/shard_map/project_heads/pallas_call | solution.py:74
  163.3 14.3 %attention.1 = (bf16[2048,128]{1,0:T(8,128)(2,1)}, f32[8,2048]{1,0:T(8,128)}) custom-call(bf16[2048,384]{1,0:T(8,128)(2,1)} %project_heads.1.refs_0_.refs_1_), custom_call_target="tpu_custom_call" | custom-call | flops 10000000 | tf_op jit(solution)/shard_map/attention/pallas_call | solution.py:74
  177.6 8.8 %weight_grad.3.refs_0_ = bf16[8,512,256]{2,1,0:T(8,128)(2,1)} custom-call(bf16[2048,128]{1,0:T(8,128)(2,1)} %get-tuple-element.71.refs_0_.refs_2_.refs_4_, bf16[2048,512]{1,0:T(8,128)(2,1)} %get-tuple-element.72.refs_1_.refs_3_, bf16[2,4,2,512,512]{4,3,2,1,0:T(8,128)(2,1)} %bitcast.98), custom_call_target="tpu_custom_call" | custom-call | flops 8589934 | tf_op jit(solution)/shard_map/weight_grad/pallas_call | solution.py:74
  186.4 6.3 %attended_gradient.1.refs_0_.refs_2_ = bf16[2048,128]{1,0:T(8,128)(2,1)} custom-call(bf16[8,512,256]{2,1,0:T(8,128)(2,1)} %weight_grad.3.refs_0_, bf16[2,4,2,512,512]{4,3,2,1,0:T(8,128)(2,1)} %bitcast.99, bf16[8,256,512]{2,1,0:T(8,128)(2,1)} %bitcast.104), custom_call_target="tpu_custom_call" | custom-call | flops 4294967 | tf_op jit(solution)/shard_map/attended_gradient/pallas_call | solution.py:74
  192.7 5.2 %all-to-all-done.2 = bf16[4,512,512]{2,1,0:T(8,128)(2,1)} async-done(((bf16[4,512,512]{2,1,0:T(8,128)(2,1)}), bf16[4,512,512]{2,1,0:T(8,128)(2,1)}, u32[]{:S(2)}, u32[]{:S(2)}) %all-to-all-start.2) | async-done | bytes 2097184 | tf_op jit(solution)/shard_map/all_to_all | solution.py:747
  197.9 5.2 %all-to-all-start.3 = ((bf16[8,512,256]{2,1,0:T(8,128)(2,1)}), bf16[8,512,256]{2,1,0:T(8,128)(2,1)}, u32[]{:S(2)}, u32[]{:S(2)}) async-start(bf16[8,512,256]{2,1,0:T(8,128)(2,1)} %weight_grad.3.refs_0_), calls=%async_computation.3 | async-start | bytes 4194304 | tf_op jit(solution)/shard_map/all_to_all | solution.py:765
  203.1 9.4 %up_gradient.1 = (bf16[2048,512]{1,0:T(8,128)(2,1)}, f32[1,512]{1,0:T(1,128)}) custom-call(bf16[2048,128]{1,0:T(8,128)(2,1)} %attended_gradient.1.refs_0_.refs_2_, bf16[2,4,2,512,512]{4,3,2,1,0:T(8,128)(2,1)} %bitcast.100, f32[2048,512]{1,0:T(8,128)} %get-tuple-element.74.refs_2_, bf16[8,256,512]{2,1,0:T(8,128)(2,1)} %bitcast.21.refs_3_.refs_7_), custom_call_target="tpu_custom_call" | custom-call | flops 8589934 | tf_op jit(solution)/shard_map/up_gradient/pallas_call | solution.py:74
  212.5 23.9 %attention_back.1 = (bf16[2048,384]{1,0:T(8,128)(2,1)}, f32[1,384]{1,0:T(1,128)}) custom-call(bf16[2048,512]{1,0:T(8,128)(2,1)} %get-tuple-element.76.refs_0_.refs_1_.refs_3_, bf16[2048,384]{1,0:T(8,128)(2,1)} %project_heads.1.refs_0_.refs_1_, bf16[2048,128]{1,0:T(8,128)(2,1)} %attended_gradient.1.refs_0_.refs_2_, f32[8,2048]{1,0:T(8,128)} %get-tuple-element.77.refs_3_, ...), custom_call_target="tpu_custom_call" | custom-call | flops 20000000 | tf_op jit(solution)/shard_map/attention_back/pallas_call | solution.py:74
  236.9 8.8 %weight_grad.4.refs_0_ = bf16[8,512,256]{2,1,0:T(8,128)(2,1)} custom-call(bf16[2048,384]{1,0:T(8,128)(2,1)} %get-tuple-element.78.refs_0_.refs_2_, bf16[2048,512]{1,0:T(8,128)(2,1)} %get-tuple-element.76.refs_0_.refs_1_.refs_3_, bf16[2048,2048]{1,0:T(8,128)(2,1)} %get-tuple-element.70.refs_1_.refs_0_.refs_2_.refs_3_), custom_call_target="tpu_custom_call" | custom-call | flops 8589934 | tf_op jit(solution)/shard_map/weight_grad/pallas_call | solution.py:74
  245.7 4.2 %all-to-all-done.3 = bf16[8,512,256]{2,1,0:T(8,128)(2,1)} async-done(((bf16[8,512,256]{2,1,0:T(8,128)(2,1)}), bf16[8,512,256]{2,1,0:T(8,128)(2,1)}, u32[]{:S(2)}, u32[]{:S(2)}) %all-to-all-start.3) | async-done | bytes 2097184 | tf_op jit(solution)/shard_map/all_to_all | solution.py:765
  250.0 4.4 %all-to-all-start.4 = ((bf16[8,512,256]{2,1,0:T(8,128)(2,1)}), bf16[8,512,256]{2,1,0:T(8,128)(2,1)}, u32[]{:S(2)}, u32[]{:S(2)}) async-start(bf16[8,512,256]{2,1,0:T(8,128)(2,1)} %weight_grad.4.refs_0_), calls=%async_computation.4 | async-start | bytes 4194304 | tf_op jit(solution)/shard_map/all_to_all | solution.py:765
  255.0 15.0 %normed_gradient.1 = (bf16[4,256,512]{2,1,0:T(8,128)(2,1)}, bf16[4,256,512]{2,1,0:T(8,128)(2,1)}, bf16[2,2,256,512]{3,2,1,0:T(8,128)(2,1)}, bf16[2,2,256,512]{3,2,1,0:T(8,128)(2,1)}) custom-call(bf16[8,512,256]{2,1,0:T(8,128)(2,1)} %weight_grad.4.refs_0_, s32[3]{0:T(128)} %pad_add_fusion.refs_1_, bf16[2048,384]{1,0:T(8,128)(2,1)} %get-tuple-element.78.refs_0_.refs_2_, ...), custom_call_target="tpu_custom_call" | custom-call | flops 15032385 | tf_op jit(solution)/shard_map/normed_gradient/pallas_call | solution.py:74
  277.4 10.9 %branch_sum.1 = (bf16[4,256,512]{2,1,0:T(8,128)(2,1)}, bf16[4,256,512]{2,1,0:T(8,128)(2,1)}, bf16[4,256,512]{2,1,0:T(8,128)(2,1)}, bf16[4,256,512]{2,1,0:T(8,128)(2,1)}) custom-call(bf16[4,256,512]{2,1,0:T(8,128)(2,1)} %get-tuple-element.80.refs_0_, s32[3]{0:T(128)} %pad_add_fusion.refs_1_, bf16[2048,128]{1,0:T(8,128)(2,1)} %get-tuple-element.71.refs_0_.refs_2_.refs_4_, ...), custom_call_target="tpu_custom_call" | custom-call | flops 10737418 | tf_op jit(solution)/shard_map/branch_sum/pallas_call | solution.py:74
  290.7 10.3 %weight_grad.5.refs_0_ = bf16[8,528,256]{2,1,0:T(8,128)(2,1)} custom-call(bf16[4,256,512]{2,1,0:T(8,128)(2,1)} %get-tuple-element.82.refs_0_, bf16[8,16,256]{2,1,0:T(8,128)(2,1)} %bitcast.139, bf16[2048,384]{1,0:T(8,128)(2,1)} %get-tuple-element.78.refs_0_.refs_2_, bf16[2048,2048]{1,0:T(8,128)(2,1)} %get-tuple-element.70.refs_1_.refs_0_.refs_2_.refs_3_, ...), custom_call_target="tpu_custom_call" | custom-call | flops 8858370 | tf_op jit(solution)/shard_map/weight_grad/pallas_call | solution.py:74
  301.2 4.4 %all-to-all-start.5 = ((bf16[4,1056,256]{2,1,0:T(8,128)(2,1)}), bf16[4,1056,256]{2,1,0:T(8,128)(2,1)S(1)}, u32[]{:S(2)}, u32[]{:S(2)}) async-start(bf16[4,1056,256]{2,1,0:T(8,128)(2,1)} %bitcast.110), calls=%async_computation.5 | async-start | bytes 4325376 | tf_op jit(solution)/shard_map/all_to_all | solution.py:818
  305.5 2.5 fold.8
  309.3 3.8 unpack.3.refs_0_
  313.1 2.5 fold.9
  317.5 3.3 collective-permute-done.14
  320.8 2.6 fold.10
  328.0 3.5 collective-permute-done.17
  337.6 4.2 %unpack.4 = f32[256,2048]{1,0:T(8,128)} custom-call(bf16[1,256,512]{2,1,0:T(8,128)(2,1)} %get-tuple-element.97.refs_0_, bf16[2,4,512,256]{3,2,1,0:T(8,128)(2,1)} %bitcast.36.refs_1_), custom_call_target="tpu_custom_call" | custom-call | tf_op jit(solution)/shard_map/unpack/pallas_call | solution.py:74
  341.8 5.6 %collective-permute-done.16 = bf16[256,512]{1,0:T(8,128)(2,1)S(1)} collective-permute-done((bf16[256,512]{1,0:T(8,128)(2,1)}, bf16[256,512]{1,0:T(8,128)(2,1)S(1)}, u32[]{:S(2)}, u32[]{:S(2)}) %collective-permute-start.16) | collective-permute-done | bytes 262176 | tf_op jit(solution)/shard_map/ppermute | solution.py:48
  347.4 4.5 %collective-permute-done.18 = bf16[256,512]{1,0:T(8,128)(2,1)} collective-permute-done((bf16[256,512]{1,0:T(8,128)(2,1)}, bf16[256,512]{1,0:T(8,128)(2,1)}, u32[]{:S(2)}, u32[]{:S(2)}) %collective-permute-start.18) | collective-permute-done | bytes 262176 | tf_op jit(solution)/shard_map/ppermute | solution.py:48
  359.3 2.5 collective-permute-start.28
  365.1 2.5 collective-permute-start.29
  367.6 2.9 multiply_add_fusion
  370.4 2.4 fold.13
  375.8 2.5 side_sums.1
  394.3 4.0 unpack.5
  399.1 2.4 finish.1
  (191 shorter events, 74.1 us)
Async XLA Ops:
  7.2 106.4 %all-gather.5.cloned.1.call-start = ((), (), s32[]{:S(2)}) async-start(), calls=%async_computation.6 | async-start | bytes 8912896 | tf_op jit(solution)/shard_map/all_gather | solution.py:977
  7.9 169.7 %all-gather.7.cloned.1.call-start = ((), (), s32[]{:S(2)}) async-start(), calls=%async_computation.7 | async-start | bytes 9437184 | tf_op jit(solution)/shard_map/all_gather | solution.py:987
  8.0 19.3 %collective-permute-start = (bf16[512,512]{1,0:T(8,128)(2,1)}, bf16[512,512]{1,0:T(8,128)(2,1)S(1)}, u32[]{:S(2)}, u32[]{:S(2)}) collective-permute-start(bf16[512,512]{1,0:T(8,128)(2,1)} %refs_3_.4), channel_id=1, source_target_pairs={{0,8},{8,0},{1,9},{9,1},{2,10},{10,2},{3,11},{11,3},{4,12},{12,4},... | collective-permute-start | bytes 1572872 | tf_op jit(solution)/shard_map/ppermute | solution.py:48
  30.2 62.7 %all-to-all-start = ((bf16[8,272,512]{2,1,0:T(8,128)(2,1)}), bf16[8,272,512]{2,1,0:T(8,128)(2,1)S(1)}, u32[]{:S(2)}, u32[]{:S(2)}) async-start(bf16[8,272,512]{2,1,0:T(8,128)(2,1)} %bitcast.109), calls=%async_computation | async-start | bytes 4456448 | tf_op jit(solution)/shard_map/all_to_all | solution.py:685
  37.0 31.4 %collective-permute-start.1 = (bf16[2,256,512]{2,1,0:T(8,128)(2,1)S(1)}, bf16[2,256,512]{2,1,0:T(8,128)(2,1)S(1)}, u32[]{:S(2)}, u32[]{:S(2)}) collective-permute-start(bf16[2,256,512]{2,1,0:T(8,128)(2,1)S(1)} %copy-done.26), channel_id=1, source_target_pairs={{0,4},{4,0},{1,5},{5,1},{2,6},{6,2},{3,7},{7,3},{8,12},{12,8},{9,1... | collective-permute-start | bytes 1572872 | tf_op jit(solution)/shard_map/ppermute | solution.py:48
  68.4 24.5 %copy-start.19 = (bf16[2,256,512]{2,1,0:T(8,128)(2,1)}, bf16[2,256,512]{2,1,0:T(8,128)(2,1)S(1)}, u32[]{:S(2)}) copy-start(bf16[2,256,512]{2,1,0:T(8,128)(2,1)S(1)} %collective-permute-done.1.refs_2_) | copy-start | bytes 1572868
  96.7 48.9 %all-to-all-start.1 = ((bf16[4,512,512]{2,1,0:T(8,128)(2,1)}), bf16[4,512,512]{2,1,0:T(8,128)(2,1)S(1)}, u32[]{:S(2)}, u32[]{:S(2)}) async-start(bf16[4,512,512]{2,1,0:T(8,128)(2,1)} %bitcast.117), calls=%async_computation.1 | async-start | bytes 4194304 | tf_op jit(solution)/shard_map/all_to_all | solution.py:747
  101.2 27.6 %collective-permute-start.6 = (bf16[2,256,512]{2,1,0:T(8,128)(2,1)}, bf16[2,256,512]{2,1,0:T(8,128)(2,1)}, u32[]{:S(2)}, u32[]{:S(2)}) collective-permute-start(bf16[2,256,512]{2,1,0:T(8,128)(2,1)} %get-tuple-element.75), channel_id=1, source_target_pairs={{0,4},{4,0},{1,5},{5,1},{2,6},{6,2},{3,7},{7,3},{8,12},{12,8},{9,1... | collective-permute-start | bytes 1572872 | tf_op jit(solution)/shard_map/ppermute | solution.py:48
  105.6 44.6 %copy-start.22 = (bf16[1,8,16,512]{3,1,2,0:T(8,128)(2,1)}, bf16[1,8,16,512]{3,1,2,0:T(8,128)(2,1)S(1)}, u32[]{:S(2)}) copy-start(bf16[1,8,16,512]{3,1,2,0:T(8,128)(2,1)S(1)} %copy.46) | copy-start | bytes 393220
  105.7 2.8 collective-permute-start.4
  108.3 5.3 %collective-permute-start.3 = (bf16[2,2,256,512]{3,2,1,0:T(8,128)(2,1)}, bf16[2,2,256,512]{3,2,1,0:T(8,128)(2,1)S(1)}, u32[]{:S(2)}, u32[]{:S(2)}) collective-permute-start(bf16[2,2,256,512]{3,2,1,0:T(8,128)(2,1)} %dynamic-slice_bitcast_fusion.1), channel_id=1, source_target_pairs={{0,1},{1,0},{2,3},{3,2},{4,5},{5,4},{6,7},{7,6},{8,9},{9,8},{10,11... | collective-permute-start | bytes 3145736 | tf_op jit(solution)/shard_map/ppermute | solution.py:48
  108.4 3.7 collective-permute-start.5
  145.6 52.2 %all-to-all-start.2 = ((bf16[4,512,512]{2,1,0:T(8,128)(2,1)}), bf16[4,512,512]{2,1,0:T(8,128)(2,1)}, u32[]{:S(2)}, u32[]{:S(2)}) async-start(bf16[4,512,512]{2,1,0:T(8,128)(2,1)} %bitcast.118), calls=%async_computation.2 | async-start | bytes 4194304 | tf_op jit(solution)/shard_map/all_to_all | solution.py:747
  150.2 2.7 collective-permute-start.2
  197.9 52.1 %all-to-all-start.3 = ((bf16[8,512,256]{2,1,0:T(8,128)(2,1)}), bf16[8,512,256]{2,1,0:T(8,128)(2,1)}, u32[]{:S(2)}, u32[]{:S(2)}) async-start(bf16[8,512,256]{2,1,0:T(8,128)(2,1)} %weight_grad.3.refs_0_), calls=%async_computation.3 | async-start | bytes 4194304 | tf_op jit(solution)/shard_map/all_to_all | solution.py:765
  212.5 33.2 %collective-permute-start.8 = (bf16[2048,512]{1,0:T(8,128)(2,1)}, bf16[2048,512]{1,0:T(8,128)(2,1)}, u32[]{:S(2)}, u32[]{:S(2)}) collective-permute-start(bf16[2048,512]{1,0:T(8,128)(2,1)} %get-tuple-element.76.refs_0_.refs_1_.refs_3_), channel_id=1, source_target_pairs={{0,1},{1,0},{2,3},{3,2},{4,5},{5,4},{6,7},{7,6},{8,9},{9,8},{10,11... | collective-permute-start | bytes 6291464 | tf_op jit(solution)/shard_map/ppermute | solution.py:48
  236.4 9.3 %collective-permute-start.7 = (bf16[2048,384]{1,0:T(8,128)(2,1)}, bf16[2048,384]{1,0:T(8,128)(2,1)}, u32[]{:S(2)}, u32[]{:S(2)}) collective-permute-start(bf16[2048,384]{1,0:T(8,128)(2,1)} %get-tuple-element.78.refs_0_.refs_2_), channel_id=1, source_target_pairs={{0,1},{1,0},{2,3},{3,2},{4,5},{5,4},{6,7},{7,6},{8,9},{9,8},{10,11... | collective-permute-start | bytes 4718600 | tf_op jit(solution)/shard_map/ppermute | solution.py:48
  245.7 8.6 %copy-start.4 = (bf16[2048,512]{1,0:T(8,128)(2,1)S(1)}, bf16[2048,512]{1,0:T(8,128)(2,1)}, u32[]{:S(2)}) copy-start(bf16[2048,512]{1,0:T(8,128)(2,1)} %get-tuple-element.72.refs_1_.refs_3_) | copy-start | bytes 6291460
  250.0 51.2 %all-to-all-start.4 = ((bf16[8,512,256]{2,1,0:T(8,128)(2,1)}), bf16[8,512,256]{2,1,0:T(8,128)(2,1)}, u32[]{:S(2)}, u32[]{:S(2)}) async-start(bf16[8,512,256]{2,1,0:T(8,128)(2,1)} %weight_grad.4.refs_0_), calls=%async_computation.4 | async-start | bytes 4194304 | tf_op jit(solution)/shard_map/all_to_all | solution.py:765
  254.3 20.6 %collective-permute-start.10 = (bf16[2048,512]{1,0:T(8,128)(2,1)S(1)}, bf16[2048,512]{1,0:T(8,128)(2,1)S(1)}, u32[]{:S(2)}, u32[]{:S(2)}) collective-permute-start(bf16[2048,512]{1,0:T(8,128)(2,1)S(1)} %copy-done.4), channel_id=1, source_target_pairs={{0,1},{1,0},{2,3},{3,2},{4,5},{5,4},{6,7},{7,6},{8,9},{9,8},{10,11... | collective-permute-start | bytes 6291464 | tf_op jit(solution)/shard_map/ppermute | solution.py:48
  271.4 3.6 collective-permute-start.11
  271.9 3.0 collective-permute-start.9
  272.0 33.5 %collective-permute-start.12 = (bf16[4,256,512]{2,1,0:T(8,128)(2,1)}, bf16[4,256,512]{2,1,0:T(8,128)(2,1)}, u32[]{:S(2)}, u32[]{:S(2)}) collective-permute-start(bf16[4,256,512]{2,1,0:T(8,128)(2,1)} %get-tuple-element.85), channel_id=1, source_target_pairs={{0,2},{2,0},{1,3},{3,1},{4,6},{6,4},{5,7},{7,5},{8,10},{10,8},{9,1... | collective-permute-start | bytes 3145736 | tf_op jit(solution)/shard_map/ppermute | solution.py:48
  272.3 16.9 %copy-start.7 = (bf16[512,512]{1,0:T(8,128)(2,1)S(1)}, bf16[512,512]{1,0:T(8,128)(2,1)}, u32[]{:S(2)}) copy-start(bf16[512,512]{1,0:T(8,128)(2,1)} %refs_3_.4) | copy-start | bytes 1572868
  272.4 17.1 %copy-start.23 = (f32[1,512]{1,0:T(1,128)S(1)}, f32[1,512]{1,0:T(1,128)}, u32[]{:S(2)}) copy-start(f32[1,512]{1,0:T(1,128)} %get-tuple-element.84) | copy-start | bytes 6148
  272.4 17.2 %copy-start.24 = (f32[1,384]{1,0:T(1,128)S(1)}, f32[1,384]{1,0:T(1,128)}, u32[]{:S(2)}) copy-start(f32[1,384]{1,0:T(1,128)} %get-tuple-element.83) | copy-start | bytes 4612
  272.4 40.8 %collective-permute-start.13 = (bf16[2,2,256,512]{3,2,1,0:T(8,128)(2,1)}, bf16[2,2,256,512]{3,2,1,0:T(8,128)(2,1)}, u32[]{:S(2)}, u32[]{:S(2)}) collective-permute-start(bf16[2,2,256,512]{3,2,1,0:T(8,128)(2,1)} %get-tuple-element.89), channel_id=1, source_target_pairs={{0,4},{4,0},{1,5},{5,1},{2,6},{6,2},{3,7},{7,3},{8,12},{12,8},{9,1... | collective-permute-start | bytes 3145736 | tf_op jit(solution)/shard_map/ppermute | solution.py:48
  288.3 32.5 %collective-permute-start.14 = (bf16[4,256,512]{2,1,0:T(8,128)(2,1)}, bf16[4,256,512]{2,1,0:T(8,128)(2,1)}, u32[]{:S(2)}, u32[]{:S(2)}) collective-permute-start(bf16[4,256,512]{2,1,0:T(8,128)(2,1)} %get-tuple-element.91), channel_id=1, source_target_pairs={{0,2},{2,0},{1,3},{3,1},{4,6},{6,4},{5,7},{7,5},{8,10},{10,8},{9,1... | collective-permute-start | bytes 3145736 | tf_op jit(solution)/shard_map/ppermute | solution.py:48
  301.2 73.3 %all-to-all-start.5 = ((bf16[4,1056,256]{2,1,0:T(8,128)(2,1)}), bf16[4,1056,256]{2,1,0:T(8,128)(2,1)S(1)}, u32[]{:S(2)}, u32[]{:S(2)}) async-start(bf16[4,1056,256]{2,1,0:T(8,128)(2,1)} %bitcast.110), calls=%async_computation.5 | async-start | bytes 4325376 | tf_op jit(solution)/shard_map/all_to_all | solution.py:818
  308.1 15.3 %collective-permute-start.15 = (bf16[2,256,512]{2,1,0:T(8,128)(2,1)}, bf16[2,256,512]{2,1,0:T(8,128)(2,1)S(1)}, u32[]{:S(2)}, u32[]{:S(2)}) collective-permute-start(bf16[2,256,512]{2,1,0:T(8,128)(2,1)} %get-tuple-element.93), channel_id=1, source_target_pairs={{0,4},{4,0},{1,5},{5,1},{2,6},{6,2},{3,7},{7,3},{8,12},{12,8},{9,1... | collective-permute-start | bytes 1572872 | tf_op jit(solution)/shard_map/ppermute | solution.py:48
  315.7 15.8 %collective-permute-start.17 = (bf16[2,256,512]{2,1,0:T(8,128)(2,1)}, bf16[2,256,512]{2,1,0:T(8,128)(2,1)S(1)}, u32[]{:S(2)}, u32[]{:S(2)}) collective-permute-start(bf16[2,256,512]{2,1,0:T(8,128)(2,1)} %get-tuple-element.96), channel_id=1, source_target_pairs={{0,2},{2,0},{1,3},{3,1},{4,6},{6,4},{5,7},{7,5},{8,10},{10,8},{9,1... | collective-permute-start | bytes 1572872 | tf_op jit(solution)/shard_map/ppermute | solution.py:48
  326.2 21.2 %collective-permute-start.16 = (bf16[256,512]{1,0:T(8,128)(2,1)}, bf16[256,512]{1,0:T(8,128)(2,1)S(1)}, u32[]{:S(2)}, u32[]{:S(2)}) collective-permute-start(bf16[256,512]{1,0:T(8,128)(2,1)} %bitcast.164), channel_id=1, source_target_pairs={{0,8},{8,0},{1,9},{9,1},{2,10},{10,2},{3,11},{11,3},{4,12},{12,4},... | collective-permute-start | bytes 786440 | tf_op jit(solution)/shard_map/ppermute | solution.py:48
  334.3 17.6 %collective-permute-start.18 = (bf16[256,512]{1,0:T(8,128)(2,1)}, bf16[256,512]{1,0:T(8,128)(2,1)}, u32[]{:S(2)}, u32[]{:S(2)}) collective-permute-start(bf16[256,512]{1,0:T(8,128)(2,1)} %bitcast.166), channel_id=1, source_target_pairs={{0,8},{8,0},{1,9},{9,1},{2,10},{10,2},{3,11},{11,3},{4,12},{12,4},... | collective-permute-start | bytes 786440 | tf_op jit(solution)/shard_map/ppermute | solution.py:48
  337.2 33.2 %collective-permute-start.19 = (bf16[4,256,512]{2,1,0:T(8,128)(2,1)}, bf16[4,256,512]{2,1,0:T(8,128)(2,1)}, u32[]{:S(2)}, u32[]{:S(2)}) collective-permute-start(bf16[4,256,512]{2,1,0:T(8,128)(2,1)} %get-tuple-element.103), channel_id=1, source_target_pairs={{0,2},{2,0},{1,3},{3,1},{4,6},{6,4},{5,7},{7,5},{8,10},{10,8},{9,1... | collective-permute-start | bytes 3145736 | tf_op jit(solution)/shard_map/ppermute | solution.py:48
  337.6 14.3 %copy-start.14 = (bf16[1,256,512]{2,1,0:T(8,128)(2,1)S(1)}, bf16[1,256,512]{2,1,0:T(8,128)(2,1)}, u32[]{:S(2)}) copy-start(bf16[1,256,512]{2,1,0:T(8,128)(2,1)} %get-tuple-element.94.refs_0_) | copy-start | bytes 786436
  337.6 14.4 %copy-start.15 = (bf16[1,256,512]{2,1,0:T(8,128)(2,1)S(1)}, bf16[1,256,512]{2,1,0:T(8,128)(2,1)}, u32[]{:S(2)}) copy-start(bf16[1,256,512]{2,1,0:T(8,128)(2,1)} %get-tuple-element.97.refs_0_) | copy-start | bytes 786436
  341.8 12.1 %copy-start.5 = (bf16[512,512]{1,0:T(8,128)(2,1)S(1)}, bf16[512,512]{1,0:T(8,128)(2,1)}, u32[]{:S(2)}) copy-start(bf16[512,512]{1,0:T(8,128)(2,1)} %refs_1_.7) | copy-start | bytes 1572868
  355.6 3.6 collective-permute-start.27
  357.1 4.7 %collective-permute-start.25 = (f32[2,512]{1,0:T(2,128)S(1)}, f32[2,512]{1,0:T(2,128)S(1)}, u32[]{:S(2)}, u32[]{:S(2)}) collective-permute-start(f32[2,512]{1,0:T(2,128)S(1)} %pad_maximum_fusion.3), channel_id=1, source_target_pairs={{0,1},{1,0},{2,3},{3,2},{4,5},{5,4},{6,7},{7,6},{8,9},{9,8},{10,11... | collective-permute-start | bytes 12296 | tf_op jit(solution)/shard_map/ppermute | solution.py:48
  359.3 5.7 %collective-permute-start.28 = (f32[8,128]{1,0:T(8,128)S(1)}, f32[8,128]{1,0:T(8,128)S(1)}, u32[]{:S(2)}, u32[]{:S(2)}) collective-permute-start(f32[8,128]{1,0:T(8,128)S(1)} %fusion.10), channel_id=1, source_target_pairs={{0,8},{8,0},{1,9},{9,1},{2,10},{10,2},{3,11},{11,3},{4,12},{12,4},... | collective-permute-start | bytes 12296 | tf_op jit(solution)/shard_map/ppermute | solution.py:48
  361.8 5.7 %collective-permute-start.26 = (f32[2,512]{1,0:T(2,128)S(1)}, f32[2,512]{1,0:T(2,128)S(1)}, u32[]{:S(2)}, u32[]{:S(2)}) collective-permute-start(f32[2,512]{1,0:T(2,128)S(1)} %fusion.3), channel_id=1, source_target_pairs={{0,2},{2,0},{1,3},{3,1},{4,6},{6,4},{5,7},{7,5},{8,10},{10,8},{9,1... | collective-permute-start | bytes 12296 | tf_op jit(solution)/shard_map/ppermute | solution.py:48
  363.6 17.2 %collective-permute-start.20 = (bf16[2,256,512]{2,1,0:T(8,128)(2,1)}, bf16[2,256,512]{2,1,0:T(8,128)(2,1)}, u32[]{:S(2)}, u32[]{:S(2)}) collective-permute-start(bf16[2,256,512]{2,1,0:T(8,128)(2,1)} %get-tuple-element.105), channel_id=1, source_target_pairs={{0,4},{4,0},{1,5},{5,1},{2,6},{6,2},{3,7},{7,3},{8,12},{12,8},{9,1... | collective-permute-start | bytes 1572872 | tf_op jit(solution)/shard_map/ppermute | solution.py:48
  365.1 18.5 %collective-permute-start.29 = (f32[8,128]{1,0:T(8,128)S(1)}, f32[8,128]{1,0:T(8,128)S(1)}, u32[]{:S(2)}, u32[]{:S(2)}) collective-permute-start(f32[8,128]{1,0:T(8,128)S(1)} %add.89), channel_id=1, source_target_pairs={{0,16},{16,0},{1,17},{17,1},{2,18},{18,2},{3,19},{19,3},{4,20},{20... | collective-permute-start | bytes 12296 | tf_op jit(solution)/shard_map/ppermute | solution.py:48
  372.8 13.1 %collective-permute-start.21 = (bf16[2,256,512]{2,1,0:T(8,128)(2,1)}, bf16[2,256,512]{2,1,0:T(8,128)(2,1)S(1)}, u32[]{:S(2)}, u32[]{:S(2)}) collective-permute-start(bf16[2,256,512]{2,1,0:T(8,128)(2,1)} %bitcast.162), channel_id=1, source_target_pairs={{0,8},{8,0},{1,9},{9,1},{2,10},{10,2},{3,11},{11,3},{4,12},{12,4},... | collective-permute-start | bytes 1572872 | tf_op jit(solution)/shard_map/ppermute | solution.py:48
  378.3 14.0 %collective-permute-start.22 = (bf16[2,528,256]{2,1,0:T(8,128)(2,1)}, bf16[2,528,256]{2,1,0:T(8,128)(2,1)S(1)}, u32[]{:S(2)}, u32[]{:S(2)}) collective-permute-start(bf16[2,528,256]{2,1,0:T(8,128)(2,1)} %get-tuple-element.110), channel_id=1, source_target_pairs={{0,4},{4,0},{1,5},{5,1},{2,6},{6,2},{3,7},{7,3},{8,12},{12,8},{9,1... | collective-permute-start | bytes 1622024 | tf_op jit(solution)/shard_map/ppermute | solution.py:48
  382.8 15.5 %collective-permute-start.23 = (bf16[256,512]{1,0:T(8,128)(2,1)}, bf16[256,512]{1,0:T(8,128)(2,1)S(1)}, u32[]{:S(2)}, u32[]{:S(2)}) collective-permute-start(bf16[256,512]{1,0:T(8,128)(2,1)} %bitcast.163), channel_id=1, source_target_pairs={{0,8},{8,0},{1,9},{9,1},{2,10},{10,2},{3,11},{11,3},{4,12},{12,4},... | collective-permute-start | bytes 786440 | tf_op jit(solution)/shard_map/ppermute | solution.py:48
  388.8 9.5 %collective-permute-start.24 = (bf16[256,512]{1,0:T(8,128)(2,1)}, bf16[256,512]{1,0:T(8,128)(2,1)S(1)}, u32[]{:S(2)}, u32[]{:S(2)}) collective-permute-start(bf16[256,512]{1,0:T(8,128)(2,1)} %bitcast.165), channel_id=1, source_target_pairs={{0,4},{4,0},{1,5},{5,1},{2,6},{6,2},{3,7},{7,3},{8,12},{12,8},{9,1... | collective-permute-start | bytes 786440 | tf_op jit(solution)/shard_map/ppermute | solution.py:48
  394.3 7.2 %copy-start.25 = (f32[64]{0:T(128)}, f32[64]{0:T(128)S(1)}, u32[]{:S(2)}) copy-start(f32[64]{0:T(128)S(1)} %get-tuple-element.183) | copy-start | bytes 772
  (18 other events, 29.2 us)
Sparse Core Ops, SparseCore 0:
  9.6 90.3 all-gather.4
  101.9 54.8 all-gather.6

commit v8 on v7

--- a/solution.py
+++ b/solution.py
@@ -385,6 +385,8 @@
     gt_ref,
     prob_ref,
     slope_ref,
+    k_ref,
+    v_ref,
     k_total,
     v_total,
 ):
@@ -398,6 +400,10 @@
         turned_into(qt_ref, qkv_ref, slice(0, width))
         turned_into(kt_ref, qkv_ref, slice(width, 2 * width))
         turned_into(gt_ref, grad_ref, slice(0, width))
+        for n in range(2):
+            for ref, begin in ((k_ref, width), (v_ref, 2 * width)):
+                begin += n * HEAD_DIM
+                ref[n] = qkv_ref[:, begin : begin + HEAD_DIM]
         k_total[...] = jnp.zeros_like(k_total)
         v_total[...] = jnp.zeros_like(v_total)
         sums_ref[...] = jnp.zeros_like(sums_ref)
@@ -410,13 +416,11 @@
         rows = rows_of(j, block)
         new = []
         for n, head in enumerate(HEADS_HERE):
-            start = width + n * HEAD_DIM
-            scores = matmul(qkv_ref[rows, start : start + HEAD_DIM], qt_ref[head, own])
+            scores = matmul(k_ref[n, rows, :], qt_ref[head, own])
             probs = jnp.exp(scores - log_sums[n])
             if diagonal:
                 probs = jnp.where(causal, probs, 0.0)
-            start += width
-            slope = matmul(qkv_ref[rows, start : start + HEAD_DIM], gt_ref[head, own])
+            slope = matmul(v_ref[n, rows, :], gt_ref[head, own])
             prob_ref[n, j] = probs
             slope_ref[n, j] = slope
             new.append(carry[n] + fold_rows(probs * slope, jnp.sum))
@@ -433,8 +437,8 @@
         for n, head in enumerate(HEADS_HERE):
             probs = prob_ref[n, j]
             score_grad = (probs * (slope_ref[n, j] - dots[n])).astype(jnp.bfloat16)
-            k_total[rows, head] += matmul(score_grad, qkv_ref[own, head])
-            v_total[rows, head] += matmul(probs.astype(jnp.bfloat16), grad_ref[own, head])
+            k_total[n, rows, :] += matmul(score_grad, qkv_ref[own, head])
+            v_total[n, rows, :] += matmul(probs.astype(jnp.bfloat16), grad_ref[own, head])
             new.append(carry[n] + matmul(kt_ref[head, rows], score_grad))
         return tuple(new)
 
@@ -449,9 +453,11 @@
     def _():
         def finish(b, carry):
             rows = rows_of(b, chunk)
-            k_pre = turn(k_total[rows, :], cosine_ref[rows, :], -sine_ref[rows, :])
+            k_sum = jnp.concatenate([k_total[0, rows, :], k_total[1, rows, :]], axis=1)
+            v_sum = jnp.concatenate([v_total[0, rows, :], v_total[1, rows, :]], axis=1)
+            k_pre = turn(k_sum, cosine_ref[rows, :], -sine_ref[rows, :])
             k_pre = k_pre.astype(jnp.bfloat16)
-            v_pre = v_total[rows, :].astype(jnp.bfloat16)
+            v_pre = v_sum.astype(jnp.bfloat16)
             pre_grad_ref[rows, width : 2 * width] = k_pre
             pre_grad_ref[rows, 2 * width :] = v_pre
             both = jnp.concatenate([k_pre, v_pre], axis=1).astype(jnp.float32)
@@ -476,7 +482,8 @@
         [struct((rows, 3 * width), jnp.bfloat16), struct((1, 3 * width), jnp.float32)],
         [pltpu.VMEM((width, rows), jnp.bfloat16)] * 3
         + [pltpu.VMEM((2, blocks, block, block), jnp.float32)] * 2
-        + [pltpu.VMEM((rows, width), jnp.float32)] * 2,
+        + [pltpu.VMEM((2, rows, HEAD_DIM), jnp.bfloat16)] * 2
+        + [pltpu.VMEM((2, rows, HEAD_DIM), jnp.float32)] * 2,
         flops=20 * 10**9,
         after=after,
     )(qkv, out_grad, log_sums, jnp.asarray(cosine), jnp.asarray(sine))

time: 411 us -> 411 us (level)
  no operation moved by 1% of the time
where the time goes in v8:
time: 411 us; the launch traced here: 409 us
  Pallas kernels  183 us (45%)
  waiting for transfers between devices  108 us (26%)
  starting transfers between devices  64.1 us (16%)
  local copies, waits for them, and re-layouts  30.5 us (7%)
  between operations  14.4 us (4%)
  other arithmetic  9.02 us (2%)
    pallas_call x15, Pallas kernels, call(): return lambda *operands: run(*after, *operands)  147 us
    ppermute x30, waiting for transfers between devices, shifted(): lax.ppermute(value, axis, [(source, (source + step) % count) for source i...  59.9 us
    pallas_call x15, Pallas kernels, prefetch_call(): run(index.astype(jnp.int32).reshape(1), *after, *operands)  36 us
    ppermute x30, starting transfers between devices, shifted(): lax.ppermute(value, axis, [(source, (source + step) % count) for source i...  34.9 us
    all_to_all x1, waiting for transfers between devices, exchanged(): return lax.all_to_all(blocks, WIDE, 0, 0)  24.5 us
    all_to_all x2, waiting for transfers between devices, exchanged_along_line(): lax.all_to_all(blocks, LINE, 0, 0).reshape(2 * count, rows // 2, width)  19.4 us
    unnamed x60, local copies, waits for them, and re-layouts  13.2 us
    all_to_all x2, starting transfers between devices, scatter_columns(): arrived = lax.all_to_all(grad, WIDE, 0, 0)  9.57 us
  transfers between devices with their start and end apart: 38, of which 17 were waited for; matrix products, arithmetic and copies ran while one was open for 6% of the time, Pallas kernels for 44%

profile of v8, /device:TPU:0, one launch (start us, length us, event | category | flops | bytes accessed | tf_op | source)
XLA Modules:
  0.0 408.8 jit_solution(4185749751115716503)
XLA Ops:
  8.0 3.1 collective-permute-start
  11.1 5.4 %concatenate.16 = bf16[704]{0:T(1024)(128)(2,1)S(1)} concatenate(bf16[64]{0:T(256)(128)(2,1)} %param.22, bf16[64]{0:T(256)(128)(2,1)} %param.23, bf16[64]{0:T(256)(128)(2,1)} %param.25, bf16[64]{0:T(256)(128)(2,1)} %param.27, bf16[64]{0:T(256)(128)(2,1)} %param.29, bf16[64]{0:T(256)(128)(2,1)} %param.31, bf16[64]{0:T(256)(128)(2,1)} %param.35, bf16[256]{0:T(256)(128)(2,1)} %param.33), dimensions={0} | concatenate | bytes 2816 | tf_op jit(solution)/shard_map/concatenate | solution.py:981
  17.1 2.2 pack.5
  19.3 3.6 pack.3
  22.9 2.2 pack.4
  25.1 2.2 collective-permute-done.refs_4_
  30.2 6.8 %all-to-all-start = ((bf16[8,272,512]{2,1,0:T(8,128)(2,1)}), bf16[8,272,512]{2,1,0:T(8,128)(2,1)S(1)}, u32[]{:S(2)}, u32[]{:S(2)}) async-start(bf16[8,272,512]{2,1,0:T(8,128)(2,1)} %bitcast.109), calls=%async_computation | async-start | bytes 4456448 | tf_op jit(solution)/shard_map/all_to_all | solution.py:692
  39.0 29.4 %collective-permute-done.1.refs_2_ = bf16[2,256,512]{2,1,0:T(8,128)(2,1)S(1)} collective-permute-done((bf16[2,256,512]{2,1,0:T(8,128)(2,1)S(1)}, bf16[2,256,512]{2,1,0:T(8,128)(2,1)S(1)}, u32[]{:S(2)}, u32[]{:S(2)}) %collective-permute-start.1) | collective-permute-done | bytes 524320 | tf_op jit(solution)/shard_map/ppermute | solution.py:48
  68.4 24.5 %all-to-all-done.refs_0_.refs_5_.refs_7_ = bf16[8,272,512]{2,1,0:T(8,128)(2,1)S(1)} async-done(((bf16[8,272,512]{2,1,0:T(8,128)(2,1)}), bf16[8,272,512]{2,1,0:T(8,128)(2,1)S(1)}, u32[]{:S(2)}, u32[]{:S(2)}) %all-to-all-start) | async-done | bytes 2228256 | tf_op jit(solution)/shard_map/all_to_all | solution.py:692
  94.3 2.4 spread.2
  96.7 4.6 %all-to-all-start.1 = ((bf16[4,512,512]{2,1,0:T(8,128)(2,1)}), bf16[4,512,512]{2,1,0:T(8,128)(2,1)S(1)}, u32[]{:S(2)}, u32[]{:S(2)}) async-start(bf16[4,512,512]{2,1,0:T(8,128)(2,1)} %bitcast.117), calls=%async_computation.1 | async-start | bytes 4194304 | tf_op jit(solution)/shard_map/all_to_all | solution.py:754
  101.2 3.4 collective-permute-start.6
  109.1 3.0 collective-permute-done.5
  114.6 14.3 %norm_up.1 = (bf16[2048,2048]{1,0:T(8,128)(2,1)}, f32[2048,128]{1,0:T(8,128)}, bf16[2048,512]{1,0:T(8,128)(2,1)}, f32[2048,512]{1,0:T(8,128)}) custom-call(bf16[2,2,256,512]{3,2,1,0:T(8,128)(2,1)} %copy-done.8, bf16[4,4,512,512]{3,2,1,0:T(8,128)(2,1)} %bitcast.116, f32[1,2048]{1,0:T(1,128)} %reshape.248.refs_2_, f32[1,2048]{1,0:T(1,128)} %reshape.249.refs_3_, ...), custom_call_target="tpu_custom_call" | custom-call | flops 12884901 | tf_op jit(solution)/shard_map/norm_up/pallas_call | solution.py:74
  128.9 2.5 spread.3
  131.4 14.2 %all-to-all-done.1 = bf16[4,512,512]{2,1,0:T(8,128)(2,1)S(1)} async-done(((bf16[4,512,512]{2,1,0:T(8,128)(2,1)}), bf16[4,512,512]{2,1,0:T(8,128)(2,1)S(1)}, u32[]{:S(2)}, u32[]{:S(2)}) %all-to-all-start.1) | async-done | bytes 2097184 | tf_op jit(solution)/shard_map/all_to_all | solution.py:754
  145.6 4.4 %all-to-all-start.2 = ((bf16[4,512,512]{2,1,0:T(8,128)(2,1)}), bf16[4,512,512]{2,1,0:T(8,128)(2,1)}, u32[]{:S(2)}, u32[]{:S(2)}) async-start(bf16[4,512,512]{2,1,0:T(8,128)(2,1)} %bitcast.118), calls=%async_computation.2 | async-start | bytes 4194304 | tf_op jit(solution)/shard_map/all_to_all | solution.py:754
  153.9 9.4 %project_heads.1.refs_0_.refs_1_ = bf16[2048,384]{1,0:T(8,128)(2,1)} custom-call(bf16[2,2,256,512]{3,2,1,0:T(8,128)(2,1)} %copy-done.2, bf16[2048,2048]{1,0:T(8,128)(2,1)} %get-tuple-element.70.refs_1_.refs_0_.refs_2_.refs_3_, f32[1,384]{1,0:T(1,128)} %reshape.250.refs_2_, f32[2048,128]{1,0:T(8,128)} %constant.83.clone.refs_3_.refs_4_, ...), custom_call_target="tpu_custom_call" | custom-call | flops 6442450 | tf_op jit(solution)/shard_map/project_heads/pallas_call | solution.py:74
  163.3 14.3 %attention.1 = (bf16[2048,128]{1,0:T(8,128)(2,1)}, f32[8,2048]{1,0:T(8,128)}) custom-call(bf16[2048,384]{1,0:T(8,128)(2,1)} %project_heads.1.refs_0_.refs_1_), custom_call_target="tpu_custom_call" | custom-call | flops 10000000 | tf_op jit(solution)/shard_map/attention/pallas_call | solution.py:74
  177.6 8.8 %weight_grad.3.refs_0_ = bf16[8,512,256]{2,1,0:T(8,128)(2,1)} custom-call(bf16[2048,128]{1,0:T(8,128)(2,1)} %get-tuple-element.71.refs_0_.refs_2_.refs_4_, bf16[2048,512]{1,0:T(8,128)(2,1)} %get-tuple-element.72.refs_1_.refs_3_, bf16[2,4,2,512,512]{4,3,2,1,0:T(8,128)(2,1)} %bitcast.98), custom_call_target="tpu_custom_call" | custom-call | flops 8589934 | tf_op jit(solution)/shard_map/weight_grad/pallas_call | solution.py:74
  186.4 6.3 %attended_gradient.1.refs_0_.refs_2_ = bf16[2048,128]{1,0:T(8,128)(2,1)} custom-call(bf16[8,512,256]{2,1,0:T(8,128)(2,1)} %weight_grad.3.refs_0_, bf16[2,4,2,512,512]{4,3,2,1,0:T(8,128)(2,1)} %bitcast.99, bf16[8,256,512]{2,1,0:T(8,128)(2,1)} %bitcast.104), custom_call_target="tpu_custom_call" | custom-call | flops 4294967 | tf_op jit(solution)/shard_map/attended_gradient/pallas_call | solution.py:74
  192.7 5.2 %all-to-all-done.2 = bf16[4,512,512]{2,1,0:T(8,128)(2,1)} async-done(((bf16[4,512,512]{2,1,0:T(8,128)(2,1)}), bf16[4,512,512]{2,1,0:T(8,128)(2,1)}, u32[]{:S(2)}, u32[]{:S(2)}) %all-to-all-start.2) | async-done | bytes 2097184 | tf_op jit(solution)/shard_map/all_to_all | solution.py:754
  197.9 5.2 %all-to-all-start.3 = ((bf16[8,512,256]{2,1,0:T(8,128)(2,1)}), bf16[8,512,256]{2,1,0:T(8,128)(2,1)}, u32[]{:S(2)}, u32[]{:S(2)}) async-start(bf16[8,512,256]{2,1,0:T(8,128)(2,1)} %weight_grad.3.refs_0_), calls=%async_computation.3 | async-start | bytes 4194304 | tf_op jit(solution)/shard_map/all_to_all | solution.py:772
  203.1 9.4 %up_gradient.1 = (bf16[2048,512]{1,0:T(8,128)(2,1)}, f32[1,512]{1,0:T(1,128)}) custom-call(bf16[2048,128]{1,0:T(8,128)(2,1)} %attended_gradient.1.refs_0_.refs_2_, bf16[2,4,2,512,512]{4,3,2,1,0:T(8,128)(2,1)} %bitcast.100, f32[2048,512]{1,0:T(8,128)} %get-tuple-element.74.refs_2_, bf16[8,256,512]{2,1,0:T(8,128)(2,1)} %bitcast.21.refs_3_.refs_7_), custom_call_target="tpu_custom_call" | custom-call | flops 8589934 | tf_op jit(solution)/shard_map/up_gradient/pallas_call | solution.py:74
  212.5 25.2 %attention_back.1 = (bf16[2048,384]{1,0:T(8,128)(2,1)}, f32[1,384]{1,0:T(1,128)}) custom-call(bf16[2048,512]{1,0:T(8,128)(2,1)} %get-tuple-element.76.refs_0_.refs_1_.refs_3_, bf16[2048,384]{1,0:T(8,128)(2,1)} %project_heads.1.refs_0_.refs_1_, bf16[2048,128]{1,0:T(8,128)(2,1)} %attended_gradient.1.refs_0_.refs_2_, f32[8,2048]{1,0:T(8,128)} %get-tuple-element.77.refs_3_, ...), custom_call_target="tpu_custom_call" | custom-call | flops 20000000 | tf_op jit(solution)/shard_map/attention_back/pallas_call | solution.py:74
  238.2 8.8 %weight_grad.4.refs_0_ = bf16[8,512,256]{2,1,0:T(8,128)(2,1)} custom-call(bf16[2048,384]{1,0:T(8,128)(2,1)} %get-tuple-element.78.refs_0_.refs_2_, bf16[2048,512]{1,0:T(8,128)(2,1)} %get-tuple-element.76.refs_0_.refs_1_.refs_3_, bf16[2048,2048]{1,0:T(8,128)(2,1)} %get-tuple-element.70.refs_1_.refs_0_.refs_2_.refs_3_), custom_call_target="tpu_custom_call" | custom-call | flops 8589934 | tf_op jit(solution)/shard_map/weight_grad/pallas_call | solution.py:74
  247.0 3.0 all-to-all-done.3
  250.0 4.4 %all-to-all-start.4 = ((bf16[8,512,256]{2,1,0:T(8,128)(2,1)}), bf16[8,512,256]{2,1,0:T(8,128)(2,1)}, u32[]{:S(2)}, u32[]{:S(2)}) async-start(bf16[8,512,256]{2,1,0:T(8,128)(2,1)} %weight_grad.4.refs_0_), calls=%async_computation.4 | async-start | bytes 4194304 | tf_op jit(solution)/shard_map/all_to_all | solution.py:772
  255.0 15.0 %normed_gradient.1 = (bf16[4,256,512]{2,1,0:T(8,128)(2,1)}, bf16[4,256,512]{2,1,0:T(8,128)(2,1)}, bf16[2,2,256,512]{3,2,1,0:T(8,128)(2,1)}, bf16[2,2,256,512]{3,2,1,0:T(8,128)(2,1)}) custom-call(bf16[8,512,256]{2,1,0:T(8,128)(2,1)} %weight_grad.4.refs_0_, s32[3]{0:T(128)} %pad_add_fusion.refs_1_, bf16[2048,384]{1,0:T(8,128)(2,1)} %get-tuple-element.78.refs_0_.refs_2_, ...), custom_call_target="tpu_custom_call" | custom-call | flops 15032385 | tf_op jit(solution)/shard_map/normed_gradient/pallas_call | solution.py:74
  277.4 10.9 %branch_sum.1 = (bf16[4,256,512]{2,1,0:T(8,128)(2,1)}, bf16[4,256,512]{2,1,0:T(8,128)(2,1)}, bf16[4,256,512]{2,1,0:T(8,128)(2,1)}, bf16[4,256,512]{2,1,0:T(8,128)(2,1)}) custom-call(bf16[4,256,512]{2,1,0:T(8,128)(2,1)} %get-tuple-element.80.refs_0_, s32[3]{0:T(128)} %pad_add_fusion.refs_1_, bf16[2048,128]{1,0:T(8,128)(2,1)} %get-tuple-element.71.refs_0_.refs_2_.refs_4_, ...), custom_call_target="tpu_custom_call" | custom-call | flops 10737418 | tf_op jit(solution)/shard_map/branch_sum/pallas_call | solution.py:74
  290.7 10.3 %weight_grad.5.refs_0_ = bf16[8,528,256]{2,1,0:T(8,128)(2,1)} custom-call(bf16[4,256,512]{2,1,0:T(8,128)(2,1)} %get-tuple-element.82.refs_0_, bf16[8,16,256]{2,1,0:T(8,128)(2,1)} %bitcast.139, bf16[2048,384]{1,0:T(8,128)(2,1)} %get-tuple-element.78.refs_0_.refs_2_, bf16[2048,2048]{1,0:T(8,128)(2,1)} %get-tuple-element.70.refs_1_.refs_0_.refs_2_.refs_3_, ...), custom_call_target="tpu_custom_call" | custom-call | flops 8858370 | tf_op jit(solution)/shard_map/weight_grad/pallas_call | solution.py:74
  301.7 3.8 all-to-all-start.5
  305.5 2.5 fold.8
  309.6 3.8 unpack.3.refs_0_
  313.4 2.5 fold.9
  317.5 3.3 collective-permute-done.14
  320.8 2.6 fold.10
  328.0 3.5 collective-permute-done.17
  337.6 4.2 %unpack.4 = f32[256,2048]{1,0:T(8,128)} custom-call(bf16[1,256,512]{2,1,0:T(8,128)(2,1)} %get-tuple-element.97.refs_0_, bf16[2,4,512,256]{3,2,1,0:T(8,128)(2,1)} %bitcast.36.refs_1_), custom_call_target="tpu_custom_call" | custom-call | tf_op jit(solution)/shard_map/unpack/pallas_call | solution.py:74
  341.8 5.6 %collective-permute-done.16 = bf16[256,512]{1,0:T(8,128)(2,1)S(1)} collective-permute-done((bf16[256,512]{1,0:T(8,128)(2,1)}, bf16[256,512]{1,0:T(8,128)(2,1)S(1)}, u32[]{:S(2)}, u32[]{:S(2)}) %collective-permute-start.16) | collective-permute-done | bytes 262176 | tf_op jit(solution)/shard_map/ppermute | solution.py:48
  347.4 4.5 %collective-permute-done.18 = bf16[256,512]{1,0:T(8,128)(2,1)} collective-permute-done((bf16[256,512]{1,0:T(8,128)(2,1)}, bf16[256,512]{1,0:T(8,128)(2,1)}, u32[]{:S(2)}, u32[]{:S(2)}) %collective-permute-start.18) | collective-permute-done | bytes 262176 | tf_op jit(solution)/shard_map/ppermute | solution.py:48
  359.3 2.5 collective-permute-start.28
  365.1 2.5 collective-permute-start.29
  367.6 2.9 multiply_add_fusion
  370.4 2.4 fold.13
  375.8 2.5 side_sums.1
  394.3 4.0 unpack.5
  399.1 2.4 finish.1
  (191 shorter events, 74.7 us)
Async XLA Ops:
  7.2 106.4 %all-gather.5.cloned.1.call-start = ((), (), s32[]{:S(2)}) async-start(), calls=%async_computation.6 | async-start | bytes 8912896 | tf_op jit(solution)/shard_map/all_gather | solution.py:984
  7.9 169.7 %all-gather.7.cloned.1.call-start = ((), (), s32[]{:S(2)}) async-start(), calls=%async_computation.7 | async-start | bytes 9437184 | tf_op jit(solution)/shard_map/all_gather | solution.py:994
  8.0 19.3 %collective-permute-start = (bf16[512,512]{1,0:T(8,128)(2,1)}, bf16[512,512]{1,0:T(8,128)(2,1)S(1)}, u32[]{:S(2)}, u32[]{:S(2)}) collective-permute-start(bf16[512,512]{1,0:T(8,128)(2,1)} %refs_3_.4), channel_id=1, source_target_pairs={{0,8},{8,0},{1,9},{9,1},{2,10},{10,2},{3,11},{11,3},{4,12},{12,4},... | collective-permute-start | bytes 1572872 | tf_op jit(solution)/shard_map/ppermute | solution.py:48
  30.2 62.7 %all-to-all-start = ((bf16[8,272,512]{2,1,0:T(8,128)(2,1)}), bf16[8,272,512]{2,1,0:T(8,128)(2,1)S(1)}, u32[]{:S(2)}, u32[]{:S(2)}) async-start(bf16[8,272,512]{2,1,0:T(8,128)(2,1)} %bitcast.109), calls=%async_computation | async-start | bytes 4456448 | tf_op jit(solution)/shard_map/all_to_all | solution.py:692
  37.0 31.4 %collective-permute-start.1 = (bf16[2,256,512]{2,1,0:T(8,128)(2,1)S(1)}, bf16[2,256,512]{2,1,0:T(8,128)(2,1)S(1)}, u32[]{:S(2)}, u32[]{:S(2)}) collective-permute-start(bf16[2,256,512]{2,1,0:T(8,128)(2,1)S(1)} %copy-done.26), channel_id=1, source_target_pairs={{0,4},{4,0},{1,5},{5,1},{2,6},{6,2},{3,7},{7,3},{8,12},{12,8},{9,1... | collective-permute-start | bytes 1572872 | tf_op jit(solution)/shard_map/ppermute | solution.py:48
  68.4 24.5 %copy-start.19 = (bf16[2,256,512]{2,1,0:T(8,128)(2,1)}, bf16[2,256,512]{2,1,0:T(8,128)(2,1)S(1)}, u32[]{:S(2)}) copy-start(bf16[2,256,512]{2,1,0:T(8,128)(2,1)S(1)} %collective-permute-done.1.refs_2_) | copy-start | bytes 1572868
  96.7 48.9 %all-to-all-start.1 = ((bf16[4,512,512]{2,1,0:T(8,128)(2,1)}), bf16[4,512,512]{2,1,0:T(8,128)(2,1)S(1)}, u32[]{:S(2)}, u32[]{:S(2)}) async-start(bf16[4,512,512]{2,1,0:T(8,128)(2,1)} %bitcast.117), calls=%async_computation.1 | async-start | bytes 4194304 | tf_op jit(solution)/shard_map/all_to_all | solution.py:754
  101.2 27.6 %collective-permute-start.6 = (bf16[2,256,512]{2,1,0:T(8,128)(2,1)}, bf16[2,256,512]{2,1,0:T(8,128)(2,1)}, u32[]{:S(2)}, u32[]{:S(2)}) collective-permute-start(bf16[2,256,512]{2,1,0:T(8,128)(2,1)} %get-tuple-element.75), channel_id=1, source_target_pairs={{0,4},{4,0},{1,5},{5,1},{2,6},{6,2},{3,7},{7,3},{8,12},{12,8},{9,1... | collective-permute-start | bytes 1572872 | tf_op jit(solution)/shard_map/ppermute | solution.py:48
  105.6 44.6 %copy-start.22 = (bf16[1,8,16,512]{3,1,2,0:T(8,128)(2,1)}, bf16[1,8,16,512]{3,1,2,0:T(8,128)(2,1)S(1)}, u32[]{:S(2)}) copy-start(bf16[1,8,16,512]{3,1,2,0:T(8,128)(2,1)S(1)} %copy.46) | copy-start | bytes 393220
  105.7 2.8 collective-permute-start.4
  108.3 5.3 %collective-permute-start.3 = (bf16[2,2,256,512]{3,2,1,0:T(8,128)(2,1)}, bf16[2,2,256,512]{3,2,1,0:T(8,128)(2,1)S(1)}, u32[]{:S(2)}, u32[]{:S(2)}) collective-permute-start(bf16[2,2,256,512]{3,2,1,0:T(8,128)(2,1)} %dynamic-slice_bitcast_fusion.1), channel_id=1, source_target_pairs={{0,1},{1,0},{2,3},{3,2},{4,5},{5,4},{6,7},{7,6},{8,9},{9,8},{10,11... | collective-permute-start | bytes 3145736 | tf_op jit(solution)/shard_map/ppermute | solution.py:48
  108.4 3.7 collective-permute-start.5
  145.6 52.2 %all-to-all-start.2 = ((bf16[4,512,512]{2,1,0:T(8,128)(2,1)}), bf16[4,512,512]{2,1,0:T(8,128)(2,1)}, u32[]{:S(2)}, u32[]{:S(2)}) async-start(bf16[4,512,512]{2,1,0:T(8,128)(2,1)} %bitcast.118), calls=%async_computation.2 | async-start | bytes 4194304 | tf_op jit(solution)/shard_map/all_to_all | solution.py:754
  150.2 2.7 collective-permute-start.2
  197.9 52.1 %all-to-all-start.3 = ((bf16[8,512,256]{2,1,0:T(8,128)(2,1)}), bf16[8,512,256]{2,1,0:T(8,128)(2,1)}, u32[]{:S(2)}, u32[]{:S(2)}) async-start(bf16[8,512,256]{2,1,0:T(8,128)(2,1)} %weight_grad.3.refs_0_), calls=%async_computation.3 | async-start | bytes 4194304 | tf_op jit(solution)/shard_map/all_to_all | solution.py:772
  212.5 34.5 %collective-permute-start.8 = (bf16[2048,512]{1,0:T(8,128)(2,1)}, bf16[2048,512]{1,0:T(8,128)(2,1)}, u32[]{:S(2)}, u32[]{:S(2)}) collective-permute-start(bf16[2048,512]{1,0:T(8,128)(2,1)} %get-tuple-element.76.refs_0_.refs_1_.refs_3_), channel_id=1, source_target_pairs={{0,1},{1,0},{2,3},{3,2},{4,5},{5,4},{6,7},{7,6},{8,9},{9,8},{10,11... | collective-permute-start | bytes 6291464 | tf_op jit(solution)/shard_map/ppermute | solution.py:48
  237.7 9.3 %collective-permute-start.7 = (bf16[2048,384]{1,0:T(8,128)(2,1)}, bf16[2048,384]{1,0:T(8,128)(2,1)}, u32[]{:S(2)}, u32[]{:S(2)}) collective-permute-start(bf16[2048,384]{1,0:T(8,128)(2,1)} %get-tuple-element.78.refs_0_.refs_2_), channel_id=1, source_target_pairs={{0,1},{1,0},{2,3},{3,2},{4,5},{5,4},{6,7},{7,6},{8,9},{9,8},{10,11... | collective-permute-start | bytes 4718600 | tf_op jit(solution)/shard_map/ppermute | solution.py:48
  247.0 7.4 %copy-start.4 = (bf16[2048,512]{1,0:T(8,128)(2,1)S(1)}, bf16[2048,512]{1,0:T(8,128)(2,1)}, u32[]{:S(2)}) copy-start(bf16[2048,512]{1,0:T(8,128)(2,1)} %get-tuple-element.72.refs_1_.refs_3_) | copy-start | bytes 6291460
  250.0 51.7 %all-to-all-start.4 = ((bf16[8,512,256]{2,1,0:T(8,128)(2,1)}), bf16[8,512,256]{2,1,0:T(8,128)(2,1)}, u32[]{:S(2)}, u32[]{:S(2)}) async-start(bf16[8,512,256]{2,1,0:T(8,128)(2,1)} %weight_grad.4.refs_0_), calls=%async_computation.4 | async-start | bytes 4194304 | tf_op jit(solution)/shard_map/all_to_all | solution.py:772
  254.3 20.6 %collective-permute-start.10 = (bf16[2048,512]{1,0:T(8,128)(2,1)S(1)}, bf16[2048,512]{1,0:T(8,128)(2,1)S(1)}, u32[]{:S(2)}, u32[]{:S(2)}) collective-permute-start(bf16[2048,512]{1,0:T(8,128)(2,1)S(1)} %copy-done.4), channel_id=1, source_target_pairs={{0,1},{1,0},{2,3},{3,2},{4,5},{5,4},{6,7},{7,6},{8,9},{9,8},{10,11... | collective-permute-start | bytes 6291464 | tf_op jit(solution)/shard_map/ppermute | solution.py:48
  271.4 3.6 collective-permute-start.11
  271.9 3.0 collective-permute-start.9
  272.0 33.5 %collective-permute-start.12 = (bf16[4,256,512]{2,1,0:T(8,128)(2,1)}, bf16[4,256,512]{2,1,0:T(8,128)(2,1)}, u32[]{:S(2)}, u32[]{:S(2)}) collective-permute-start(bf16[4,256,512]{2,1,0:T(8,128)(2,1)} %get-tuple-element.85), channel_id=1, source_target_pairs={{0,2},{2,0},{1,3},{3,1},{4,6},{6,4},{5,7},{7,5},{8,10},{10,8},{9,1... | collective-permute-start | bytes 3145736 | tf_op jit(solution)/shard_map/ppermute | solution.py:48
  272.3 16.9 %copy-start.7 = (bf16[512,512]{1,0:T(8,128)(2,1)S(1)}, bf16[512,512]{1,0:T(8,128)(2,1)}, u32[]{:S(2)}) copy-start(bf16[512,512]{1,0:T(8,128)(2,1)} %refs_3_.4) | copy-start | bytes 1572868
  272.4 17.1 %copy-start.23 = (f32[1,512]{1,0:T(1,128)S(1)}, f32[1,512]{1,0:T(1,128)}, u32[]{:S(2)}) copy-start(f32[1,512]{1,0:T(1,128)} %get-tuple-element.84) | copy-start | bytes 6148
  272.4 17.2 %copy-start.24 = (f32[1,384]{1,0:T(1,128)S(1)}, f32[1,384]{1,0:T(1,128)}, u32[]{:S(2)}) copy-start(f32[1,384]{1,0:T(1,128)} %get-tuple-element.83) | copy-start | bytes 4612
  272.4 41.0 %collective-permute-start.13 = (bf16[2,2,256,512]{3,2,1,0:T(8,128)(2,1)}, bf16[2,2,256,512]{3,2,1,0:T(8,128)(2,1)}, u32[]{:S(2)}, u32[]{:S(2)}) collective-permute-start(bf16[2,2,256,512]{3,2,1,0:T(8,128)(2,1)} %get-tuple-element.89), channel_id=1, source_target_pairs={{0,4},{4,0},{1,5},{5,1},{2,6},{6,2},{3,7},{7,3},{8,12},{12,8},{9,1... | collective-permute-start | bytes 3145736 | tf_op jit(solution)/shard_map/ppermute | solution.py:48
  288.3 32.5 %collective-permute-start.14 = (bf16[4,256,512]{2,1,0:T(8,128)(2,1)}, bf16[4,256,512]{2,1,0:T(8,128)(2,1)}, u32[]{:S(2)}, u32[]{:S(2)}) collective-permute-start(bf16[4,256,512]{2,1,0:T(8,128)(2,1)} %get-tuple-element.91), channel_id=1, source_target_pairs={{0,2},{2,0},{1,3},{3,1},{4,6},{6,4},{5,7},{7,5},{8,10},{10,8},{9,1... | collective-permute-start | bytes 3145736 | tf_op jit(solution)/shard_map/ppermute | solution.py:48
  301.7 72.8 %all-to-all-start.5 = ((bf16[4,1056,256]{2,1,0:T(8,128)(2,1)}), bf16[4,1056,256]{2,1,0:T(8,128)(2,1)S(1)}, u32[]{:S(2)}, u32[]{:S(2)}) async-start(bf16[4,1056,256]{2,1,0:T(8,128)(2,1)} %bitcast.110), calls=%async_computation.5 | async-start | bytes 4325376 | tf_op jit(solution)/shard_map/all_to_all | solution.py:825
  308.1 15.3 %collective-permute-start.15 = (bf16[2,256,512]{2,1,0:T(8,128)(2,1)}, bf16[2,256,512]{2,1,0:T(8,128)(2,1)S(1)}, u32[]{:S(2)}, u32[]{:S(2)}) collective-permute-start(bf16[2,256,512]{2,1,0:T(8,128)(2,1)} %get-tuple-element.93), channel_id=1, source_target_pairs={{0,4},{4,0},{1,5},{5,1},{2,6},{6,2},{3,7},{7,3},{8,12},{12,8},{9,1... | collective-permute-start | bytes 1572872 | tf_op jit(solution)/shard_map/ppermute | solution.py:48
  315.9 15.5 %collective-permute-start.17 = (bf16[2,256,512]{2,1,0:T(8,128)(2,1)}, bf16[2,256,512]{2,1,0:T(8,128)(2,1)S(1)}, u32[]{:S(2)}, u32[]{:S(2)}) collective-permute-start(bf16[2,256,512]{2,1,0:T(8,128)(2,1)} %get-tuple-element.96), channel_id=1, source_target_pairs={{0,2},{2,0},{1,3},{3,1},{4,6},{6,4},{5,7},{7,5},{8,10},{10,8},{9,1... | collective-permute-start | bytes 1572872 | tf_op jit(solution)/shard_map/ppermute | solution.py:48
  326.2 21.2 %collective-permute-start.16 = (bf16[256,512]{1,0:T(8,128)(2,1)}, bf16[256,512]{1,0:T(8,128)(2,1)S(1)}, u32[]{:S(2)}, u32[]{:S(2)}) collective-permute-start(bf16[256,512]{1,0:T(8,128)(2,1)} %bitcast.164), channel_id=1, source_target_pairs={{0,8},{8,0},{1,9},{9,1},{2,10},{10,2},{3,11},{11,3},{4,12},{12,4},... | collective-permute-start | bytes 786440 | tf_op jit(solution)/shard_map/ppermute | solution.py:48
  334.3 17.6 %collective-permute-start.18 = (bf16[256,512]{1,0:T(8,128)(2,1)}, bf16[256,512]{1,0:T(8,128)(2,1)}, u32[]{:S(2)}, u32[]{:S(2)}) collective-permute-start(bf16[256,512]{1,0:T(8,128)(2,1)} %bitcast.166), channel_id=1, source_target_pairs={{0,8},{8,0},{1,9},{9,1},{2,10},{10,2},{3,11},{11,3},{4,12},{12,4},... | collective-permute-start | bytes 786440 | tf_op jit(solution)/shard_map/ppermute | solution.py:48
  337.2 33.2 %collective-permute-start.19 = (bf16[4,256,512]{2,1,0:T(8,128)(2,1)}, bf16[4,256,512]{2,1,0:T(8,128)(2,1)}, u32[]{:S(2)}, u32[]{:S(2)}) collective-permute-start(bf16[4,256,512]{2,1,0:T(8,128)(2,1)} %get-tuple-element.103), channel_id=1, source_target_pairs={{0,2},{2,0},{1,3},{3,1},{4,6},{6,4},{5,7},{7,5},{8,10},{10,8},{9,1... | collective-permute-start | bytes 3145736 | tf_op jit(solution)/shard_map/ppermute | solution.py:48
  337.6 14.3 %copy-start.14 = (bf16[1,256,512]{2,1,0:T(8,128)(2,1)S(1)}, bf16[1,256,512]{2,1,0:T(8,128)(2,1)}, u32[]{:S(2)}) copy-start(bf16[1,256,512]{2,1,0:T(8,128)(2,1)} %get-tuple-element.94.refs_0_) | copy-start | bytes 786436
  337.6 14.4 %copy-start.15 = (bf16[1,256,512]{2,1,0:T(8,128)(2,1)S(1)}, bf16[1,256,512]{2,1,0:T(8,128)(2,1)}, u32[]{:S(2)}) copy-start(bf16[1,256,512]{2,1,0:T(8,128)(2,1)} %get-tuple-element.97.refs_0_) | copy-start | bytes 786436
  341.8 12.1 %copy-start.5 = (bf16[512,512]{1,0:T(8,128)(2,1)S(1)}, bf16[512,512]{1,0:T(8,128)(2,1)}, u32[]{:S(2)}) copy-start(bf16[512,512]{1,0:T(8,128)(2,1)} %refs_1_.7) | copy-start | bytes 1572868
  355.6 3.6 collective-permute-start.27
  357.1 4.7 %collective-permute-start.25 = (f32[2,512]{1,0:T(2,128)S(1)}, f32[2,512]{1,0:T(2,128)S(1)}, u32[]{:S(2)}, u32[]{:S(2)}) collective-permute-start(f32[2,512]{1,0:T(2,128)S(1)} %pad_maximum_fusion.3), channel_id=1, source_target_pairs={{0,1},{1,0},{2,3},{3,2},{4,5},{5,4},{6,7},{7,6},{8,9},{9,8},{10,11... | collective-permute-start | bytes 12296 | tf_op jit(solution)/shard_map/ppermute | solution.py:48
  359.3 5.7 %collective-permute-start.28 = (f32[8,128]{1,0:T(8,128)S(1)}, f32[8,128]{1,0:T(8,128)S(1)}, u32[]{:S(2)}, u32[]{:S(2)}) collective-permute-start(f32[8,128]{1,0:T(8,128)S(1)} %fusion.10), channel_id=1, source_target_pairs={{0,8},{8,0},{1,9},{9,1},{2,10},{10,2},{3,11},{11,3},{4,12},{12,4},... | collective-permute-start | bytes 12296 | tf_op jit(solution)/shard_map/ppermute | solution.py:48
  361.8 5.7 %collective-permute-start.26 = (f32[2,512]{1,0:T(2,128)S(1)}, f32[2,512]{1,0:T(2,128)S(1)}, u32[]{:S(2)}, u32[]{:S(2)}) collective-permute-start(f32[2,512]{1,0:T(2,128)S(1)} %fusion.3), channel_id=1, source_target_pairs={{0,2},{2,0},{1,3},{3,1},{4,6},{6,4},{5,7},{7,5},{8,10},{10,8},{9,1... | collective-permute-start | bytes 12296 | tf_op jit(solution)/shard_map/ppermute | solution.py:48
  363.6 17.2 %collective-permute-start.20 = (bf16[2,256,512]{2,1,0:T(8,128)(2,1)}, bf16[2,256,512]{2,1,0:T(8,128)(2,1)}, u32[]{:S(2)}, u32[]{:S(2)}) collective-permute-start(bf16[2,256,512]{2,1,0:T(8,128)(2,1)} %get-tuple-element.105), channel_id=1, source_target_pairs={{0,4},{4,0},{1,5},{5,1},{2,6},{6,2},{3,7},{7,3},{8,12},{12,8},{9,1... | collective-permute-start | bytes 1572872 | tf_op jit(solution)/shard_map/ppermute | solution.py:48
  365.1 18.5 %collective-permute-start.29 = (f32[8,128]{1,0:T(8,128)S(1)}, f32[8,128]{1,0:T(8,128)S(1)}, u32[]{:S(2)}, u32[]{:S(2)}) collective-permute-start(f32[8,128]{1,0:T(8,128)S(1)} %add.89), channel_id=1, source_target_pairs={{0,16},{16,0},{1,17},{17,1},{2,18},{18,2},{3,19},{19,3},{4,20},{20... | collective-permute-start | bytes 12296 | tf_op jit(solution)/shard_map/ppermute | solution.py:48
  372.8 13.1 %collective-permute-start.21 = (bf16[2,256,512]{2,1,0:T(8,128)(2,1)}, bf16[2,256,512]{2,1,0:T(8,128)(2,1)S(1)}, u32[]{:S(2)}, u32[]{:S(2)}) collective-permute-start(bf16[2,256,512]{2,1,0:T(8,128)(2,1)} %bitcast.162), channel_id=1, source_target_pairs={{0,8},{8,0},{1,9},{9,1},{2,10},{10,2},{3,11},{11,3},{4,12},{12,4},... | collective-permute-start | bytes 1572872 | tf_op jit(solution)/shard_map/ppermute | solution.py:48
  378.3 14.0 %collective-permute-start.22 = (bf16[2,528,256]{2,1,0:T(8,128)(2,1)}, bf16[2,528,256]{2,1,0:T(8,128)(2,1)S(1)}, u32[]{:S(2)}, u32[]{:S(2)}) collective-permute-start(bf16[2,528,256]{2,1,0:T(8,128)(2,1)} %get-tuple-element.110), channel_id=1, source_target_pairs={{0,4},{4,0},{1,5},{5,1},{2,6},{6,2},{3,7},{7,3},{8,12},{12,8},{9,1... | collective-permute-start | bytes 1622024 | tf_op jit(solution)/shard_map/ppermute | solution.py:48
  382.8 15.5 %collective-permute-start.23 = (bf16[256,512]{1,0:T(8,128)(2,1)}, bf16[256,512]{1,0:T(8,128)(2,1)S(1)}, u32[]{:S(2)}, u32[]{:S(2)}) collective-permute-start(bf16[256,512]{1,0:T(8,128)(2,1)} %bitcast.163), channel_id=1, source_target_pairs={{0,8},{8,0},{1,9},{9,1},{2,10},{10,2},{3,11},{11,3},{4,12},{12,4},... | collective-permute-start | bytes 786440 | tf_op jit(solution)/shard_map/ppermute | solution.py:48
  388.8 9.5 %collective-permute-start.24 = (bf16[256,512]{1,0:T(8,128)(2,1)}, bf16[256,512]{1,0:T(8,128)(2,1)S(1)}, u32[]{:S(2)}, u32[]{:S(2)}) collective-permute-start(bf16[256,512]{1,0:T(8,128)(2,1)} %bitcast.165), channel_id=1, source_target_pairs={{0,4},{4,0},{1,5},{5,1},{2,6},{6,2},{3,7},{7,3},{8,12},{12,8},{9,1... | collective-permute-start | bytes 786440 | tf_op jit(solution)/shard_map/ppermute | solution.py:48
  394.3 7.2 %copy-start.25 = (f32[64]{0:T(128)}, f32[64]{0:T(128)S(1)}, u32[]{:S(2)}) copy-start(f32[64]{0:T(128)S(1)} %get-tuple-element.183) | copy-start | bytes 772
  (18 other events, 29.2 us)
Sparse Core Ops, SparseCore 0:
  9.6 90.3 all-gather.4
  101.9 54.8 all-gather.6
